TPU v7x, 512 devices: a whole 4x8x8 slice. The times are simulated.
512 devices in a mesh: gx: 16 (over y, z_lo), gy: 4 (over z_hi), gz: 8 (over x, core).
Axes of the slice: x: 4, y: 8, z: 8 (z_hi: 4, z_lo: 2; z = z_hi * 2 + z_lo), core: 2. Of those that a mesh axis runs over, the one named last changes fastest.
Arguments:
- stiffness: float32 [128, 384, 512], P('gz', 'gx', 'gy'), may hold values from 0.03 to 0.1
- older_wave: float32 [128, 384, 512], P('gz', 'gx', 'gy'), may hold values from -4 to 4
- wave_now: float32 [128, 384, 512], P('gz', 'gx', 'gy'), may hold values from -5.2 to 5.2
- forward_wave: bfloat16 [4, 128, 384, 512], P(None, 'gz', 'gx', 'gy'), may hold values from -6 to 6
- residuals: float32 [4, 65536], P(None, ('gx', 'gy', 'gz')), may hold values from -6 to 6
- owners: int32 [65536, 1], P(('gx', 'gy', 'gz')), may hold values from 0 to 63; in each aligned block of 128 rows (0 to 127, 128 to 255, ...) at most 8 rows name the same one
- receivers: int32 [65536], P(('gx', 'gy', 'gz')), may hold values from 0 to 3071
- source_cell: int32 [1], replicated, may hold values from 0 to 196607
Outputs:
- image: float32 [128, 384, 512], P('gz', 'gx', 'gy')
- last_older: float32 [128, 384, 512], P('gz', 'gx', 'gy')
- last_wave: float32 [128, 384, 512], P('gz', 'gx', 'gy')
Inputs may be any that keep to these rules, and one draw needn't show every extreme that they name: `owners`: in the rows of one device (aligned blocks of 128 rows) no owner is named more than 8 times, a bound that some block reaches.
All inputs are finite; a program needn't handle non-finite values.
Results may differ from a plain program's by a relative error of at most 0.0003.
Values sent between devices are 32-bit elements; how exact they have to be, the bound alone decides.
No kernel may reach another device: no remote copies, remote signals or barrier semaphores. Data moves between devices by JAX's collectives and lax.ppermute only.
A program may use at most 64 MiB of HBM per device.

v0:
```python
import math

import jax
import jax.numpy as jnp
from jax import lax
from jax.sharding import PartitionSpec as P

STEPS = 4


def extended(block, sides, width):
    for axis, dim in sides:
        count = lax.axis_size(axis)
        forward = [(i, i + 1) for i in range(count - 1)]
        backward = [(target, source) for source, target in forward]
        low = lax.ppermute(
            lax.slice_in_dim(block, block.shape[dim] - width, None, axis=dim), axis, forward
        )
        high = lax.ppermute(lax.slice_in_dim(block, 0, width, axis=dim), axis, backward)
        block = jnp.concatenate([low, block, high], axis=dim)
    return block


def stencil_weights():
    radius = 8
    window = [math.cos(math.pi * offset / 20.0) for offset in range(1, radius + 1)]
    alternating = sum(
        ((-1.0) ** (offset + 1) * window[offset - 1] for offset in range(1, radius + 1))
    )
    factor = 1.0 / (2.0 * alternating)
    weights = []
    for offset in range(1, radius + 1):
        weights.append(
            factor * 2.0 * (-1.0) ** (offset + 1) * window[offset - 1] / (offset * offset)
        )
    return (weights, -2.0 * sum(weights))


def laplace(field):
    weights, center = stencil_weights()
    depth, rows, cols = field.shape
    total = 3.0 * center * field[8 : depth - 8, 8 : rows - 8, 8 : cols - 8]
    for offset in range(1, 9):
        near = (
            field[8 + offset : depth - 8 + offset, 8 : rows - 8, 8 : cols - 8]
            + field[8 - offset : depth - 8 - offset, 8 : rows - 8, 8 : cols - 8]
        )
        near = (
            near
            + field[8 : depth - 8, 8 + offset : rows - 8 + offset, 8 : cols - 8]
            + field[8 : depth - 8, 8 - offset : rows - 8 - offset, 8 : cols - 8]
        )
        near = (
            near
            + field[8 : depth - 8, 8 : rows - 8, 8 + offset : cols - 8 + offset]
            + field[8 : depth - 8, 8 : rows - 8, 8 - offset : cols - 8 - offset]
        )
        total = total + weights[offset - 1] * near
    return total


def on_device(
    stiffness, older_wave, wave_now, forward_wave, residuals, owners, receivers, source_cell
):
    depth, rows, cols = wave_now.shape
    span_y = lax.axis_size("gy")
    own_tile = lax.axis_index("gx") * span_y + lax.axis_index("gy")
    at_surface = (lax.axis_index("gz") == 0).astype(jnp.float32)
    surface = rows * cols
    empty_plane = jnp.zeros((STEPS, surface), jnp.float32)
    packet = jnp.concatenate(
        [
            residuals,
            owners[:, 0].astype(jnp.float32)[None, :],
            receivers.astype(jnp.float32)[None, :],
        ],
        axis=0,
    )
    piece = lax.all_gather(packet, ("gx", "gy"), axis=1, tiled=True)
    owner_row = piece[STEPS].astype(jnp.int32)
    target = jnp.where(owner_row == own_tile, piece[STEPS + 1].astype(jnp.int32), surface)
    local_plane = empty_plane.at[:, target].add(piece[:STEPS], mode="drop")
    plane = lax.psum(local_plane, "gz").reshape(STEPS, rows, cols)
    image_sum = jnp.zeros((depth, rows, cols), jnp.float32)
    for moment in range(STEPS):
        padded = extended(wave_now, (("gx", 1), ("gy", 2), ("gz", 0)), 8)
        laplacian = laplace(padded).at[0].add(plane[moment] * at_surface)
        fresh = 2.0 * wave_now - older_wave + stiffness * laplacian
        image_sum = image_sum + forward_wave[moment].astype(jnp.float32) * fresh
        older_wave, wave_now = (wave_now, fresh)
    total_y = cols * span_y
    shot_x = source_cell[0] // total_y
    shot_y = source_cell[0] % total_y
    depth_gap = (lax.axis_index("gz") * depth + jnp.arange(depth, dtype=jnp.int32)).astype(
        jnp.float32
    )
    gap_x = (lax.axis_index("gx") * rows + jnp.arange(rows, dtype=jnp.int32) - shot_x).astype(
        jnp.float32
    )
    gap_y = (lax.axis_index("gy") * cols + jnp.arange(cols, dtype=jnp.int32) - shot_y).astype(
        jnp.float32
    )
    distance = (
        (depth_gap * depth_gap)[:, None, None]
        + (gap_x * gap_x)[None, :, None]
        + (gap_y * gap_y)[None, None, :]
    )
    weight = jnp.minimum(1.0, distance / 576.0)
    return (weight * image_sum, older_wave, wave_now)


def solution(mesh):
    in_specs = (
        P("gz", "gx", "gy"),
        P("gz", "gx", "gy"),
        P("gz", "gx", "gy"),
        P(None, "gz", "gx", "gy"),
        P(None, ("gx", "gy", "gz")),
        P(("gx", "gy", "gz"), None),
        P(("gx", "gy", "gz")),
        P(),
    )
    out_specs = (P("gz", "gx", "gy"), P("gz", "gx", "gy"), P("gz", "gx", "gy"))
    return jax.shard_map(
        on_device, mesh=mesh, in_specs=in_specs, out_specs=out_specs, check_vma=False
    )
```

profile of v0, /device:TPU:1, one launch (start us, length us, event | category | flops | bytes accessed | tf_op | source)
XLA Modules:
  0.0 406.4 jit_solution(8653303154033240810)
XLA Ops:
  1.5 4.8 %collective-permute-start = (f32[16,8,128]{2,1,0:T(8,128)S(1)}, f32[16,8,128]{2,1,0:T(8,128)S(1)}, u32[]{:S(2)}, u32[]{:S(2)}) collective-permute-start(f32[16,8,128]{2,1,0:T(8,128)S(1)} %get-tuple-element.97), channel_id=1, source_target_pairs={{0,32},{32,64},{64,96},{96,128},{128,160},{160,192},{192,224},{224... | collective-permute-start | bytes 196616 | tf_op jit(solution)/shard_map/ppermute | solution.py:16
  9.7 120.9 %all_gather.3 = f32[6,8192]{1,0:T(8,128)S(1)} all-gather(f32[6,128]{1,0:T(8,128)S(1)} %pad_maximum_fusion.22), channel_id=1, replica_groups=mesh['gx'=16,'gy'=4,'gz'=8] {'gx','gy'}, dimensions={1}, use_global_device_ids=true | all-gather | bytes 199680 | tf_op jit(solution)/shard_map/all_gather | solution.py:79
  130.8 2.7 copy.12
  133.4 45.5 %scatter_custom_fusion = f32[4,3072]{0,1:T(8,128)} fusion(s32[8192]{0:T(1024)S(1)} %bitcast.36, f32[8192,4]{1,0:T(8,128)} %copy.12, f32[]{:T(128)} %constant.163.clone.1), kind=kCustom, calls=%fused_computation.45 | custom fusion | flops 32768 | bytes 49664 | tf_op jit(solution)/shard_map/scatter-add | solution.py:82
  182.5 79.3 %psum.7 = f32[4,3072]{0,1:T(8,128)S(1)} all-reduce(f32[4,3072]{0,1:T(8,128)} %scatter_custom_fusion), channel_id=1, replica_groups=mesh['gx'=16,'gy'=4,'gz'=8] {'gz'}, use_global_device_ids=true, to_apply=%region_1.2 | all-reduce | flops 12288 | bytes 98304 | tf_op jit(solution)/shard_map/psum | solution.py:83
  263.2 3.2 collective-permute-start.4
  268.8 2.9 fusion
  274.5 4.4 %fusion.181 = f32[16,24,128]{2,1,0:T(8,128)S(1)} fusion(f32[16,40,8]{2,1,0:T(8,128)S(1)} %collective-permute-done.2, f32[16,40,128]{2,1,0:T(8,128)S(1)} %get-tuple-element.99, f32[16,40,8]{2,1,0:T(8,128)} %collective-permute-done.3, f32[16,32,128]{2,1,0:T(8,128)S(1)} %get-tuple-element.95, f32[16,32,128]{2,1,0:T(8,128)S(1)} %get-tuple-element.98, ...), kind=kLoop, calls=%fused_computation.319 | loop fusion | flops 3588096 | bytes 7053312 | tf_op jit(solution)/shard_map/add | solution.py:58
  281.6 3.9 collective-permute-done.7
  285.6 5.5 %collective-permute-start.8 = (f32[16,40,8]{2,1,0:T(8,128)S(1)}, f32[16,40,8]{2,1,0:T(8,128)S(1)}, u32[]{:S(2)}, u32[]{:S(2)}) collective-permute-start(f32[16,40,8]{2,1,0:T(8,128)S(1)} %get-tuple-element.84), channel_id=1, source_target_pairs={{0,8},{8,16},{16,24},{1,9},{9,17},{17,25},{2,10},{10,18},{18,26},{... | collective-permute-start | bytes 61448 | tf_op jit(solution)/shard_map/ppermute | solution.py:16
  292.5 5.7 %collective-permute-done.8 = f32[16,40,8]{2,1,0:T(8,128)S(1)} collective-permute-done((f32[16,40,8]{2,1,0:T(8,128)S(1)}, f32[16,40,8]{2,1,0:T(8,128)S(1)}, u32[]{:S(2)}, u32[]{:S(2)}) %collective-permute-start.8) | collective-permute-done | bytes 20512 | tf_op jit(solution)/shard_map/ppermute | solution.py:16
  298.2 12.3 %collective-permute-done.9 = f32[16,40,8]{2,1,0:T(8,128)S(1)} collective-permute-done((f32[16,40,8]{2,1,0:T(8,128)S(1)}, f32[16,40,8]{2,1,0:T(8,128)S(1)}, u32[]{:S(2)}, u32[]{:S(2)}) %collective-permute-start.9) | collective-permute-done | bytes 20512 | tf_op jit(solution)/shard_map/ppermute | solution.py:19
  313.2 3.4 collective-permute-start.11
  326.0 3.1 collective-permute-done.13
  329.3 5.8 %collective-permute-start.14 = (f32[16,40,8]{2,1,0:T(8,128)S(1)}, f32[16,40,8]{2,1,0:T(8,128)S(1)}, u32[]{:S(2)}, u32[]{:S(2)}) collective-permute-start(f32[16,40,8]{2,1,0:T(8,128)S(1)} %get-tuple-element.80), channel_id=1, source_target_pairs={{0,8},{8,16},{16,24},{1,9},{9,17},{17,25},{2,10},{10,18},{18,26},{... | collective-permute-start | bytes 61448 | tf_op jit(solution)/shard_map/ppermute | solution.py:16
  336.4 5.2 %collective-permute-done.14 = f32[16,40,8]{2,1,0:T(8,128)S(1)} collective-permute-done((f32[16,40,8]{2,1,0:T(8,128)S(1)}, f32[16,40,8]{2,1,0:T(8,128)S(1)}, u32[]{:S(2)}, u32[]{:S(2)}) %collective-permute-start.14) | collective-permute-done | bytes 20512 | tf_op jit(solution)/shard_map/ppermute | solution.py:16
  341.6 10.1 %collective-permute-done.15 = f32[16,40,8]{2,1,0:T(8,128)S(1)} collective-permute-done((f32[16,40,8]{2,1,0:T(8,128)S(1)}, f32[16,40,8]{2,1,0:T(8,128)S(1)}, u32[]{:S(2)}, u32[]{:S(2)}) %collective-permute-start.15) | collective-permute-done | bytes 20512 | tf_op jit(solution)/shard_map/ppermute | solution.py:19
  354.1 3.7 collective-permute-start.17
  364.1 4.9 %collective-permute-start.18 = (f32[16,8,128]{2,1,0:T(8,128)S(1)}, f32[16,8,128]{2,1,0:T(8,128)S(1)}, u32[]{:S(2)}, u32[]{:S(2)}) collective-permute-start(f32[16,8,128]{2,1,0:T(8,128)S(1)} %get-tuple-element.88), channel_id=1, source_target_pairs={{0,32},{32,64},{64,96},{96,128},{128,160},{160,192},{192,224},{224... | collective-permute-start | bytes 196616 | tf_op jit(solution)/shard_map/ppermute | solution.py:16
  370.3 3.7 collective-permute-done.19
  378.0 3.6 collective-permute-done.20
  381.6 9.8 %collective-permute-done.21 = f32[16,40,8]{2,1,0:T(8,128)S(1)} collective-permute-done((f32[16,40,8]{2,1,0:T(8,128)S(1)}, f32[16,40,8]{2,1,0:T(8,128)S(1)}, u32[]{:S(2)}, u32[]{:S(2)}) %collective-permute-start.21) | collective-permute-done | bytes 20512 | tf_op jit(solution)/shard_map/ppermute | solution.py:19
  393.8 5.4 %collective-permute-start.23 = (f32[8,40,144]{2,1,0:T(8,128)S(1)}, f32[8,40,144]{2,1,0:T(8,128)S(1)}, u32[]{:S(2)}, u32[]{:S(2)}) collective-permute-start(f32[8,40,144]{2,1,0:T(8,128)S(1)} %get-tuple-element.66), channel_id=1, source_target_pairs={{0,1},{1,2},{2,3},{3,4},{4,5},{5,6},{6,7},{8,9},{9,10},{10,11},{11... | collective-permute-start | bytes 552968 | tf_op jit(solution)/shard_map/ppermute | solution.py:16
  399.5 2.6 collective-permute-done.22
  (89 shorter events, 52.0 us)
Async XLA Ops:
  1.5 177.4 %collective-permute-start = (f32[16,8,128]{2,1,0:T(8,128)S(1)}, f32[16,8,128]{2,1,0:T(8,128)S(1)}, u32[]{:S(2)}, u32[]{:S(2)}) collective-permute-start(f32[16,8,128]{2,1,0:T(8,128)S(1)} %get-tuple-element.97), channel_id=1, source_target_pairs={{0,32},{32,64},{64,96},{96,128},{128,160},{160,192},{192,224},{224... | collective-permute-start | bytes 196616 | tf_op jit(solution)/shard_map/ppermute | solution.py:16
  6.4 172.7 %collective-permute-start.1 = (f32[16,8,128]{2,1,0:T(8,128)S(1)}, f32[16,8,128]{2,1,0:T(8,128)S(1)}, u32[]{:S(2)}, u32[]{:S(2)}) collective-permute-start(f32[16,8,128]{2,1,0:T(8,128)S(1)} %get-tuple-element.96), channel_id=1, source_target_pairs={{32,0},{64,32},{96,64},{128,96},{160,128},{192,160},{224,192},{256... | collective-permute-start | bytes 196616 | tf_op jit(solution)/shard_map/ppermute | solution.py:19
  179.9 81.9 %collective-permute-start.2 = (f32[16,40,8]{2,1,0:T(8,128)}, f32[16,40,8]{2,1,0:T(8,128)S(1)}, u32[]{:S(2)}, u32[]{:S(2)}) collective-permute-start(f32[16,40,8]{2,1,0:T(8,128)} %get-tuple-element.86), channel_id=1, source_target_pairs={{0,8},{8,16},{16,24},{1,9},{9,17},{17,25},{2,10},{10,18},{18,26},{... | collective-permute-start | bytes 61448 | tf_op jit(solution)/shard_map/ppermute | solution.py:16
  181.2 80.6 %collective-permute-start.3 = (f32[16,40,8]{2,1,0:T(8,128)}, f32[16,40,8]{2,1,0:T(8,128)}, u32[]{:S(2)}, u32[]{:S(2)}) collective-permute-start(f32[16,40,8]{2,1,0:T(8,128)} %get-tuple-element.85), channel_id=1, source_target_pairs={{8,0},{16,8},{24,16},{9,1},{17,9},{25,17},{10,2},{18,10},{26,18},{... | collective-permute-start | bytes 61448 | tf_op jit(solution)/shard_map/ppermute | solution.py:19
  263.2 8.5 %collective-permute-start.4 = (f32[8,40,144]{2,1,0:T(8,128)S(1)}, f32[8,40,144]{2,1,0:T(8,128)S(1)}, u32[]{:S(2)}, u32[]{:S(2)}) collective-permute-start(f32[8,40,144]{2,1,0:T(8,128)S(1)} %get-tuple-element.71), channel_id=1, source_target_pairs={{1,0},{2,1},{3,2},{4,3},{5,4},{6,5},{7,6},{9,8},{10,9},{11,10},{12... | collective-permute-start | bytes 552968 | tf_op jit(solution)/shard_map/ppermute | solution.py:19
  266.4 6.4 %collective-permute-start.5 = (f32[8,40,144]{2,1,0:T(8,128)S(1)}, f32[8,40,144]{2,1,0:T(8,128)S(1)}, u32[]{:S(2)}, u32[]{:S(2)}) collective-permute-start(f32[8,40,144]{2,1,0:T(8,128)S(1)} %get-tuple-element.72), channel_id=1, source_target_pairs={{0,1},{1,2},{2,3},{3,4},{4,5},{5,6},{6,7},{8,9},{9,10},{10,11},{11... | collective-permute-start | bytes 552968 | tf_op jit(solution)/shard_map/ppermute | solution.py:16
  279.0 2.6 collective-permute-start.6
  280.3 5.2 %collective-permute-start.7 = (f32[16,8,128]{2,1,0:T(8,128)S(1)}, f32[16,8,128]{2,1,0:T(8,128)S(1)}, u32[]{:S(2)}, u32[]{:S(2)}) collective-permute-start(f32[16,8,128]{2,1,0:T(8,128)S(1)} %get-tuple-element.91), channel_id=1, source_target_pairs={{32,0},{64,32},{96,64},{128,96},{160,128},{192,160},{224,192},{256... | collective-permute-start | bytes 196616 | tf_op jit(solution)/shard_map/ppermute | solution.py:19
  285.6 12.5 %collective-permute-start.8 = (f32[16,40,8]{2,1,0:T(8,128)S(1)}, f32[16,40,8]{2,1,0:T(8,128)S(1)}, u32[]{:S(2)}, u32[]{:S(2)}) collective-permute-start(f32[16,40,8]{2,1,0:T(8,128)S(1)} %get-tuple-element.84), channel_id=1, source_target_pairs={{0,8},{8,16},{16,24},{1,9},{9,17},{17,25},{2,10},{10,18},{18,26},{... | collective-permute-start | bytes 61448 | tf_op jit(solution)/shard_map/ppermute | solution.py:16
  291.2 19.3 %collective-permute-start.9 = (f32[16,40,8]{2,1,0:T(8,128)S(1)}, f32[16,40,8]{2,1,0:T(8,128)S(1)}, u32[]{:S(2)}, u32[]{:S(2)}) collective-permute-start(f32[16,40,8]{2,1,0:T(8,128)S(1)} %get-tuple-element.83), channel_id=1, source_target_pairs={{8,0},{16,8},{24,16},{9,1},{17,9},{25,17},{10,2},{18,10},{26,18},{... | collective-permute-start | bytes 61448 | tf_op jit(solution)/shard_map/ppermute | solution.py:19
  310.9 8.4 %collective-permute-start.10 = (f32[8,40,144]{2,1,0:T(8,128)S(1)}, f32[8,40,144]{2,1,0:T(8,128)S(1)}, u32[]{:S(2)}, u32[]{:S(2)}) collective-permute-start(f32[8,40,144]{2,1,0:T(8,128)S(1)} %get-tuple-element.69), channel_id=1, source_target_pairs={{1,0},{2,1},{3,2},{4,3},{5,4},{6,5},{7,6},{9,8},{10,9},{11,10},{12... | collective-permute-start | bytes 552968 | tf_op jit(solution)/shard_map/ppermute | solution.py:19
  313.2 7.2 %collective-permute-start.11 = (f32[8,40,144]{2,1,0:T(8,128)S(1)}, f32[8,40,144]{2,1,0:T(8,128)S(1)}, u32[]{:S(2)}, u32[]{:S(2)}) collective-permute-start(f32[8,40,144]{2,1,0:T(8,128)S(1)} %get-tuple-element.70), channel_id=1, source_target_pairs={{0,1},{1,2},{2,3},{3,4},{4,5},{5,6},{6,7},{8,9},{9,10},{10,11},{11... | collective-permute-start | bytes 552968 | tf_op jit(solution)/shard_map/ppermute | solution.py:16
  322.8 3.2 collective-permute-start.12
  324.1 5.0 %collective-permute-start.13 = (f32[16,8,128]{2,1,0:T(8,128)S(1)}, f32[16,8,128]{2,1,0:T(8,128)S(1)}, u32[]{:S(2)}, u32[]{:S(2)}) collective-permute-start(f32[16,8,128]{2,1,0:T(8,128)S(1)} %get-tuple-element.89), channel_id=1, source_target_pairs={{32,0},{64,32},{96,64},{128,96},{160,128},{192,160},{224,192},{256... | collective-permute-start | bytes 196616 | tf_op jit(solution)/shard_map/ppermute | solution.py:19
  329.3 12.3 %collective-permute-start.14 = (f32[16,40,8]{2,1,0:T(8,128)S(1)}, f32[16,40,8]{2,1,0:T(8,128)S(1)}, u32[]{:S(2)}, u32[]{:S(2)}) collective-permute-start(f32[16,40,8]{2,1,0:T(8,128)S(1)} %get-tuple-element.80), channel_id=1, source_target_pairs={{0,8},{8,16},{16,24},{1,9},{9,17},{17,25},{2,10},{10,18},{18,26},{... | collective-permute-start | bytes 61448 | tf_op jit(solution)/shard_map/ppermute | solution.py:16
  335.1 16.6 %collective-permute-start.15 = (f32[16,40,8]{2,1,0:T(8,128)S(1)}, f32[16,40,8]{2,1,0:T(8,128)S(1)}, u32[]{:S(2)}, u32[]{:S(2)}) collective-permute-start(f32[16,40,8]{2,1,0:T(8,128)S(1)} %get-tuple-element.79), channel_id=1, source_target_pairs={{8,0},{16,8},{24,16},{9,1},{17,9},{25,17},{10,2},{18,10},{26,18},{... | collective-permute-start | bytes 61448 | tf_op jit(solution)/shard_map/ppermute | solution.py:19
  352.0 8.6 %collective-permute-start.16 = (f32[8,40,144]{2,1,0:T(8,128)S(1)}, f32[8,40,144]{2,1,0:T(8,128)S(1)}, u32[]{:S(2)}, u32[]{:S(2)}) collective-permute-start(f32[8,40,144]{2,1,0:T(8,128)S(1)} %get-tuple-element.67), channel_id=1, source_target_pairs={{1,0},{2,1},{3,2},{4,3},{5,4},{6,5},{7,6},{9,8},{10,9},{11,10},{12... | collective-permute-start | bytes 552968 | tf_op jit(solution)/shard_map/ppermute | solution.py:19
  354.1 7.7 %collective-permute-start.17 = (f32[8,40,144]{2,1,0:T(8,128)S(1)}, f32[8,40,144]{2,1,0:T(8,128)S(1)}, u32[]{:S(2)}, u32[]{:S(2)}) collective-permute-start(f32[8,40,144]{2,1,0:T(8,128)S(1)} %get-tuple-element.68), channel_id=1, source_target_pairs={{0,1},{1,2},{2,3},{3,4},{4,5},{5,6},{6,7},{8,9},{9,10},{10,11},{11... | collective-permute-start | bytes 552968 | tf_op jit(solution)/shard_map/ppermute | solution.py:16
  364.1 6.2 %collective-permute-start.18 = (f32[16,8,128]{2,1,0:T(8,128)S(1)}, f32[16,8,128]{2,1,0:T(8,128)S(1)}, u32[]{:S(2)}, u32[]{:S(2)}) collective-permute-start(f32[16,8,128]{2,1,0:T(8,128)S(1)} %get-tuple-element.88), channel_id=1, source_target_pairs={{0,32},{32,64},{64,96},{96,128},{128,160},{160,192},{192,224},{224... | collective-permute-start | bytes 196616 | tf_op jit(solution)/shard_map/ppermute | solution.py:16
  369.0 5.0 %collective-permute-start.19 = (f32[16,8,128]{2,1,0:T(8,128)S(1)}, f32[16,8,128]{2,1,0:T(8,128)S(1)}, u32[]{:S(2)}, u32[]{:S(2)}) collective-permute-start(f32[16,8,128]{2,1,0:T(8,128)S(1)} %get-tuple-element.87), channel_id=1, source_target_pairs={{32,0},{64,32},{96,64},{128,96},{160,128},{192,160},{224,192},{256... | collective-permute-start | bytes 196616 | tf_op jit(solution)/shard_map/ppermute | solution.py:19
  374.2 7.4 %collective-permute-start.20 = (f32[16,40,8]{2,1,0:T(8,128)S(1)}, f32[16,40,8]{2,1,0:T(8,128)S(1)}, u32[]{:S(2)}, u32[]{:S(2)}) collective-permute-start(f32[16,40,8]{2,1,0:T(8,128)S(1)} %get-tuple-element.76), channel_id=1, source_target_pairs={{0,8},{8,16},{16,24},{1,9},{9,17},{17,25},{2,10},{10,18},{18,26},{... | collective-permute-start | bytes 61448 | tf_op jit(solution)/shard_map/ppermute | solution.py:16
  376.6 14.8 %collective-permute-start.21 = (f32[16,40,8]{2,1,0:T(8,128)S(1)}, f32[16,40,8]{2,1,0:T(8,128)S(1)}, u32[]{:S(2)}, u32[]{:S(2)}) collective-permute-start(f32[16,40,8]{2,1,0:T(8,128)S(1)} %get-tuple-element.75), channel_id=1, source_target_pairs={{8,0},{16,8},{24,16},{9,1},{17,9},{25,17},{10,2},{18,10},{26,18},{... | collective-permute-start | bytes 61448 | tf_op jit(solution)/shard_map/ppermute | solution.py:19
  391.8 10.2 %collective-permute-start.22 = (f32[8,40,144]{2,1,0:T(8,128)S(1)}, f32[8,40,144]{2,1,0:T(8,128)S(1)}, u32[]{:S(2)}, u32[]{:S(2)}) collective-permute-start(f32[8,40,144]{2,1,0:T(8,128)S(1)} %get-tuple-element.65), channel_id=1, source_target_pairs={{1,0},{2,1},{3,2},{4,3},{5,4},{6,5},{7,6},{9,8},{10,9},{11,10},{12... | collective-permute-start | bytes 552968 | tf_op jit(solution)/shard_map/ppermute | solution.py:19
  393.8 9.5 %collective-permute-start.23 = (f32[8,40,144]{2,1,0:T(8,128)S(1)}, f32[8,40,144]{2,1,0:T(8,128)S(1)}, u32[]{:S(2)}, u32[]{:S(2)}) collective-permute-start(f32[8,40,144]{2,1,0:T(8,128)S(1)} %get-tuple-element.66), channel_id=1, source_target_pairs={{0,1},{1,2},{2,3},{3,4},{4,5},{5,6},{6,7},{8,9},{9,10},{10,11},{11... | collective-permute-start | bytes 552968 | tf_op jit(solution)/shard_map/ppermute | solution.py:16
  (5 other events, 97.5 us)
where the time goes:
time: 411 us; the launch traced here: 406 us
  blocking collectives  200 us (49%)
  waiting for transfers between devices  69.5 us (17%)
  other arithmetic  67.4 us (16%)
  starting transfers between devices  62.1 us (15%)
  local copies, waits for them, and re-layouts  5.23 us (1%)
    all_gather x1, blocking collectives, on_device(): piece = lax.all_gather(packet, ('gx', 'gy'), axis=1, tiled=True)  121 us
    psum x1, blocking collectives, on_device(): plane = lax.psum(local_plane, 'gz').reshape(STEPS, rows, cols)  79.3 us
    ppermute x12, waiting for transfers between devices, extended(): lax.ppermute(lax.slice_in_dim(block, 0, width, axis=dim), axis, backward)  49.8 us
    scatter-add x1, other arithmetic, on_device(): local_plane = empty_plane.at[:, target].add(piece[:STEPS], mode='drop')  45.5 us
    ppermute x12, starting transfers between devices, extended(): lax.ppermute(lax.slice_in_dim(block, block.shape[dim] - width, None, axis...  42.2 us
    ppermute x12, starting transfers between devices, extended(): lax.ppermute(lax.slice_in_dim(block, 0, width, axis=dim), axis, backward)  19.9 us
    ppermute x12, waiting for transfers between devices, extended(): lax.ppermute(lax.slice_in_dim(block, block.shape[dim] - width, None, axis...  19.7 us
    add x4, other arithmetic, laplace(): total = total + weights[offset - 1] * near  9.35 us
  transfers between devices with their start and end apart: 24, of which 17 were waited for; matrix products, arithmetic and copies ran while one was open for 13% of the time, Pallas kernels for 0%

commit v1 on v0

v1 whole, which is shorter than its diff:
```python
import functools
import math

import jax
import jax.numpy as jnp
import numpy as np
from jax import lax
from jax.experimental import pallas as pl
from jax.experimental.pallas import tpu as pltpu
from jax.sharding import PartitionSpec as P

STEPS = 4
RADIUS = 8
LANES = 128
STRIP = 32
CAP = 8
SLOTS = 3 * CAP
F32 = jnp.float32
BF16 = jnp.bfloat16


def stencil_weights():
    window = [math.cos(math.pi * offset / 20.0) for offset in range(1, RADIUS + 1)]
    alternating = sum(
        ((-1.0) ** (offset + 1) * window[offset - 1] for offset in range(1, RADIUS + 1))
    )
    factor = 1.0 / (2.0 * alternating)
    weights = []
    for offset in range(1, RADIUS + 1):
        weights.append(
            factor * 2.0 * (-1.0) ** (offset + 1) * window[offset - 1] / (offset * offset)
        )
    return (weights, -2.0 * sum(weights))


WEIGHTS, CENTER = stencil_weights()


def band():
    size = 2 * LANES
    matrix = np.zeros((size, size), np.float64)
    for column in range(size):
        matrix[column, column] = 3.0 * CENTER
        for offset in range(1, RADIUS + 1):
            matrix[(column + offset) % size, column] = WEIGHTS[offset - 1]
            matrix[(column - offset) % size, column] = WEIGHTS[offset - 1]
    matrix = matrix.astype(np.float32)
    high = matrix.astype(jnp.bfloat16)
    low = (matrix - high.astype(np.float32)).astype(jnp.bfloat16)
    return high, low


def lane_of(shape):
    return lax.broadcasted_iota(jnp.int32, shape, len(shape) - 1)


def vmem():
    return pl.BlockSpec(memory_space=pltpu.VMEM)


def smem():
    return pl.BlockSpec(memory_space=pltpu.SMEM)


def call(body, outs, ins, scratch=(), flops=1_000_000, in_specs=None):
    return pl.pallas_call(
        body,
        out_shape=outs,
        in_specs=in_specs or [smem()] + [vmem()] * (len(ins) - 1),
        out_specs=jax.tree.map(lambda _: vmem(), outs),
        scratch_shapes=list(scratch),
        compiler_params=pltpu.CompilerParams(vmem_limit_bytes=32 * 1024 * 1024),
        cost_estimate=pl.CostEstimate(flops=flops, bytes_accessed=2_000_000, transcendentals=0),
    )(*ins)


def shaped(*shape):
    return jax.ShapeDtypeStruct(shape, F32)


def split3(value):
    high = value.astype(BF16)
    rest = value - high.astype(F32)
    middle = rest.astype(BF16)
    return high, middle, (rest - middle.astype(F32)).astype(BF16)


def dot_nt(left, right):
    return lax.dot_general(left, right, (((1,), (1,)), ((), ())), preferred_element_type=F32)


def slot_kernel(span_y, tiles, ids, residuals, owner_column, owner_row, cell_row, out):
    rows = residuals.shape[1]
    owner = owner_row[...]
    earlier = (owner_column[...] == owner) & (
        lax.broadcasted_iota(jnp.int32, (rows, rows), 0)
        < lax.broadcasted_iota(jnp.int32, (rows, rows), 1)
    )
    rank = jnp.sum(earlier.astype(jnp.int32), axis=0, keepdims=True)
    cell = cell_row[...]
    along = cell & (LANES - 1)
    fields = [residuals[pl.ds(field, 1), :] for field in range(STEPS)] + [cell.astype(F32)]
    stacked = jnp.concatenate(
        [jnp.broadcast_to(field, (SLOTS, rows)) for field in fields]
        + [jnp.zeros((LANES - SLOTS * len(fields), rows), F32)],
        axis=0,
    )
    line = lax.broadcasted_iota(jnp.int32, (LANES, rows), 0)
    slot = line - SLOTS * (line // SLOTS)
    tile = lax.broadcasted_iota(jnp.int32, (tiles, rows), 0)
    place = tile & (span_y - 1)
    total = jnp.zeros((tiles, LANES), F32)
    for group in range(3):
        named = owner == tile + (group - 1)
        wanted = slot == rank + CAP * group
        if group == 0:
            named = named & (place != 0)
            wanted = wanted & (along >= LANES - STRIP)
        if group == 2:
            named = named & (place != span_y - 1)
            wanted = wanted & (along < STRIP)
        chosen = named.astype(F32).astype(BF16)
        for part in split3(jnp.where(wanted, stacked, 0.0)):
            total = total + dot_nt(chosen, part)
    out[...] = total


def plane_kernel(rows, ids, packets, main, side, turned):
    main[...] = jnp.zeros(main.shape, F32)
    side[...] = jnp.zeros(side.shape, F32)

    @pl.when(ids[0] == 0)
    def _():
        turned[...] = jnp.transpose(packets[...])
        count = packets.shape[0]
        line = lax.broadcasted_iota(jnp.int32, (rows, count), 0)
        spot = lax.broadcasted_iota(jnp.int32, (LANES, count), 0)

        def product(slot):
            cell = turned[pl.ds(SLOTS * STEPS + slot, 1), :].astype(jnp.int32)
            hit = (cell >> 7) == line
            highs, lows = [], []
            for step in range(STEPS):
                value = turned[pl.ds(SLOTS * step + slot, 1), :]
                high = value.astype(BF16).astype(F32)
                highs.append(jnp.where(hit, high, 0.0))
                lows.append(jnp.where(hit, value - high, 0.0))
            left = jnp.concatenate(highs + lows, axis=0).astype(BF16)
            right = jnp.where((cell & (LANES - 1)) == spot, 1.0, 0.0).astype(BF16)
            both = dot_nt(left, right)
            return both[: STEPS * rows] + both[STEPS * rows :]

        for slot in range(SLOTS):
            target = main if slot // CAP == 1 else side
            target[...] += product(slot).reshape(target.shape)


def strip_pack_kernel(ids, wave, older, stiff, even, odd):
    parity = ids[2] & 1
    quarter = lane_of(wave.shape[1:]) // STRIP
    low, high = quarter == 0, quarter == 3
    quarters = LANES // STRIP
    for number, field in enumerate((wave, older, stiff)):
        for chunk in range(field.shape[0] // quarters):
            lows = highs = None
            for turn in range(quarters):
                value = field[quarters * chunk + turn]
                one = jnp.where(low, value, 0.0)
                two = jnp.where(high, value, 0.0)
                if turn:
                    one = pltpu.roll(one, STRIP * turn, 1)
                    two = pltpu.roll(two, STRIP * turn, 1)
                lows = one if lows is None else lows + one
                highs = two if highs is None else highs + two
            place = number * (field.shape[0] // quarters) + chunk
            even[place] = jnp.where(parity == 0, highs, lows)
            odd[place] = jnp.where(parity == 0, lows, highs)


def fold(first, second):
    return first + pltpu.roll(second, LANES // 2, 1)


def write_faces(ids, main, side, z_even, z_odd, x_even, x_odd):
    z_parity, x_parity = ids[0] & 1, ids[1] & 1
    depth, rows, _ = main.shape
    half = RADIUS // 2
    for face, start in (
        (z_even, (depth - RADIUS) * (1 - z_parity)),
        (z_odd, (depth - RADIUS) * z_parity),
    ):
        face[pl.ds(0, RADIUS)] = main[pl.ds(start, RADIUS)]
        for plane in range(half):
            face[RADIUS + plane] = fold(side[start + plane], side[start + half + plane])
    for face, start in (
        (x_even, (rows - RADIUS) * (1 - x_parity)),
        (x_odd, (rows - RADIUS) * x_parity),
    ):
        start = pl.multiple_of(start, RADIUS)
        face[pl.ds(0, depth)] = main[:, pl.ds(start, RADIUS), :]
        for plane in range(depth // 2):
            face[depth + plane] = fold(
                side[plane, pl.ds(start, RADIUS), :],
                side[plane + depth // 2, pl.ds(start, RADIUS), :],
            )


def strip_unpack_kernel(
    ids, even, odd, wave, wave_side, older_side, stiff_side, z_even, z_odd, x_even, x_odd
):
    parity = ids[2] & 1
    quarters = LANES // STRIP
    quarter = lane_of(wave.shape[1:]) // STRIP
    from_even = quarter == 3 * parity
    from_odd = quarter == 3 * (1 - parity)
    chunks = wave.shape[0] // quarters
    for number, side in enumerate((wave_side, older_side, stiff_side)):
        for chunk in range(chunks):
            one, two = even[number * chunks + chunk], odd[number * chunks + chunk]
            for turn in range(quarters):
                back = (LANES - STRIP * turn) % LANES
                first = pltpu.roll(one, back, 1) if back else one
                second = pltpu.roll(two, back, 1) if back else two
                side[quarters * chunk + turn] = jnp.where(
                    from_even, first, jnp.where(from_odd, second, 0.0)
                )
    write_faces(ids, wave, wave_side, z_even, z_odd, x_even, x_odd)


def fill(ids, wave, side, z_even, z_odd, x_even, x_odd, z_ext, x_ext):
    z_parity, x_parity = ids[0] & 1, ids[1] & 1
    depth, rows, _ = wave.shape
    half = RADIUS // 2
    outer = lane_of((RADIUS, LANES))
    kept = (outer < STRIP) | (outer >= LANES - STRIP)
    kept_plane = lane_of((rows, LANES))
    kept_plane = (kept_plane < STRIP) | (kept_plane >= LANES - STRIP)
    for part, field in enumerate((wave, side)):
        z_ext[part, pl.ds(RADIUS, depth)] = field[...]
        x_ext[part, :, pl.ds(RADIUS, rows), :] = field[...]
    pair = z_even.at[1 - z_parity]
    for face, start in (
        (pair, (depth + RADIUS) * (1 - z_parity)),
        (z_odd, (depth + RADIUS) * z_parity),
    ):
        z_ext[0, pl.ds(start, RADIUS)] = face[pl.ds(0, RADIUS)]
        for plane in range(half):
            both = face[RADIUS + plane]
            z_ext[1, start + plane] = jnp.where(kept_plane, both, 0.0)
            z_ext[1, start + half + plane] = jnp.where(
                kept_plane, pltpu.roll(both, LANES // 2, 1), 0.0
            )
    for face, start in (
        (x_even, (rows + RADIUS) * (1 - x_parity)),
        (x_odd, (rows + RADIUS) * x_parity),
    ):
        start = pl.multiple_of(start, RADIUS)
        x_ext[0, :, pl.ds(start, RADIUS), :] = face[pl.ds(0, depth)]
        for plane in range(depth // 2):
            both = face[depth + plane]
            x_ext[1, plane, pl.ds(start, RADIUS), :] = jnp.where(kept, both, 0.0)
            x_ext[1, plane + depth // 2, pl.ds(start, RADIUS), :] = jnp.where(
                kept, pltpu.roll(both, LANES // 2, 1), 0.0
            )


def advance(step, ids, refs, wave, side, older, older_side, stiff, stiff_side, forward, image_in,
            plane, plane_side, band_high, band_low, fresh, fresh_side, image, z_ext, x_ext, y_terms):
    depth, rows, _ = wave.shape
    last = step == STEPS - 1
    width = LANES if last else 2 * LANES
    both = jnp.concatenate(
        [wave[...].reshape(depth * rows, LANES), side[...].reshape(depth * rows, LANES)], axis=1
    )
    high = both.astype(BF16)
    low = (both - high.astype(F32)).astype(BF16)
    matrix, rest = band_high[:, :width], band_low[:, :width]
    y_terms[:, :width] = (
        jnp.dot(high, matrix, preferred_element_type=F32)
        + jnp.dot(low, matrix, preferred_element_type=F32)
        + jnp.dot(high, rest, preferred_element_type=F32)
    )

    def one(z, part, field, before, speed, source, target):
        column = x_ext[part, z]
        turned = [None] + [
            pltpu.roll(column, rows + 2 * RADIUS - offset, 0) for offset in range(1, RADIUS)
        ]
        total = y_terms[z * rows : (z + 1) * rows, part * LANES : (part + 1) * LANES]
        for offset in range(1, RADIUS + 1):
            near = z_ext[part, RADIUS + z + offset] + z_ext[part, RADIUS + z - offset]
            if offset < RADIUS:
                near = near + turned[offset][RADIUS : RADIUS + rows]
                near = near + turned[RADIUS - offset][:rows]
            else:
                near = near + column[2 * RADIUS :] + column[:rows]
            total = total + WEIGHTS[offset - 1] * near
        if z == 0:
            total = total + source[step]
        value = 2.0 * field[z] - before[z] + speed[z] * total
        target[z] = value
        return value

    for z in range(depth):
        value = one(z, 0, wave, older, stiff, plane, fresh)
        product = forward[step, z].astype(F32) * value
        if step:
            product = product + image_in[z]
        if last:
            product = product * muting(ids, z, depth, rows)
        image[z] = product
        if not last:
            one(z, 1, side, older_side, stiff_side, plane_side, fresh_side)


def muting(ids, z, depth, rows):
    gap_z = (ids[0] * depth + z).astype(F32)
    gap_x = (
        ids[1] * rows + lax.broadcasted_iota(jnp.int32, (rows, LANES), 0) - ids[3]
    ).astype(F32)
    gap_y = (ids[2] * LANES + lane_of((rows, LANES)) - ids[4]).astype(F32)
    distance = gap_z * gap_z + gap_x * gap_x + gap_y * gap_y
    return jnp.minimum(1.0, distance / 576.0)


def step_kernel(step, ids, z_even_in, z_odd_in, x_even_in, x_odd_in, wave, side, older,
                older_side, stiff, stiff_side, forward, plane, plane_side, band_high, band_low,
                *rest):
    image_in = None
    if step:
        image_in, *rest = rest
    last = step == STEPS - 1
    if last:
        image, fresh, z_ext, x_ext, y_terms = rest
        fresh_side = None
    else:
        (image, fresh, fresh_side, z_even, z_odd, x_even, x_odd, z_ext, x_ext, y_terms) = rest
    fill(ids, wave, side, z_even_in, z_odd_in, x_even_in, x_odd_in, z_ext, x_ext)
    advance(step, ids, None, wave, side, older, older_side, stiff, stiff_side, forward, image_in,
            plane, plane_side, band_high, band_low, fresh, fresh_side, image, z_ext, x_ext,
            y_terms)
    if not last:
        write_faces(ids, fresh, fresh_side, z_even, z_odd, x_even, x_odd)


def swap(block, axis, parity):
    count = lax.axis_size(axis)
    pairs = []
    for left in range(parity, count - 1, 2):
        pairs += [(left, left + 1), (left + 1, left)]
    return lax.ppermute(block, axis, pairs)


def exchange(faces):
    z_even, z_odd, x_even, x_odd = faces
    count = lax.axis_size("gz")
    groups = [[2 * chip, 2 * chip + 1] for chip in range(count // 2)]
    x_odd = swap(x_odd, "gx", 1)
    x_even = swap(x_even, "gx", 0)
    z_odd = swap(z_odd, "gz", 1)
    z_even = lax.all_gather(z_even, "gz", axis=0, tiled=False, axis_index_groups=groups)
    return z_even, z_odd, x_even, x_odd


def on_device(
    stiffness, older_wave, wave_now, forward_wave, residuals, owners, receivers, source_cell
):
    depth, rows, cols = wave_now.shape
    span_x, span_y, span_z = (lax.axis_size(axis) for axis in ("gx", "gy", "gz"))
    tiles = span_x * span_y
    total_y = cols * span_y
    ids = jnp.stack(
        [
            lax.axis_index("gz"),
            lax.axis_index("gx"),
            lax.axis_index("gy"),
            source_cell[0] // total_y,
            source_cell[0] % total_y,
        ]
    ).astype(jnp.int32)
    band_high, band_low = (jnp.asarray(part) for part in band())
    block = shaped(depth, rows, LANES)
    z_face = shaped(RADIUS + RADIUS // 2, rows, LANES)
    x_face = shaped(depth + depth // 2, RADIUS, LANES)
    faces_out = [z_face, z_face, x_face, x_face]

    packets = call(
        functools.partial(slot_kernel, span_y, tiles),
        shaped(tiles, LANES),
        [ids, residuals, owners, owners.reshape(1, -1), receivers.reshape(1, -1)],
    )
    strips = shaped(3 * depth * STRIP // LANES, rows, LANES)
    even, odd = call(strip_pack_kernel, [strips, strips], [ids, wave_now, older_wave, stiffness])

    packets = lax.all_to_all(packets, ("gx", "gy"), 0, 0, tiled=True)
    odd = swap(odd, "gy", 1)
    even = swap(even, "gy", 0)
    side, older_side, stiff_side, *faces = call(
        strip_unpack_kernel, [block] * 3 + faces_out, [ids, even, odd, wave_now]
    )
    packets = jnp.broadcast_to(packets[None], (span_z, tiles, LANES))
    packets = lax.all_to_all(packets, "gz", 0, 0, tiled=True).reshape(span_z * tiles, LANES)
    plane_out = shaped(STEPS, rows, LANES)
    plane, plane_side = call(
        functools.partial(plane_kernel, rows),
        [plane_out, plane_out],
        [ids, packets],
        scratch=[pltpu.VMEM((LANES, span_z * tiles), F32)],
    )

    scratch = [
        pltpu.VMEM((2, depth + 2 * RADIUS, rows, LANES), F32),
        pltpu.VMEM((2, depth, rows + 2 * RADIUS, LANES), F32),
        pltpu.VMEM((depth * rows, 2 * LANES), F32),
    ]
    wave, older = wave_now, older_wave
    image = None
    for step in range(STEPS):
        faces = exchange(faces)
        ins = [ids, *faces, wave, side, older, older_side, stiffness, stiff_side, forward_wave,
               plane, plane_side, band_high, band_low]
        if step:
            ins.append(image)
        outs = [block, block]
        if step < STEPS - 1:
            outs += [block] + faces_out
        image, fresh, *rest = call(functools.partial(step_kernel, step), outs, ins, scratch)
        older, wave = wave, fresh
        if step < STEPS - 1:
            older_side, side = side, rest[0]
            faces = rest[1:]
    return image, older, wave


def solution(mesh):
    in_specs = (
        P("gz", "gx", "gy"),
        P("gz", "gx", "gy"),
        P("gz", "gx", "gy"),
        P(None, "gz", "gx", "gy"),
        P(None, ("gx", "gy", "gz")),
        P(("gx", "gy", "gz"), None),
        P(("gx", "gy", "gz")),
        P(),
    )
    out_specs = (P("gz", "gx", "gy"), P("gz", "gx", "gy"), P("gz", "gx", "gy"))
    return jax.shard_map(
        on_device, mesh=mesh, in_specs=in_specs, out_specs=out_specs, check_vma=False
    )
```

time: 411 us -> 111 us (0.27)
  the two profiles are of different devices: /device:TPU:1 before, /device:TPU:27 now
where the time goes in v1:
time: 111 us; the launch traced here: 110 us
  starting transfers between devices  50.5 us (45%)
  blocking collectives  33.1 us (30%)
  Pallas kernels  11.4 us (10%)
  waiting for transfers between devices  8.87 us (8%)
  local copies, waits for them, and re-layouts  4.41 us (4%)
  between operations  1.58 us (1%)
    ppermute x14, starting transfers between devices, swap(): return lax.ppermute(block, axis, pairs)  43.3 us
    all_to_all x1, blocking collectives, on_device(): packets = lax.all_to_all(packets, ('gx', 'gy'), 0, 0, tiled=True)  24.7 us
    pallas_call x8, Pallas kernels, call(): pl.pallas_call(body, out_shape=outs, in_specs=in_specs or [smem()] + [vme...  11.4 us
    ppermute x14, waiting for transfers between devices, swap(): return lax.ppermute(block, axis, pairs)  8.86 us
    all_gather x4, blocking collectives, exchange(): lax.all_gather(z_even, 'gz', axis=0, tiled=False, axis_index_groups=groups)  8.33 us
    all_to_all x1, starting transfers between devices, on_device(): lax.all_to_all(packets, 'gz', 0, 0, tiled=True)  7.27 us
    unnamed x27, local copies, waits for them, and re-layouts  3.61 us
  transfers between devices with their start and end apart: 15, of which 4 were waited for; matrix products, arithmetic and copies ran while one was open for 1% of the time, Pallas kernels for 2%

profile of v1, /device:TPU:27, one launch (start us, length us, event | category | flops | bytes accessed | tf_op | source)
XLA Modules:
  0.0 109.9 jit_solution(14508320488968548066)
XLA Ops:
  5.0 5.8 %collective-permute-start = (f32[12,24,128]{2,1,0:T(8,128)S(1)}, f32[12,24,128]{2,1,0:T(8,128)S(1)}, u32[]{:S(2)}, u32[]{:S(2)}) collective-permute-start(f32[12,24,128]{2,1,0:T(8,128)S(1)} %get-tuple-element.37), channel_id=1, source_target_pairs={{0,8},{8,0},{16,24},{24,16},{1,9},{9,1},{17,25},{25,17},{2,10},{10... | collective-permute-start | bytes 442376 | tf_op jit(solution)/shard_map/ppermute | solution.py:351
  13.3 24.7 %all_to_all.14 = f32[64,1,128]{2,1,0:T(1,128)S(1)} all-to-all(f32[64,1,128]{2,1,0:T(1,128)S(1)} %bitcast.26), channel_id=1, replica_groups=mesh['gx'=16,'gy'=4,'gz'=8] {'gx','gy'}, dimensions={0} | all-to-all | bytes 65536 | tf_op jit(solution)/shard_map/all_to_all | solution.py:395
  38.7 7.3 %all-to-all-start.1 = ((f32[8,64,128]{2,1,0:T(8,128)}), f32[8,64,128]{2,1,0:T(8,128)S(1)}, u32[]{:S(2)}, u32[]{:S(2)}) async-start(f32[8,64,128]{2,1,0:T(8,128)} %broadcast_in_dim.9), calls=%async_computation.1 | async-start | bytes 524288 | tf_op jit(solution)/shard_map/all_to_all | solution.py:402
  46.9 3.5 %collective-permute-start.2 = (f32[12,24,128]{2,1,0:T(8,128)S(1)}, f32[12,24,128]{2,1,0:T(8,128)S(1)}, u32[]{:S(2)}, u32[]{:S(2)}) collective-permute-start(f32[12,24,128]{2,1,0:T(8,128)S(1)} %get-tuple-element.40), channel_id=1, source_target_pairs={{1,2},{2,1},{3,4},{4,3},{5,6},{6,5},{9,10},{10,9},{11,12},{12,11},... | collective-permute-start | bytes 442376 | tf_op jit(solution)/shard_map/ppermute | solution.py:351
  50.4 2.2 %collective-permute-start.3 = (f32[24,8,128]{2,1,0:T(8,128)S(1)}, f32[24,8,128]{2,1,0:T(8,128)S(1)}, u32[]{:S(2)}, u32[]{:S(2)}) collective-permute-start(f32[24,8,128]{2,1,0:T(8,128)S(1)} %get-tuple-element.41), channel_id=1, source_target_pairs={{0,32},{32,0},{64,96},{96,64},{128,160},{160,128},{192,224},{224,1... | collective-permute-start | bytes 294920 | tf_op jit(solution)/shard_map/ppermute | solution.py:351
  52.6 3.9 %collective-permute-start.4 = (f32[24,8,128]{2,1,0:T(8,128)S(1)}, f32[24,8,128]{2,1,0:T(8,128)S(1)}, u32[]{:S(2)}, u32[]{:S(2)}) collective-permute-start(f32[24,8,128]{2,1,0:T(8,128)S(1)} %get-tuple-element.42), channel_id=1, source_target_pairs={{32,64},{64,32},{96,128},{128,96},{160,192},{192,160},{224,256},{2... | collective-permute-start | bytes 294920 | tf_op jit(solution)/shard_map/ppermute | solution.py:351
  56.6 2.1 %all-gather = f32[24,24,128]{2,1,0:T(8,128)S(1)} all-gather(f32[12,24,128]{2,1,0:T(8,128)S(1)} %get-tuple-element.39), channel_id=2, replica_groups={{0,1},{2,3},{4,5},{6,7},{8,9},{10,11},{12,13},{14,15},{16,17},{18,19},{..., dimensions={0}, use_global_device_ids=true | all-gather | bytes 442368 | tf_op jit(solution)/shard_map/all_gather | solution.py:361
  61.7 3.5 %collective-permute-start.5 = (f32[12,24,128]{2,1,0:T(8,128)S(1)}, f32[12,24,128]{2,1,0:T(8,128)S(1)}, u32[]{:S(2)}, u32[]{:S(2)}) collective-permute-start(f32[12,24,128]{2,1,0:T(8,128)S(1)} %get-tuple-element.49), channel_id=1, source_target_pairs={{1,2},{2,1},{3,4},{4,3},{5,6},{6,5},{9,10},{10,9},{11,12},{12,11},... | collective-permute-start | bytes 442376 | tf_op jit(solution)/shard_map/ppermute | solution.py:351
  65.2 4.3 %collective-permute-start.6 = (f32[24,8,128]{2,1,0:T(8,128)S(1)}, f32[24,8,128]{2,1,0:T(8,128)S(1)}, u32[]{:S(2)}, u32[]{:S(2)}) collective-permute-start(f32[24,8,128]{2,1,0:T(8,128)S(1)} %get-tuple-element.50), channel_id=1, source_target_pairs={{0,32},{32,0},{64,96},{96,64},{128,160},{160,128},{192,224},{224,1... | collective-permute-start | bytes 294920 | tf_op jit(solution)/shard_map/ppermute | solution.py:351
  69.5 1.9 %collective-permute-start.7 = (f32[24,8,128]{2,1,0:T(8,128)S(1)}, f32[24,8,128]{2,1,0:T(8,128)S(1)}, u32[]{:S(2)}, u32[]{:S(2)}) collective-permute-start(f32[24,8,128]{2,1,0:T(8,128)S(1)} %get-tuple-element.51), channel_id=1, source_target_pairs={{32,64},{64,32},{96,128},{128,96},{160,192},{192,160},{224,256},{2... | collective-permute-start | bytes 294920 | tf_op jit(solution)/shard_map/ppermute | solution.py:351
  71.4 2.0 %all-gather.1 = f32[24,24,128]{2,1,0:T(8,128)S(1)} all-gather(f32[12,24,128]{2,1,0:T(8,128)S(1)} %get-tuple-element.48), channel_id=3, replica_groups={{0,1},{2,3},{4,5},{6,7},{8,9},{10,11},{12,13},{14,15},{16,17},{18,19},{..., dimensions={0}, use_global_device_ids=true | all-gather | bytes 442368 | tf_op jit(solution)/shard_map/all_gather | solution.py:361
  73.4 2.9 %collective-permute-done.7.x_odd_in = f32[24,8,128]{2,1,0:T(8,128)S(1)} collective-permute-done((f32[24,8,128]{2,1,0:T(8,128)S(1)}, f32[24,8,128]{2,1,0:T(8,128)S(1)}, u32[]{:S(2)}, u32[]{:S(2)}) %collective-permute-start.7) | collective-permute-done | bytes 98336 | tf_op jit(solution)/shard_map/ppermute | solution.py:351
  78.2 3.4 %collective-permute-start.8 = (f32[12,24,128]{2,1,0:T(8,128)S(1)}, f32[12,24,128]{2,1,0:T(8,128)S(1)}, u32[]{:S(2)}, u32[]{:S(2)}) collective-permute-start(f32[12,24,128]{2,1,0:T(8,128)S(1)} %get-tuple-element.56), channel_id=1, source_target_pairs={{1,2},{2,1},{3,4},{4,3},{5,6},{6,5},{9,10},{10,9},{11,12},{12,11},... | collective-permute-start | bytes 442376 | tf_op jit(solution)/shard_map/ppermute | solution.py:351
  81.5 3.1 %collective-permute-start.9 = (f32[24,8,128]{2,1,0:T(8,128)S(1)}, f32[24,8,128]{2,1,0:T(8,128)S(1)}, u32[]{:S(2)}, u32[]{:S(2)}) collective-permute-start(f32[24,8,128]{2,1,0:T(8,128)S(1)} %get-tuple-element.57), channel_id=1, source_target_pairs={{0,32},{32,0},{64,96},{96,64},{128,160},{160,128},{192,224},{224,1... | collective-permute-start | bytes 294920 | tf_op jit(solution)/shard_map/ppermute | solution.py:351
  84.7 1.9 %collective-permute-start.10 = (f32[24,8,128]{2,1,0:T(8,128)S(1)}, f32[24,8,128]{2,1,0:T(8,128)S(1)}, u32[]{:S(2)}, u32[]{:S(2)}) collective-permute-start(f32[24,8,128]{2,1,0:T(8,128)S(1)} %get-tuple-element.58), channel_id=1, source_target_pairs={{32,64},{64,32},{96,128},{128,96},{160,192},{192,160},{224,256},{2... | collective-permute-start | bytes 294920 | tf_op jit(solution)/shard_map/ppermute | solution.py:351
  86.6 2.0 %all-gather.2 = f32[24,24,128]{2,1,0:T(8,128)S(1)} all-gather(f32[12,24,128]{2,1,0:T(8,128)S(1)} %get-tuple-element.55), channel_id=4, replica_groups={{0,1},{2,3},{4,5},{6,7},{8,9},{10,11},{12,13},{14,15},{16,17},{18,19},{..., dimensions={0}, use_global_device_ids=true | all-gather | bytes 442368 | tf_op jit(solution)/shard_map/all_gather | solution.py:361
  88.6 2.6 %collective-permute-done.10.x_odd_in = f32[24,8,128]{2,1,0:T(8,128)S(1)} collective-permute-done((f32[24,8,128]{2,1,0:T(8,128)S(1)}, f32[24,8,128]{2,1,0:T(8,128)S(1)}, u32[]{:S(2)}, u32[]{:S(2)}) %collective-permute-start.10) | collective-permute-done | bytes 98336 | tf_op jit(solution)/shard_map/ppermute | solution.py:351
  91.2 2.5 %shard_map.127 = (f32[16,24,128]{2,1,0:T(8,128)S(1)}, f32[16,24,128]{2,1,0:T(8,128)}, f32[16,24,128]{2,1,0:T(8,128)S(1)}, f32[12,24,128]{2,1,0:T(8,128)S(1)}, f3...) custom-call(s32[5]{0:T(128)S(1)} %stack.23.ids, f32[2,12,24,128]{3,2,1,0:T(8,128)S(1)} %bitcast.22, ...), custom_call_target="tpu_custom_call" | custom-call | flops 1000000 | bytes 2000000 | tf_op jit(solution)/shard_map/pallas_call | solution.py:66
  93.7 3.5 %collective-permute-start.11 = (f32[12,24,128]{2,1,0:T(8,128)S(1)}, f32[12,24,128]{2,1,0:T(8,128)S(1)}, u32[]{:S(2)}, u32[]{:S(2)}) collective-permute-start(f32[12,24,128]{2,1,0:T(8,128)S(1)} %get-tuple-element.63), channel_id=1, source_target_pairs={{1,2},{2,1},{3,4},{4,3},{5,6},{6,5},{9,10},{10,9},{11,12},{12,11},... | collective-permute-start | bytes 442376 | tf_op jit(solution)/shard_map/ppermute | solution.py:351
  97.2 3.6 %collective-permute-start.12 = (f32[24,8,128]{2,1,0:T(8,128)S(1)}, f32[24,8,128]{2,1,0:T(8,128)S(1)}, u32[]{:S(2)}, u32[]{:S(2)}) collective-permute-start(f32[24,8,128]{2,1,0:T(8,128)S(1)} %get-tuple-element.64), channel_id=1, source_target_pairs={{0,32},{32,0},{64,96},{96,64},{128,160},{160,128},{192,224},{224,1... | collective-permute-start | bytes 294920 | tf_op jit(solution)/shard_map/ppermute | solution.py:351
  100.9 1.9 %collective-permute-start.13 = (f32[24,8,128]{2,1,0:T(8,128)S(1)}, f32[24,8,128]{2,1,0:T(8,128)S(1)}, u32[]{:S(2)}, u32[]{:S(2)}) collective-permute-start(f32[24,8,128]{2,1,0:T(8,128)S(1)} %get-tuple-element.65), channel_id=1, source_target_pairs={{32,64},{64,32},{96,128},{128,96},{160,192},{192,160},{224,256},{2... | collective-permute-start | bytes 294920 | tf_op jit(solution)/shard_map/ppermute | solution.py:351
  102.8 2.1 %all-gather.3 = f32[24,24,128]{2,1,0:T(8,128)S(1)} all-gather(f32[12,24,128]{2,1,0:T(8,128)S(1)} %get-tuple-element.62), channel_id=5, replica_groups={{0,1},{2,3},{4,5},{6,7},{8,9},{10,11},{12,13},{14,15},{16,17},{18,19},{..., dimensions={0}, use_global_device_ids=true | all-gather | bytes 442368 | tf_op jit(solution)/shard_map/all_gather | solution.py:361
  105.0 2.8 %collective-permute-done.13.x_odd_in = f32[24,8,128]{2,1,0:T(8,128)S(1)} collective-permute-done((f32[24,8,128]{2,1,0:T(8,128)S(1)}, f32[24,8,128]{2,1,0:T(8,128)S(1)}, u32[]{:S(2)}, u32[]{:S(2)}) %collective-permute-start.13) | collective-permute-done | bytes 98336 | tf_op jit(solution)/shard_map/ppermute | solution.py:351
  107.8 2.1 %shard_map.128 = (f32[16,24,128]{2,1,0:T(8,128)}, f32[16,24,128]{2,1,0:T(8,128)}) custom-call(s32[5]{0:T(128)S(1)} %stack.23.ids, f32[2,12,24,128]{3,2,1,0:T(8,128)S(1)} %bitcast.21, f32[12,24,128]{2,1,0:T(8,128)S(1)} %collective-permute-done.11.z_odd_in, f32[24,8,128]{2,1,0:T(8,128)S(1)} %collective-permute-done.12.x_even_in, ...), custom_call_target="tpu_custom_call" | custom-call | flops 1000000 | bytes 2000000 | tf_op jit(solution)/shard_map/pallas_call | solution.py:66
  (48 shorter events, 12.5 us)
Async XLA Ops:
  1.4 0.9 copy-start.1
  5.0 6.5 %copy-start.10 = (s32[128,1]{0,1:T(1,128)S(1)}, s32[128,1]{0,1:T(1,128)}, u32[]{:S(2)}) copy-start(s32[128,1]{0,1:T(1,128)} %param.15) | copy-start | bytes 1540
  5.0 41.0 %collective-permute-start = (f32[12,24,128]{2,1,0:T(8,128)S(1)}, f32[12,24,128]{2,1,0:T(8,128)S(1)}, u32[]{:S(2)}, u32[]{:S(2)}) collective-permute-start(f32[12,24,128]{2,1,0:T(8,128)S(1)} %get-tuple-element.37), channel_id=1, source_target_pairs={{0,8},{8,0},{16,24},{24,16},{1,9},{9,1},{17,25},{25,17},{2,10},{10... | collective-permute-start | bytes 442376 | tf_op jit(solution)/shard_map/ppermute | solution.py:351
  10.8 35.1 %collective-permute-start.1 = (f32[12,24,128]{2,1,0:T(8,128)S(1)}, f32[12,24,128]{2,1,0:T(8,128)S(1)}, u32[]{:S(2)}, u32[]{:S(2)}) collective-permute-start(f32[12,24,128]{2,1,0:T(8,128)S(1)} %get-tuple-element.38), channel_id=1, source_target_pairs={{8,16},{16,8},{9,17},{17,9},{10,18},{18,10},{11,19},{19,11},{12,20... | collective-permute-start | bytes 442376 | tf_op jit(solution)/shard_map/ppermute | solution.py:351
  38.7 7.3 %copy-start.4 = (f32[16,24,128]{2,1,0:T(8,128)S(1)}, f32[16,24,128]{2,1,0:T(8,128)}, u32[]{:S(2)}) copy-start(f32[16,24,128]{2,1,0:T(8,128)} %older.5) | copy-start | bytes 589828
  38.7 20.0 %all-to-all-start.1 = ((f32[8,64,128]{2,1,0:T(8,128)}), f32[8,64,128]{2,1,0:T(8,128)S(1)}, u32[]{:S(2)}, u32[]{:S(2)}) async-start(f32[8,64,128]{2,1,0:T(8,128)} %broadcast_in_dim.9), calls=%async_computation.1 | async-start | bytes 524288 | tf_op jit(solution)/shard_map/all_to_all | solution.py:402
  46.0 13.8 %copy-start.6 = (bf16[256,256]{1,0:T(8,128)(2,1)S(1)}, bf16[256,256]{1,0:T(8,128)(2,1)}, u32[]{:S(2)}) copy-start(bf16[256,256]{1,0:T(8,128)(2,1)} %constant.44.clone.band_high) | copy-start | bytes 393220
  46.0 13.8 %copy-start.8 = (f32[16,24,128]{2,1,0:T(8,128)S(1)}, f32[16,24,128]{2,1,0:T(8,128)}, u32[]{:S(2)}) copy-start(f32[16,24,128]{2,1,0:T(8,128)} %older.4) | copy-start | bytes 589828
  46.9 12.9 %copy-start = (bf16[4,16,24,128]{3,2,1,0:T(8,128)(2,1)S(1)}, bf16[4,16,24,128]{3,2,1,0:T(8,128)(2,1)}, u32[]{:S(2)}) copy-start(bf16[4,16,24,128]{3,2,1,0:T(8,128)(2,1)} %forward.7) | copy-start | bytes 1179652
  46.9 12.9 %collective-permute-start.2 = (f32[12,24,128]{2,1,0:T(8,128)S(1)}, f32[12,24,128]{2,1,0:T(8,128)S(1)}, u32[]{:S(2)}, u32[]{:S(2)}) collective-permute-start(f32[12,24,128]{2,1,0:T(8,128)S(1)} %get-tuple-element.40), channel_id=1, source_target_pairs={{1,2},{2,1},{3,4},{4,3},{5,6},{6,5},{9,10},{10,9},{11,12},{12,11},... | collective-permute-start | bytes 442376 | tf_op jit(solution)/shard_map/ppermute | solution.py:351
  50.4 8.9 %collective-permute-start.3 = (f32[24,8,128]{2,1,0:T(8,128)S(1)}, f32[24,8,128]{2,1,0:T(8,128)S(1)}, u32[]{:S(2)}, u32[]{:S(2)}) collective-permute-start(f32[24,8,128]{2,1,0:T(8,128)S(1)} %get-tuple-element.41), channel_id=1, source_target_pairs={{0,32},{32,0},{64,96},{96,64},{128,160},{160,128},{192,224},{224,1... | collective-permute-start | bytes 294920 | tf_op jit(solution)/shard_map/ppermute | solution.py:351
  52.6 7.2 %collective-permute-start.4 = (f32[24,8,128]{2,1,0:T(8,128)S(1)}, f32[24,8,128]{2,1,0:T(8,128)S(1)}, u32[]{:S(2)}, u32[]{:S(2)}) collective-permute-start(f32[24,8,128]{2,1,0:T(8,128)S(1)} %get-tuple-element.42), channel_id=1, source_target_pairs={{32,64},{64,32},{96,128},{128,96},{160,192},{192,160},{224,256},{2... | collective-permute-start | bytes 294920 | tf_op jit(solution)/shard_map/ppermute | solution.py:351
  56.5 3.3 %copy-start.5 = (bf16[256,256]{1,0:T(8,128)(2,1)S(1)}, bf16[256,256]{1,0:T(8,128)(2,1)}, u32[]{:S(2)}) copy-start(bf16[256,256]{1,0:T(8,128)(2,1)} %constant.45.clone.band_low) | copy-start | bytes 393220
  58.7 1.1 %copy-start.2 = (f32[16,24,128]{2,1,0:T(8,128)S(1)}, f32[16,24,128]{2,1,0:T(8,128)}, u32[]{:S(2)}) copy-start(f32[16,24,128]{2,1,0:T(8,128)} %stiff.9) | copy-start | bytes 589828
  61.7 14.6 %collective-permute-start.5 = (f32[12,24,128]{2,1,0:T(8,128)S(1)}, f32[12,24,128]{2,1,0:T(8,128)S(1)}, u32[]{:S(2)}, u32[]{:S(2)}) collective-permute-start(f32[12,24,128]{2,1,0:T(8,128)S(1)} %get-tuple-element.49), channel_id=1, source_target_pairs={{1,2},{2,1},{3,4},{4,3},{5,6},{6,5},{9,10},{10,9},{11,12},{12,11},... | collective-permute-start | bytes 442376 | tf_op jit(solution)/shard_map/ppermute | solution.py:351
  65.2 8.2 %collective-permute-start.6 = (f32[24,8,128]{2,1,0:T(8,128)S(1)}, f32[24,8,128]{2,1,0:T(8,128)S(1)}, u32[]{:S(2)}, u32[]{:S(2)}) collective-permute-start(f32[24,8,128]{2,1,0:T(8,128)S(1)} %get-tuple-element.50), channel_id=1, source_target_pairs={{0,32},{32,0},{64,96},{96,64},{128,160},{160,128},{192,224},{224,1... | collective-permute-start | bytes 294920 | tf_op jit(solution)/shard_map/ppermute | solution.py:351
  69.5 6.8 %collective-permute-start.7 = (f32[24,8,128]{2,1,0:T(8,128)S(1)}, f32[24,8,128]{2,1,0:T(8,128)S(1)}, u32[]{:S(2)}, u32[]{:S(2)}) collective-permute-start(f32[24,8,128]{2,1,0:T(8,128)S(1)} %get-tuple-element.51), channel_id=1, source_target_pairs={{32,64},{64,32},{96,128},{128,96},{160,192},{192,160},{224,256},{2... | collective-permute-start | bytes 294920 | tf_op jit(solution)/shard_map/ppermute | solution.py:351
  78.2 13.0 %collective-permute-start.8 = (f32[12,24,128]{2,1,0:T(8,128)S(1)}, f32[12,24,128]{2,1,0:T(8,128)S(1)}, u32[]{:S(2)}, u32[]{:S(2)}) collective-permute-start(f32[12,24,128]{2,1,0:T(8,128)S(1)} %get-tuple-element.56), channel_id=1, source_target_pairs={{1,2},{2,1},{3,4},{4,3},{5,6},{6,5},{9,10},{10,9},{11,12},{12,11},... | collective-permute-start | bytes 442376 | tf_op jit(solution)/shard_map/ppermute | solution.py:351
  81.5 7.1 %collective-permute-start.9 = (f32[24,8,128]{2,1,0:T(8,128)S(1)}, f32[24,8,128]{2,1,0:T(8,128)S(1)}, u32[]{:S(2)}, u32[]{:S(2)}) collective-permute-start(f32[24,8,128]{2,1,0:T(8,128)S(1)} %get-tuple-element.57), channel_id=1, source_target_pairs={{0,32},{32,0},{64,96},{96,64},{128,160},{160,128},{192,224},{224,1... | collective-permute-start | bytes 294920 | tf_op jit(solution)/shard_map/ppermute | solution.py:351
  84.7 6.5 %collective-permute-start.10 = (f32[24,8,128]{2,1,0:T(8,128)S(1)}, f32[24,8,128]{2,1,0:T(8,128)S(1)}, u32[]{:S(2)}, u32[]{:S(2)}) collective-permute-start(f32[24,8,128]{2,1,0:T(8,128)S(1)} %get-tuple-element.58), channel_id=1, source_target_pairs={{32,64},{64,32},{96,128},{128,96},{160,192},{192,160},{224,256},{2... | collective-permute-start | bytes 294920 | tf_op jit(solution)/shard_map/ppermute | solution.py:351
  93.7 14.1 %collective-permute-start.11 = (f32[12,24,128]{2,1,0:T(8,128)S(1)}, f32[12,24,128]{2,1,0:T(8,128)S(1)}, u32[]{:S(2)}, u32[]{:S(2)}) collective-permute-start(f32[12,24,128]{2,1,0:T(8,128)S(1)} %get-tuple-element.63), channel_id=1, source_target_pairs={{1,2},{2,1},{3,4},{4,3},{5,6},{6,5},{9,10},{10,9},{11,12},{12,11},... | collective-permute-start | bytes 442376 | tf_op jit(solution)/shard_map/ppermute | solution.py:351
  97.2 7.7 %collective-permute-start.12 = (f32[24,8,128]{2,1,0:T(8,128)S(1)}, f32[24,8,128]{2,1,0:T(8,128)S(1)}, u32[]{:S(2)}, u32[]{:S(2)}) collective-permute-start(f32[24,8,128]{2,1,0:T(8,128)S(1)} %get-tuple-element.64), channel_id=1, source_target_pairs={{0,32},{32,0},{64,96},{96,64},{128,160},{160,128},{192,224},{224,1... | collective-permute-start | bytes 294920 | tf_op jit(solution)/shard_map/ppermute | solution.py:351
  100.9 6.9 %collective-permute-start.13 = (f32[24,8,128]{2,1,0:T(8,128)S(1)}, f32[24,8,128]{2,1,0:T(8,128)S(1)}, u32[]{:S(2)}, u32[]{:S(2)}) collective-permute-start(f32[24,8,128]{2,1,0:T(8,128)S(1)} %get-tuple-element.65), channel_id=1, source_target_pairs={{32,64},{64,32},{96,128},{128,96},{160,192},{192,160},{224,256},{2... | collective-permute-start | bytes 294920 | tf_op jit(solution)/shard_map/ppermute | solution.py:351
  102.8 5.0 %copy-start.9 = (f32[16,24,128]{2,1,0:T(8,128)S(1)}, f32[16,24,128]{2,1,0:T(8,128)}, u32[]{:S(2)}) copy-start(f32[16,24,128]{2,1,0:T(8,128)} %get-tuple-element.35.wave) | copy-start | bytes 589828
  (4 other events, 3.2 us)

commit v2 on v1

--- a/solution.py
+++ b/solution.py
@@ -125,14 +125,17 @@
     out[...] = total
 
 
-def plane_kernel(rows, ids, packets, main, side, turned):
+def plane_kernel(rows, ids, *refs):
+    *packets, main, side, turned = refs
     main[...] = jnp.zeros(main.shape, F32)
     side[...] = jnp.zeros(side.shape, F32)
 
     @pl.when(ids[0] == 0)
     def _():
-        turned[...] = jnp.transpose(packets[...])
-        count = packets.shape[0]
+        count = turned.shape[1]
+        share = count // len(packets)
+        for number, packet in enumerate(packets):
+            turned[:, share * number : share * (number + 1)] = jnp.transpose(packet[...])
         line = lax.broadcasted_iota(jnp.int32, (rows, count), 0)
         spot = lax.broadcasted_iota(jnp.int32, (LANES, count), 0)
 
@@ -177,31 +180,64 @@
             odd[place] = jnp.where(parity == 0, lows, highs)
 
 
-def fold(first, second):
-    return first + pltpu.roll(second, LANES // 2, 1)
-
-
-def write_faces(ids, main, side, z_even, z_odd, x_even, x_odd):
+def strip_width(step):
+    return {0: STRIP, 1: STRIP // 2, 2: STRIP // 4}.get(step, 0)
+
+
+def folds(width):
+    return LANES // (2 * width) if width else 0
+
+
+def folded(length, width):
+    return length // folds(width) if width else 0
+
+
+def kept_lanes(shape, width):
+    lane = lane_of(shape)
+    return (lane < width) | (lane >= LANES - width)
+
+
+def fold(pieces, width):
+    total = None
+    for turn, piece in enumerate(pieces):
+        piece = jnp.where(kept_lanes(piece.shape, width), piece, 0.0)
+        if turn:
+            piece = pltpu.roll(piece, 2 * width * turn, 1)
+        total = piece if total is None else total + piece
+    return total
+
+
+def unfold(both, turn, width):
+    if turn:
+        both = pltpu.roll(both, LANES - 2 * width * turn, 1)
+    return jnp.where(kept_lanes(both.shape, width), both, 0.0)
+
+
+def write_faces(width, ids, main, side, z_even, z_odd, x_even, x_odd):
     z_parity, x_parity = ids[0] & 1, ids[1] & 1
     depth, rows, _ = main.shape
-    half = RADIUS // 2
+    count = folds(width)
     for face, start in (
         (z_even, (depth - RADIUS) * (1 - z_parity)),
         (z_odd, (depth - RADIUS) * z_parity),
     ):
         face[pl.ds(0, RADIUS)] = main[pl.ds(start, RADIUS)]
-        for plane in range(half):
-            face[RADIUS + plane] = fold(side[start + plane], side[start + half + plane])
+        span = folded(RADIUS, width)
+        for plane in range(span):
+            face[RADIUS + plane] = fold(
+                [side[start + plane + span * turn] for turn in range(count)], width
+            )
     for face, start in (
         (x_even, (rows - RADIUS) * (1 - x_parity)),
         (x_odd, (rows - RADIUS) * x_parity),
     ):
         start = pl.multiple_of(start, RADIUS)
         face[pl.ds(0, depth)] = main[:, pl.ds(start, RADIUS), :]
-        for plane in range(depth // 2):
+        span = folded(depth, width)
+        for plane in range(span):
             face[depth + plane] = fold(
-                side[plane, pl.ds(start, RADIUS), :],
-                side[plane + depth // 2, pl.ds(start, RADIUS), :],
+                [side[plane + span * turn, pl.ds(start, RADIUS), :] for turn in range(count)],
+                width,
             )
 
 
@@ -224,18 +260,14 @@
                 side[quarters * chunk + turn] = jnp.where(
                     from_even, first, jnp.where(from_odd, second, 0.0)
                 )
-    write_faces(ids, wave, wave_side, z_even, z_odd, x_even, x_odd)
-
-
-def fill(ids, wave, side, z_even, z_odd, x_even, x_odd, z_ext, x_ext):
+    write_faces(STRIP, ids, wave, wave_side, z_even, z_odd, x_even, x_odd)
+
+
+def fill(width, ids, wave, side, z_even, z_odd, x_even, x_odd, z_ext, x_ext):
     z_parity, x_parity = ids[0] & 1, ids[1] & 1
     depth, rows, _ = wave.shape
-    half = RADIUS // 2
-    outer = lane_of((RADIUS, LANES))
-    kept = (outer < STRIP) | (outer >= LANES - STRIP)
-    kept_plane = lane_of((rows, LANES))
-    kept_plane = (kept_plane < STRIP) | (kept_plane >= LANES - STRIP)
-    for part, field in enumerate((wave, side)):
+    count = folds(width)
+    for part, field in enumerate((wave, side) if width else (wave,)):
         z_ext[part, pl.ds(RADIUS, depth)] = field[...]
         x_ext[part, :, pl.ds(RADIUS, rows), :] = field[...]
     pair = z_even.at[1 - z_parity]
@@ -244,24 +276,22 @@
         (z_odd, (depth + RADIUS) * z_parity),
     ):
         z_ext[0, pl.ds(start, RADIUS)] = face[pl.ds(0, RADIUS)]
-        for plane in range(half):
+        span = folded(RADIUS, width)
+        for plane in range(span):
             both = face[RADIUS + plane]
-            z_ext[1, start + plane] = jnp.where(kept_plane, both, 0.0)
-            z_ext[1, start + half + plane] = jnp.where(
-                kept_plane, pltpu.roll(both, LANES // 2, 1), 0.0
-            )
+            for turn in range(count):
+                z_ext[1, start + plane + span * turn] = unfold(both, turn, width)
     for face, start in (
         (x_even, (rows + RADIUS) * (1 - x_parity)),
         (x_odd, (rows + RADIUS) * x_parity),
     ):
         start = pl.multiple_of(start, RADIUS)
         x_ext[0, :, pl.ds(start, RADIUS), :] = face[pl.ds(0, depth)]
-        for plane in range(depth // 2):
+        span = folded(depth, width)
+        for plane in range(span):
             both = face[depth + plane]
-            x_ext[1, plane, pl.ds(start, RADIUS), :] = jnp.where(kept, both, 0.0)
-            x_ext[1, plane + depth // 2, pl.ds(start, RADIUS), :] = jnp.where(
-                kept, pltpu.roll(both, LANES // 2, 1), 0.0
-            )
+            for turn in range(count):
+                x_ext[1, plane + span * turn, pl.ds(start, RADIUS), :] = unfold(both, turn, width)
 
 
 def advance(step, ids, refs, wave, side, older, older_side, stiff, stiff_side, forward, image_in,
@@ -323,7 +353,7 @@
     return jnp.minimum(1.0, distance / 576.0)
 
 
-def step_kernel(step, ids, z_even_in, z_odd_in, x_even_in, x_odd_in, wave, side, older,
+def step_kernel(step, ids, x_odd_in, x_even_in, z_odd_in, z_even_in, wave, side, older,
                 older_side, stiff, stiff_side, forward, plane, plane_side, band_high, band_low,
                 *rest):
     image_in = None
@@ -335,12 +365,12 @@
         fresh_side = None
     else:
         (image, fresh, fresh_side, z_even, z_odd, x_even, x_odd, z_ext, x_ext, y_terms) = rest
-    fill(ids, wave, side, z_even_in, z_odd_in, x_even_in, x_odd_in, z_ext, x_ext)
+    fill(strip_width(step), ids, wave, side, z_even_in, z_odd_in, x_even_in, x_odd_in, z_ext, x_ext)
     advance(step, ids, None, wave, side, older, older_side, stiff, stiff_side, forward, image_in,
             plane, plane_side, band_high, band_low, fresh, fresh_side, image, z_ext, x_ext,
             y_terms)
     if not last:
-        write_faces(ids, fresh, fresh_side, z_even, z_odd, x_even, x_odd)
+        write_faces(strip_width(step + 1), ids, fresh, fresh_side, z_even, z_odd, x_even, x_odd)
 
 
 def swap(block, axis, parity):
@@ -351,13 +381,17 @@
     return lax.ppermute(block, axis, pairs)
 
 
+def core_pairs(count):
+    return [[2 * chip, 2 * chip + 1] for chip in range(count // 2)]
+
+
 def exchange(faces):
     z_even, z_odd, x_even, x_odd = faces
     count = lax.axis_size("gz")
-    groups = [[2 * chip, 2 * chip + 1] for chip in range(count // 2)]
+    groups = core_pairs(count)
+    z_odd = swap(z_odd, "gz", 1)
+    x_even = swap(x_even, "gx", 0)
     x_odd = swap(x_odd, "gx", 1)
-    x_even = swap(x_even, "gx", 0)
-    z_odd = swap(z_odd, "gz", 1)
     z_even = lax.all_gather(z_even, "gz", axis=0, tiled=False, axis_index_groups=groups)
     return z_even, z_odd, x_even, x_odd
 
@@ -380,31 +414,39 @@
     ).astype(jnp.int32)
     band_high, band_low = (jnp.asarray(part) for part in band())
     block = shaped(depth, rows, LANES)
-    z_face = shaped(RADIUS + RADIUS // 2, rows, LANES)
-    x_face = shaped(depth + depth // 2, RADIUS, LANES)
-    faces_out = [z_face, z_face, x_face, x_face]
+
+    def faces_out(step):
+        width = strip_width(step)
+        z_face = shaped(RADIUS + folded(RADIUS, width), rows, LANES)
+        x_face = shaped(depth + folded(depth, width), RADIUS, LANES)
+        return [z_face, z_face, x_face, x_face]
 
     packets = call(
         functools.partial(slot_kernel, span_y, tiles),
         shaped(tiles, LANES),
         [ids, residuals, owners, owners.reshape(1, -1), receivers.reshape(1, -1)],
     )
+    packets = lax.all_to_all(packets, ("gx", "gy"), 0, 0, tiled=True)
+    ids, packets = lax.optimization_barrier((ids, packets))
     strips = shaped(3 * depth * STRIP // LANES, rows, LANES)
     even, odd = call(strip_pack_kernel, [strips, strips], [ids, wave_now, older_wave, stiffness])
 
-    packets = lax.all_to_all(packets, ("gx", "gy"), 0, 0, tiled=True)
     odd = swap(odd, "gy", 1)
     even = swap(even, "gy", 0)
     side, older_side, stiff_side, *faces = call(
-        strip_unpack_kernel, [block] * 3 + faces_out, [ids, even, odd, wave_now]
-    )
-    packets = jnp.broadcast_to(packets[None], (span_z, tiles, LANES))
-    packets = lax.all_to_all(packets, "gz", 0, 0, tiled=True).reshape(span_z * tiles, LANES)
+        strip_unpack_kernel, [block] * 3 + faces_out(0), [ids, even, odd, wave_now]
+    )
+    packets = lax.all_gather(
+        packets, "gz", axis=0, tiled=True, axis_index_groups=core_pairs(span_z)
+    )
+    packets = [packets] + [
+        lax.ppermute(packets, "gz", [(layer, 0)]) for layer in range(2, span_z, 2)
+    ]
     plane_out = shaped(STEPS, rows, LANES)
     plane, plane_side = call(
         functools.partial(plane_kernel, rows),
         [plane_out, plane_out],
-        [ids, packets],
+        [ids, *packets],
         scratch=[pltpu.VMEM((LANES, span_z * tiles), F32)],
     )
 
@@ -417,13 +459,13 @@
     image = None
     for step in range(STEPS):
         faces = exchange(faces)
-        ins = [ids, *faces, wave, side, older, older_side, stiffness, stiff_side, forward_wave,
+        ins = [ids, *faces[::-1], wave, side, older, older_side, stiffness, stiff_side, forward_wave,
                plane, plane_side, band_high, band_low]
         if step:
             ins.append(image)
         outs = [block, block]
         if step < STEPS - 1:
-            outs += [block] + faces_out
+            outs += [block] + faces_out(step + 1)
         image, fresh, *rest = call(functools.partial(step_kernel, step), outs, ins, scratch)
         older, wave = wave, fresh
         if step < STEPS - 1:

time: 111 us -> 108 us (0.973)
  the two profiles are of different devices: /device:TPU:27 before, /device:TPU:1 now
where the time goes in v2:
time: 108 us; the launch traced here: 107 us
  starting transfers between devices  44.9 us (42%)
  blocking collectives  40.6 us (38%)
  Pallas kernels  11.5 us (11%)
  local copies, waits for them, and re-layouts  4.73 us (4%)
  waiting for transfers between devices  3.34 us (3%)
  between operations  1.66 us (2%)
    ppermute x14, starting transfers between devices, swap(): return lax.ppermute(block, axis, pairs)  42.9 us
    all_to_all x1, blocking collectives, on_device(): packets = lax.all_to_all(packets, ('gx', 'gy'), 0, 0, tiled=True)  27.8 us
    pallas_call x8, Pallas kernels, call(): pl.pallas_call(body, out_shape=outs, in_specs=in_specs or [smem()] + [vme...  11.5 us
    all_gather x4, blocking collectives, exchange(): lax.all_gather(z_even, 'gz', axis=0, tiled=False, axis_index_groups=groups)  8.88 us
    unnamed x25, local copies, waits for them, and re-layouts  4.64 us
    all_gather x1, blocking collectives, on_device(): lax.all_gather(packets, 'gz', axis=0, tiled=True, axis_index_groups=core_...  3.89 us
    ppermute x14, waiting for transfers between devices, swap(): return lax.ppermute(block, axis, pairs)  3.33 us
  transfers between devices with their start and end apart: 17, of which 1 were waited for; matrix products, arithmetic and copies ran while one was open for 0% of the time, Pallas kernels for 1%

profile of v2, /device:TPU:1, one launch (start us, length us, event | category | flops | bytes accessed | tf_op | source)
XLA Modules:
  0.0 106.7 jit_solution(17645902087898892609)
XLA Ops:
  4.2 0.9 shard_map.121
  5.1 27.8 %all_to_all.12 = f32[64,1,128]{2,1,0:T(1,128)S(1)} all-to-all(f32[64,1,128]{2,1,0:T(1,128)S(1)} %bitcast.24), channel_id=1, replica_groups=mesh['gx'=16,'gy'=4,'gz'=8] {'gx','gy'}, dimensions={0} | all-to-all | bytes 65536 | tf_op jit(solution)/shard_map/all_to_all | solution.py:429
  33.0 0.9 copy-done.2
  33.9 0.9 copy-done.6
  35.7 2.2 %collective-permute-start = (f32[12,24,128]{2,1,0:T(8,128)S(1)}, f32[12,24,128]{2,1,0:T(8,128)S(1)}, u32[]{:S(2)}, u32[]{:S(2)}) collective-permute-start(f32[12,24,128]{2,1,0:T(8,128)S(1)} %get-tuple-element.40), channel_id=1, source_target_pairs={{0,8},{8,0},{16,24},{24,16},{1,9},{9,1},{17,25},{25,17},{2,10},{10... | collective-permute-start | bytes 442376 | tf_op jit(solution)/shard_map/ppermute | solution.py:381
  38.6 3.9 %all_gather.29.refs_0_ = f32[128,128]{1,0:T(8,128)S(1)} all-gather(f32[64,128]{1,0:T(8,128)S(1)} %bitcast.27), channel_id=1, replica_groups={{0,1},{2,3},{4,5},{6,7},{8,9},{10,11},{12,13},{14,15},{16,17},{18,19},{..., dimensions={0}, use_global_device_ids=true | all-gather | bytes 98304 | tf_op jit(solution)/shard_map/all_gather | solution.py:439
  43.2 3.3 %collective-permute-done.even = f32[12,24,128]{2,1,0:T(8,128)S(1)} collective-permute-done((f32[12,24,128]{2,1,0:T(8,128)S(1)}, f32[12,24,128]{2,1,0:T(8,128)S(1)}, u32[]{:S(2)}, u32[]{:S(2)}) %collective-permute-start) | collective-permute-done | bytes 147488 | tf_op jit(solution)/shard_map/ppermute | solution.py:381
  46.5 0.9 shard_map.123
  47.4 4.6 %collective-permute-start.4 = (f32[12,24,128]{2,1,0:T(8,128)S(1)}, f32[12,24,128]{2,1,0:T(8,128)S(1)}, u32[]{:S(2)}, u32[]{:S(2)}) collective-permute-start(f32[12,24,128]{2,1,0:T(8,128)S(1)} %get-tuple-element.44), channel_id=1, source_target_pairs={{1,2},{2,1},{3,4},{4,3},{5,6},{6,5},{9,10},{10,9},{11,12},{12,11},... | collective-permute-start | bytes 442376 | tf_op jit(solution)/shard_map/ppermute | solution.py:381
  54.0 4.7 %collective-permute-start.3 = (f32[24,8,128]{2,1,0:T(8,128)S(1)}, f32[24,8,128]{2,1,0:T(8,128)S(1)}, u32[]{:S(2)}, u32[]{:S(2)}) collective-permute-start(f32[24,8,128]{2,1,0:T(8,128)S(1)} %get-tuple-element.43), channel_id=1, source_target_pairs={{0,32},{32,0},{64,96},{96,64},{128,160},{160,128},{192,224},{224,1... | collective-permute-start | bytes 294920 | tf_op jit(solution)/shard_map/ppermute | solution.py:381
  59.3 3.0 %all-gather = f32[24,24,128]{2,1,0:T(8,128)S(1)} all-gather(f32[12,24,128]{2,1,0:T(8,128)S(1)} %get-tuple-element.45), channel_id=2, replica_groups={{0,1},{2,3},{4,5},{6,7},{8,9},{10,11},{12,13},{14,15},{16,17},{18,19},{..., dimensions={0}, use_global_device_ids=true | all-gather | bytes 442368 | tf_op jit(solution)/shard_map/all_gather | solution.py:395
  62.3 1.9 %shard_map.125 = (f32[16,24,128]{2,1,0:T(8,128)S(1)}, f32[16,24,128]{2,1,0:T(8,128)S(1)}, f32[16,24,128]{2,1,0:T(8,128)S(1)}, f32[10,24,128]{2,1,0:T(8,128)S(1)}...) custom-call(s32[5]{0:T(128)S(1)} %stack.23.ids, ...), custom_call_target="tpu_custom_call" | custom-call | flops 1000000 | bytes 2000000 | tf_op jit(solution)/shard_map/pallas_call | solution.py:66
  64.2 3.1 %collective-permute-start.10 = (f32[10,24,128]{2,1,0:T(8,128)S(1)}, f32[10,24,128]{2,1,0:T(8,128)S(1)}, u32[]{:S(2)}, u32[]{:S(2)}) collective-permute-start(f32[10,24,128]{2,1,0:T(8,128)S(1)} %get-tuple-element.54), channel_id=1, source_target_pairs={{1,2},{2,1},{3,4},{4,3},{5,6},{6,5},{9,10},{10,9},{11,12},{12,11},... | collective-permute-start | bytes 368648 | tf_op jit(solution)/shard_map/ppermute | solution.py:381
  68.0 5.7 %collective-permute-start.9 = (f32[20,8,128]{2,1,0:T(8,128)S(1)}, f32[20,8,128]{2,1,0:T(8,128)S(1)}, u32[]{:S(2)}, u32[]{:S(2)}) collective-permute-start(f32[20,8,128]{2,1,0:T(8,128)S(1)} %get-tuple-element.53), channel_id=1, source_target_pairs={{0,32},{32,0},{64,96},{96,64},{128,160},{160,128},{192,224},{224,1... | collective-permute-start | bytes 245768 | tf_op jit(solution)/shard_map/ppermute | solution.py:381
  73.7 2.0 %all-gather.1 = f32[20,24,128]{2,1,0:T(8,128)S(1)} all-gather(f32[10,24,128]{2,1,0:T(8,128)S(1)} %get-tuple-element.55), channel_id=3, replica_groups={{0,1},{2,3},{4,5},{6,7},{8,9},{10,11},{12,13},{14,15},{16,17},{18,19},{..., dimensions={0}, use_global_device_ids=true | all-gather | bytes 368640 | tf_op jit(solution)/shard_map/all_gather | solution.py:395
  75.7 1.9 %shard_map.126 = (f32[16,24,128]{2,1,0:T(8,128)S(1)}, f32[16,24,128]{2,1,0:T(8,128)S(1)}, f32[16,24,128]{2,1,0:T(8,128)S(1)}, f32[9,24,128]{2,1,0:T(8,128)S(1)},...) custom-call(s32[5]{0:T(128)S(1)} %stack.23.ids, ...), custom_call_target="tpu_custom_call" | custom-call | flops 1000000 | bytes 2000000 | tf_op jit(solution)/shard_map/pallas_call | solution.py:66
  77.6 3.4 %collective-permute-start.13 = (f32[9,24,128]{2,1,0:T(8,128)S(1)}, f32[9,24,128]{2,1,0:T(8,128)S(1)}, u32[]{:S(2)}, u32[]{:S(2)}) collective-permute-start(f32[9,24,128]{2,1,0:T(8,128)S(1)} %get-tuple-element.61), channel_id=1, source_target_pairs={{1,2},{2,1},{3,4},{4,3},{5,6},{6,5},{9,10},{10,9},{11,12},{12,11},... | collective-permute-start | bytes 331784 | tf_op jit(solution)/shard_map/ppermute | solution.py:381
  81.7 6.4 %collective-permute-start.12 = (f32[18,8,128]{2,1,0:T(8,128)S(1)}, f32[18,8,128]{2,1,0:T(8,128)S(1)}, u32[]{:S(2)}, u32[]{:S(2)}) collective-permute-start(f32[18,8,128]{2,1,0:T(8,128)S(1)} %get-tuple-element.60), channel_id=1, source_target_pairs={{0,32},{32,0},{64,96},{96,64},{128,160},{160,128},{192,224},{224,1... | collective-permute-start | bytes 221192 | tf_op jit(solution)/shard_map/ppermute | solution.py:381
  88.2 2.0 %all-gather.2 = f32[18,24,128]{2,1,0:T(8,128)S(1)} all-gather(f32[9,24,128]{2,1,0:T(8,128)S(1)} %get-tuple-element.62), channel_id=4, replica_groups={{0,1},{2,3},{4,5},{6,7},{8,9},{10,11},{12,13},{14,15},{16,17},{18,19},{..., dimensions={0}, use_global_device_ids=true | all-gather | bytes 331776 | tf_op jit(solution)/shard_map/all_gather | solution.py:395
  90.2 2.5 %shard_map.127 = (f32[16,24,128]{2,1,0:T(8,128)S(1)}, f32[16,24,128]{2,1,0:T(8,128)}, f32[16,24,128]{2,1,0:T(8,128)S(1)}, f32[8,24,128]{2,1,0:T(8,128)S(1)}, f32...) custom-call(s32[5]{0:T(128)S(1)} %stack.23.ids, ...), custom_call_target="tpu_custom_call" | custom-call | flops 1000000 | bytes 2000000 | tf_op jit(solution)/shard_map/pallas_call | solution.py:66
  92.6 3.2 %collective-permute-start.16 = (f32[8,24,128]{2,1,0:T(8,128)S(1)}, f32[8,24,128]{2,1,0:T(8,128)S(1)}, u32[]{:S(2)}, u32[]{:S(2)}) collective-permute-start(f32[8,24,128]{2,1,0:T(8,128)S(1)} %get-tuple-element.68), channel_id=1, source_target_pairs={{1,2},{2,1},{3,4},{4,3},{5,6},{6,5},{9,10},{10,9},{11,12},{12,11},... | collective-permute-start | bytes 294920 | tf_op jit(solution)/shard_map/ppermute | solution.py:381
  96.5 6.2 %collective-permute-start.15 = (f32[16,8,128]{2,1,0:T(8,128)S(1)}, f32[16,8,128]{2,1,0:T(8,128)S(1)}, u32[]{:S(2)}, u32[]{:S(2)}) collective-permute-start(f32[16,8,128]{2,1,0:T(8,128)S(1)} %get-tuple-element.67), channel_id=1, source_target_pairs={{0,32},{32,0},{64,96},{96,64},{128,160},{160,128},{192,224},{224,1... | collective-permute-start | bytes 196616 | tf_op jit(solution)/shard_map/ppermute | solution.py:381
  102.7 1.9 %all-gather.3 = f32[16,24,128]{2,1,0:T(8,128)S(1)} all-gather(f32[8,24,128]{2,1,0:T(8,128)S(1)} %get-tuple-element.69), channel_id=5, replica_groups={{0,1},{2,3},{4,5},{6,7},{8,9},{10,11},{12,13},{14,15},{16,17},{18,19},{..., dimensions={0}, use_global_device_ids=true | all-gather | bytes 294912 | tf_op jit(solution)/shard_map/all_gather | solution.py:395
  104.7 2.0 %shard_map.128 = (f32[16,24,128]{2,1,0:T(8,128)}, f32[16,24,128]{2,1,0:T(8,128)}) custom-call(s32[5]{0:T(128)S(1)} %stack.23.ids, f32[16,8,128]{2,1,0:T(8,128)S(1)} %collective-permute-done.14.x_odd_in, f32[16,8,128]{2,1,0:T(8,128)S(1)} %collective-permute-done.15.x_even_in, f32[8,24,128]{2,1,0:T(8,128)S(1)} %collective-permute-done.16.z_odd_in, ...), custom_call_target="tpu_custom_call" | custom-call | flops 1000000 | bytes 2000000 | tf_op jit(solution)/shard_map/pallas_call | solution.py:66
  (50 shorter events, 9.6 us)
Async XLA Ops:
  0.6 32.4 %copy-start.1 = (f32[16,24,128]{2,1,0:T(8,128)S(1)}, f32[16,24,128]{2,1,0:T(8,128)}, u32[]{:S(2)}) copy-start(f32[16,24,128]{2,1,0:T(8,128)} %stiff.9) | copy-start | bytes 589828
  35.7 10.8 %collective-permute-start = (f32[12,24,128]{2,1,0:T(8,128)S(1)}, f32[12,24,128]{2,1,0:T(8,128)S(1)}, u32[]{:S(2)}, u32[]{:S(2)}) collective-permute-start(f32[12,24,128]{2,1,0:T(8,128)S(1)} %get-tuple-element.40), channel_id=1, source_target_pairs={{0,8},{8,0},{16,24},{24,16},{1,9},{9,1},{17,25},{25,17},{2,10},{10... | collective-permute-start | bytes 442376 | tf_op jit(solution)/shard_map/ppermute | solution.py:381
  37.9 8.5 %collective-permute-start.1 = (f32[12,24,128]{2,1,0:T(8,128)S(1)}, f32[12,24,128]{2,1,0:T(8,128)S(1)}, u32[]{:S(2)}, u32[]{:S(2)}) collective-permute-start(f32[12,24,128]{2,1,0:T(8,128)S(1)} %get-tuple-element.41), channel_id=1, source_target_pairs={{8,16},{16,8},{9,17},{17,9},{10,18},{18,10},{11,19},{19,11},{12,20... | collective-permute-start | bytes 442376 | tf_op jit(solution)/shard_map/ppermute | solution.py:381
  42.5 11.5 %collective-permute-start.7 = (f32[128,128]{1,0:T(8,128)S(1)}, f32[128,128]{1,0:T(8,128)S(1)}, u32[]{:S(2)}, u32[]{:S(2)}) collective-permute-start(f32[128,128]{1,0:T(8,128)S(1)} %all_gather.29.refs_0_), channel_id=1, source_target_pairs={{6,0},{14,8},{22,16},{30,24},{38,32},{46,40},{54,48},{62,56},{70,6... | collective-permute-start | bytes 196616 | tf_op jit(solution)/shard_map/ppermute | solution.py:443
  46.5 15.8 %copy-start.5 = (bf16[256,256]{1,0:T(8,128)(2,1)S(1)}, bf16[256,256]{1,0:T(8,128)(2,1)}, u32[]{:S(2)}) copy-start(bf16[256,256]{1,0:T(8,128)(2,1)} %constant.44.clone.band_high) | copy-start | bytes 393220
  46.5 15.8 %copy-start.7 = (f32[16,24,128]{2,1,0:T(8,128)S(1)}, f32[16,24,128]{2,1,0:T(8,128)}, u32[]{:S(2)}) copy-start(f32[16,24,128]{2,1,0:T(8,128)} %older.4) | copy-start | bytes 589828
  47.3 14.9 %copy-start = (bf16[4,16,24,128]{3,2,1,0:T(8,128)(2,1)S(1)}, bf16[4,16,24,128]{3,2,1,0:T(8,128)(2,1)}, u32[]{:S(2)}) copy-start(bf16[4,16,24,128]{3,2,1,0:T(8,128)(2,1)} %forward.7) | copy-start | bytes 1179652
  47.4 14.9 %collective-permute-start.4 = (f32[12,24,128]{2,1,0:T(8,128)S(1)}, f32[12,24,128]{2,1,0:T(8,128)S(1)}, u32[]{:S(2)}, u32[]{:S(2)}) collective-permute-start(f32[12,24,128]{2,1,0:T(8,128)S(1)} %get-tuple-element.44), channel_id=1, source_target_pairs={{1,2},{2,1},{3,4},{4,3},{5,6},{6,5},{9,10},{10,9},{11,12},{12,11},... | collective-permute-start | bytes 442376 | tf_op jit(solution)/shard_map/ppermute | solution.py:381
  51.9 6.7 %collective-permute-start.6 = (f32[128,128]{1,0:T(8,128)S(1)}, f32[128,128]{1,0:T(8,128)S(1)}, u32[]{:S(2)}, u32[]{:S(2)}) collective-permute-start(f32[128,128]{1,0:T(8,128)S(1)} %all_gather.29.refs_0_), channel_id=1, source_target_pairs={{4,0},{12,8},{20,16},{28,24},{36,32},{44,40},{52,48},{60,56},{68,6... | collective-permute-start | bytes 196616 | tf_op jit(solution)/shard_map/ppermute | solution.py:443
  52.6 6.1 %collective-permute-start.5 = (f32[128,128]{1,0:T(8,128)S(1)}, f32[128,128]{1,0:T(8,128)S(1)}, u32[]{:S(2)}, u32[]{:S(2)}) collective-permute-start(f32[128,128]{1,0:T(8,128)S(1)} %all_gather.29.refs_0_), channel_id=1, source_target_pairs={{2,0},{10,8},{18,16},{26,24},{34,32},{42,40},{50,48},{58,56},{66,6... | collective-permute-start | bytes 196616 | tf_op jit(solution)/shard_map/ppermute | solution.py:443
  53.3 9.0 %collective-permute-start.2 = (f32[24,8,128]{2,1,0:T(8,128)S(1)}, f32[24,8,128]{2,1,0:T(8,128)S(1)}, u32[]{:S(2)}, u32[]{:S(2)}) collective-permute-start(f32[24,8,128]{2,1,0:T(8,128)S(1)} %get-tuple-element.42), channel_id=1, source_target_pairs={{32,64},{64,32},{96,128},{128,96},{160,192},{192,160},{224,256},{2... | collective-permute-start | bytes 294920 | tf_op jit(solution)/shard_map/ppermute | solution.py:381
  54.0 8.3 %collective-permute-start.3 = (f32[24,8,128]{2,1,0:T(8,128)S(1)}, f32[24,8,128]{2,1,0:T(8,128)S(1)}, u32[]{:S(2)}, u32[]{:S(2)}) collective-permute-start(f32[24,8,128]{2,1,0:T(8,128)S(1)} %get-tuple-element.43), channel_id=1, source_target_pairs={{0,32},{32,0},{64,96},{96,64},{128,160},{160,128},{192,224},{224,1... | collective-permute-start | bytes 294920 | tf_op jit(solution)/shard_map/ppermute | solution.py:381
  59.2 3.1 %copy-start.3 = (f32[16,24,128]{2,1,0:T(8,128)S(1)}, f32[16,24,128]{2,1,0:T(8,128)}, u32[]{:S(2)}) copy-start(f32[16,24,128]{2,1,0:T(8,128)} %older.5) | copy-start | bytes 589828
  59.2 3.1 %copy-start.4 = (bf16[256,256]{1,0:T(8,128)(2,1)S(1)}, bf16[256,256]{1,0:T(8,128)(2,1)}, u32[]{:S(2)}) copy-start(bf16[256,256]{1,0:T(8,128)(2,1)} %constant.45.clone.band_low) | copy-start | bytes 393220
  64.2 11.5 %collective-permute-start.10 = (f32[10,24,128]{2,1,0:T(8,128)S(1)}, f32[10,24,128]{2,1,0:T(8,128)S(1)}, u32[]{:S(2)}, u32[]{:S(2)}) collective-permute-start(f32[10,24,128]{2,1,0:T(8,128)S(1)} %get-tuple-element.54), channel_id=1, source_target_pairs={{1,2},{2,1},{3,4},{4,3},{5,6},{6,5},{9,10},{10,9},{11,12},{12,11},... | collective-permute-start | bytes 368648 | tf_op jit(solution)/shard_map/ppermute | solution.py:381
  67.3 8.3 %collective-permute-start.8 = (f32[20,8,128]{2,1,0:T(8,128)S(1)}, f32[20,8,128]{2,1,0:T(8,128)S(1)}, u32[]{:S(2)}, u32[]{:S(2)}) collective-permute-start(f32[20,8,128]{2,1,0:T(8,128)S(1)} %get-tuple-element.52), channel_id=1, source_target_pairs={{32,64},{64,32},{96,128},{128,96},{160,192},{192,160},{224,256},{2... | collective-permute-start | bytes 245768 | tf_op jit(solution)/shard_map/ppermute | solution.py:381
  68.0 7.7 %collective-permute-start.9 = (f32[20,8,128]{2,1,0:T(8,128)S(1)}, f32[20,8,128]{2,1,0:T(8,128)S(1)}, u32[]{:S(2)}, u32[]{:S(2)}) collective-permute-start(f32[20,8,128]{2,1,0:T(8,128)S(1)} %get-tuple-element.53), channel_id=1, source_target_pairs={{0,32},{32,0},{64,96},{96,64},{128,160},{160,128},{192,224},{224,1... | collective-permute-start | bytes 245768 | tf_op jit(solution)/shard_map/ppermute | solution.py:381
  77.6 12.5 %collective-permute-start.13 = (f32[9,24,128]{2,1,0:T(8,128)S(1)}, f32[9,24,128]{2,1,0:T(8,128)S(1)}, u32[]{:S(2)}, u32[]{:S(2)}) collective-permute-start(f32[9,24,128]{2,1,0:T(8,128)S(1)} %get-tuple-element.61), channel_id=1, source_target_pairs={{1,2},{2,1},{3,4},{4,3},{5,6},{6,5},{9,10},{10,9},{11,12},{12,11},... | collective-permute-start | bytes 331784 | tf_op jit(solution)/shard_map/ppermute | solution.py:381
  81.1 9.1 %collective-permute-start.11 = (f32[18,8,128]{2,1,0:T(8,128)S(1)}, f32[18,8,128]{2,1,0:T(8,128)S(1)}, u32[]{:S(2)}, u32[]{:S(2)}) collective-permute-start(f32[18,8,128]{2,1,0:T(8,128)S(1)} %get-tuple-element.59), channel_id=1, source_target_pairs={{32,64},{64,32},{96,128},{128,96},{160,192},{192,160},{224,256},{2... | collective-permute-start | bytes 221192 | tf_op jit(solution)/shard_map/ppermute | solution.py:381
  81.7 8.4 %collective-permute-start.12 = (f32[18,8,128]{2,1,0:T(8,128)S(1)}, f32[18,8,128]{2,1,0:T(8,128)S(1)}, u32[]{:S(2)}, u32[]{:S(2)}) collective-permute-start(f32[18,8,128]{2,1,0:T(8,128)S(1)} %get-tuple-element.60), channel_id=1, source_target_pairs={{0,32},{32,0},{64,96},{96,64},{128,160},{160,128},{192,224},{224,1... | collective-permute-start | bytes 221192 | tf_op jit(solution)/shard_map/ppermute | solution.py:381
  92.6 12.1 %copy-start.8 = (f32[16,24,128]{2,1,0:T(8,128)S(1)}, f32[16,24,128]{2,1,0:T(8,128)}, u32[]{:S(2)}) copy-start(f32[16,24,128]{2,1,0:T(8,128)} %get-tuple-element.37.wave) | copy-start | bytes 589828
  92.6 12.0 %collective-permute-start.16 = (f32[8,24,128]{2,1,0:T(8,128)S(1)}, f32[8,24,128]{2,1,0:T(8,128)S(1)}, u32[]{:S(2)}, u32[]{:S(2)}) collective-permute-start(f32[8,24,128]{2,1,0:T(8,128)S(1)} %get-tuple-element.68), channel_id=1, source_target_pairs={{1,2},{2,1},{3,4},{4,3},{5,6},{6,5},{9,10},{10,9},{11,12},{12,11},... | collective-permute-start | bytes 294920 | tf_op jit(solution)/shard_map/ppermute | solution.py:381
  95.9 8.8 %collective-permute-start.14 = (f32[16,8,128]{2,1,0:T(8,128)S(1)}, f32[16,8,128]{2,1,0:T(8,128)S(1)}, u32[]{:S(2)}, u32[]{:S(2)}) collective-permute-start(f32[16,8,128]{2,1,0:T(8,128)S(1)} %get-tuple-element.66), channel_id=1, source_target_pairs={{32,64},{64,32},{96,128},{128,96},{160,192},{192,160},{224,256},{2... | collective-permute-start | bytes 196616 | tf_op jit(solution)/shard_map/ppermute | solution.py:381
  96.5 8.1 %collective-permute-start.15 = (f32[16,8,128]{2,1,0:T(8,128)S(1)}, f32[16,8,128]{2,1,0:T(8,128)S(1)}, u32[]{:S(2)}, u32[]{:S(2)}) collective-permute-start(f32[16,8,128]{2,1,0:T(8,128)S(1)} %get-tuple-element.67), channel_id=1, source_target_pairs={{0,32},{32,0},{64,96},{96,64},{128,160},{160,128},{192,224},{224,1... | collective-permute-start | bytes 196616 | tf_op jit(solution)/shard_map/ppermute | solution.py:381
  (5 other events, 3.8 us)

commit v3 on v2

--- a/solution.py
+++ b/solution.py
@@ -89,10 +89,17 @@
     return lax.dot_general(left, right, (((1,), (1,)), ((), ())), preferred_element_type=F32)
 
 
-def slot_kernel(span_y, tiles, ids, residuals, owner_column, owner_row, cell_row, out):
+def prepare_kernel(span_y, tiles, ids, residuals, owners, cells, wave, older, stiff, packets,
+                   even, odd):
+    pack_slots(span_y, tiles, residuals, owners, cells, packets)
+    pack_strips(ids, wave, older, stiff, even, odd)
+
+
+def pack_slots(span_y, tiles, residuals, owner_row, cell_row, out):
     rows = residuals.shape[1]
     owner = owner_row[...]
-    earlier = (owner_column[...] == owner) & (
+    owner_column = jnp.transpose(jnp.broadcast_to(owner.astype(F32), (rows, rows)))
+    earlier = (owner_column.astype(jnp.int32) == owner) & (
         lax.broadcasted_iota(jnp.int32, (rows, rows), 0)
         < lax.broadcasted_iota(jnp.int32, (rows, rows), 1)
     )
@@ -158,7 +165,7 @@
             target[...] += product(slot).reshape(target.shape)
 
 
-def strip_pack_kernel(ids, wave, older, stiff, even, odd):
+def pack_strips(ids, wave, older, stiff, even, odd):
     parity = ids[2] & 1
     quarter = lane_of(wave.shape[1:]) // STRIP
     low, high = quarter == 0, quarter == 3
@@ -242,17 +249,19 @@
 
 
 def strip_unpack_kernel(
-    ids, even, odd, wave, wave_side, older_side, stiff_side, z_even, z_odd, x_even, x_odd
+    span_y, ids, even, odd, wave, wave_side, older_side, stiff_side, z_even, z_odd, x_even, x_odd
 ):
     parity = ids[2] & 1
     quarters = LANES // STRIP
     quarter = lane_of(wave.shape[1:]) // STRIP
     from_even = quarter == 3 * parity
-    from_odd = quarter == 3 * (1 - parity)
+    edge = jnp.where(parity == 0, ids[2] == 0, ids[2] == span_y - 1)
+    from_odd = quarter == jnp.where(edge, -1, 3 * (1 - parity))
     chunks = wave.shape[0] // quarters
     for number, side in enumerate((wave_side, older_side, stiff_side)):
         for chunk in range(chunks):
-            one, two = even[number * chunks + chunk], odd[number * chunks + chunk]
+            one = even[1 - parity, number * chunks + chunk]
+            two = odd[parity, number * chunks + chunk]
             for turn in range(quarters):
                 back = (LANES - STRIP * turn) % LANES
                 first = pltpu.roll(one, back, 1) if back else one
@@ -381,18 +390,21 @@
     return lax.ppermute(block, axis, pairs)
 
 
-def core_pairs(count):
-    return [[2 * chip, 2 * chip + 1] for chip in range(count // 2)]
+def pair_gather(block, axis, parity):
+    count = lax.axis_size(axis)
+    groups = [
+        [(2 * pair + parity) % count, (2 * pair + parity + 1) % count]
+        for pair in range(count // 2)
+    ]
+    return lax.all_gather(block, axis, axis=0, tiled=False, axis_index_groups=groups)
 
 
 def exchange(faces):
     z_even, z_odd, x_even, x_odd = faces
-    count = lax.axis_size("gz")
-    groups = core_pairs(count)
     z_odd = swap(z_odd, "gz", 1)
     x_even = swap(x_even, "gx", 0)
     x_odd = swap(x_odd, "gx", 1)
-    z_even = lax.all_gather(z_even, "gz", axis=0, tiled=False, axis_index_groups=groups)
+    z_even = pair_gather(z_even, "gz", 0)
     return z_even, z_odd, x_even, x_odd
 
 
@@ -421,24 +433,23 @@
         x_face = shaped(depth + folded(depth, width), RADIUS, LANES)
         return [z_face, z_face, x_face, x_face]
 
-    packets = call(
-        functools.partial(slot_kernel, span_y, tiles),
-        shaped(tiles, LANES),
-        [ids, residuals, owners, owners.reshape(1, -1), receivers.reshape(1, -1)],
+    strips = shaped(3 * depth * STRIP // LANES, rows, LANES)
+    packets, even, odd = call(
+        functools.partial(prepare_kernel, span_y, tiles),
+        [shaped(tiles, LANES), strips, strips],
+        [ids, residuals, owners.reshape(1, -1), receivers.reshape(1, -1), wave_now, older_wave,
+         stiffness],
+        in_specs=[smem()] + [pl.BlockSpec()] * 6,
     )
     packets = lax.all_to_all(packets, ("gx", "gy"), 0, 0, tiled=True)
-    ids, packets = lax.optimization_barrier((ids, packets))
-    strips = shaped(3 * depth * STRIP // LANES, rows, LANES)
-    even, odd = call(strip_pack_kernel, [strips, strips], [ids, wave_now, older_wave, stiffness])
-
-    odd = swap(odd, "gy", 1)
-    even = swap(even, "gy", 0)
+    even, odd = (pair_gather(strip, "gy", parity) for parity, strip in enumerate((even, odd)))
     side, older_side, stiff_side, *faces = call(
-        strip_unpack_kernel, [block] * 3 + faces_out(0), [ids, even, odd, wave_now]
-    )
-    packets = lax.all_gather(
-        packets, "gz", axis=0, tiled=True, axis_index_groups=core_pairs(span_z)
-    )
+        functools.partial(strip_unpack_kernel, span_y),
+        [block] * 3 + faces_out(0),
+        [ids, even, odd, wave_now],
+    )
+    packets, faces = lax.optimization_barrier((packets, faces))
+    packets = pair_gather(packets, "gz", 0).reshape(2 * tiles, LANES)
     packets = [packets] + [
         lax.ppermute(packets, "gz", [(layer, 0)]) for layer in range(2, span_z, 2)
     ]

time: 108 us -> 111 us (1.028)
  starting transfers between devices: 44.9 us -> 59.8 us
  blocking collectives: 40.6 us -> 33.4 us
  waiting for transfers between devices: 3.34 us -> 0.04 us
    all_to_all x1 -> x0, blocking collectives: 27.8 us -> none  [on_device(): packets = lax.all_to_all(packets, ('gx', 'gy'), 0, 0, tiled=True)]
    all_gather x5 -> x7, blocking collectives: 12.8 us -> 33.4 us  [pair_gather(): lax.all_gather(block, axis, axis=0, tiled=False, axis_index_groups=groups)]
    all_to_all x0 -> x1, starting transfers between devices: none -> 17.1 us  [on_device(): packets = lax.all_to_all(packets, ('gx', 'gy'), 0, 0, tiled=True)]
    ppermute x14 -> x12, waiting for transfers between devices: 3.33 us -> 0.03 us  [swap(): return lax.ppermute(block, axis, pairs)]
    ppermute x14 -> x12, starting transfers between devices: 42.9 us -> 40.7 us  [swap(): return lax.ppermute(block, axis, pairs)]
    unnamed x25 -> x26, local copies, waits for them, and re-layouts: 4.64 us -> 3.78 us
    pallas_call x8 -> x7, Pallas kernels: 11.5 us -> 11.4 us  [call(): pl.pallas_call(body, out_shape=outs, in_specs=in_specs or [smem()] + [vme...]
  transfers between devices with their start and end apart: 17 -> 16, of which waited for: 1 -> 0; matrix products, arithmetic and copies ran while one was open for 0% -> 0% of each run, Pallas kernels for 1% -> 1%
where the time goes in v3:
time: 111 us; the launch traced here: 110 us
  starting transfers between devices  59.8 us (54%)
  blocking collectives  33.4 us (30%)
  Pallas kernels  11.4 us (10%)
  local copies, waits for them, and re-layouts  3.87 us (3%)
  between operations  1.58 us (1%)
    ppermute x12, starting transfers between devices, swap(): return lax.ppermute(block, axis, pairs)  40.7 us
    all_gather x7, blocking collectives, pair_gather(): lax.all_gather(block, axis, axis=0, tiled=False, axis_index_groups=groups)  33.4 us
    all_to_all x1, starting transfers between devices, on_device(): packets = lax.all_to_all(packets, ('gx', 'gy'), 0, 0, tiled=True)  17.1 us
    pallas_call x7, Pallas kernels, call(): pl.pallas_call(body, out_shape=outs, in_specs=in_specs or [smem()] + [vme...  11.4 us
    unnamed x26, local copies, waits for them, and re-layouts  3.78 us
  transfers between devices with their start and end apart: 16, of which 0 were waited for; matrix products, arithmetic and copies ran while one was open for 0% of the time, Pallas kernels for 1%

profile of v3, /device:TPU:1, one launch (start us, length us, event | category | flops | bytes accessed | tf_op | source)
XLA Modules:
  0.0 110.0 jit_solution(7985941615809904645)
XLA Ops:
  2.1 0.9 copy-done.1
  3.0 0.9 copy-done.3
  3.9 0.9 copy-done.7
  4.9 1.6 %shard_map.121 = (f32[64,128]{1,0:T(8,128)}, f32[12,24,128]{2,1,0:T(8,128)S(1)}, f32[12,24,128]{2,1,0:T(8,128)S(1)}) custom-call(s32[5]{0:T(128)S(1)} %stack.23.ids, f32[4,128]{1,0:T(4,128)S(1)} %copy-done.10, s32[1,128]{1,0:T(1,128)S(1)} %bitcast.28, s32[1,128]{1,0:T(1,128)S(1)} %bitcast.29, f32[16,24,128]{2,1,0:T(8,128)S(1)} %copy-done.3, ...), custom_call_target="tpu_custom_call" | custom-call | flops 1000000 | bytes 2000000 | tf_op jit(solution)/shard_map/pallas_call | solution.py:66
  6.5 17.1 %all-to-all-start = ((f32[64,1,128]{2,1,0:T(1,128)}), f32[64,1,128]{2,1,0:T(1,128)S(1)}, u32[]{:S(2)}, u32[]{:S(2)}) async-start(f32[64,1,128]{2,1,0:T(1,128)} %bitcast.9), calls=%async_computation | async-start | bytes 65536 | tf_op jit(solution)/shard_map/all_to_all | solution.py:444
  23.6 10.5 %all-gather = f32[24,24,128]{2,1,0:T(8,128)S(1)} all-gather(f32[12,24,128]{2,1,0:T(8,128)S(1)} %get-tuple-element.44), channel_id=2, replica_groups={{0,8},{16,24},{1,9},{17,25},{2,10},{18,26},{3,11},{19,27},{4,12},{20,28..., dimensions={0}, use_global_device_ids=true | all-gather | bytes 442368 | tf_op jit(solution)/shard_map/all_gather | solution.py:399
  34.1 9.7 %all-gather.1 = f32[24,24,128]{2,1,0:T(8,128)S(1)} all-gather(f32[12,24,128]{2,1,0:T(8,128)S(1)} %get-tuple-element.45), channel_id=3, replica_groups={{8,16},{24,0},{9,17},{25,1},{10,18},{26,2},{11,19},{27,3},{12,20},{28,4..., dimensions={0}, use_global_device_ids=true | all-gather | bytes 442368 | tf_op jit(solution)/shard_map/all_gather | solution.py:399
  44.7 4.0 %collective-permute-start.2 = (f32[12,24,128]{2,1,0:T(8,128)S(1)}, f32[12,24,128]{2,1,0:T(8,128)S(1)}, u32[]{:S(2)}, u32[]{:S(2)}) collective-permute-start(f32[12,24,128]{2,1,0:T(8,128)S(1)} %get-tuple-element.52), channel_id=1, source_target_pairs={{1,2},{2,1},{3,4},{4,3},{5,6},{6,5},{9,10},{10,9},{11,12},{12,11},... | collective-permute-start | bytes 442376 | tf_op jit(solution)/shard_map/ppermute | solution.py:390
  48.7 1.9 %all-gather.3.refs_0_ = f32[128,128]{1,0:T(8,128)S(1)} all-gather(f32[64,128]{1,0:T(8,128)S(1)} %bitcast.30), channel_id=5, replica_groups={{0,1},{2,3},{4,5},{6,7},{8,9},{10,11},{12,13},{14,15},{16,17},{18,19},{..., dimensions={0}, use_global_device_ids=true | all-gather | bytes 98304 | tf_op jit(solution)/shard_map/all_gather | solution.py:399
  51.9 5.5 %collective-permute-start.1 = (f32[24,8,128]{2,1,0:T(8,128)S(1)}, f32[24,8,128]{2,1,0:T(8,128)S(1)}, u32[]{:S(2)}, u32[]{:S(2)}) collective-permute-start(f32[24,8,128]{2,1,0:T(8,128)S(1)} %get-tuple-element.51), channel_id=1, source_target_pairs={{0,32},{32,0},{64,96},{96,64},{128,160},{160,128},{192,224},{224,1... | collective-permute-start | bytes 294920 | tf_op jit(solution)/shard_map/ppermute | solution.py:390
  58.8 4.4 %all-gather.2 = f32[24,24,128]{2,1,0:T(8,128)S(1)} all-gather(f32[12,24,128]{2,1,0:T(8,128)S(1)} %get-tuple-element.53), channel_id=4, replica_groups={{0,1},{2,3},{4,5},{6,7},{8,9},{10,11},{12,13},{14,15},{16,17},{18,19},{..., dimensions={0}, use_global_device_ids=true | all-gather | bytes 442368 | tf_op jit(solution)/shard_map/all_gather | solution.py:399
  64.1 1.9 %shard_map.124 = (f32[16,24,128]{2,1,0:T(8,128)S(1)}, f32[16,24,128]{2,1,0:T(8,128)S(1)}, f32[16,24,128]{2,1,0:T(8,128)S(1)}, f32[10,24,128]{2,1,0:T(8,128)S(1)}...) custom-call(s32[5]{0:T(128)S(1)} %stack.23.ids, ...), custom_call_target="tpu_custom_call" | custom-call | flops 1000000 | bytes 2000000 | tf_op jit(solution)/shard_map/pallas_call | solution.py:66
  65.9 4.5 %collective-permute-start.8 = (f32[10,24,128]{2,1,0:T(8,128)S(1)}, f32[10,24,128]{2,1,0:T(8,128)S(1)}, u32[]{:S(2)}, u32[]{:S(2)}) collective-permute-start(f32[10,24,128]{2,1,0:T(8,128)S(1)} %get-tuple-element.62), channel_id=1, source_target_pairs={{1,2},{2,1},{3,4},{4,3},{5,6},{6,5},{9,10},{10,9},{11,12},{12,11},... | collective-permute-start | bytes 368648 | tf_op jit(solution)/shard_map/ppermute | solution.py:390
  71.1 5.5 %collective-permute-start.7 = (f32[20,8,128]{2,1,0:T(8,128)S(1)}, f32[20,8,128]{2,1,0:T(8,128)S(1)}, u32[]{:S(2)}, u32[]{:S(2)}) collective-permute-start(f32[20,8,128]{2,1,0:T(8,128)S(1)} %get-tuple-element.61), channel_id=1, source_target_pairs={{0,32},{32,0},{64,96},{96,64},{128,160},{160,128},{192,224},{224,1... | collective-permute-start | bytes 245768 | tf_op jit(solution)/shard_map/ppermute | solution.py:390
  76.6 3.0 %all-gather.4 = f32[20,24,128]{2,1,0:T(8,128)S(1)} all-gather(f32[10,24,128]{2,1,0:T(8,128)S(1)} %get-tuple-element.63), channel_id=6, replica_groups={{0,1},{2,3},{4,5},{6,7},{8,9},{10,11},{12,13},{14,15},{16,17},{18,19},{..., dimensions={0}, use_global_device_ids=true | all-gather | bytes 368640 | tf_op jit(solution)/shard_map/all_gather | solution.py:399
  79.7 1.9 %shard_map.125 = (f32[16,24,128]{2,1,0:T(8,128)S(1)}, f32[16,24,128]{2,1,0:T(8,128)S(1)}, f32[16,24,128]{2,1,0:T(8,128)S(1)}, f32[9,24,128]{2,1,0:T(8,128)S(1)},...) custom-call(s32[5]{0:T(128)S(1)} %stack.23.ids, ...), custom_call_target="tpu_custom_call" | custom-call | flops 1000000 | bytes 2000000 | tf_op jit(solution)/shard_map/pallas_call | solution.py:66
  81.6 2.7 %collective-permute-start.11 = (f32[9,24,128]{2,1,0:T(8,128)S(1)}, f32[9,24,128]{2,1,0:T(8,128)S(1)}, u32[]{:S(2)}, u32[]{:S(2)}) collective-permute-start(f32[9,24,128]{2,1,0:T(8,128)S(1)} %get-tuple-element.69), channel_id=1, source_target_pairs={{1,2},{2,1},{3,4},{4,3},{5,6},{6,5},{9,10},{10,9},{11,12},{12,11},... | collective-permute-start | bytes 331784 | tf_op jit(solution)/shard_map/ppermute | solution.py:390
  84.9 5.4 %collective-permute-start.10 = (f32[18,8,128]{2,1,0:T(8,128)S(1)}, f32[18,8,128]{2,1,0:T(8,128)S(1)}, u32[]{:S(2)}, u32[]{:S(2)}) collective-permute-start(f32[18,8,128]{2,1,0:T(8,128)S(1)} %get-tuple-element.68), channel_id=1, source_target_pairs={{0,32},{32,0},{64,96},{96,64},{128,160},{160,128},{192,224},{224,1... | collective-permute-start | bytes 221192 | tf_op jit(solution)/shard_map/ppermute | solution.py:390
  90.4 2.0 %all-gather.5 = f32[18,24,128]{2,1,0:T(8,128)S(1)} all-gather(f32[9,24,128]{2,1,0:T(8,128)S(1)} %get-tuple-element.70), channel_id=7, replica_groups={{0,1},{2,3},{4,5},{6,7},{8,9},{10,11},{12,13},{14,15},{16,17},{18,19},{..., dimensions={0}, use_global_device_ids=true | all-gather | bytes 331776 | tf_op jit(solution)/shard_map/all_gather | solution.py:399
  92.4 2.5 %shard_map.126 = (f32[16,24,128]{2,1,0:T(8,128)S(1)}, f32[16,24,128]{2,1,0:T(8,128)}, f32[16,24,128]{2,1,0:T(8,128)S(1)}, f32[8,24,128]{2,1,0:T(8,128)S(1)}, f32...) custom-call(s32[5]{0:T(128)S(1)} %stack.23.ids, ...), custom_call_target="tpu_custom_call" | custom-call | flops 1000000 | bytes 2000000 | tf_op jit(solution)/shard_map/pallas_call | solution.py:66
  94.8 3.9 %collective-permute-start.14 = (f32[8,24,128]{2,1,0:T(8,128)S(1)}, f32[8,24,128]{2,1,0:T(8,128)S(1)}, u32[]{:S(2)}, u32[]{:S(2)}) collective-permute-start(f32[8,24,128]{2,1,0:T(8,128)S(1)} %get-tuple-element.76), channel_id=1, source_target_pairs={{1,2},{2,1},{3,4},{4,3},{5,6},{6,5},{9,10},{10,9},{11,12},{12,11},... | collective-permute-start | bytes 294920 | tf_op jit(solution)/shard_map/ppermute | solution.py:390
  99.4 6.6 %collective-permute-start.13 = (f32[16,8,128]{2,1,0:T(8,128)S(1)}, f32[16,8,128]{2,1,0:T(8,128)S(1)}, u32[]{:S(2)}, u32[]{:S(2)}) collective-permute-start(f32[16,8,128]{2,1,0:T(8,128)S(1)} %get-tuple-element.75), channel_id=1, source_target_pairs={{0,32},{32,0},{64,96},{96,64},{128,160},{160,128},{192,224},{224,1... | collective-permute-start | bytes 196616 | tf_op jit(solution)/shard_map/ppermute | solution.py:390
  106.0 1.9 %all-gather.6 = f32[16,24,128]{2,1,0:T(8,128)S(1)} all-gather(f32[8,24,128]{2,1,0:T(8,128)S(1)} %get-tuple-element.77), channel_id=8, replica_groups={{0,1},{2,3},{4,5},{6,7},{8,9},{10,11},{12,13},{14,15},{16,17},{18,19},{..., dimensions={0}, use_global_device_ids=true | all-gather | bytes 294912 | tf_op jit(solution)/shard_map/all_gather | solution.py:399
  108.0 2.1 %shard_map.127 = (f32[16,24,128]{2,1,0:T(8,128)}, f32[16,24,128]{2,1,0:T(8,128)}) custom-call(s32[5]{0:T(128)S(1)} %stack.23.ids, f32[16,8,128]{2,1,0:T(8,128)S(1)} %collective-permute-done.12.x_odd_in, f32[16,8,128]{2,1,0:T(8,128)S(1)} %collective-permute-done.13.x_even_in, f32[8,24,128]{2,1,0:T(8,128)S(1)} %collective-permute-done.14.z_odd_in, ...), custom_call_target="tpu_custom_call" | custom-call | flops 1000000 | bytes 2000000 | tf_op jit(solution)/shard_map/pallas_call | solution.py:66
  (49 shorter events, 7.2 us)
Async XLA Ops:
  2.1 0.9 copy-start.1
  3.0 0.9 copy-start.3
  6.5 38.2 %all-to-all-start = ((f32[64,1,128]{2,1,0:T(1,128)}), f32[64,1,128]{2,1,0:T(1,128)S(1)}, u32[]{:S(2)}, u32[]{:S(2)}) async-start(f32[64,1,128]{2,1,0:T(1,128)} %bitcast.9), calls=%async_computation | async-start | bytes 65536 | tf_op jit(solution)/shard_map/all_to_all | solution.py:444
  34.1 9.7 %copy-start.4 = (f32[16,24,128]{2,1,0:T(8,128)S(1)}, f32[16,24,128]{2,1,0:T(8,128)}, u32[]{:S(2)}) copy-start(f32[16,24,128]{2,1,0:T(8,128)} %older.5) | copy-start | bytes 589828
  43.8 19.9 %copy-start.6 = (bf16[256,256]{1,0:T(8,128)(2,1)S(1)}, bf16[256,256]{1,0:T(8,128)(2,1)}, u32[]{:S(2)}) copy-start(bf16[256,256]{1,0:T(8,128)(2,1)} %constant.44.clone.band_high) | copy-start | bytes 393220
  43.8 19.9 %copy-start.8 = (f32[16,24,128]{2,1,0:T(8,128)S(1)}, f32[16,24,128]{2,1,0:T(8,128)}, u32[]{:S(2)}) copy-start(f32[16,24,128]{2,1,0:T(8,128)} %older.4) | copy-start | bytes 589828
  44.7 19.0 %copy-start = (bf16[4,16,24,128]{3,2,1,0:T(8,128)(2,1)S(1)}, bf16[4,16,24,128]{3,2,1,0:T(8,128)(2,1)}, u32[]{:S(2)}) copy-start(bf16[4,16,24,128]{3,2,1,0:T(8,128)(2,1)} %forward.7) | copy-start | bytes 1179652
  44.7 19.0 %collective-permute-start.2 = (f32[12,24,128]{2,1,0:T(8,128)S(1)}, f32[12,24,128]{2,1,0:T(8,128)S(1)}, u32[]{:S(2)}, u32[]{:S(2)}) collective-permute-start(f32[12,24,128]{2,1,0:T(8,128)S(1)} %get-tuple-element.52), channel_id=1, source_target_pairs={{1,2},{2,1},{3,4},{4,3},{5,6},{6,5},{9,10},{10,9},{11,12},{12,11},... | collective-permute-start | bytes 442376 | tf_op jit(solution)/shard_map/ppermute | solution.py:390
  50.6 7.5 %collective-permute-start.5 = (f32[128,128]{1,0:T(8,128)S(1)}, f32[128,128]{1,0:T(8,128)S(1)}, u32[]{:S(2)}, u32[]{:S(2)}) collective-permute-start(f32[128,128]{1,0:T(8,128)S(1)} %all-gather.3.refs_0_), channel_id=1, source_target_pairs={{6,0},{14,8},{22,16},{30,24},{38,32},{46,40},{54,48},{62,56},{70,6... | collective-permute-start | bytes 196616 | tf_op jit(solution)/shard_map/ppermute | solution.py:454
  51.2 12.5 %collective-permute-start = (f32[24,8,128]{2,1,0:T(8,128)S(1)}, f32[24,8,128]{2,1,0:T(8,128)S(1)}, u32[]{:S(2)}, u32[]{:S(2)}) collective-permute-start(f32[24,8,128]{2,1,0:T(8,128)S(1)} %get-tuple-element.50), channel_id=1, source_target_pairs={{32,64},{64,32},{96,128},{128,96},{160,192},{192,160},{224,256},{2... | collective-permute-start | bytes 294920 | tf_op jit(solution)/shard_map/ppermute | solution.py:390
  51.9 11.8 %collective-permute-start.1 = (f32[24,8,128]{2,1,0:T(8,128)S(1)}, f32[24,8,128]{2,1,0:T(8,128)S(1)}, u32[]{:S(2)}, u32[]{:S(2)}) collective-permute-start(f32[24,8,128]{2,1,0:T(8,128)S(1)} %get-tuple-element.51), channel_id=1, source_target_pairs={{0,32},{32,0},{64,96},{96,64},{128,160},{160,128},{192,224},{224,1... | collective-permute-start | bytes 294920 | tf_op jit(solution)/shard_map/ppermute | solution.py:390
  57.4 5.8 %collective-permute-start.4 = (f32[128,128]{1,0:T(8,128)S(1)}, f32[128,128]{1,0:T(8,128)S(1)}, u32[]{:S(2)}, u32[]{:S(2)}) collective-permute-start(f32[128,128]{1,0:T(8,128)S(1)} %all-gather.3.refs_0_), channel_id=1, source_target_pairs={{4,0},{12,8},{20,16},{28,24},{36,32},{44,40},{52,48},{60,56},{68,6... | collective-permute-start | bytes 196616 | tf_op jit(solution)/shard_map/ppermute | solution.py:454
  58.1 5.1 %collective-permute-start.3 = (f32[128,128]{1,0:T(8,128)S(1)}, f32[128,128]{1,0:T(8,128)S(1)}, u32[]{:S(2)}, u32[]{:S(2)}) collective-permute-start(f32[128,128]{1,0:T(8,128)S(1)} %all-gather.3.refs_0_), channel_id=1, source_target_pairs={{2,0},{10,8},{18,16},{26,24},{34,32},{42,40},{50,48},{58,56},{66,6... | collective-permute-start | bytes 196616 | tf_op jit(solution)/shard_map/ppermute | solution.py:454
  58.7 5.0 %copy-start.5 = (bf16[256,256]{1,0:T(8,128)(2,1)S(1)}, bf16[256,256]{1,0:T(8,128)(2,1)}, u32[]{:S(2)}) copy-start(bf16[256,256]{1,0:T(8,128)(2,1)} %constant.45.clone.band_low) | copy-start | bytes 393220
  65.9 13.7 %collective-permute-start.8 = (f32[10,24,128]{2,1,0:T(8,128)S(1)}, f32[10,24,128]{2,1,0:T(8,128)S(1)}, u32[]{:S(2)}, u32[]{:S(2)}) collective-permute-start(f32[10,24,128]{2,1,0:T(8,128)S(1)} %get-tuple-element.62), channel_id=1, source_target_pairs={{1,2},{2,1},{3,4},{4,3},{5,6},{6,5},{9,10},{10,9},{11,12},{12,11},... | collective-permute-start | bytes 368648 | tf_op jit(solution)/shard_map/ppermute | solution.py:390
  70.5 9.2 %collective-permute-start.6 = (f32[20,8,128]{2,1,0:T(8,128)S(1)}, f32[20,8,128]{2,1,0:T(8,128)S(1)}, u32[]{:S(2)}, u32[]{:S(2)}) collective-permute-start(f32[20,8,128]{2,1,0:T(8,128)S(1)} %get-tuple-element.60), channel_id=1, source_target_pairs={{32,64},{64,32},{96,128},{128,96},{160,192},{192,160},{224,256},{2... | collective-permute-start | bytes 245768 | tf_op jit(solution)/shard_map/ppermute | solution.py:390
  71.1 8.5 %collective-permute-start.7 = (f32[20,8,128]{2,1,0:T(8,128)S(1)}, f32[20,8,128]{2,1,0:T(8,128)S(1)}, u32[]{:S(2)}, u32[]{:S(2)}) collective-permute-start(f32[20,8,128]{2,1,0:T(8,128)S(1)} %get-tuple-element.61), channel_id=1, source_target_pairs={{0,32},{32,0},{64,96},{96,64},{128,160},{160,128},{192,224},{224,1... | collective-permute-start | bytes 245768 | tf_op jit(solution)/shard_map/ppermute | solution.py:390
  81.6 10.8 %collective-permute-start.11 = (f32[9,24,128]{2,1,0:T(8,128)S(1)}, f32[9,24,128]{2,1,0:T(8,128)S(1)}, u32[]{:S(2)}, u32[]{:S(2)}) collective-permute-start(f32[9,24,128]{2,1,0:T(8,128)S(1)} %get-tuple-element.69), channel_id=1, source_target_pairs={{1,2},{2,1},{3,4},{4,3},{5,6},{6,5},{9,10},{10,9},{11,12},{12,11},... | collective-permute-start | bytes 331784 | tf_op jit(solution)/shard_map/ppermute | solution.py:390
  84.3 8.1 %collective-permute-start.9 = (f32[18,8,128]{2,1,0:T(8,128)S(1)}, f32[18,8,128]{2,1,0:T(8,128)S(1)}, u32[]{:S(2)}, u32[]{:S(2)}) collective-permute-start(f32[18,8,128]{2,1,0:T(8,128)S(1)} %get-tuple-element.67), channel_id=1, source_target_pairs={{32,64},{64,32},{96,128},{128,96},{160,192},{192,160},{224,256},{2... | collective-permute-start | bytes 221192 | tf_op jit(solution)/shard_map/ppermute | solution.py:390
  84.9 7.4 %collective-permute-start.10 = (f32[18,8,128]{2,1,0:T(8,128)S(1)}, f32[18,8,128]{2,1,0:T(8,128)S(1)}, u32[]{:S(2)}, u32[]{:S(2)}) collective-permute-start(f32[18,8,128]{2,1,0:T(8,128)S(1)} %get-tuple-element.68), channel_id=1, source_target_pairs={{0,32},{32,0},{64,96},{96,64},{128,160},{160,128},{192,224},{224,1... | collective-permute-start | bytes 221192 | tf_op jit(solution)/shard_map/ppermute | solution.py:390
  94.8 13.1 %copy-start.9 = (f32[16,24,128]{2,1,0:T(8,128)S(1)}, f32[16,24,128]{2,1,0:T(8,128)}, u32[]{:S(2)}) copy-start(f32[16,24,128]{2,1,0:T(8,128)} %get-tuple-element.41.wave) | copy-start | bytes 589828
  94.8 13.1 %collective-permute-start.14 = (f32[8,24,128]{2,1,0:T(8,128)S(1)}, f32[8,24,128]{2,1,0:T(8,128)S(1)}, u32[]{:S(2)}, u32[]{:S(2)}) collective-permute-start(f32[8,24,128]{2,1,0:T(8,128)S(1)} %get-tuple-element.76), channel_id=1, source_target_pairs={{1,2},{2,1},{3,4},{4,3},{5,6},{6,5},{9,10},{10,9},{11,12},{12,11},... | collective-permute-start | bytes 294920 | tf_op jit(solution)/shard_map/ppermute | solution.py:390
  98.8 9.2 %collective-permute-start.12 = (f32[16,8,128]{2,1,0:T(8,128)S(1)}, f32[16,8,128]{2,1,0:T(8,128)S(1)}, u32[]{:S(2)}, u32[]{:S(2)}) collective-permute-start(f32[16,8,128]{2,1,0:T(8,128)S(1)} %get-tuple-element.74), channel_id=1, source_target_pairs={{32,64},{64,32},{96,128},{128,96},{160,192},{192,160},{224,256},{2... | collective-permute-start | bytes 196616 | tf_op jit(solution)/shard_map/ppermute | solution.py:390
  99.4 8.5 %collective-permute-start.13 = (f32[16,8,128]{2,1,0:T(8,128)S(1)}, f32[16,8,128]{2,1,0:T(8,128)S(1)}, u32[]{:S(2)}, u32[]{:S(2)}) collective-permute-start(f32[16,8,128]{2,1,0:T(8,128)S(1)} %get-tuple-element.75), channel_id=1, source_target_pairs={{0,32},{32,0},{64,96},{96,64},{128,160},{160,128},{192,224},{224,1... | collective-permute-start | bytes 196616 | tf_op jit(solution)/shard_map/ppermute | solution.py:390
  (5 other events, 3.9 us)

commit v4 on v3

--- a/solution.py
+++ b/solution.py
@@ -62,15 +62,15 @@
     return pl.BlockSpec(memory_space=pltpu.SMEM)
 
 
-def call(body, outs, ins, scratch=(), flops=1_000_000, in_specs=None):
+def call(body, outs, ins, scratch=(), in_specs=None, grant=32):
     return pl.pallas_call(
         body,
         out_shape=outs,
         in_specs=in_specs or [smem()] + [vmem()] * (len(ins) - 1),
         out_specs=jax.tree.map(lambda _: vmem(), outs),
         scratch_shapes=list(scratch),
-        compiler_params=pltpu.CompilerParams(vmem_limit_bytes=32 * 1024 * 1024),
-        cost_estimate=pl.CostEstimate(flops=flops, bytes_accessed=2_000_000, transcendentals=0),
+        compiler_params=pltpu.CompilerParams(vmem_limit_bytes=grant * 1024 * 1024),
+        cost_estimate=pl.CostEstimate(flops=1_000_000, bytes_accessed=2_000_000, transcendentals=0),
     )(*ins)
 
 
@@ -132,12 +132,12 @@
     out[...] = total
 
 
-def plane_kernel(rows, ids, *refs):
-    *packets, main, side, turned = refs
-    main[...] = jnp.zeros(main.shape, F32)
-    side[...] = jnp.zeros(side.shape, F32)
-
-    @pl.when(ids[0] == 0)
+def plane_kernel(face, rows, ids, z_even, *refs):
+    *packets, out, turned = refs
+    out[pl.ds(0, face)] = z_even[...]
+    out[pl.ds(face, 2 * STEPS)] = jnp.zeros((2 * STEPS, rows, LANES), F32)
+
+    @pl.when(ids[0] < 2)
     def _():
         count = turned.shape[1]
         share = count // len(packets)
@@ -160,9 +160,11 @@
             both = dot_nt(left, right)
             return both[: STEPS * rows] + both[STEPS * rows :]
 
-        for slot in range(SLOTS):
-            target = main if slot // CAP == 1 else side
-            target[...] += product(slot).reshape(target.shape)
+        for part, groups in enumerate(((1,), (0, 2))):
+            total = None
+            for slot in [CAP * group + rank for group in groups for rank in range(CAP)]:
+                total = product(slot) if total is None else total + product(slot)
+            out[pl.ds(face + STEPS * part, STEPS)] = total.reshape(STEPS, rows, LANES)
 
 
 def pack_strips(ids, wave, older, stiff, even, odd):
@@ -249,19 +251,17 @@
 
 
 def strip_unpack_kernel(
-    span_y, ids, even, odd, wave, wave_side, older_side, stiff_side, z_even, z_odd, x_even, x_odd
+    ids, even, odd, wave, wave_side, older_side, stiff_side, z_even, z_odd, x_even, x_odd
 ):
     parity = ids[2] & 1
     quarters = LANES // STRIP
     quarter = lane_of(wave.shape[1:]) // STRIP
     from_even = quarter == 3 * parity
-    edge = jnp.where(parity == 0, ids[2] == 0, ids[2] == span_y - 1)
-    from_odd = quarter == jnp.where(edge, -1, 3 * (1 - parity))
+    from_odd = quarter == 3 * (1 - parity)
     chunks = wave.shape[0] // quarters
     for number, side in enumerate((wave_side, older_side, stiff_side)):
         for chunk in range(chunks):
-            one = even[1 - parity, number * chunks + chunk]
-            two = odd[parity, number * chunks + chunk]
+            one, two = even[number * chunks + chunk], odd[number * chunks + chunk]
             for turn in range(quarters):
                 back = (LANES - STRIP * turn) % LANES
                 first = pltpu.roll(one, back, 1) if back else one
@@ -303,8 +303,8 @@
                 x_ext[1, plane + span * turn, pl.ds(start, RADIUS), :] = unfold(both, turn, width)
 
 
-def advance(step, ids, refs, wave, side, older, older_side, stiff, stiff_side, forward, image_in,
-            plane, plane_side, band_high, band_low, fresh, fresh_side, image, z_ext, x_ext, y_terms):
+def advance(step, ids, wave, side, older, older_side, stiff, stiff_side, forward, image_in,
+            planes, band_high, band_low, fresh, fresh_side, image, z_ext, x_ext, y_terms):
     depth, rows, _ = wave.shape
     last = step == STEPS - 1
     width = LANES if last else 2 * LANES
@@ -320,7 +320,7 @@
         + jnp.dot(high, rest, preferred_element_type=F32)
     )
 
-    def one(z, part, field, before, speed, source, target):
+    def one(z, part, field, before, speed, target):
         column = x_ext[part, z]
         turned = [None] + [
             pltpu.roll(column, rows + 2 * RADIUS - offset, 0) for offset in range(1, RADIUS)
@@ -335,13 +335,13 @@
                 near = near + column[2 * RADIUS :] + column[:rows]
             total = total + WEIGHTS[offset - 1] * near
         if z == 0:
-            total = total + source[step]
+            total = total + planes[STEPS * part + step]
         value = 2.0 * field[z] - before[z] + speed[z] * total
         target[z] = value
         return value
 
     for z in range(depth):
-        value = one(z, 0, wave, older, stiff, plane, fresh)
+        value = one(z, 0, wave, older, stiff, fresh)
         product = forward[step, z].astype(F32) * value
         if step:
             product = product + image_in[z]
@@ -349,7 +349,7 @@
             product = product * muting(ids, z, depth, rows)
         image[z] = product
         if not last:
-            one(z, 1, side, older_side, stiff_side, plane_side, fresh_side)
+            one(z, 1, side, older_side, stiff_side, fresh_side)
 
 
 def muting(ids, z, depth, rows):
@@ -363,11 +363,15 @@
 
 
 def step_kernel(step, ids, x_odd_in, x_even_in, z_odd_in, z_even_in, wave, side, older,
-                older_side, stiff, stiff_side, forward, plane, plane_side, band_high, band_low,
-                *rest):
+                older_side, stiff, stiff_side, forward, band_high, band_low, *rest):
     image_in = None
     if step:
-        image_in, *rest = rest
+        planes, image_in, *rest = rest
+    else:
+        planes, *rest = rest
+        face = z_even_in.shape[1] - 2 * STEPS
+        both = z_even_in[0, pl.ds(face, 2 * STEPS)] + z_even_in[1, pl.ds(face, 2 * STEPS)]
+        planes[...] = jnp.where(ids[0] == 0, both, 0.0)
     last = step == STEPS - 1
     if last:
         image, fresh, z_ext, x_ext, y_terms = rest
@@ -375,9 +379,8 @@
     else:
         (image, fresh, fresh_side, z_even, z_odd, x_even, x_odd, z_ext, x_ext, y_terms) = rest
     fill(strip_width(step), ids, wave, side, z_even_in, z_odd_in, x_even_in, x_odd_in, z_ext, x_ext)
-    advance(step, ids, None, wave, side, older, older_side, stiff, stiff_side, forward, image_in,
-            plane, plane_side, band_high, band_low, fresh, fresh_side, image, z_ext, x_ext,
-            y_terms)
+    advance(step, ids, wave, side, older, older_side, stiff, stiff_side, forward, image_in,
+            planes, band_high, band_low, fresh, fresh_side, image, z_ext, x_ext, y_terms)
     if not last:
         write_faces(strip_width(step + 1), ids, fresh, fresh_side, z_even, z_odd, x_even, x_odd)
 
@@ -440,25 +443,26 @@
         [ids, residuals, owners.reshape(1, -1), receivers.reshape(1, -1), wave_now, older_wave,
          stiffness],
         in_specs=[smem()] + [pl.BlockSpec()] * 6,
+        grant=60,
     )
     packets = lax.all_to_all(packets, ("gx", "gy"), 0, 0, tiled=True)
-    even, odd = (pair_gather(strip, "gy", parity) for parity, strip in enumerate((even, odd)))
+    even, odd = (swap(strip, "gy", parity) for parity, strip in enumerate((even, odd)))
     side, older_side, stiff_side, *faces = call(
-        functools.partial(strip_unpack_kernel, span_y),
+        strip_unpack_kernel,
         [block] * 3 + faces_out(0),
         [ids, even, odd, wave_now],
     )
-    packets, faces = lax.optimization_barrier((packets, faces))
-    packets = pair_gather(packets, "gz", 0).reshape(2 * tiles, LANES)
+    cores = 2
     packets = [packets] + [
-        lax.ppermute(packets, "gz", [(layer, 0)]) for layer in range(2, span_z, 2)
+        lax.ppermute(packets, "gz", [(chip + core, core) for core in range(cores)])
+        for chip in range(cores, span_z, cores)
     ]
-    plane_out = shaped(STEPS, rows, LANES)
-    plane, plane_side = call(
-        functools.partial(plane_kernel, rows),
-        [plane_out, plane_out],
-        [ids, *packets],
-        scratch=[pltpu.VMEM((LANES, span_z * tiles), F32)],
+    face = faces[0].shape[0]
+    faces[0] = call(
+        functools.partial(plane_kernel, face, rows),
+        shaped(face + 2 * STEPS, rows, LANES),
+        [ids, faces[0], *packets],
+        scratch=[pltpu.VMEM((LANES, span_z // cores * tiles), F32)],
     )
 
     scratch = [
@@ -471,13 +475,18 @@
     for step in range(STEPS):
         faces = exchange(faces)
         ins = [ids, *faces[::-1], wave, side, older, older_side, stiffness, stiff_side, forward_wave,
-               plane, plane_side, band_high, band_low]
+               band_high, band_low]
+        outs = [block, block]
         if step:
-            ins.append(image)
-        outs = [block, block]
+            ins += [planes, image]
+        else:
+            outs = [shaped(2 * STEPS, rows, LANES)] + outs
         if step < STEPS - 1:
             outs += [block] + faces_out(step + 1)
-        image, fresh, *rest = call(functools.partial(step_kernel, step), outs, ins, scratch)
+        rest = call(functools.partial(step_kernel, step), outs, ins, scratch)
+        if not step:
+            planes, *rest = rest
+        image, fresh, *rest = rest
         older, wave = wave, fresh
         if step < STEPS - 1:
             older_side, side = side, rest[0]

time: 111 us -> 104 us (0.937)
  starting transfers between devices: 59.8 us -> 52.3 us
  local copies, waits for them, and re-layouts: 3.87 us -> 0.64 us
  blocking collectives: 33.4 us -> 35.9 us
  Pallas kernels: 11.4 us -> 13.1 us
    all_to_all x0 -> x1, blocking collectives: none -> 27.7 us  [on_device(): packets = lax.all_to_all(packets, ('gx', 'gy'), 0, 0, tiled=True)]
    all_gather x7 -> x4, blocking collectives: 33.4 us -> 8.18 us  [pair_gather(): lax.all_gather(block, axis, axis=0, tiled=False, axis_index_groups=groups)]
    all_to_all x1 -> x0, starting transfers between devices: 17.1 us -> none  [on_device(): packets = lax.all_to_all(packets, ('gx', 'gy'), 0, 0, tiled=True)]
    ppermute x12 -> x14, starting transfers between devices: 40.7 us -> 48.3 us  [swap(): return lax.ppermute(block, axis, pairs)]
    unnamed x26 -> x16, local copies, waits for them, and re-layouts: 3.78 us -> 0.04 us
    ppermute x3, starting transfers between devices: 1.98 us -> 4 us  [on_device(): lax.ppermute(packets, 'gz', [(chip + core, core) for core in range(cores)])]
    pallas_call x7, Pallas kernels: 11.4 us -> 13.1 us  [call(): pl.pallas_call(body, out_shape=outs, in_specs=in_specs or [smem()] + [vme...]
  transfers between devices with their start and end apart: 16 -> 17, of which waited for: 0 -> 0; matrix products, arithmetic and copies ran while one was open for 0% -> 0% of each run, Pallas kernels for 1% -> 2%
where the time goes in v4:
time: 104 us
  starting transfers between devices  52.3 us (50%)
  blocking collectives  35.9 us (35%)
  Pallas kernels  13.1 us (13%)
  between operations  1.63 us (2%)
    ppermute x14, starting transfers between devices, swap(): return lax.ppermute(block, axis, pairs)  48.3 us
    all_to_all x1, blocking collectives, on_device(): packets = lax.all_to_all(packets, ('gx', 'gy'), 0, 0, tiled=True)  27.7 us
    pallas_call x7, Pallas kernels, call(): pl.pallas_call(body, out_shape=outs, in_specs=in_specs or [smem()] + [vme...  13.1 us
    all_gather x4, blocking collectives, pair_gather(): lax.all_gather(block, axis, axis=0, tiled=False, axis_index_groups=groups)  8.18 us
    ppermute x3, starting transfers between devices, on_device(): lax.ppermute(packets, 'gz', [(chip + core, core) for core in range(cores)])  4 us
  transfers between devices with their start and end apart: 17, of which 0 were waited for; matrix products, arithmetic and copies ran while one was open for 0% of the time, Pallas kernels for 2%

profile of v4, /device:TPU:1, one launch (start us, length us, event | category | flops | bytes accessed | tf_op | source)
XLA Modules:
  0.0 103.7 jit_solution(9762202482595345112)
XLA Ops:
  1.9 2.3 %shard_map.121 = (f32[64,128]{1,0:T(8,128)}, f32[12,24,128]{2,1,0:T(8,128)}, f32[12,24,128]{2,1,0:T(8,128)}) custom-call(s32[5]{0:T(128)} %stack.23.ids, f32[4,128]{1,0:T(4,128)} %residuals.1, s32[1,128]{1,0:T(1,128)} %bitcast.29, s32[1,128]{1,0:T(1,128)} %bitcast.30, f32[16,24,128]{2,1,0:T(8,128)} %older.5, f32[16,24,128]{2,1,0:T(8,128)} %older.4, ...), custom_call_target="tpu_custom_call" | custom-call | flops 1000000 | bytes 2000000 | tf_op jit(solution)/shard_map/pallas_call | solution.py:66
  4.2 6.6 %collective-permute-start = (f32[12,24,128]{2,1,0:T(8,128)}, f32[12,24,128]{2,1,0:T(8,128)S(1)}, u32[]{:S(2)}, u32[]{:S(2)}) collective-permute-start(f32[12,24,128]{2,1,0:T(8,128)} %get-tuple-element.37), channel_id=1, source_target_pairs={{0,8},{8,0},{16,24},{24,16},{1,9},{9,1},{17,25},{25,17},{2,10},{10... | collective-permute-start | bytes 442376 | tf_op jit(solution)/shard_map/ppermute | solution.py:393
  11.5 27.7 %all_to_all.11 = f32[64,1,128]{2,1,0:T(1,128)S(1)} all-to-all(f32[64,1,128]{2,1,0:T(1,128)} %bitcast.28), channel_id=1, replica_groups=mesh['gx'=16,'gy'=4,'gz'=8] {'gx','gy'}, dimensions={0} | all-to-all | bytes 65536 | tf_op jit(solution)/shard_map/all_to_all | solution.py:448
  39.3 1.4 %collective-permute-start.7 = (f32[64,128]{1,0:T(8,128)S(1)}, f32[64,128]{1,0:T(8,128)S(1)}, u32[]{:S(2)}, u32[]{:S(2)}) collective-permute-start(f32[64,128]{1,0:T(8,128)S(1)} %bitcast.24), channel_id=1, source_target_pairs={{6,0},{7,1},{14,8},{15,9},{22,16},{23,17},{30,24},{31,25},{38,32},... | collective-permute-start | bytes 98312 | tf_op jit(solution)/shard_map/ppermute | solution.py:457
  40.7 1.3 %collective-permute-start.6 = (f32[64,128]{1,0:T(8,128)S(1)}, f32[64,128]{1,0:T(8,128)S(1)}, u32[]{:S(2)}, u32[]{:S(2)}) collective-permute-start(f32[64,128]{1,0:T(8,128)S(1)} %bitcast.25), channel_id=1, source_target_pairs={{4,0},{5,1},{12,8},{13,9},{20,16},{21,17},{28,24},{29,25},{36,32},... | collective-permute-start | bytes 98312 | tf_op jit(solution)/shard_map/ppermute | solution.py:457
  42.0 1.3 %collective-permute-start.5 = (f32[64,128]{1,0:T(8,128)S(1)}, f32[64,128]{1,0:T(8,128)S(1)}, u32[]{:S(2)}, u32[]{:S(2)}) collective-permute-start(f32[64,128]{1,0:T(8,128)S(1)} %bitcast.26), channel_id=1, source_target_pairs={{2,0},{3,1},{10,8},{11,9},{18,16},{19,17},{26,24},{27,25},{34,32},... | collective-permute-start | bytes 98312 | tf_op jit(solution)/shard_map/ppermute | solution.py:457
  43.3 0.9 shard_map.122
  44.2 6.8 %collective-permute-start.4 = (f32[12,24,128]{2,1,0:T(8,128)S(1)}, f32[12,24,128]{2,1,0:T(8,128)S(1)}, u32[]{:S(2)}, u32[]{:S(2)}) collective-permute-start(f32[12,24,128]{2,1,0:T(8,128)S(1)} %get-tuple-element.41), channel_id=1, source_target_pairs={{1,2},{2,1},{3,4},{4,3},{5,6},{6,5},{9,10},{10,9},{11,12},{12,11},... | collective-permute-start | bytes 442376 | tf_op jit(solution)/shard_map/ppermute | solution.py:393
  51.7 4.7 %collective-permute-start.3 = (f32[24,8,128]{2,1,0:T(8,128)S(1)}, f32[24,8,128]{2,1,0:T(8,128)S(1)}, u32[]{:S(2)}, u32[]{:S(2)}) collective-permute-start(f32[24,8,128]{2,1,0:T(8,128)S(1)} %get-tuple-element.40), channel_id=1, source_target_pairs={{0,32},{32,0},{64,96},{96,64},{128,160},{160,128},{192,224},{224,1... | collective-permute-start | bytes 294920 | tf_op jit(solution)/shard_map/ppermute | solution.py:393
  56.5 1.6 %shard_map.123 = f32[20,24,128]{2,1,0:T(8,128)S(1)} custom-call(s32[5]{0:T(128)S(1)} %copy-done.7, f32[12,24,128]{2,1,0:T(8,128)S(1)} %get-tuple-element.42.z_even, f32[64,128]{1,0:T(8,128)S(1)} %bitcast.27, f32[64,128]{1,0:T(8,128)S(1)} %collective-permute-done.5.refs_1_, f32[64,128]{1,0:T(8,128)S(1)} %collective-permute-done.6.refs_2_, ...), custom_call_target="tpu_custom_call" | custom-call | flops 1000000 | bytes 2000000 | tf_op jit(solution)/shard_map/pallas_call | solution.py:66
  58.1 2.3 %all-gather = f32[40,24,128]{2,1,0:T(8,128)S(1)} all-gather(f32[20,24,128]{2,1,0:T(8,128)S(1)} %shard_map.123), channel_id=2, replica_groups={{0,1},{2,3},{4,5},{6,7},{8,9},{10,11},{12,13},{14,15},{16,17},{18,19},{..., dimensions={0}, use_global_device_ids=true | all-gather | bytes 737280 | tf_op jit(solution)/shard_map/all_gather | solution.py:402
  60.4 1.9 %shard_map.124 = (f32[8,24,128]{2,1,0:T(8,128)S(1)}, f32[16,24,128]{2,1,0:T(8,128)S(1)}, f32[16,24,128]{2,1,0:T(8,128)S(1)}, f32[16,24,128]{2,1,0:T(8,128)S(1)},...) custom-call(s32[5]{0:T(128)S(1)} %copy-done.7, ...), custom_call_target="tpu_custom_call" | custom-call | flops 1000000 | bytes 2000000 | tf_op jit(solution)/shard_map/pallas_call | solution.py:66
  62.3 2.1 %collective-permute-start.10 = (f32[10,24,128]{2,1,0:T(8,128)S(1)}, f32[10,24,128]{2,1,0:T(8,128)S(1)}, u32[]{:S(2)}, u32[]{:S(2)}) collective-permute-start(f32[10,24,128]{2,1,0:T(8,128)S(1)} %get-tuple-element.49), channel_id=1, source_target_pairs={{1,2},{2,1},{3,4},{4,3},{5,6},{6,5},{9,10},{10,9},{11,12},{12,11},... | collective-permute-start | bytes 368648 | tf_op jit(solution)/shard_map/ppermute | solution.py:393
  65.1 5.7 %collective-permute-start.9 = (f32[20,8,128]{2,1,0:T(8,128)S(1)}, f32[20,8,128]{2,1,0:T(8,128)S(1)}, u32[]{:S(2)}, u32[]{:S(2)}) collective-permute-start(f32[20,8,128]{2,1,0:T(8,128)S(1)} %get-tuple-element.48), channel_id=1, source_target_pairs={{0,32},{32,0},{64,96},{96,64},{128,160},{160,128},{192,224},{224,1... | collective-permute-start | bytes 245768 | tf_op jit(solution)/shard_map/ppermute | solution.py:393
  70.9 2.0 %all-gather.1 = f32[20,24,128]{2,1,0:T(8,128)S(1)} all-gather(f32[10,24,128]{2,1,0:T(8,128)S(1)} %get-tuple-element.50), channel_id=3, replica_groups={{0,1},{2,3},{4,5},{6,7},{8,9},{10,11},{12,13},{14,15},{16,17},{18,19},{..., dimensions={0}, use_global_device_ids=true | all-gather | bytes 368640 | tf_op jit(solution)/shard_map/all_gather | solution.py:402
  72.9 1.9 %shard_map.125 = (f32[16,24,128]{2,1,0:T(8,128)S(1)}, f32[16,24,128]{2,1,0:T(8,128)S(1)}, f32[16,24,128]{2,1,0:T(8,128)S(1)}, f32[9,24,128]{2,1,0:T(8,128)S(1)},...) custom-call(s32[5]{0:T(128)S(1)} %copy-done.7, ...), custom_call_target="tpu_custom_call" | custom-call | flops 1000000 | bytes 2000000 | tf_op jit(solution)/shard_map/pallas_call | solution.py:66
  74.8 3.4 %collective-permute-start.13 = (f32[9,24,128]{2,1,0:T(8,128)S(1)}, f32[9,24,128]{2,1,0:T(8,128)S(1)}, u32[]{:S(2)}, u32[]{:S(2)}) collective-permute-start(f32[9,24,128]{2,1,0:T(8,128)S(1)} %get-tuple-element.57), channel_id=1, source_target_pairs={{1,2},{2,1},{3,4},{4,3},{5,6},{6,5},{9,10},{10,9},{11,12},{12,11},... | collective-permute-start | bytes 331784 | tf_op jit(solution)/shard_map/ppermute | solution.py:393
  78.9 5.8 %collective-permute-start.12 = (f32[18,8,128]{2,1,0:T(8,128)S(1)}, f32[18,8,128]{2,1,0:T(8,128)S(1)}, u32[]{:S(2)}, u32[]{:S(2)}) collective-permute-start(f32[18,8,128]{2,1,0:T(8,128)S(1)} %get-tuple-element.56), channel_id=1, source_target_pairs={{0,32},{32,0},{64,96},{96,64},{128,160},{160,128},{192,224},{224,1... | collective-permute-start | bytes 221192 | tf_op jit(solution)/shard_map/ppermute | solution.py:393
  84.7 2.0 %all-gather.2 = f32[18,24,128]{2,1,0:T(8,128)S(1)} all-gather(f32[9,24,128]{2,1,0:T(8,128)S(1)} %get-tuple-element.58), channel_id=4, replica_groups={{0,1},{2,3},{4,5},{6,7},{8,9},{10,11},{12,13},{14,15},{16,17},{18,19},{..., dimensions={0}, use_global_device_ids=true | all-gather | bytes 331776 | tf_op jit(solution)/shard_map/all_gather | solution.py:402
  86.7 2.5 %shard_map.126 = (f32[16,24,128]{2,1,0:T(8,128)S(1)}, f32[16,24,128]{2,1,0:T(8,128)}, f32[16,24,128]{2,1,0:T(8,128)S(1)}, f32[8,24,128]{2,1,0:T(8,128)S(1)}, f32...) custom-call(s32[5]{0:T(128)S(1)} %copy-done.7, ...), custom_call_target="tpu_custom_call" | custom-call | flops 1000000 | bytes 2000000 | tf_op jit(solution)/shard_map/pallas_call | solution.py:66
  89.2 3.5 %collective-permute-start.16 = (f32[8,24,128]{2,1,0:T(8,128)S(1)}, f32[8,24,128]{2,1,0:T(8,128)S(1)}, u32[]{:S(2)}, u32[]{:S(2)}) collective-permute-start(f32[8,24,128]{2,1,0:T(8,128)S(1)} %get-tuple-element.64), channel_id=1, source_target_pairs={{1,2},{2,1},{3,4},{4,3},{5,6},{6,5},{9,10},{10,9},{11,12},{12,11},... | collective-permute-start | bytes 294920 | tf_op jit(solution)/shard_map/ppermute | solution.py:393
  93.4 6.3 %collective-permute-start.15 = (f32[16,8,128]{2,1,0:T(8,128)S(1)}, f32[16,8,128]{2,1,0:T(8,128)S(1)}, u32[]{:S(2)}, u32[]{:S(2)}) collective-permute-start(f32[16,8,128]{2,1,0:T(8,128)S(1)} %get-tuple-element.63), channel_id=1, source_target_pairs={{0,32},{32,0},{64,96},{96,64},{128,160},{160,128},{192,224},{224,1... | collective-permute-start | bytes 196616 | tf_op jit(solution)/shard_map/ppermute | solution.py:393
  99.7 1.9 %all-gather.3 = f32[16,24,128]{2,1,0:T(8,128)S(1)} all-gather(f32[8,24,128]{2,1,0:T(8,128)S(1)} %get-tuple-element.65), channel_id=5, replica_groups={{0,1},{2,3},{4,5},{6,7},{8,9},{10,11},{12,13},{14,15},{16,17},{18,19},{..., dimensions={0}, use_global_device_ids=true | all-gather | bytes 294912 | tf_op jit(solution)/shard_map/all_gather | solution.py:402
  101.6 2.1 %shard_map.127 = (f32[16,24,128]{2,1,0:T(8,128)}, f32[16,24,128]{2,1,0:T(8,128)}) custom-call(s32[5]{0:T(128)S(1)} %copy-done.7, f32[16,8,128]{2,1,0:T(8,128)S(1)} %collective-permute-done.14.x_odd_in, f32[16,8,128]{2,1,0:T(8,128)S(1)} %collective-permute-done.15.x_even_in, f32[8,24,128]{2,1,0:T(8,128)S(1)} %collective-permute-done.16.z_odd_in, ...), custom_call_target="tpu_custom_call" | custom-call | flops 1000000 | bytes 2000000 | tf_op jit(solution)/shard_map/pallas_call | solution.py:66
  (39 shorter events, 4.0 us)
Async XLA Ops:
  1.9 41.4 %copy-start.2 = (f32[16,24,128]{2,1,0:T(8,128)S(1)}, f32[16,24,128]{2,1,0:T(8,128)}, u32[]{:S(2)}) copy-start(f32[16,24,128]{2,1,0:T(8,128)} %older.5) | copy-start | bytes 589828
  4.2 39.1 %collective-permute-start = (f32[12,24,128]{2,1,0:T(8,128)}, f32[12,24,128]{2,1,0:T(8,128)S(1)}, u32[]{:S(2)}, u32[]{:S(2)}) collective-permute-start(f32[12,24,128]{2,1,0:T(8,128)} %get-tuple-element.37), channel_id=1, source_target_pairs={{0,8},{8,0},{16,24},{24,16},{1,9},{9,1},{17,25},{25,17},{2,10},{10... | collective-permute-start | bytes 442376 | tf_op jit(solution)/shard_map/ppermute | solution.py:393
  10.9 32.4 %collective-permute-start.1 = (f32[12,24,128]{2,1,0:T(8,128)}, f32[12,24,128]{2,1,0:T(8,128)S(1)}, u32[]{:S(2)}, u32[]{:S(2)}) collective-permute-start(f32[12,24,128]{2,1,0:T(8,128)} %get-tuple-element.38), channel_id=1, source_target_pairs={{8,16},{16,8},{9,17},{17,9},{10,18},{18,10},{11,19},{19,11},{12,20... | collective-permute-start | bytes 442376 | tf_op jit(solution)/shard_map/ppermute | solution.py:393
  39.3 4.1 %copy-start.7 = (s32[5]{0:T(128)S(1)}, s32[5]{0:T(128)}, u32[]{:S(2)}) copy-start(s32[5]{0:T(128)} %stack.23.ids) | copy-start | bytes 64
  39.3 12.4 %collective-permute-start.7 = (f32[64,128]{1,0:T(8,128)S(1)}, f32[64,128]{1,0:T(8,128)S(1)}, u32[]{:S(2)}, u32[]{:S(2)}) collective-permute-start(f32[64,128]{1,0:T(8,128)S(1)} %bitcast.24), channel_id=1, source_target_pairs={{6,0},{7,1},{14,8},{15,9},{22,16},{23,17},{30,24},{31,25},{38,32},... | collective-permute-start | bytes 98312 | tf_op jit(solution)/shard_map/ppermute | solution.py:457
  40.7 15.7 %collective-permute-start.6 = (f32[64,128]{1,0:T(8,128)S(1)}, f32[64,128]{1,0:T(8,128)S(1)}, u32[]{:S(2)}, u32[]{:S(2)}) collective-permute-start(f32[64,128]{1,0:T(8,128)S(1)} %bitcast.25), channel_id=1, source_target_pairs={{4,0},{5,1},{12,8},{13,9},{20,16},{21,17},{28,24},{29,25},{36,32},... | collective-permute-start | bytes 98312 | tf_op jit(solution)/shard_map/ppermute | solution.py:457
  42.0 14.4 %collective-permute-start.5 = (f32[64,128]{1,0:T(8,128)S(1)}, f32[64,128]{1,0:T(8,128)S(1)}, u32[]{:S(2)}, u32[]{:S(2)}) collective-permute-start(f32[64,128]{1,0:T(8,128)S(1)} %bitcast.26), channel_id=1, source_target_pairs={{2,0},{3,1},{10,8},{11,9},{18,16},{19,17},{26,24},{27,25},{34,32},... | collective-permute-start | bytes 98312 | tf_op jit(solution)/shard_map/ppermute | solution.py:457
  44.2 16.2 %collective-permute-start.4 = (f32[12,24,128]{2,1,0:T(8,128)S(1)}, f32[12,24,128]{2,1,0:T(8,128)S(1)}, u32[]{:S(2)}, u32[]{:S(2)}) collective-permute-start(f32[12,24,128]{2,1,0:T(8,128)S(1)} %get-tuple-element.41), channel_id=1, source_target_pairs={{1,2},{2,1},{3,4},{4,3},{5,6},{6,5},{9,10},{10,9},{11,12},{12,11},... | collective-permute-start | bytes 442376 | tf_op jit(solution)/shard_map/ppermute | solution.py:393
  51.0 9.3 %collective-permute-start.2 = (f32[24,8,128]{2,1,0:T(8,128)S(1)}, f32[24,8,128]{2,1,0:T(8,128)S(1)}, u32[]{:S(2)}, u32[]{:S(2)}) collective-permute-start(f32[24,8,128]{2,1,0:T(8,128)S(1)} %get-tuple-element.39), channel_id=1, source_target_pairs={{32,64},{64,32},{96,128},{128,96},{160,192},{192,160},{224,256},{2... | collective-permute-start | bytes 294920 | tf_op jit(solution)/shard_map/ppermute | solution.py:393
  51.7 8.6 %collective-permute-start.3 = (f32[24,8,128]{2,1,0:T(8,128)S(1)}, f32[24,8,128]{2,1,0:T(8,128)S(1)}, u32[]{:S(2)}, u32[]{:S(2)}) collective-permute-start(f32[24,8,128]{2,1,0:T(8,128)S(1)} %get-tuple-element.40), channel_id=1, source_target_pairs={{0,32},{32,0},{64,96},{96,64},{128,160},{160,128},{192,224},{224,1... | collective-permute-start | bytes 294920 | tf_op jit(solution)/shard_map/ppermute | solution.py:393
  56.4 3.9 %copy-start.4 = (bf16[256,256]{1,0:T(8,128)(2,1)S(1)}, bf16[256,256]{1,0:T(8,128)(2,1)}, u32[]{:S(2)}) copy-start(bf16[256,256]{1,0:T(8,128)(2,1)} %constant.44.clone.band_high) | copy-start | bytes 393220
  56.4 3.9 %copy-start.5 = (f32[16,24,128]{2,1,0:T(8,128)S(1)}, f32[16,24,128]{2,1,0:T(8,128)}, u32[]{:S(2)}) copy-start(f32[16,24,128]{2,1,0:T(8,128)} %older.4) | copy-start | bytes 589828
  58.0 2.4 %copy-start = (bf16[4,16,24,128]{3,2,1,0:T(8,128)(2,1)S(1)}, bf16[4,16,24,128]{3,2,1,0:T(8,128)(2,1)}, u32[]{:S(2)}) copy-start(bf16[4,16,24,128]{3,2,1,0:T(8,128)(2,1)} %forward.7) | copy-start | bytes 1179652
  58.0 2.4 %copy-start.1 = (f32[16,24,128]{2,1,0:T(8,128)S(1)}, f32[16,24,128]{2,1,0:T(8,128)}, u32[]{:S(2)}) copy-start(f32[16,24,128]{2,1,0:T(8,128)} %stiff.9) | copy-start | bytes 589828
  62.3 10.5 %collective-permute-start.10 = (f32[10,24,128]{2,1,0:T(8,128)S(1)}, f32[10,24,128]{2,1,0:T(8,128)S(1)}, u32[]{:S(2)}, u32[]{:S(2)}) collective-permute-start(f32[10,24,128]{2,1,0:T(8,128)S(1)} %get-tuple-element.49), channel_id=1, source_target_pairs={{1,2},{2,1},{3,4},{4,3},{5,6},{6,5},{9,10},{10,9},{11,12},{12,11},... | collective-permute-start | bytes 368648 | tf_op jit(solution)/shard_map/ppermute | solution.py:393
  64.5 8.4 %collective-permute-start.8 = (f32[20,8,128]{2,1,0:T(8,128)S(1)}, f32[20,8,128]{2,1,0:T(8,128)S(1)}, u32[]{:S(2)}, u32[]{:S(2)}) collective-permute-start(f32[20,8,128]{2,1,0:T(8,128)S(1)} %get-tuple-element.47), channel_id=1, source_target_pairs={{32,64},{64,32},{96,128},{128,96},{160,192},{192,160},{224,256},{2... | collective-permute-start | bytes 245768 | tf_op jit(solution)/shard_map/ppermute | solution.py:393
  65.1 7.7 %collective-permute-start.9 = (f32[20,8,128]{2,1,0:T(8,128)S(1)}, f32[20,8,128]{2,1,0:T(8,128)S(1)}, u32[]{:S(2)}, u32[]{:S(2)}) collective-permute-start(f32[20,8,128]{2,1,0:T(8,128)S(1)} %get-tuple-element.48), channel_id=1, source_target_pairs={{0,32},{32,0},{64,96},{96,64},{128,160},{160,128},{192,224},{224,1... | collective-permute-start | bytes 245768 | tf_op jit(solution)/shard_map/ppermute | solution.py:393
  74.8 11.9 %collective-permute-start.13 = (f32[9,24,128]{2,1,0:T(8,128)S(1)}, f32[9,24,128]{2,1,0:T(8,128)S(1)}, u32[]{:S(2)}, u32[]{:S(2)}) collective-permute-start(f32[9,24,128]{2,1,0:T(8,128)S(1)} %get-tuple-element.57), channel_id=1, source_target_pairs={{1,2},{2,1},{3,4},{4,3},{5,6},{6,5},{9,10},{10,9},{11,12},{12,11},... | collective-permute-start | bytes 331784 | tf_op jit(solution)/shard_map/ppermute | solution.py:393
  78.3 8.4 %collective-permute-start.11 = (f32[18,8,128]{2,1,0:T(8,128)S(1)}, f32[18,8,128]{2,1,0:T(8,128)S(1)}, u32[]{:S(2)}, u32[]{:S(2)}) collective-permute-start(f32[18,8,128]{2,1,0:T(8,128)S(1)} %get-tuple-element.55), channel_id=1, source_target_pairs={{32,64},{64,32},{96,128},{128,96},{160,192},{192,160},{224,256},{2... | collective-permute-start | bytes 221192 | tf_op jit(solution)/shard_map/ppermute | solution.py:393
  78.9 7.8 %collective-permute-start.12 = (f32[18,8,128]{2,1,0:T(8,128)S(1)}, f32[18,8,128]{2,1,0:T(8,128)S(1)}, u32[]{:S(2)}, u32[]{:S(2)}) collective-permute-start(f32[18,8,128]{2,1,0:T(8,128)S(1)} %get-tuple-element.56), channel_id=1, source_target_pairs={{0,32},{32,0},{64,96},{96,64},{128,160},{160,128},{192,224},{224,1... | collective-permute-start | bytes 221192 | tf_op jit(solution)/shard_map/ppermute | solution.py:393
  89.2 12.4 %copy-start.6 = (f32[16,24,128]{2,1,0:T(8,128)S(1)}, f32[16,24,128]{2,1,0:T(8,128)}, u32[]{:S(2)}) copy-start(f32[16,24,128]{2,1,0:T(8,128)} %get-tuple-element.35.wave) | copy-start | bytes 589828
  89.2 12.4 %collective-permute-start.16 = (f32[8,24,128]{2,1,0:T(8,128)S(1)}, f32[8,24,128]{2,1,0:T(8,128)S(1)}, u32[]{:S(2)}, u32[]{:S(2)}) collective-permute-start(f32[8,24,128]{2,1,0:T(8,128)S(1)} %get-tuple-element.64), channel_id=1, source_target_pairs={{1,2},{2,1},{3,4},{4,3},{5,6},{6,5},{9,10},{10,9},{11,12},{12,11},... | collective-permute-start | bytes 294920 | tf_op jit(solution)/shard_map/ppermute | solution.py:393
  92.7 8.9 %collective-permute-start.14 = (f32[16,8,128]{2,1,0:T(8,128)S(1)}, f32[16,8,128]{2,1,0:T(8,128)S(1)}, u32[]{:S(2)}, u32[]{:S(2)}) collective-permute-start(f32[16,8,128]{2,1,0:T(8,128)S(1)} %get-tuple-element.62), channel_id=1, source_target_pairs={{32,64},{64,32},{96,128},{128,96},{160,192},{192,160},{224,256},{2... | collective-permute-start | bytes 196616 | tf_op jit(solution)/shard_map/ppermute | solution.py:393
  93.4 8.2 %collective-permute-start.15 = (f32[16,8,128]{2,1,0:T(8,128)S(1)}, f32[16,8,128]{2,1,0:T(8,128)S(1)}, u32[]{:S(2)}, u32[]{:S(2)}) collective-permute-start(f32[16,8,128]{2,1,0:T(8,128)S(1)} %get-tuple-element.63), channel_id=1, source_target_pairs={{0,32},{32,0},{64,96},{96,64},{128,160},{160,128},{192,224},{224,1... | collective-permute-start | bytes 196616 | tf_op jit(solution)/shard_map/ppermute | solution.py:393
  (1 other events, 2.4 us)

commit v5 on v4

--- a/solution.py
+++ b/solution.py
@@ -446,6 +446,7 @@
         grant=60,
     )
     packets = lax.all_to_all(packets, ("gx", "gy"), 0, 0, tiled=True)
+    packets, even, odd = lax.optimization_barrier((packets, even, odd))
     even, odd = (swap(strip, "gy", parity) for parity, strip in enumerate((even, odd)))
     side, older_side, stiff_side, *faces = call(
         strip_unpack_kernel,

time: 104 us -> 103 us (level); the launches traced: 104 us -> 101 us
  starting transfers between devices: 52.3 us -> 45.8 us
  waiting for transfers between devices: 0.04 us -> 4.2 us
    ppermute x14, starting transfers between devices: 48.3 us -> 41.9 us  [swap(): return lax.ppermute(block, axis, pairs)]
    ppermute x14, waiting for transfers between devices: 0.04 us -> 4.2 us  [swap(): return lax.ppermute(block, axis, pairs)]
  transfers between devices with their start and end apart: 17 -> 17, of which waited for: 0 -> 1; matrix products, arithmetic and copies ran while one was open for 0% -> 0% of each run, Pallas kernels for 2% -> 2%
where the time goes in v5:
time: 103 us; the launch traced here: 101 us
  starting transfers between devices  45.8 us (44%)
  blocking collectives  36.1 us (35%)
  Pallas kernels  13.1 us (13%)
  waiting for transfers between devices  4.2 us (4%)
  between operations  1.6 us (2%)
    ppermute x14, starting transfers between devices, swap(): return lax.ppermute(block, axis, pairs)  41.9 us
    all_to_all x1, blocking collectives, on_device(): packets = lax.all_to_all(packets, ('gx', 'gy'), 0, 0, tiled=True)  27.9 us
    pallas_call x7, Pallas kernels, call(): pl.pallas_call(body, out_shape=outs, in_specs=in_specs or [smem()] + [vme...  13.1 us
    all_gather x4, blocking collectives, pair_gather(): lax.all_gather(block, axis, axis=0, tiled=False, axis_index_groups=groups)  8.18 us
    ppermute x14, waiting for transfers between devices, swap(): return lax.ppermute(block, axis, pairs)  4.2 us
    ppermute x3, starting transfers between devices, on_device(): lax.ppermute(packets, 'gz', [(chip + core, core) for core in range(cores)])  3.88 us
  transfers between devices with their start and end apart: 17, of which 1 were waited for; matrix products, arithmetic and copies ran while one was open for 0% of the time, Pallas kernels for 2%

profile of v5, /device:TPU:1, one launch (start us, length us, event | category | flops | bytes accessed | tf_op | source)
XLA Modules:
  0.0 101.5 jit_solution(18019838273069248417)
XLA Ops:
  1.9 2.3 %shard_map.121 = (f32[64,128]{1,0:T(8,128)}, f32[12,24,128]{2,1,0:T(8,128)}, f32[12,24,128]{2,1,0:T(8,128)}) custom-call(s32[5]{0:T(128)} %stack.23.ids, f32[4,128]{1,0:T(4,128)} %residuals.1, s32[1,128]{1,0:T(1,128)} %bitcast.29, s32[1,128]{1,0:T(1,128)} %bitcast.30, f32[16,24,128]{2,1,0:T(8,128)} %older.5, f32[16,24,128]{2,1,0:T(8,128)} %older.4, ...), custom_call_target="tpu_custom_call" | custom-call | flops 1000000 | bytes 2000000 | tf_op jit(solution)/shard_map/pallas_call | solution.py:66
  4.2 27.9 %all_to_all.12 = f32[64,1,128]{2,1,0:T(1,128)S(1)} all-to-all(f32[64,1,128]{2,1,0:T(1,128)} %bitcast.28), channel_id=1, replica_groups=mesh['gx'=16,'gy'=4,'gz'=8] {'gx','gy'}, dimensions={0} | all-to-all | bytes 65536 | tf_op jit(solution)/shard_map/all_to_all | solution.py:448
  32.2 2.4 %collective-permute-start = (f32[12,24,128]{2,1,0:T(8,128)}, f32[12,24,128]{2,1,0:T(8,128)S(1)}, u32[]{:S(2)}, u32[]{:S(2)}) collective-permute-start(f32[12,24,128]{2,1,0:T(8,128)} %get-tuple-element.43), channel_id=1, source_target_pairs={{0,8},{8,0},{16,24},{24,16},{1,9},{9,1},{17,25},{25,17},{2,10},{10... | collective-permute-start | bytes 442376 | tf_op jit(solution)/shard_map/ppermute | solution.py:393
  35.2 1.3 %collective-permute-start.7 = (f32[64,128]{1,0:T(8,128)S(1)}, f32[64,128]{1,0:T(8,128)S(1)}, u32[]{:S(2)}, u32[]{:S(2)}) collective-permute-start(f32[64,128]{1,0:T(8,128)S(1)} %bitcast.24), channel_id=1, source_target_pairs={{6,0},{7,1},{14,8},{15,9},{22,16},{23,17},{30,24},{31,25},{38,32},... | collective-permute-start | bytes 98312 | tf_op jit(solution)/shard_map/ppermute | solution.py:458
  36.5 1.3 %collective-permute-start.6 = (f32[64,128]{1,0:T(8,128)S(1)}, f32[64,128]{1,0:T(8,128)S(1)}, u32[]{:S(2)}, u32[]{:S(2)}) collective-permute-start(f32[64,128]{1,0:T(8,128)S(1)} %bitcast.25), channel_id=1, source_target_pairs={{4,0},{5,1},{12,8},{13,9},{20,16},{21,17},{28,24},{29,25},{36,32},... | collective-permute-start | bytes 98312 | tf_op jit(solution)/shard_map/ppermute | solution.py:458
  37.8 1.3 %collective-permute-start.5 = (f32[64,128]{1,0:T(8,128)S(1)}, f32[64,128]{1,0:T(8,128)S(1)}, u32[]{:S(2)}, u32[]{:S(2)}) collective-permute-start(f32[64,128]{1,0:T(8,128)S(1)} %bitcast.26), channel_id=1, source_target_pairs={{2,0},{3,1},{10,8},{11,9},{18,16},{19,17},{26,24},{27,25},{34,32},... | collective-permute-start | bytes 98312 | tf_op jit(solution)/shard_map/ppermute | solution.py:458
  39.1 4.2 %collective-permute-done.even = f32[12,24,128]{2,1,0:T(8,128)S(1)} collective-permute-done((f32[12,24,128]{2,1,0:T(8,128)}, f32[12,24,128]{2,1,0:T(8,128)S(1)}, u32[]{:S(2)}, u32[]{:S(2)}) %collective-permute-start) | collective-permute-done | bytes 147488 | tf_op jit(solution)/shard_map/ppermute | solution.py:393
  44.2 4.5 %collective-permute-start.4 = (f32[12,24,128]{2,1,0:T(8,128)S(1)}, f32[12,24,128]{2,1,0:T(8,128)S(1)}, u32[]{:S(2)}, u32[]{:S(2)}) collective-permute-start(f32[12,24,128]{2,1,0:T(8,128)S(1)} %get-tuple-element.47), channel_id=1, source_target_pairs={{1,2},{2,1},{3,4},{4,3},{5,6},{6,5},{9,10},{10,9},{11,12},{12,11},... | collective-permute-start | bytes 442376 | tf_op jit(solution)/shard_map/ppermute | solution.py:393
  49.3 4.7 %collective-permute-start.3 = (f32[24,8,128]{2,1,0:T(8,128)S(1)}, f32[24,8,128]{2,1,0:T(8,128)S(1)}, u32[]{:S(2)}, u32[]{:S(2)}) collective-permute-start(f32[24,8,128]{2,1,0:T(8,128)S(1)} %get-tuple-element.46), channel_id=1, source_target_pairs={{0,32},{32,0},{64,96},{96,64},{128,160},{160,128},{192,224},{224,1... | collective-permute-start | bytes 294920 | tf_op jit(solution)/shard_map/ppermute | solution.py:393
  54.0 1.6 %shard_map.123 = f32[20,24,128]{2,1,0:T(8,128)S(1)} custom-call(s32[5]{0:T(128)S(1)} %copy-done.7, f32[12,24,128]{2,1,0:T(8,128)S(1)} %get-tuple-element.48.z_even, f32[64,128]{1,0:T(8,128)S(1)} %bitcast.27, f32[64,128]{1,0:T(8,128)S(1)} %collective-permute-done.5.refs_1_, f32[64,128]{1,0:T(8,128)S(1)} %collective-permute-done.6.refs_2_, ...), custom_call_target="tpu_custom_call" | custom-call | flops 1000000 | bytes 2000000 | tf_op jit(solution)/shard_map/pallas_call | solution.py:66
  55.6 2.3 %all-gather = f32[40,24,128]{2,1,0:T(8,128)S(1)} all-gather(f32[20,24,128]{2,1,0:T(8,128)S(1)} %shard_map.123), channel_id=2, replica_groups={{0,1},{2,3},{4,5},{6,7},{8,9},{10,11},{12,13},{14,15},{16,17},{18,19},{..., dimensions={0}, use_global_device_ids=true | all-gather | bytes 737280 | tf_op jit(solution)/shard_map/all_gather | solution.py:402
  58.0 1.9 %shard_map.124 = (f32[8,24,128]{2,1,0:T(8,128)S(1)}, f32[16,24,128]{2,1,0:T(8,128)S(1)}, f32[16,24,128]{2,1,0:T(8,128)S(1)}, f32[16,24,128]{2,1,0:T(8,128)S(1)},...) custom-call(s32[5]{0:T(128)S(1)} %copy-done.7, ...), custom_call_target="tpu_custom_call" | custom-call | flops 1000000 | bytes 2000000 | tf_op jit(solution)/shard_map/pallas_call | solution.py:66
  59.9 2.1 %collective-permute-start.10 = (f32[10,24,128]{2,1,0:T(8,128)S(1)}, f32[10,24,128]{2,1,0:T(8,128)S(1)}, u32[]{:S(2)}, u32[]{:S(2)}) collective-permute-start(f32[10,24,128]{2,1,0:T(8,128)S(1)} %get-tuple-element.55), channel_id=1, source_target_pairs={{1,2},{2,1},{3,4},{4,3},{5,6},{6,5},{9,10},{10,9},{11,12},{12,11},... | collective-permute-start | bytes 368648 | tf_op jit(solution)/shard_map/ppermute | solution.py:393
  62.7 5.6 %collective-permute-start.9 = (f32[20,8,128]{2,1,0:T(8,128)S(1)}, f32[20,8,128]{2,1,0:T(8,128)S(1)}, u32[]{:S(2)}, u32[]{:S(2)}) collective-permute-start(f32[20,8,128]{2,1,0:T(8,128)S(1)} %get-tuple-element.54), channel_id=1, source_target_pairs={{0,32},{32,0},{64,96},{96,64},{128,160},{160,128},{192,224},{224,1... | collective-permute-start | bytes 245768 | tf_op jit(solution)/shard_map/ppermute | solution.py:393
  68.4 2.0 %all-gather.1 = f32[20,24,128]{2,1,0:T(8,128)S(1)} all-gather(f32[10,24,128]{2,1,0:T(8,128)S(1)} %get-tuple-element.56), channel_id=3, replica_groups={{0,1},{2,3},{4,5},{6,7},{8,9},{10,11},{12,13},{14,15},{16,17},{18,19},{..., dimensions={0}, use_global_device_ids=true | all-gather | bytes 368640 | tf_op jit(solution)/shard_map/all_gather | solution.py:402
  70.4 1.9 %shard_map.125 = (f32[16,24,128]{2,1,0:T(8,128)S(1)}, f32[16,24,128]{2,1,0:T(8,128)S(1)}, f32[16,24,128]{2,1,0:T(8,128)S(1)}, f32[9,24,128]{2,1,0:T(8,128)S(1)},...) custom-call(s32[5]{0:T(128)S(1)} %copy-done.7, ...), custom_call_target="tpu_custom_call" | custom-call | flops 1000000 | bytes 2000000 | tf_op jit(solution)/shard_map/pallas_call | solution.py:66
  72.3 4.2 %collective-permute-start.13 = (f32[9,24,128]{2,1,0:T(8,128)S(1)}, f32[9,24,128]{2,1,0:T(8,128)S(1)}, u32[]{:S(2)}, u32[]{:S(2)}) collective-permute-start(f32[9,24,128]{2,1,0:T(8,128)S(1)} %get-tuple-element.63), channel_id=1, source_target_pairs={{1,2},{2,1},{3,4},{4,3},{5,6},{6,5},{9,10},{10,9},{11,12},{12,11},... | collective-permute-start | bytes 331784 | tf_op jit(solution)/shard_map/ppermute | solution.py:393
  77.2 5.4 %collective-permute-start.12 = (f32[18,8,128]{2,1,0:T(8,128)S(1)}, f32[18,8,128]{2,1,0:T(8,128)S(1)}, u32[]{:S(2)}, u32[]{:S(2)}) collective-permute-start(f32[18,8,128]{2,1,0:T(8,128)S(1)} %get-tuple-element.62), channel_id=1, source_target_pairs={{0,32},{32,0},{64,96},{96,64},{128,160},{160,128},{192,224},{224,1... | collective-permute-start | bytes 221192 | tf_op jit(solution)/shard_map/ppermute | solution.py:393
  82.6 2.0 %all-gather.2 = f32[18,24,128]{2,1,0:T(8,128)S(1)} all-gather(f32[9,24,128]{2,1,0:T(8,128)S(1)} %get-tuple-element.64), channel_id=4, replica_groups={{0,1},{2,3},{4,5},{6,7},{8,9},{10,11},{12,13},{14,15},{16,17},{18,19},{..., dimensions={0}, use_global_device_ids=true | all-gather | bytes 331776 | tf_op jit(solution)/shard_map/all_gather | solution.py:402
  84.6 2.5 %shard_map.126 = (f32[16,24,128]{2,1,0:T(8,128)S(1)}, f32[16,24,128]{2,1,0:T(8,128)}, f32[16,24,128]{2,1,0:T(8,128)S(1)}, f32[8,24,128]{2,1,0:T(8,128)S(1)}, f32...) custom-call(s32[5]{0:T(128)S(1)} %copy-done.7, ...), custom_call_target="tpu_custom_call" | custom-call | flops 1000000 | bytes 2000000 | tf_op jit(solution)/shard_map/pallas_call | solution.py:66
  87.0 3.4 %collective-permute-start.16 = (f32[8,24,128]{2,1,0:T(8,128)S(1)}, f32[8,24,128]{2,1,0:T(8,128)S(1)}, u32[]{:S(2)}, u32[]{:S(2)}) collective-permute-start(f32[8,24,128]{2,1,0:T(8,128)S(1)} %get-tuple-element.70), channel_id=1, source_target_pairs={{1,2},{2,1},{3,4},{4,3},{5,6},{6,5},{9,10},{10,9},{11,12},{12,11},... | collective-permute-start | bytes 294920 | tf_op jit(solution)/shard_map/ppermute | solution.py:393
  91.2 6.3 %collective-permute-start.15 = (f32[16,8,128]{2,1,0:T(8,128)S(1)}, f32[16,8,128]{2,1,0:T(8,128)S(1)}, u32[]{:S(2)}, u32[]{:S(2)}) collective-permute-start(f32[16,8,128]{2,1,0:T(8,128)S(1)} %get-tuple-element.69), channel_id=1, source_target_pairs={{0,32},{32,0},{64,96},{96,64},{128,160},{160,128},{192,224},{224,1... | collective-permute-start | bytes 196616 | tf_op jit(solution)/shard_map/ppermute | solution.py:393
  97.5 1.9 %all-gather.3 = f32[16,24,128]{2,1,0:T(8,128)S(1)} all-gather(f32[8,24,128]{2,1,0:T(8,128)S(1)} %get-tuple-element.71), channel_id=5, replica_groups={{0,1},{2,3},{4,5},{6,7},{8,9},{10,11},{12,13},{14,15},{16,17},{18,19},{..., dimensions={0}, use_global_device_ids=true | all-gather | bytes 294912 | tf_op jit(solution)/shard_map/all_gather | solution.py:402
  99.4 2.1 %shard_map.127 = (f32[16,24,128]{2,1,0:T(8,128)}, f32[16,24,128]{2,1,0:T(8,128)}) custom-call(s32[5]{0:T(128)S(1)} %copy-done.7, f32[16,8,128]{2,1,0:T(8,128)S(1)} %collective-permute-done.14.x_odd_in, f32[16,8,128]{2,1,0:T(8,128)S(1)} %collective-permute-done.15.x_even_in, f32[8,24,128]{2,1,0:T(8,128)S(1)} %collective-permute-done.16.z_odd_in, ...), custom_call_target="tpu_custom_call" | custom-call | flops 1000000 | bytes 2000000 | tf_op jit(solution)/shard_map/pallas_call | solution.py:66
  (39 shorter events, 4.9 us)
Async XLA Ops:
  1.9 41.4 %copy-start.2 = (f32[16,24,128]{2,1,0:T(8,128)S(1)}, f32[16,24,128]{2,1,0:T(8,128)}, u32[]{:S(2)}) copy-start(f32[16,24,128]{2,1,0:T(8,128)} %older.5) | copy-start | bytes 589828
  32.2 11.1 %copy-start.7 = (s32[5]{0:T(128)S(1)}, s32[5]{0:T(128)}, u32[]{:S(2)}) copy-start(s32[5]{0:T(128)} %stack.23.ids) | copy-start | bytes 64
  32.2 11.1 %collective-permute-start = (f32[12,24,128]{2,1,0:T(8,128)}, f32[12,24,128]{2,1,0:T(8,128)S(1)}, u32[]{:S(2)}, u32[]{:S(2)}) collective-permute-start(f32[12,24,128]{2,1,0:T(8,128)} %get-tuple-element.43), channel_id=1, source_target_pairs={{0,8},{8,0},{16,24},{24,16},{1,9},{9,1},{17,25},{25,17},{2,10},{10... | collective-permute-start | bytes 442376 | tf_op jit(solution)/shard_map/ppermute | solution.py:393
  34.5 8.7 %collective-permute-start.1 = (f32[12,24,128]{2,1,0:T(8,128)}, f32[12,24,128]{2,1,0:T(8,128)S(1)}, u32[]{:S(2)}, u32[]{:S(2)}) collective-permute-start(f32[12,24,128]{2,1,0:T(8,128)} %get-tuple-element.44), channel_id=1, source_target_pairs={{8,16},{16,8},{9,17},{17,9},{10,18},{18,10},{11,19},{19,11},{12,20... | collective-permute-start | bytes 442376 | tf_op jit(solution)/shard_map/ppermute | solution.py:393
  35.2 14.1 %collective-permute-start.7 = (f32[64,128]{1,0:T(8,128)S(1)}, f32[64,128]{1,0:T(8,128)S(1)}, u32[]{:S(2)}, u32[]{:S(2)}) collective-permute-start(f32[64,128]{1,0:T(8,128)S(1)} %bitcast.24), channel_id=1, source_target_pairs={{6,0},{7,1},{14,8},{15,9},{22,16},{23,17},{30,24},{31,25},{38,32},... | collective-permute-start | bytes 98312 | tf_op jit(solution)/shard_map/ppermute | solution.py:458
  36.5 17.5 %collective-permute-start.6 = (f32[64,128]{1,0:T(8,128)S(1)}, f32[64,128]{1,0:T(8,128)S(1)}, u32[]{:S(2)}, u32[]{:S(2)}) collective-permute-start(f32[64,128]{1,0:T(8,128)S(1)} %bitcast.25), channel_id=1, source_target_pairs={{4,0},{5,1},{12,8},{13,9},{20,16},{21,17},{28,24},{29,25},{36,32},... | collective-permute-start | bytes 98312 | tf_op jit(solution)/shard_map/ppermute | solution.py:458
  37.8 16.2 %collective-permute-start.5 = (f32[64,128]{1,0:T(8,128)S(1)}, f32[64,128]{1,0:T(8,128)S(1)}, u32[]{:S(2)}, u32[]{:S(2)}) collective-permute-start(f32[64,128]{1,0:T(8,128)S(1)} %bitcast.26), channel_id=1, source_target_pairs={{2,0},{3,1},{10,8},{11,9},{18,16},{19,17},{26,24},{27,25},{34,32},... | collective-permute-start | bytes 98312 | tf_op jit(solution)/shard_map/ppermute | solution.py:458
  44.2 13.8 %collective-permute-start.4 = (f32[12,24,128]{2,1,0:T(8,128)S(1)}, f32[12,24,128]{2,1,0:T(8,128)S(1)}, u32[]{:S(2)}, u32[]{:S(2)}) collective-permute-start(f32[12,24,128]{2,1,0:T(8,128)S(1)} %get-tuple-element.47), channel_id=1, source_target_pairs={{1,2},{2,1},{3,4},{4,3},{5,6},{6,5},{9,10},{10,9},{11,12},{12,11},... | collective-permute-start | bytes 442376 | tf_op jit(solution)/shard_map/ppermute | solution.py:393
  48.6 9.3 %collective-permute-start.2 = (f32[24,8,128]{2,1,0:T(8,128)S(1)}, f32[24,8,128]{2,1,0:T(8,128)S(1)}, u32[]{:S(2)}, u32[]{:S(2)}) collective-permute-start(f32[24,8,128]{2,1,0:T(8,128)S(1)} %get-tuple-element.45), channel_id=1, source_target_pairs={{32,64},{64,32},{96,128},{128,96},{160,192},{192,160},{224,256},{2... | collective-permute-start | bytes 294920 | tf_op jit(solution)/shard_map/ppermute | solution.py:393
  49.3 8.6 %collective-permute-start.3 = (f32[24,8,128]{2,1,0:T(8,128)S(1)}, f32[24,8,128]{2,1,0:T(8,128)S(1)}, u32[]{:S(2)}, u32[]{:S(2)}) collective-permute-start(f32[24,8,128]{2,1,0:T(8,128)S(1)} %get-tuple-element.46), channel_id=1, source_target_pairs={{0,32},{32,0},{64,96},{96,64},{128,160},{160,128},{192,224},{224,1... | collective-permute-start | bytes 294920 | tf_op jit(solution)/shard_map/ppermute | solution.py:393
  54.0 3.9 %copy-start.4 = (bf16[256,256]{1,0:T(8,128)(2,1)S(1)}, bf16[256,256]{1,0:T(8,128)(2,1)}, u32[]{:S(2)}) copy-start(bf16[256,256]{1,0:T(8,128)(2,1)} %constant.44.clone.band_high) | copy-start | bytes 393220
  54.0 3.9 %copy-start.5 = (f32[16,24,128]{2,1,0:T(8,128)S(1)}, f32[16,24,128]{2,1,0:T(8,128)}, u32[]{:S(2)}) copy-start(f32[16,24,128]{2,1,0:T(8,128)} %older.4) | copy-start | bytes 589828
  55.6 2.4 %copy-start = (bf16[4,16,24,128]{3,2,1,0:T(8,128)(2,1)S(1)}, bf16[4,16,24,128]{3,2,1,0:T(8,128)(2,1)}, u32[]{:S(2)}) copy-start(bf16[4,16,24,128]{3,2,1,0:T(8,128)(2,1)} %forward.7) | copy-start | bytes 1179652
  55.6 2.4 %copy-start.1 = (f32[16,24,128]{2,1,0:T(8,128)S(1)}, f32[16,24,128]{2,1,0:T(8,128)}, u32[]{:S(2)}) copy-start(f32[16,24,128]{2,1,0:T(8,128)} %stiff.9) | copy-start | bytes 589828
  59.9 10.5 %collective-permute-start.10 = (f32[10,24,128]{2,1,0:T(8,128)S(1)}, f32[10,24,128]{2,1,0:T(8,128)S(1)}, u32[]{:S(2)}, u32[]{:S(2)}) collective-permute-start(f32[10,24,128]{2,1,0:T(8,128)S(1)} %get-tuple-element.55), channel_id=1, source_target_pairs={{1,2},{2,1},{3,4},{4,3},{5,6},{6,5},{9,10},{10,9},{11,12},{12,11},... | collective-permute-start | bytes 368648 | tf_op jit(solution)/shard_map/ppermute | solution.py:393
  62.1 8.3 %collective-permute-start.8 = (f32[20,8,128]{2,1,0:T(8,128)S(1)}, f32[20,8,128]{2,1,0:T(8,128)S(1)}, u32[]{:S(2)}, u32[]{:S(2)}) collective-permute-start(f32[20,8,128]{2,1,0:T(8,128)S(1)} %get-tuple-element.53), channel_id=1, source_target_pairs={{32,64},{64,32},{96,128},{128,96},{160,192},{192,160},{224,256},{2... | collective-permute-start | bytes 245768 | tf_op jit(solution)/shard_map/ppermute | solution.py:393
  62.7 7.6 %collective-permute-start.9 = (f32[20,8,128]{2,1,0:T(8,128)S(1)}, f32[20,8,128]{2,1,0:T(8,128)S(1)}, u32[]{:S(2)}, u32[]{:S(2)}) collective-permute-start(f32[20,8,128]{2,1,0:T(8,128)S(1)} %get-tuple-element.54), channel_id=1, source_target_pairs={{0,32},{32,0},{64,96},{96,64},{128,160},{160,128},{192,224},{224,1... | collective-permute-start | bytes 245768 | tf_op jit(solution)/shard_map/ppermute | solution.py:393
  72.3 12.3 %collective-permute-start.13 = (f32[9,24,128]{2,1,0:T(8,128)S(1)}, f32[9,24,128]{2,1,0:T(8,128)S(1)}, u32[]{:S(2)}, u32[]{:S(2)}) collective-permute-start(f32[9,24,128]{2,1,0:T(8,128)S(1)} %get-tuple-element.63), channel_id=1, source_target_pairs={{1,2},{2,1},{3,4},{4,3},{5,6},{6,5},{9,10},{10,9},{11,12},{12,11},... | collective-permute-start | bytes 331784 | tf_op jit(solution)/shard_map/ppermute | solution.py:393
  76.5 8.1 %collective-permute-start.11 = (f32[18,8,128]{2,1,0:T(8,128)S(1)}, f32[18,8,128]{2,1,0:T(8,128)S(1)}, u32[]{:S(2)}, u32[]{:S(2)}) collective-permute-start(f32[18,8,128]{2,1,0:T(8,128)S(1)} %get-tuple-element.61), channel_id=1, source_target_pairs={{32,64},{64,32},{96,128},{128,96},{160,192},{192,160},{224,256},{2... | collective-permute-start | bytes 221192 | tf_op jit(solution)/shard_map/ppermute | solution.py:393
  77.2 7.4 %collective-permute-start.12 = (f32[18,8,128]{2,1,0:T(8,128)S(1)}, f32[18,8,128]{2,1,0:T(8,128)S(1)}, u32[]{:S(2)}, u32[]{:S(2)}) collective-permute-start(f32[18,8,128]{2,1,0:T(8,128)S(1)} %get-tuple-element.62), channel_id=1, source_target_pairs={{0,32},{32,0},{64,96},{96,64},{128,160},{160,128},{192,224},{224,1... | collective-permute-start | bytes 221192 | tf_op jit(solution)/shard_map/ppermute | solution.py:393
  87.0 12.4 %copy-start.6 = (f32[16,24,128]{2,1,0:T(8,128)S(1)}, f32[16,24,128]{2,1,0:T(8,128)}, u32[]{:S(2)}) copy-start(f32[16,24,128]{2,1,0:T(8,128)} %get-tuple-element.38.wave) | copy-start | bytes 589828
  87.0 12.4 %collective-permute-start.16 = (f32[8,24,128]{2,1,0:T(8,128)S(1)}, f32[8,24,128]{2,1,0:T(8,128)S(1)}, u32[]{:S(2)}, u32[]{:S(2)}) collective-permute-start(f32[8,24,128]{2,1,0:T(8,128)S(1)} %get-tuple-element.70), channel_id=1, source_target_pairs={{1,2},{2,1},{3,4},{4,3},{5,6},{6,5},{9,10},{10,9},{11,12},{12,11},... | collective-permute-start | bytes 294920 | tf_op jit(solution)/shard_map/ppermute | solution.py:393
  90.5 8.9 %collective-permute-start.14 = (f32[16,8,128]{2,1,0:T(8,128)S(1)}, f32[16,8,128]{2,1,0:T(8,128)S(1)}, u32[]{:S(2)}, u32[]{:S(2)}) collective-permute-start(f32[16,8,128]{2,1,0:T(8,128)S(1)} %get-tuple-element.68), channel_id=1, source_target_pairs={{32,64},{64,32},{96,128},{128,96},{160,192},{192,160},{224,256},{2... | collective-permute-start | bytes 196616 | tf_op jit(solution)/shard_map/ppermute | solution.py:393
  91.2 8.2 %collective-permute-start.15 = (f32[16,8,128]{2,1,0:T(8,128)S(1)}, f32[16,8,128]{2,1,0:T(8,128)S(1)}, u32[]{:S(2)}, u32[]{:S(2)}) collective-permute-start(f32[16,8,128]{2,1,0:T(8,128)S(1)} %get-tuple-element.69), channel_id=1, source_target_pairs={{0,32},{32,0},{64,96},{96,64},{128,160},{160,128},{192,224},{224,1... | collective-permute-start | bytes 196616 | tf_op jit(solution)/shard_map/ppermute | solution.py:393
  (1 other events, 2.4 us)

commit v6 on v5

--- a/solution.py
+++ b/solution.py
@@ -272,76 +272,102 @@
     write_faces(STRIP, ids, wave, wave_side, z_even, z_odd, x_even, x_odd)
 
 
-def fill(width, ids, wave, side, z_even, z_odd, x_even, x_odd, z_ext, x_ext):
+def fill(width, ids, z_even, z_odd, x_even, x_odd, z_halo, x_halo):
     z_parity, x_parity = ids[0] & 1, ids[1] & 1
-    depth, rows, _ = wave.shape
+    depth = x_halo.shape[1]
     count = folds(width)
-    for part, field in enumerate((wave, side) if width else (wave,)):
-        z_ext[part, pl.ds(RADIUS, depth)] = field[...]
-        x_ext[part, :, pl.ds(RADIUS, rows), :] = field[...]
     pair = z_even.at[1 - z_parity]
-    for face, start in (
-        (pair, (depth + RADIUS) * (1 - z_parity)),
-        (z_odd, (depth + RADIUS) * z_parity),
-    ):
-        z_ext[0, pl.ds(start, RADIUS)] = face[pl.ds(0, RADIUS)]
+    for face, start in ((pair, RADIUS * (1 - z_parity)), (z_odd, RADIUS * z_parity)):
+        z_halo[0, pl.ds(start, RADIUS)] = face[pl.ds(0, RADIUS)]
         span = folded(RADIUS, width)
         for plane in range(span):
             both = face[RADIUS + plane]
             for turn in range(count):
-                z_ext[1, start + plane + span * turn] = unfold(both, turn, width)
-    for face, start in (
-        (x_even, (rows + RADIUS) * (1 - x_parity)),
-        (x_odd, (rows + RADIUS) * x_parity),
-    ):
+                z_halo[1, start + plane + span * turn] = unfold(both, turn, width)
+    for face, start in ((x_even, RADIUS * (1 - x_parity)), (x_odd, RADIUS * x_parity)):
         start = pl.multiple_of(start, RADIUS)
-        x_ext[0, :, pl.ds(start, RADIUS), :] = face[pl.ds(0, depth)]
+        x_halo[0, :, pl.ds(start, RADIUS), :] = face[pl.ds(0, depth)]
         span = folded(depth, width)
         for plane in range(span):
             both = face[depth + plane]
             for turn in range(count):
-                x_ext[1, plane + span * turn, pl.ds(start, RADIUS), :] = unfold(both, turn, width)
-
-
-def advance(step, ids, wave, side, older, older_side, stiff, stiff_side, forward, image_in,
-            planes, band_high, band_low, fresh, fresh_side, image, z_ext, x_ext, y_terms):
+                x_halo[1, plane + span * turn, pl.ds(start, RADIUS), :] = unfold(both, turn, width)
+
+
+def own_kernel(last, wave, side, band_high, band_low, *rest):
+    *outs, y_terms = rest
     depth, rows, _ = wave.shape
-    last = step == STEPS - 1
-    width = LANES if last else 2 * LANES
+    width = LANES * len(outs)
     both = jnp.concatenate(
         [wave[...].reshape(depth * rows, LANES), side[...].reshape(depth * rows, LANES)], axis=1
     )
     high = both.astype(BF16)
     low = (both - high.astype(F32)).astype(BF16)
-    matrix, rest = band_high[:, :width], band_low[:, :width]
+    matrix, remainder = band_high[:, :width], band_low[:, :width]
     y_terms[:, :width] = (
         jnp.dot(high, matrix, preferred_element_type=F32)
         + jnp.dot(low, matrix, preferred_element_type=F32)
-        + jnp.dot(high, rest, preferred_element_type=F32)
-    )
-
-    def one(z, part, field, before, speed, target):
-        column = x_ext[part, z]
-        turned = [None] + [
-            pltpu.roll(column, rows + 2 * RADIUS - offset, 0) for offset in range(1, RADIUS)
-        ]
-        total = y_terms[z * rows : (z + 1) * rows, part * LANES : (part + 1) * LANES]
+        + jnp.dot(high, remainder, preferred_element_type=F32)
+    )
+    beyond = jnp.zeros((RADIUS, LANES), F32)
+    for z in range(depth):
+        for part, (field, out) in enumerate(zip((wave, side), outs)):
+            column = jnp.concatenate([beyond, field[z], beyond], axis=0)
+            turned = [None] + [
+                pltpu.roll(column, rows + 2 * RADIUS - offset, 0) for offset in range(1, RADIUS)
+            ]
+            total = y_terms[z * rows : (z + 1) * rows, part * LANES : (part + 1) * LANES]
+            for offset in range(1, RADIUS + 1):
+                if offset < RADIUS:
+                    near = turned[offset][RADIUS : RADIUS + rows] + turned[RADIUS - offset][:rows]
+                else:
+                    near = column[2 * RADIUS :] + column[:rows]
+                if z + offset < depth:
+                    near = near + field[z + offset]
+                if z >= offset:
+                    near = near + field[z - offset]
+                total = total + WEIGHTS[offset - 1] * near
+            out[z] = total
+
+
+def advance(step, ids, wave, side, older, older_side, stiff, stiff_side, forward, image_in,
+            planes, own, own_side, fresh, fresh_side, image, z_halo, x_halo):
+    depth, rows, _ = wave.shape
+    last = step == STEPS - 1
+    line = lax.broadcasted_iota(jnp.int32, (RADIUS, LANES), 0)
+    before_tile = [
+        jnp.where(line < offset, WEIGHTS[offset - 1], 0.0) for offset in range(1, RADIUS + 1)
+    ]
+    behind_tile = [
+        jnp.where(line >= RADIUS - offset, WEIGHTS[offset - 1], 0.0)
+        for offset in range(1, RADIUS + 1)
+    ]
+    between = jnp.zeros((rows - 2 * RADIUS, LANES), F32)
+
+    def one(z, part, partial, field, previous, speed, target):
+        total = partial[z]
+        first = last_rows = None
+        head, tail = x_halo[part, z, :RADIUS], x_halo[part, z, RADIUS:]
         for offset in range(1, RADIUS + 1):
-            near = z_ext[part, RADIUS + z + offset] + z_ext[part, RADIUS + z - offset]
-            if offset < RADIUS:
-                near = near + turned[offset][RADIUS : RADIUS + rows]
-                near = near + turned[RADIUS - offset][:rows]
-            else:
-                near = near + column[2 * RADIUS :] + column[:rows]
-            total = total + WEIGHTS[offset - 1] * near
+            if z < offset:
+                total = total + WEIGHTS[offset - 1] * z_halo[part, RADIUS + z - offset]
+            if z + offset >= depth:
+                total = total + WEIGHTS[offset - 1] * z_halo[part, RADIUS + z + offset - depth]
+            above = pltpu.roll(head, offset, 0) if offset < RADIUS else head
+            below = pltpu.roll(tail, RADIUS - offset, 0) if offset < RADIUS else tail
+            above = before_tile[offset - 1] * above
+            below = behind_tile[offset - 1] * below
+            first = above if first is None else first + above
+            last_rows = below if last_rows is None else last_rows + below
+        total = total + jnp.concatenate([first, between, last_rows], axis=0)
         if z == 0:
             total = total + planes[STEPS * part + step]
-        value = 2.0 * field[z] - before[z] + speed[z] * total
+        value = 2.0 * field[z] - previous[z] + speed[z] * total
         target[z] = value
         return value
 
     for z in range(depth):
-        value = one(z, 0, wave, older, stiff, fresh)
+        value = one(z, 0, own, wave, older, stiff, fresh)
         product = forward[step, z].astype(F32) * value
         if step:
             product = product + image_in[z]
@@ -349,7 +375,7 @@
             product = product * muting(ids, z, depth, rows)
         image[z] = product
         if not last:
-            one(z, 1, side, older_side, stiff_side, fresh_side)
+            one(z, 1, own_side, side, older_side, stiff_side, fresh_side)
 
 
 def muting(ids, z, depth, rows):
@@ -363,8 +389,11 @@
 
 
 def step_kernel(step, ids, x_odd_in, x_even_in, z_odd_in, z_even_in, wave, side, older,
-                older_side, stiff, stiff_side, forward, band_high, band_low, *rest):
-    image_in = None
+                older_side, stiff, stiff_side, forward, own, *rest):
+    last = step == STEPS - 1
+    own_side = image_in = None
+    if not last:
+        own_side, *rest = rest
     if step:
         planes, image_in, *rest = rest
     else:
@@ -372,15 +401,14 @@
         face = z_even_in.shape[1] - 2 * STEPS
         both = z_even_in[0, pl.ds(face, 2 * STEPS)] + z_even_in[1, pl.ds(face, 2 * STEPS)]
         planes[...] = jnp.where(ids[0] == 0, both, 0.0)
-    last = step == STEPS - 1
     if last:
-        image, fresh, z_ext, x_ext, y_terms = rest
+        image, fresh, z_halo, x_halo = rest
         fresh_side = None
     else:
-        (image, fresh, fresh_side, z_even, z_odd, x_even, x_odd, z_ext, x_ext, y_terms) = rest
-    fill(strip_width(step), ids, wave, side, z_even_in, z_odd_in, x_even_in, x_odd_in, z_ext, x_ext)
+        image, fresh, fresh_side, z_even, z_odd, x_even, x_odd, z_halo, x_halo = rest
+    fill(strip_width(step), ids, z_even_in, z_odd_in, x_even_in, x_odd_in, z_halo, x_halo)
     advance(step, ids, wave, side, older, older_side, stiff, stiff_side, forward, image_in,
-            planes, band_high, band_low, fresh, fresh_side, image, z_ext, x_ext, y_terms)
+            planes, own, own_side, fresh, fresh_side, image, z_halo, x_halo)
     if not last:
         write_faces(strip_width(step + 1), ids, fresh, fresh_side, z_even, z_odd, x_even, x_odd)
 
@@ -467,29 +495,36 @@
     )
 
     scratch = [
-        pltpu.VMEM((2, depth + 2 * RADIUS, rows, LANES), F32),
-        pltpu.VMEM((2, depth, rows + 2 * RADIUS, LANES), F32),
-        pltpu.VMEM((depth * rows, 2 * LANES), F32),
+        pltpu.VMEM((2, 2 * RADIUS, rows, LANES), F32),
+        pltpu.VMEM((2, depth, 2 * RADIUS, LANES), F32),
     ]
     wave, older = wave_now, older_wave
     image = None
     for step in range(STEPS):
+        last = step == STEPS - 1
+        own = call(
+            functools.partial(own_kernel, last),
+            [block] if last else [block, block],
+            [wave, side, band_high, band_low],
+            scratch=[pltpu.VMEM((depth * rows, 2 * LANES), F32)],
+            in_specs=[vmem()] * 4,
+        )
         faces = exchange(faces)
         ins = [ids, *faces[::-1], wave, side, older, older_side, stiffness, stiff_side, forward_wave,
-               band_high, band_low]
+               *own]
         outs = [block, block]
         if step:
             ins += [planes, image]
         else:
             outs = [shaped(2 * STEPS, rows, LANES)] + outs
-        if step < STEPS - 1:
+        if not last:
             outs += [block] + faces_out(step + 1)
         rest = call(functools.partial(step_kernel, step), outs, ins, scratch)
         if not step:
             planes, *rest = rest
         image, fresh, *rest = rest
         older, wave = wave, fresh
-        if step < STEPS - 1:
+        if not last:
             older_side, side = side, rest[0]
             faces = rest[1:]
     return image, older, wave

time: 103 us -> 102 us (level)
  starting transfers between devices: 45.8 us -> 43.3 us
    ppermute x14, starting transfers between devices: 41.9 us -> 39.5 us  [swap(): return lax.ppermute(block, axis, pairs)]
    pallas_call x7 -> x11, Pallas kernels: 13.1 us -> 13.8 us  [call(): pl.pallas_call(body, out_shape=outs, in_specs=in_specs or [smem()] + [vme...]
  transfers between devices with their start and end apart: 17 -> 17, of which waited for: 1 -> 1; matrix products, arithmetic and copies ran while one was open for 0% -> 0% of each run, Pallas kernels for 2% -> 6%
where the time goes in v6:
time: 102 us; the launch traced here: 101 us
  starting transfers between devices  43.3 us (42%)
  blocking collectives  36.1 us (35%)
  Pallas kernels  13.8 us (14%)
  waiting for transfers between devices  4.2 us (4%)
  between operations  1.61 us (2%)
  local copies, waits for them, and re-layouts  1.55 us (2%)
    ppermute x14, starting transfers between devices, swap(): return lax.ppermute(block, axis, pairs)  39.5 us
    all_to_all x1, blocking collectives, on_device(): packets = lax.all_to_all(packets, ('gx', 'gy'), 0, 0, tiled=True)  27.9 us
    pallas_call x11, Pallas kernels, call(): pl.pallas_call(body, out_shape=outs, in_specs=in_specs or [smem()] + [vme...  13.8 us
    all_gather x4, blocking collectives, pair_gather(): lax.all_gather(block, axis, axis=0, tiled=False, axis_index_groups=groups)  8.18 us
    ppermute x14, waiting for transfers between devices, swap(): return lax.ppermute(block, axis, pairs)  4.2 us
    ppermute x3, starting transfers between devices, on_device(): lax.ppermute(packets, 'gz', [(chip + core, core) for core in range(cores)])  3.88 us
  transfers between devices with their start and end apart: 17, of which 1 were waited for; matrix products, arithmetic and copies ran while one was open for 0% of the time, Pallas kernels for 6%

profile of v6, /device:TPU:1, one launch (start us, length us, event | category | flops | bytes accessed | tf_op | source)
XLA Modules:
  0.0 100.6 jit_solution(4709088995600464572)
XLA Ops:
  1.9 2.3 %shard_map.121 = (f32[64,128]{1,0:T(8,128)}, f32[12,24,128]{2,1,0:T(8,128)}, f32[12,24,128]{2,1,0:T(8,128)}) custom-call(s32[5]{0:T(128)} %stack.23.ids, f32[4,128]{1,0:T(4,128)} %residuals.1, s32[1,128]{1,0:T(1,128)} %bitcast.29, s32[1,128]{1,0:T(1,128)} %bitcast.30, f32[16,24,128]{2,1,0:T(8,128)} %older.5, f32[16,24,128]{2,1,0:T(8,128)} %older.4, ...), custom_call_target="tpu_custom_call" | custom-call | flops 1000000 | bytes 2000000 | tf_op jit(solution)/shard_map/pallas_call | solution.py:66
  4.2 27.9 %all_to_all.12 = f32[64,1,128]{2,1,0:T(1,128)S(1)} all-to-all(f32[64,1,128]{2,1,0:T(1,128)} %bitcast.28), channel_id=1, replica_groups=mesh['gx'=16,'gy'=4,'gz'=8] {'gx','gy'}, dimensions={0} | all-to-all | bytes 65536 | tf_op jit(solution)/shard_map/all_to_all | solution.py:476
  32.2 2.4 %collective-permute-start = (f32[12,24,128]{2,1,0:T(8,128)}, f32[12,24,128]{2,1,0:T(8,128)S(1)}, u32[]{:S(2)}, u32[]{:S(2)}) collective-permute-start(f32[12,24,128]{2,1,0:T(8,128)} %get-tuple-element.49), channel_id=1, source_target_pairs={{0,8},{8,0},{16,24},{24,16},{1,9},{9,1},{17,25},{25,17},{2,10},{10... | collective-permute-start | bytes 442376 | tf_op jit(solution)/shard_map/ppermute | solution.py:421
  35.2 1.3 %collective-permute-start.7 = (f32[64,128]{1,0:T(8,128)S(1)}, f32[64,128]{1,0:T(8,128)S(1)}, u32[]{:S(2)}, u32[]{:S(2)}) collective-permute-start(f32[64,128]{1,0:T(8,128)S(1)} %bitcast.24), channel_id=1, source_target_pairs={{6,0},{7,1},{14,8},{15,9},{22,16},{23,17},{30,24},{31,25},{38,32},... | collective-permute-start | bytes 98312 | tf_op jit(solution)/shard_map/ppermute | solution.py:486
  36.5 1.3 %collective-permute-start.6 = (f32[64,128]{1,0:T(8,128)S(1)}, f32[64,128]{1,0:T(8,128)S(1)}, u32[]{:S(2)}, u32[]{:S(2)}) collective-permute-start(f32[64,128]{1,0:T(8,128)S(1)} %bitcast.25), channel_id=1, source_target_pairs={{4,0},{5,1},{12,8},{13,9},{20,16},{21,17},{28,24},{29,25},{36,32},... | collective-permute-start | bytes 98312 | tf_op jit(solution)/shard_map/ppermute | solution.py:486
  37.8 1.3 %collective-permute-start.5 = (f32[64,128]{1,0:T(8,128)S(1)}, f32[64,128]{1,0:T(8,128)S(1)}, u32[]{:S(2)}, u32[]{:S(2)}) collective-permute-start(f32[64,128]{1,0:T(8,128)S(1)} %bitcast.26), channel_id=1, source_target_pairs={{2,0},{3,1},{10,8},{11,9},{18,16},{19,17},{26,24},{27,25},{34,32},... | collective-permute-start | bytes 98312 | tf_op jit(solution)/shard_map/ppermute | solution.py:486
  39.1 4.2 %collective-permute-done.even = f32[12,24,128]{2,1,0:T(8,128)S(1)} collective-permute-done((f32[12,24,128]{2,1,0:T(8,128)}, f32[12,24,128]{2,1,0:T(8,128)S(1)}, u32[]{:S(2)}, u32[]{:S(2)}) %collective-permute-start) | collective-permute-done | bytes 147488 | tf_op jit(solution)/shard_map/ppermute | solution.py:421
  44.2 4.5 %collective-permute-start.4 = (f32[12,24,128]{2,1,0:T(8,128)S(1)}, f32[12,24,128]{2,1,0:T(8,128)S(1)}, u32[]{:S(2)}, u32[]{:S(2)}) collective-permute-start(f32[12,24,128]{2,1,0:T(8,128)S(1)} %get-tuple-element.53), channel_id=1, source_target_pairs={{1,2},{2,1},{3,4},{4,3},{5,6},{6,5},{9,10},{10,9},{11,12},{12,11},... | collective-permute-start | bytes 442376 | tf_op jit(solution)/shard_map/ppermute | solution.py:421
  50.3 4.7 %collective-permute-start.3 = (f32[24,8,128]{2,1,0:T(8,128)S(1)}, f32[24,8,128]{2,1,0:T(8,128)S(1)}, u32[]{:S(2)}, u32[]{:S(2)}) collective-permute-start(f32[24,8,128]{2,1,0:T(8,128)S(1)} %get-tuple-element.52), channel_id=1, source_target_pairs={{0,32},{32,0},{64,96},{96,64},{128,160},{160,128},{192,224},{224,1... | collective-permute-start | bytes 294920 | tf_op jit(solution)/shard_map/ppermute | solution.py:421
  55.0 1.6 %shard_map.123 = f32[20,24,128]{2,1,0:T(8,128)S(1)} custom-call(s32[5]{0:T(128)S(1)} %copy-done.7, f32[12,24,128]{2,1,0:T(8,128)S(1)} %get-tuple-element.54.z_even, f32[64,128]{1,0:T(8,128)S(1)} %bitcast.27, f32[64,128]{1,0:T(8,128)S(1)} %collective-permute-done.5.refs_1_, f32[64,128]{1,0:T(8,128)S(1)} %collective-permute-done.6.refs_2_, ...), custom_call_target="tpu_custom_call" | custom-call | flops 1000000 | bytes 2000000 | tf_op jit(solution)/shard_map/pallas_call | solution.py:66
  56.6 2.3 %all-gather = f32[40,24,128]{2,1,0:T(8,128)S(1)} all-gather(f32[20,24,128]{2,1,0:T(8,128)S(1)} %shard_map.123), channel_id=2, replica_groups={{0,1},{2,3},{4,5},{6,7},{8,9},{10,11},{12,13},{14,15},{16,17},{18,19},{..., dimensions={0}, use_global_device_ids=true | all-gather | bytes 737280 | tf_op jit(solution)/shard_map/all_gather | solution.py:430
  58.9 1.2 %shard_map.125 = (f32[8,24,128]{2,1,0:T(8,128)S(1)}, f32[16,24,128]{2,1,0:T(8,128)S(1)}, f32[16,24,128]{2,1,0:T(8,128)S(1)}, f32[16,24,128]{2,1,0:T(8,128)S(1)},...) custom-call(s32[5]{0:T(128)S(1)} %copy-done.7, ...), custom_call_target="tpu_custom_call" | custom-call | flops 1000000 | bytes 2000000 | tf_op jit(solution)/shard_map/pallas_call | solution.py:66
  60.1 2.1 %collective-permute-start.10 = (f32[10,24,128]{2,1,0:T(8,128)S(1)}, f32[10,24,128]{2,1,0:T(8,128)S(1)}, u32[]{:S(2)}, u32[]{:S(2)}) collective-permute-start(f32[10,24,128]{2,1,0:T(8,128)S(1)} %get-tuple-element.63), channel_id=1, source_target_pairs={{1,2},{2,1},{3,4},{4,3},{5,6},{6,5},{9,10},{10,9},{11,12},{12,11},... | collective-permute-start | bytes 368648 | tf_op jit(solution)/shard_map/ppermute | solution.py:421
  63.0 4.7 %collective-permute-start.9 = (f32[20,8,128]{2,1,0:T(8,128)S(1)}, f32[20,8,128]{2,1,0:T(8,128)S(1)}, u32[]{:S(2)}, u32[]{:S(2)}) collective-permute-start(f32[20,8,128]{2,1,0:T(8,128)S(1)} %get-tuple-element.62), channel_id=1, source_target_pairs={{0,32},{32,0},{64,96},{96,64},{128,160},{160,128},{192,224},{224,1... | collective-permute-start | bytes 245768 | tf_op jit(solution)/shard_map/ppermute | solution.py:421
  68.6 2.0 %all-gather.1 = f32[20,24,128]{2,1,0:T(8,128)S(1)} all-gather(f32[10,24,128]{2,1,0:T(8,128)S(1)} %get-tuple-element.64), channel_id=3, replica_groups={{0,1},{2,3},{4,5},{6,7},{8,9},{10,11},{12,13},{14,15},{16,17},{18,19},{..., dimensions={0}, use_global_device_ids=true | all-gather | bytes 368640 | tf_op jit(solution)/shard_map/all_gather | solution.py:430
  70.6 1.3 %shard_map.127 = (f32[16,24,128]{2,1,0:T(8,128)S(1)}, f32[16,24,128]{2,1,0:T(8,128)S(1)}, f32[16,24,128]{2,1,0:T(8,128)S(1)}, f32[9,24,128]{2,1,0:T(8,128)S(1)},...) custom-call(s32[5]{0:T(128)S(1)} %copy-done.7, ...), custom_call_target="tpu_custom_call" | custom-call | flops 1000000 | bytes 2000000 | tf_op jit(solution)/shard_map/pallas_call | solution.py:66
  71.9 4.0 %collective-permute-start.13 = (f32[9,24,128]{2,1,0:T(8,128)S(1)}, f32[9,24,128]{2,1,0:T(8,128)S(1)}, u32[]{:S(2)}, u32[]{:S(2)}) collective-permute-start(f32[9,24,128]{2,1,0:T(8,128)S(1)} %get-tuple-element.73), channel_id=1, source_target_pairs={{1,2},{2,1},{3,4},{4,3},{5,6},{6,5},{9,10},{10,9},{11,12},{12,11},... | collective-permute-start | bytes 331784 | tf_op jit(solution)/shard_map/ppermute | solution.py:421
  76.6 5.6 %collective-permute-start.12 = (f32[18,8,128]{2,1,0:T(8,128)S(1)}, f32[18,8,128]{2,1,0:T(8,128)S(1)}, u32[]{:S(2)}, u32[]{:S(2)}) collective-permute-start(f32[18,8,128]{2,1,0:T(8,128)S(1)} %get-tuple-element.72), channel_id=1, source_target_pairs={{0,32},{32,0},{64,96},{96,64},{128,160},{160,128},{192,224},{224,1... | collective-permute-start | bytes 221192 | tf_op jit(solution)/shard_map/ppermute | solution.py:421
  83.1 2.0 %all-gather.2 = f32[18,24,128]{2,1,0:T(8,128)S(1)} all-gather(f32[9,24,128]{2,1,0:T(8,128)S(1)} %get-tuple-element.74), channel_id=4, replica_groups={{0,1},{2,3},{4,5},{6,7},{8,9},{10,11},{12,13},{14,15},{16,17},{18,19},{..., dimensions={0}, use_global_device_ids=true | all-gather | bytes 331776 | tf_op jit(solution)/shard_map/all_gather | solution.py:430
  85.1 1.5 %shard_map.129 = (f32[16,24,128]{2,1,0:T(8,128)S(1)}, f32[16,24,128]{2,1,0:T(8,128)}, f32[16,24,128]{2,1,0:T(8,128)S(1)}, f32[8,24,128]{2,1,0:T(8,128)S(1)}, f32...) custom-call(s32[5]{0:T(128)S(1)} %copy-done.7, ...), custom_call_target="tpu_custom_call" | custom-call | flops 1000000 | bytes 2000000 | tf_op jit(solution)/shard_map/pallas_call | solution.py:66
  86.7 2.9 %collective-permute-start.16 = (f32[8,24,128]{2,1,0:T(8,128)S(1)}, f32[8,24,128]{2,1,0:T(8,128)S(1)}, u32[]{:S(2)}, u32[]{:S(2)}) collective-permute-start(f32[8,24,128]{2,1,0:T(8,128)S(1)} %get-tuple-element.82), channel_id=1, source_target_pairs={{1,2},{2,1},{3,4},{4,3},{5,6},{6,5},{9,10},{10,9},{11,12},{12,11},... | collective-permute-start | bytes 294920 | tf_op jit(solution)/shard_map/ppermute | solution.py:421
  90.3 5.3 %collective-permute-start.15 = (f32[16,8,128]{2,1,0:T(8,128)S(1)}, f32[16,8,128]{2,1,0:T(8,128)S(1)}, u32[]{:S(2)}, u32[]{:S(2)}) collective-permute-start(f32[16,8,128]{2,1,0:T(8,128)S(1)} %get-tuple-element.81), channel_id=1, source_target_pairs={{0,32},{32,0},{64,96},{96,64},{128,160},{160,128},{192,224},{224,1... | collective-permute-start | bytes 196616 | tf_op jit(solution)/shard_map/ppermute | solution.py:421
  97.1 1.9 %all-gather.3 = f32[16,24,128]{2,1,0:T(8,128)S(1)} all-gather(f32[8,24,128]{2,1,0:T(8,128)S(1)} %get-tuple-element.83), channel_id=5, replica_groups={{0,1},{2,3},{4,5},{6,7},{8,9},{10,11},{12,13},{14,15},{16,17},{18,19},{..., dimensions={0}, use_global_device_ids=true | all-gather | bytes 294912 | tf_op jit(solution)/shard_map/all_gather | solution.py:430
  99.1 1.6 %shard_map.131 = (f32[16,24,128]{2,1,0:T(8,128)}, f32[16,24,128]{2,1,0:T(8,128)}) custom-call(s32[5]{0:T(128)S(1)} %copy-done.7, f32[16,8,128]{2,1,0:T(8,128)S(1)} %collective-permute-done.14.x_odd_in, f32[16,8,128]{2,1,0:T(8,128)S(1)} %collective-permute-done.15.x_even_in, f32[8,24,128]{2,1,0:T(8,128)S(1)} %collective-permute-done.16.z_odd_in, ...), custom_call_target="tpu_custom_call" | custom-call | flops 1000000 | bytes 2000000 | tf_op jit(solution)/shard_map/pallas_call | solution.py:66
  (43 shorter events, 9.2 us)
Async XLA Ops:
  1.9 41.4 %copy-start.1 = (f32[16,24,128]{2,1,0:T(8,128)S(1)}, f32[16,24,128]{2,1,0:T(8,128)}, u32[]{:S(2)}) copy-start(f32[16,24,128]{2,1,0:T(8,128)} %older.5) | copy-start | bytes 589828
  32.2 11.1 %copy-start.7 = (s32[5]{0:T(128)S(1)}, s32[5]{0:T(128)}, u32[]{:S(2)}) copy-start(s32[5]{0:T(128)} %stack.23.ids) | copy-start | bytes 64
  32.2 17.1 %copy-start.3 = (bf16[256,256]{1,0:T(8,128)(2,1)S(1)}, bf16[256,256]{1,0:T(8,128)(2,1)}, u32[]{:S(2)}) copy-start(bf16[256,256]{1,0:T(8,128)(2,1)} %constant.45.clone.band_low) | copy-start | bytes 393220
  32.2 17.1 %copy-start.4 = (bf16[256,256]{1,0:T(8,128)(2,1)S(1)}, bf16[256,256]{1,0:T(8,128)(2,1)}, u32[]{:S(2)}) copy-start(bf16[256,256]{1,0:T(8,128)(2,1)} %constant.44.clone.band_high) | copy-start | bytes 393220
  32.2 11.1 %collective-permute-start = (f32[12,24,128]{2,1,0:T(8,128)}, f32[12,24,128]{2,1,0:T(8,128)S(1)}, u32[]{:S(2)}, u32[]{:S(2)}) collective-permute-start(f32[12,24,128]{2,1,0:T(8,128)} %get-tuple-element.49), channel_id=1, source_target_pairs={{0,8},{8,0},{16,24},{24,16},{1,9},{9,1},{17,25},{25,17},{2,10},{10... | collective-permute-start | bytes 442376 | tf_op jit(solution)/shard_map/ppermute | solution.py:421
  34.5 8.7 %collective-permute-start.1 = (f32[12,24,128]{2,1,0:T(8,128)}, f32[12,24,128]{2,1,0:T(8,128)S(1)}, u32[]{:S(2)}, u32[]{:S(2)}) collective-permute-start(f32[12,24,128]{2,1,0:T(8,128)} %get-tuple-element.50), channel_id=1, source_target_pairs={{8,16},{16,8},{9,17},{17,9},{10,18},{18,10},{11,19},{19,11},{12,20... | collective-permute-start | bytes 442376 | tf_op jit(solution)/shard_map/ppermute | solution.py:421
  35.2 15.1 %collective-permute-start.7 = (f32[64,128]{1,0:T(8,128)S(1)}, f32[64,128]{1,0:T(8,128)S(1)}, u32[]{:S(2)}, u32[]{:S(2)}) collective-permute-start(f32[64,128]{1,0:T(8,128)S(1)} %bitcast.24), channel_id=1, source_target_pairs={{6,0},{7,1},{14,8},{15,9},{22,16},{23,17},{30,24},{31,25},{38,32},... | collective-permute-start | bytes 98312 | tf_op jit(solution)/shard_map/ppermute | solution.py:486
  36.5 18.4 %collective-permute-start.6 = (f32[64,128]{1,0:T(8,128)S(1)}, f32[64,128]{1,0:T(8,128)S(1)}, u32[]{:S(2)}, u32[]{:S(2)}) collective-permute-start(f32[64,128]{1,0:T(8,128)S(1)} %bitcast.25), channel_id=1, source_target_pairs={{4,0},{5,1},{12,8},{13,9},{20,16},{21,17},{28,24},{29,25},{36,32},... | collective-permute-start | bytes 98312 | tf_op jit(solution)/shard_map/ppermute | solution.py:486
  37.8 17.2 %collective-permute-start.5 = (f32[64,128]{1,0:T(8,128)S(1)}, f32[64,128]{1,0:T(8,128)S(1)}, u32[]{:S(2)}, u32[]{:S(2)}) collective-permute-start(f32[64,128]{1,0:T(8,128)S(1)} %bitcast.26), channel_id=1, source_target_pairs={{2,0},{3,1},{10,8},{11,9},{18,16},{19,17},{26,24},{27,25},{34,32},... | collective-permute-start | bytes 98312 | tf_op jit(solution)/shard_map/ppermute | solution.py:486
  44.2 14.7 %collective-permute-start.4 = (f32[12,24,128]{2,1,0:T(8,128)S(1)}, f32[12,24,128]{2,1,0:T(8,128)S(1)}, u32[]{:S(2)}, u32[]{:S(2)}) collective-permute-start(f32[12,24,128]{2,1,0:T(8,128)S(1)} %get-tuple-element.53), channel_id=1, source_target_pairs={{1,2},{2,1},{3,4},{4,3},{5,6},{6,5},{9,10},{10,9},{11,12},{12,11},... | collective-permute-start | bytes 442376 | tf_op jit(solution)/shard_map/ppermute | solution.py:421
  48.6 10.3 %collective-permute-start.2 = (f32[24,8,128]{2,1,0:T(8,128)S(1)}, f32[24,8,128]{2,1,0:T(8,128)S(1)}, u32[]{:S(2)}, u32[]{:S(2)}) collective-permute-start(f32[24,8,128]{2,1,0:T(8,128)S(1)} %get-tuple-element.51), channel_id=1, source_target_pairs={{32,64},{64,32},{96,128},{128,96},{160,192},{192,160},{224,256},{2... | collective-permute-start | bytes 294920 | tf_op jit(solution)/shard_map/ppermute | solution.py:421
  50.3 8.6 %collective-permute-start.3 = (f32[24,8,128]{2,1,0:T(8,128)S(1)}, f32[24,8,128]{2,1,0:T(8,128)S(1)}, u32[]{:S(2)}, u32[]{:S(2)}) collective-permute-start(f32[24,8,128]{2,1,0:T(8,128)S(1)} %get-tuple-element.52), channel_id=1, source_target_pairs={{0,32},{32,0},{64,96},{96,64},{128,160},{160,128},{192,224},{224,1... | collective-permute-start | bytes 294920 | tf_op jit(solution)/shard_map/ppermute | solution.py:421
  55.0 3.9 %copy-start.5 = (f32[16,24,128]{2,1,0:T(8,128)S(1)}, f32[16,24,128]{2,1,0:T(8,128)}, u32[]{:S(2)}) copy-start(f32[16,24,128]{2,1,0:T(8,128)} %older.4) | copy-start | bytes 589828
  56.6 2.3 %copy-start = (bf16[4,16,24,128]{3,2,1,0:T(8,128)(2,1)S(1)}, bf16[4,16,24,128]{3,2,1,0:T(8,128)(2,1)}, u32[]{:S(2)}) copy-start(bf16[4,16,24,128]{3,2,1,0:T(8,128)(2,1)} %forward.7) | copy-start | bytes 1179652
  56.6 2.3 %copy-start.2 = (f32[16,24,128]{2,1,0:T(8,128)S(1)}, f32[16,24,128]{2,1,0:T(8,128)}, u32[]{:S(2)}) copy-start(f32[16,24,128]{2,1,0:T(8,128)} %stiff.9) | copy-start | bytes 589828
  60.1 10.4 %collective-permute-start.10 = (f32[10,24,128]{2,1,0:T(8,128)S(1)}, f32[10,24,128]{2,1,0:T(8,128)S(1)}, u32[]{:S(2)}, u32[]{:S(2)}) collective-permute-start(f32[10,24,128]{2,1,0:T(8,128)S(1)} %get-tuple-element.63), channel_id=1, source_target_pairs={{1,2},{2,1},{3,4},{4,3},{5,6},{6,5},{9,10},{10,9},{11,12},{12,11},... | collective-permute-start | bytes 368648 | tf_op jit(solution)/shard_map/ppermute | solution.py:421
  62.3 8.3 %collective-permute-start.8 = (f32[20,8,128]{2,1,0:T(8,128)S(1)}, f32[20,8,128]{2,1,0:T(8,128)S(1)}, u32[]{:S(2)}, u32[]{:S(2)}) collective-permute-start(f32[20,8,128]{2,1,0:T(8,128)S(1)} %get-tuple-element.61), channel_id=1, source_target_pairs={{32,64},{64,32},{96,128},{128,96},{160,192},{192,160},{224,256},{2... | collective-permute-start | bytes 245768 | tf_op jit(solution)/shard_map/ppermute | solution.py:421
  63.0 7.6 %collective-permute-start.9 = (f32[20,8,128]{2,1,0:T(8,128)S(1)}, f32[20,8,128]{2,1,0:T(8,128)S(1)}, u32[]{:S(2)}, u32[]{:S(2)}) collective-permute-start(f32[20,8,128]{2,1,0:T(8,128)S(1)} %get-tuple-element.62), channel_id=1, source_target_pairs={{0,32},{32,0},{64,96},{96,64},{128,160},{160,128},{192,224},{224,1... | collective-permute-start | bytes 245768 | tf_op jit(solution)/shard_map/ppermute | solution.py:421
  71.9 13.2 %collective-permute-start.13 = (f32[9,24,128]{2,1,0:T(8,128)S(1)}, f32[9,24,128]{2,1,0:T(8,128)S(1)}, u32[]{:S(2)}, u32[]{:S(2)}) collective-permute-start(f32[9,24,128]{2,1,0:T(8,128)S(1)} %get-tuple-element.73), channel_id=1, source_target_pairs={{1,2},{2,1},{3,4},{4,3},{5,6},{6,5},{9,10},{10,9},{11,12},{12,11},... | collective-permute-start | bytes 331784 | tf_op jit(solution)/shard_map/ppermute | solution.py:421
  75.9 9.2 %collective-permute-start.11 = (f32[18,8,128]{2,1,0:T(8,128)S(1)}, f32[18,8,128]{2,1,0:T(8,128)S(1)}, u32[]{:S(2)}, u32[]{:S(2)}) collective-permute-start(f32[18,8,128]{2,1,0:T(8,128)S(1)} %get-tuple-element.71), channel_id=1, source_target_pairs={{32,64},{64,32},{96,128},{128,96},{160,192},{192,160},{224,256},{2... | collective-permute-start | bytes 221192 | tf_op jit(solution)/shard_map/ppermute | solution.py:421
  76.6 8.5 %collective-permute-start.12 = (f32[18,8,128]{2,1,0:T(8,128)S(1)}, f32[18,8,128]{2,1,0:T(8,128)S(1)}, u32[]{:S(2)}, u32[]{:S(2)}) collective-permute-start(f32[18,8,128]{2,1,0:T(8,128)S(1)} %get-tuple-element.72), channel_id=1, source_target_pairs={{0,32},{32,0},{64,96},{96,64},{128,160},{160,128},{192,224},{224,1... | collective-permute-start | bytes 221192 | tf_op jit(solution)/shard_map/ppermute | solution.py:421
  86.7 12.4 %collective-permute-start.16 = (f32[8,24,128]{2,1,0:T(8,128)S(1)}, f32[8,24,128]{2,1,0:T(8,128)S(1)}, u32[]{:S(2)}, u32[]{:S(2)}) collective-permute-start(f32[8,24,128]{2,1,0:T(8,128)S(1)} %get-tuple-element.82), channel_id=1, source_target_pairs={{1,2},{2,1},{3,4},{4,3},{5,6},{6,5},{9,10},{10,9},{11,12},{12,11},... | collective-permute-start | bytes 294920 | tf_op jit(solution)/shard_map/ppermute | solution.py:421
  89.6 9.4 %collective-permute-start.14 = (f32[16,8,128]{2,1,0:T(8,128)S(1)}, f32[16,8,128]{2,1,0:T(8,128)S(1)}, u32[]{:S(2)}, u32[]{:S(2)}) collective-permute-start(f32[16,8,128]{2,1,0:T(8,128)S(1)} %get-tuple-element.80), channel_id=1, source_target_pairs={{32,64},{64,32},{96,128},{128,96},{160,192},{192,160},{224,256},{2... | collective-permute-start | bytes 196616 | tf_op jit(solution)/shard_map/ppermute | solution.py:421
  90.3 8.8 %collective-permute-start.15 = (f32[16,8,128]{2,1,0:T(8,128)S(1)}, f32[16,8,128]{2,1,0:T(8,128)S(1)}, u32[]{:S(2)}, u32[]{:S(2)}) collective-permute-start(f32[16,8,128]{2,1,0:T(8,128)S(1)} %get-tuple-element.81), channel_id=1, source_target_pairs={{0,32},{32,0},{64,96},{96,64},{128,160},{160,128},{192,224},{224,1... | collective-permute-start | bytes 196616 | tf_op jit(solution)/shard_map/ppermute | solution.py:421
  (1 other events, 0.9 us)

commit v7 on v6

--- a/solution.py
+++ b/solution.py
@@ -14,6 +14,7 @@
 LANES = 128
 STRIP = 32
 CAP = 8
+CHUNK = 4
 SLOTS = 3 * CAP
 F32 = jnp.float32
 BF16 = jnp.bfloat16
@@ -62,12 +63,12 @@
     return pl.BlockSpec(memory_space=pltpu.SMEM)
 
 
-def call(body, outs, ins, scratch=(), in_specs=None, grant=32):
+def call(body, outs, ins, scratch=(), in_specs=None, grant=32, out_specs=None):
     return pl.pallas_call(
         body,
         out_shape=outs,
         in_specs=in_specs or [smem()] + [vmem()] * (len(ins) - 1),
-        out_specs=jax.tree.map(lambda _: vmem(), outs),
+        out_specs=out_specs or jax.tree.map(lambda _: vmem(), outs),
         scratch_shapes=list(scratch),
         compiler_params=pltpu.CompilerParams(vmem_limit_bytes=grant * 1024 * 1024),
         cost_estimate=pl.CostEstimate(flops=1_000_000, bytes_accessed=2_000_000, transcendentals=0),
@@ -90,9 +91,17 @@
 
 
 def prepare_kernel(span_y, tiles, ids, residuals, owners, cells, wave, older, stiff, packets,
-                   even, odd):
+                   even, odd, held, sems):
+    copies = [
+        pltpu.make_async_copy(field, held.at[number], sems.at[number])
+        for number, field in enumerate((wave, older, stiff))
+    ]
+    for copy in copies:
+        copy.start()
     pack_slots(span_y, tiles, residuals, owners, cells, packets)
-    pack_strips(ids, wave, older, stiff, even, odd)
+    for copy in copies:
+        copy.wait()
+    pack_strips(ids, held.at[0], held.at[1], held.at[2], even, odd)
 
 
 def pack_slots(span_y, tiles, residuals, owner_row, cell_row, out):
@@ -297,6 +306,9 @@
 def own_kernel(last, wave, side, band_high, band_low, *rest):
     *outs, y_terms = rest
     depth, rows, _ = wave.shape
+    if last:
+        outs, kept = outs[:1], outs[1]
+        kept[...] = wave[...]
     width = LANES * len(outs)
     both = jnp.concatenate(
         [wave[...].reshape(depth * rows, LANES), side[...].reshape(depth * rows, LANES)], axis=1
@@ -330,8 +342,8 @@
             out[z] = total
 
 
-def advance(step, ids, wave, side, older, older_side, stiff, stiff_side, forward, image_in,
-            planes, own, own_side, fresh, fresh_side, image, z_halo, x_halo):
+def advance(step, shot, ids, wave, side, older, older_side, stiff, stiff_side, forward, image_in,
+            planes, own, own_side, fresh, fresh_side, image, z_halo, x_halo, done=None):
     depth, rows, _ = wave.shape
     last = step == STEPS - 1
     line = lax.broadcasted_iota(jnp.int32, (RADIUS, LANES), 0)
@@ -372,23 +384,25 @@
         if step:
             product = product + image_in[z]
         if last:
-            product = product * muting(ids, z, depth, rows)
+            product = product * muting(ids, *shot, z, depth, rows)
         image[z] = product
+        if done is not None:
+            done(z)
         if not last:
             one(z, 1, own_side, side, older_side, stiff_side, fresh_side)
 
 
-def muting(ids, z, depth, rows):
+def muting(ids, shot_x, shot_y, z, depth, rows):
     gap_z = (ids[0] * depth + z).astype(F32)
     gap_x = (
-        ids[1] * rows + lax.broadcasted_iota(jnp.int32, (rows, LANES), 0) - ids[3]
+        ids[1] * rows + lax.broadcasted_iota(jnp.int32, (rows, LANES), 0) - shot_x
     ).astype(F32)
-    gap_y = (ids[2] * LANES + lane_of((rows, LANES)) - ids[4]).astype(F32)
+    gap_y = (ids[2] * LANES + lane_of((rows, LANES)) - shot_y).astype(F32)
     distance = gap_z * gap_z + gap_x * gap_x + gap_y * gap_y
     return jnp.minimum(1.0, distance / 576.0)
 
 
-def step_kernel(step, ids, x_odd_in, x_even_in, z_odd_in, z_even_in, wave, side, older,
+def step_kernel(step, total_y, ids, x_odd_in, x_even_in, z_odd_in, z_even_in, wave, side, older,
                 older_side, stiff, stiff_side, forward, own, *rest):
     last = step == STEPS - 1
     own_side = image_in = None
@@ -401,14 +415,32 @@
         face = z_even_in.shape[1] - 2 * STEPS
         both = z_even_in[0, pl.ds(face, 2 * STEPS)] + z_even_in[1, pl.ds(face, 2 * STEPS)]
         planes[...] = jnp.where(ids[0] == 0, both, 0.0)
+    shot = done = None
+    copies = []
     if last:
-        image, fresh, z_halo, x_halo = rest
+        (source, image_out, wave_out, z_halo, x_halo, image, fresh, sems) = rest
         fresh_side = None
+        shot = (lax.div(source[0], total_y), lax.rem(source[0], total_y))
+
+        def done(z):
+            if (z + 1) % CHUNK:
+                return
+            chunk = pl.ds(z + 1 - CHUNK, CHUNK)
+            for number, (held, out) in enumerate(((image, image_out), (fresh, wave_out))):
+                copies.append(
+                    pltpu.make_async_copy(
+                        held.at[chunk], out.at[chunk], sems.at[number, z // CHUNK]
+                    )
+                )
+                copies[-1].start()
+
     else:
         image, fresh, fresh_side, z_even, z_odd, x_even, x_odd, z_halo, x_halo = rest
     fill(strip_width(step), ids, z_even_in, z_odd_in, x_even_in, x_odd_in, z_halo, x_halo)
-    advance(step, ids, wave, side, older, older_side, stiff, stiff_side, forward, image_in,
-            planes, own, own_side, fresh, fresh_side, image, z_halo, x_halo)
+    advance(step, shot, ids, wave, side, older, older_side, stiff, stiff_side, forward, image_in,
+            planes, own, own_side, fresh, fresh_side, image, z_halo, x_halo, done)
+    for copy in copies:
+        copy.wait()
     if not last:
         write_faces(strip_width(step + 1), ids, fresh, fresh_side, z_even, z_odd, x_even, x_odd)
 
@@ -445,14 +477,11 @@
     depth, rows, cols = wave_now.shape
     span_x, span_y, span_z = (lax.axis_size(axis) for axis in ("gx", "gy", "gz"))
     tiles = span_x * span_y
-    total_y = cols * span_y
     ids = jnp.stack(
         [
             lax.axis_index("gz"),
             lax.axis_index("gx"),
             lax.axis_index("gy"),
-            source_cell[0] // total_y,
-            source_cell[0] % total_y,
         ]
     ).astype(jnp.int32)
     band_high, band_low = (jnp.asarray(part) for part in band())
@@ -470,7 +499,8 @@
         [shaped(tiles, LANES), strips, strips],
         [ids, residuals, owners.reshape(1, -1), receivers.reshape(1, -1), wave_now, older_wave,
          stiffness],
-        in_specs=[smem()] + [pl.BlockSpec()] * 6,
+        scratch=[pltpu.VMEM((3, depth, rows, LANES), F32), pltpu.SemaphoreType.DMA((3,))],
+        in_specs=[smem()] + [pl.BlockSpec()] * 3 + [pl.BlockSpec(memory_space=pl.ANY)] * 3,
         grant=60,
     )
     packets = lax.all_to_all(packets, ("gx", "gy"), 0, 0, tiled=True)
@@ -504,11 +534,13 @@
         last = step == STEPS - 1
         own = call(
             functools.partial(own_kernel, last),
-            [block] if last else [block, block],
+            [block, block],
             [wave, side, band_high, band_low],
             scratch=[pltpu.VMEM((depth * rows, 2 * LANES), F32)],
             in_specs=[vmem()] * 4,
         )
+        if last:
+            *own, last_older = own
         faces = exchange(faces)
         ins = [ids, *faces[::-1], wave, side, older, older_side, stiffness, stiff_side, forward_wave,
                *own]
@@ -519,7 +551,17 @@
             outs = [shaped(2 * STEPS, rows, LANES)] + outs
         if not last:
             outs += [block] + faces_out(step + 1)
-        rest = call(functools.partial(step_kernel, step), outs, ins, scratch)
+        room, in_specs, out_specs = scratch, None, None
+        if last:
+            ins.append(source_cell)
+            in_specs = [smem()] + [vmem()] * (len(ins) - 2) + [smem()]
+            out_specs = [pl.BlockSpec(memory_space=pl.ANY)] * 2
+            held = pltpu.VMEM((depth, rows, LANES), F32)
+            room = scratch + [held, held, pltpu.SemaphoreType.DMA((2, depth // CHUNK))]
+        rest = call(
+            functools.partial(step_kernel, step, cols * span_y), outs, ins, room, in_specs,
+            out_specs=out_specs,
+        )
         if not step:
             planes, *rest = rest
         image, fresh, *rest = rest
@@ -527,7 +569,7 @@
         if not last:
             older_side, side = side, rest[0]
             faces = rest[1:]
-    return image, older, wave
+    return image, last_older, wave
 
 
 def solution(mesh):

time: 102 us -> 102 us (level)
  local copies, waits for them, and re-layouts: 1.55 us -> 0.03 us
where the time goes in v7:
time: 102 us; the launch traced here: 101 us
  starting transfers between devices  43.4 us (43%)
  blocking collectives  36.1 us (35%)
  Pallas kernels  14.5 us (14%)
  waiting for transfers between devices  4.2 us (4%)
  between operations  1.59 us (2%)
    ppermute x14, starting transfers between devices, swap(): return lax.ppermute(block, axis, pairs)  39.5 us
    all_to_all x1, blocking collectives, on_device(): packets = lax.all_to_all(packets, ('gx', 'gy'), 0, 0, tiled=True)  28 us
    pallas_call x11, Pallas kernels, call(): pl.pallas_call(body, out_shape=outs, in_specs=in_specs or [smem()] + [vme...  14.5 us
    all_gather x4, blocking collectives, pair_gather(): lax.all_gather(block, axis, axis=0, tiled=False, axis_index_groups=groups)  8.17 us
    ppermute x14, waiting for transfers between devices, swap(): return lax.ppermute(block, axis, pairs)  4.2 us
    ppermute x3, starting transfers between devices, on_device(): lax.ppermute(packets, 'gz', [(chip + core, core) for core in range(cores)])  3.88 us
  transfers between devices with their start and end apart: 17, of which 1 were waited for; matrix products, arithmetic and copies ran while one was open for 0% of the time, Pallas kernels for 6%

profile of v7, /device:TPU:1, one launch (start us, length us, event | category | flops | bytes accessed | tf_op | source)
XLA Modules:
  0.0 100.5 jit_solution(10171526528181142083)
XLA Ops:
  1.3 3.0 %shard_map.121 = (f32[64,128]{1,0:T(8,128)}, f32[12,24,128]{2,1,0:T(8,128)}, f32[12,24,128]{2,1,0:T(8,128)}) custom-call(s32[3]{0:T(128)} %pad_add_fusion.ids, f32[4,128]{1,0:T(4,128)} %residuals.1, s32[1,128]{1,0:T(1,128)} %bitcast.22, s32[1,128]{1,0:T(1,128)} %bitcast.23, f32[16,24,128]{2,1,0:T(8,128)} %older.5, f32[16,24,128]{2,1,0:T(8,128)} %older.4, ...), custom_call_target="tpu_custom_call" | custom-call | flops 1000000 | bytes 2000000 | tf_op jit(solution)/shard_map/pallas_call | solution.py:67
  4.3 28.0 %all_to_all.12 = f32[64,1,128]{2,1,0:T(1,128)S(1)} all-to-all(f32[64,1,128]{2,1,0:T(1,128)} %bitcast.21), channel_id=1, replica_groups=mesh['gx'=16,'gy'=4,'gz'=8] {'gx','gy'}, dimensions={0} | all-to-all | bytes 65536 | tf_op jit(solution)/shard_map/all_to_all | solution.py:506
  32.2 2.4 %collective-permute-start = (f32[12,24,128]{2,1,0:T(8,128)}, f32[12,24,128]{2,1,0:T(8,128)S(1)}, u32[]{:S(2)}, u32[]{:S(2)}) collective-permute-start(f32[12,24,128]{2,1,0:T(8,128)} %get-tuple-element.51), channel_id=1, source_target_pairs={{0,8},{8,0},{16,24},{24,16},{1,9},{9,1},{17,25},{25,17},{2,10},{10... | collective-permute-start | bytes 442376 | tf_op jit(solution)/shard_map/ppermute | solution.py:453
  35.3 1.3 %collective-permute-start.5 = (f32[64,128]{1,0:T(8,128)S(1)}, f32[64,128]{1,0:T(8,128)S(1)}, u32[]{:S(2)}, u32[]{:S(2)}) collective-permute-start(f32[64,128]{1,0:T(8,128)S(1)} %bitcast.17), channel_id=1, source_target_pairs={{2,0},{3,1},{10,8},{11,9},{18,16},{19,17},{26,24},{27,25},{34,32},... | collective-permute-start | bytes 98312 | tf_op jit(solution)/shard_map/ppermute | solution.py:516
  36.6 1.3 %collective-permute-start.6 = (f32[64,128]{1,0:T(8,128)S(1)}, f32[64,128]{1,0:T(8,128)S(1)}, u32[]{:S(2)}, u32[]{:S(2)}) collective-permute-start(f32[64,128]{1,0:T(8,128)S(1)} %bitcast.18), channel_id=1, source_target_pairs={{4,0},{5,1},{12,8},{13,9},{20,16},{21,17},{28,24},{29,25},{36,32},... | collective-permute-start | bytes 98312 | tf_op jit(solution)/shard_map/ppermute | solution.py:516
  37.9 1.3 %collective-permute-start.7 = (f32[64,128]{1,0:T(8,128)S(1)}, f32[64,128]{1,0:T(8,128)S(1)}, u32[]{:S(2)}, u32[]{:S(2)}) collective-permute-start(f32[64,128]{1,0:T(8,128)S(1)} %bitcast.19), channel_id=1, source_target_pairs={{6,0},{7,1},{14,8},{15,9},{22,16},{23,17},{30,24},{31,25},{38,32},... | collective-permute-start | bytes 98312 | tf_op jit(solution)/shard_map/ppermute | solution.py:516
  39.2 4.2 %collective-permute-done.even = f32[12,24,128]{2,1,0:T(8,128)S(1)} collective-permute-done((f32[12,24,128]{2,1,0:T(8,128)}, f32[12,24,128]{2,1,0:T(8,128)S(1)}, u32[]{:S(2)}, u32[]{:S(2)}) %collective-permute-start) | collective-permute-done | bytes 147488 | tf_op jit(solution)/shard_map/ppermute | solution.py:453
  44.2 4.5 %collective-permute-start.4 = (f32[12,24,128]{2,1,0:T(8,128)S(1)}, f32[12,24,128]{2,1,0:T(8,128)S(1)}, u32[]{:S(2)}, u32[]{:S(2)}) collective-permute-start(f32[12,24,128]{2,1,0:T(8,128)S(1)} %get-tuple-element.55), channel_id=1, source_target_pairs={{1,2},{2,1},{3,4},{4,3},{5,6},{6,5},{9,10},{10,9},{11,12},{12,11},... | collective-permute-start | bytes 442376 | tf_op jit(solution)/shard_map/ppermute | solution.py:453
  50.3 4.7 %collective-permute-start.3 = (f32[24,8,128]{2,1,0:T(8,128)S(1)}, f32[24,8,128]{2,1,0:T(8,128)S(1)}, u32[]{:S(2)}, u32[]{:S(2)}) collective-permute-start(f32[24,8,128]{2,1,0:T(8,128)S(1)} %get-tuple-element.54), channel_id=1, source_target_pairs={{0,32},{32,0},{64,96},{96,64},{128,160},{160,128},{192,224},{224,1... | collective-permute-start | bytes 294920 | tf_op jit(solution)/shard_map/ppermute | solution.py:453
  55.0 1.6 %shard_map.123 = f32[20,24,128]{2,1,0:T(8,128)S(1)} custom-call(s32[3]{0:T(128)S(1)} %copy-done.6, f32[12,24,128]{2,1,0:T(8,128)S(1)} %get-tuple-element.56.z_even, f32[64,128]{1,0:T(8,128)S(1)} %bitcast.20, f32[64,128]{1,0:T(8,128)S(1)} %collective-permute-done.5.refs_1_, f32[64,128]{1,0:T(8,128)S(1)} %collective-permute-done.6.refs_2_, ...), custom_call_target="tpu_custom_call" | custom-call | flops 1000000 | bytes 2000000 | tf_op jit(solution)/shard_map/pallas_call | solution.py:67
  56.6 2.3 %all-gather = f32[40,24,128]{2,1,0:T(8,128)S(1)} all-gather(f32[20,24,128]{2,1,0:T(8,128)S(1)} %shard_map.123), channel_id=2, replica_groups={{0,1},{2,3},{4,5},{6,7},{8,9},{10,11},{12,13},{14,15},{16,17},{18,19},{..., dimensions={0}, use_global_device_ids=true | all-gather | bytes 737280 | tf_op jit(solution)/shard_map/all_gather | solution.py:462
  59.0 1.2 %shard_map.125 = (f32[8,24,128]{2,1,0:T(8,128)S(1)}, f32[16,24,128]{2,1,0:T(8,128)S(1)}, f32[16,24,128]{2,1,0:T(8,128)S(1)}, f32[16,24,128]{2,1,0:T(8,128)S(1)},...) custom-call(s32[3]{0:T(128)S(1)} %copy-done.6, ...), custom_call_target="tpu_custom_call" | custom-call | flops 1000000 | bytes 2000000 | tf_op jit(solution)/shard_map/pallas_call | solution.py:67
  60.2 2.1 %collective-permute-start.10 = (f32[10,24,128]{2,1,0:T(8,128)S(1)}, f32[10,24,128]{2,1,0:T(8,128)S(1)}, u32[]{:S(2)}, u32[]{:S(2)}) collective-permute-start(f32[10,24,128]{2,1,0:T(8,128)S(1)} %get-tuple-element.65), channel_id=1, source_target_pairs={{1,2},{2,1},{3,4},{4,3},{5,6},{6,5},{9,10},{10,9},{11,12},{12,11},... | collective-permute-start | bytes 368648 | tf_op jit(solution)/shard_map/ppermute | solution.py:453
  63.0 4.7 %collective-permute-start.9 = (f32[20,8,128]{2,1,0:T(8,128)S(1)}, f32[20,8,128]{2,1,0:T(8,128)S(1)}, u32[]{:S(2)}, u32[]{:S(2)}) collective-permute-start(f32[20,8,128]{2,1,0:T(8,128)S(1)} %get-tuple-element.64), channel_id=1, source_target_pairs={{0,32},{32,0},{64,96},{96,64},{128,160},{160,128},{192,224},{224,1... | collective-permute-start | bytes 245768 | tf_op jit(solution)/shard_map/ppermute | solution.py:453
  68.6 2.0 %all-gather.1 = f32[20,24,128]{2,1,0:T(8,128)S(1)} all-gather(f32[10,24,128]{2,1,0:T(8,128)S(1)} %get-tuple-element.66), channel_id=3, replica_groups={{0,1},{2,3},{4,5},{6,7},{8,9},{10,11},{12,13},{14,15},{16,17},{18,19},{..., dimensions={0}, use_global_device_ids=true | all-gather | bytes 368640 | tf_op jit(solution)/shard_map/all_gather | solution.py:462
  70.6 1.3 %shard_map.127 = (f32[16,24,128]{2,1,0:T(8,128)S(1)}, f32[16,24,128]{2,1,0:T(8,128)S(1)}, f32[16,24,128]{2,1,0:T(8,128)S(1)}, f32[9,24,128]{2,1,0:T(8,128)S(1)},...) custom-call(s32[3]{0:T(128)S(1)} %copy-done.6, ...), custom_call_target="tpu_custom_call" | custom-call | flops 1000000 | bytes 2000000 | tf_op jit(solution)/shard_map/pallas_call | solution.py:67
  71.9 4.0 %collective-permute-start.13 = (f32[9,24,128]{2,1,0:T(8,128)S(1)}, f32[9,24,128]{2,1,0:T(8,128)S(1)}, u32[]{:S(2)}, u32[]{:S(2)}) collective-permute-start(f32[9,24,128]{2,1,0:T(8,128)S(1)} %get-tuple-element.75), channel_id=1, source_target_pairs={{1,2},{2,1},{3,4},{4,3},{5,6},{6,5},{9,10},{10,9},{11,12},{12,11},... | collective-permute-start | bytes 331784 | tf_op jit(solution)/shard_map/ppermute | solution.py:453
  76.6 5.6 %collective-permute-start.12 = (f32[18,8,128]{2,1,0:T(8,128)S(1)}, f32[18,8,128]{2,1,0:T(8,128)S(1)}, u32[]{:S(2)}, u32[]{:S(2)}) collective-permute-start(f32[18,8,128]{2,1,0:T(8,128)S(1)} %get-tuple-element.74), channel_id=1, source_target_pairs={{0,32},{32,0},{64,96},{96,64},{128,160},{160,128},{192,224},{224,1... | collective-permute-start | bytes 221192 | tf_op jit(solution)/shard_map/ppermute | solution.py:453
  83.1 2.0 %all-gather.2 = f32[18,24,128]{2,1,0:T(8,128)S(1)} all-gather(f32[9,24,128]{2,1,0:T(8,128)S(1)} %get-tuple-element.76), channel_id=4, replica_groups={{0,1},{2,3},{4,5},{6,7},{8,9},{10,11},{12,13},{14,15},{16,17},{18,19},{..., dimensions={0}, use_global_device_ids=true | all-gather | bytes 331776 | tf_op jit(solution)/shard_map/all_gather | solution.py:462
  86.2 3.0 %collective-permute-start.16 = (f32[8,24,128]{2,1,0:T(8,128)S(1)}, f32[8,24,128]{2,1,0:T(8,128)S(1)}, u32[]{:S(2)}, u32[]{:S(2)}) collective-permute-start(f32[8,24,128]{2,1,0:T(8,128)S(1)} %get-tuple-element.84), channel_id=1, source_target_pairs={{1,2},{2,1},{3,4},{4,3},{5,6},{6,5},{9,10},{10,9},{11,12},{12,11},... | collective-permute-start | bytes 294920 | tf_op jit(solution)/shard_map/ppermute | solution.py:453
  89.9 5.4 %collective-permute-start.15 = (f32[16,8,128]{2,1,0:T(8,128)S(1)}, f32[16,8,128]{2,1,0:T(8,128)S(1)}, u32[]{:S(2)}, u32[]{:S(2)}) collective-permute-start(f32[16,8,128]{2,1,0:T(8,128)S(1)} %get-tuple-element.83), channel_id=1, source_target_pairs={{0,32},{32,0},{64,96},{96,64},{128,160},{160,128},{192,224},{224,1... | collective-permute-start | bytes 196616 | tf_op jit(solution)/shard_map/ppermute | solution.py:453
  95.9 1.2 %shard_map.130 = (f32[16,24,128]{2,1,0:T(8,128)S(1)}, f32[16,24,128]{2,1,0:T(8,128)}) custom-call(f32[16,24,128]{2,1,0:T(8,128)S(1)} %get-tuple-element.86.wave, f32[16,24,128]{2,1,0:T(8,128)S(1)} %get-tuple-element.87.side, bf16[256,256]{1,0:T(8,128)(2,1)S(1)} %copy-done.3, bf16[256,256]{1,0:T(8,128)(2,1)S(1)} %copy-done.4), custom_call_target="tpu_custom_call" | custom-call | flops 1000000 | bytes 2000000 | tf_op jit(solution)/shard_map/pallas_call | solution.py:67
  97.0 1.9 %all-gather.3 = f32[16,24,128]{2,1,0:T(8,128)S(1)} all-gather(f32[8,24,128]{2,1,0:T(8,128)S(1)} %get-tuple-element.85), channel_id=5, replica_groups={{0,1},{2,3},{4,5},{6,7},{8,9},{10,11},{12,13},{14,15},{16,17},{18,19},{..., dimensions={0}, use_global_device_ids=true | all-gather | bytes 294912 | tf_op jit(solution)/shard_map/all_gather | solution.py:462
  99.0 1.5 %shard_map.131 = (f32[16,24,128]{2,1,0:T(8,128)}, f32[16,24,128]{2,1,0:T(8,128)}) custom-call(s32[3]{0:T(128)S(1)} %copy-done.6, f32[16,8,128]{2,1,0:T(8,128)S(1)} %collective-permute-done.14.x_odd_in, f32[16,8,128]{2,1,0:T(8,128)S(1)} %collective-permute-done.15.x_even_in, f32[8,24,128]{2,1,0:T(8,128)S(1)} %collective-permute-done.16.z_odd_in, ...), custom_call_target="tpu_custom_call" | custom-call | flops 1000000 | bytes 2000000 | tf_op jit(solution)/shard_map/pallas_call | solution.py:67
  (41 shorter events, 8.9 us)
Async XLA Ops:
  1.3 42.0 %copy-start.2 = (f32[16,24,128]{2,1,0:T(8,128)S(1)}, f32[16,24,128]{2,1,0:T(8,128)}, u32[]{:S(2)}) copy-start(f32[16,24,128]{2,1,0:T(8,128)} %older.5) | copy-start | bytes 589828
  32.2 11.1 %copy-start.6 = (s32[3]{0:T(128)S(1)}, s32[3]{0:T(128)}, u32[]{:S(2)}) copy-start(s32[3]{0:T(128)} %pad_add_fusion.ids) | copy-start | bytes 40
  32.2 17.1 %copy-start.3 = (bf16[256,256]{1,0:T(8,128)(2,1)S(1)}, bf16[256,256]{1,0:T(8,128)(2,1)}, u32[]{:S(2)}) copy-start(bf16[256,256]{1,0:T(8,128)(2,1)} %constant.18.clone.band_high) | copy-start | bytes 393220
  32.2 17.1 %copy-start.4 = (bf16[256,256]{1,0:T(8,128)(2,1)S(1)}, bf16[256,256]{1,0:T(8,128)(2,1)}, u32[]{:S(2)}) copy-start(bf16[256,256]{1,0:T(8,128)(2,1)} %constant.19.clone.band_low) | copy-start | bytes 393220
  32.2 11.1 %collective-permute-start = (f32[12,24,128]{2,1,0:T(8,128)}, f32[12,24,128]{2,1,0:T(8,128)S(1)}, u32[]{:S(2)}, u32[]{:S(2)}) collective-permute-start(f32[12,24,128]{2,1,0:T(8,128)} %get-tuple-element.51), channel_id=1, source_target_pairs={{0,8},{8,0},{16,24},{24,16},{1,9},{9,1},{17,25},{25,17},{2,10},{10... | collective-permute-start | bytes 442376 | tf_op jit(solution)/shard_map/ppermute | solution.py:453
  34.6 8.7 %collective-permute-start.1 = (f32[12,24,128]{2,1,0:T(8,128)}, f32[12,24,128]{2,1,0:T(8,128)S(1)}, u32[]{:S(2)}, u32[]{:S(2)}) collective-permute-start(f32[12,24,128]{2,1,0:T(8,128)} %get-tuple-element.52), channel_id=1, source_target_pairs={{8,16},{16,8},{9,17},{17,9},{10,18},{18,10},{11,19},{19,11},{12,20... | collective-permute-start | bytes 442376 | tf_op jit(solution)/shard_map/ppermute | solution.py:453
  35.3 15.0 %collective-permute-start.5 = (f32[64,128]{1,0:T(8,128)S(1)}, f32[64,128]{1,0:T(8,128)S(1)}, u32[]{:S(2)}, u32[]{:S(2)}) collective-permute-start(f32[64,128]{1,0:T(8,128)S(1)} %bitcast.17), channel_id=1, source_target_pairs={{2,0},{3,1},{10,8},{11,9},{18,16},{19,17},{26,24},{27,25},{34,32},... | collective-permute-start | bytes 98312 | tf_op jit(solution)/shard_map/ppermute | solution.py:516
  36.6 18.5 %collective-permute-start.6 = (f32[64,128]{1,0:T(8,128)S(1)}, f32[64,128]{1,0:T(8,128)S(1)}, u32[]{:S(2)}, u32[]{:S(2)}) collective-permute-start(f32[64,128]{1,0:T(8,128)S(1)} %bitcast.18), channel_id=1, source_target_pairs={{4,0},{5,1},{12,8},{13,9},{20,16},{21,17},{28,24},{29,25},{36,32},... | collective-permute-start | bytes 98312 | tf_op jit(solution)/shard_map/ppermute | solution.py:516
  37.9 17.2 %collective-permute-start.7 = (f32[64,128]{1,0:T(8,128)S(1)}, f32[64,128]{1,0:T(8,128)S(1)}, u32[]{:S(2)}, u32[]{:S(2)}) collective-permute-start(f32[64,128]{1,0:T(8,128)S(1)} %bitcast.19), channel_id=1, source_target_pairs={{6,0},{7,1},{14,8},{15,9},{22,16},{23,17},{30,24},{31,25},{38,32},... | collective-permute-start | bytes 98312 | tf_op jit(solution)/shard_map/ppermute | solution.py:516
  44.2 14.7 %collective-permute-start.4 = (f32[12,24,128]{2,1,0:T(8,128)S(1)}, f32[12,24,128]{2,1,0:T(8,128)S(1)}, u32[]{:S(2)}, u32[]{:S(2)}) collective-permute-start(f32[12,24,128]{2,1,0:T(8,128)S(1)} %get-tuple-element.55), channel_id=1, source_target_pairs={{1,2},{2,1},{3,4},{4,3},{5,6},{6,5},{9,10},{10,9},{11,12},{12,11},... | collective-permute-start | bytes 442376 | tf_op jit(solution)/shard_map/ppermute | solution.py:453
  48.7 10.3 %collective-permute-start.2 = (f32[24,8,128]{2,1,0:T(8,128)S(1)}, f32[24,8,128]{2,1,0:T(8,128)S(1)}, u32[]{:S(2)}, u32[]{:S(2)}) collective-permute-start(f32[24,8,128]{2,1,0:T(8,128)S(1)} %get-tuple-element.53), channel_id=1, source_target_pairs={{32,64},{64,32},{96,128},{128,96},{160,192},{192,160},{224,256},{2... | collective-permute-start | bytes 294920 | tf_op jit(solution)/shard_map/ppermute | solution.py:453
  50.3 8.6 %collective-permute-start.3 = (f32[24,8,128]{2,1,0:T(8,128)S(1)}, f32[24,8,128]{2,1,0:T(8,128)S(1)}, u32[]{:S(2)}, u32[]{:S(2)}) collective-permute-start(f32[24,8,128]{2,1,0:T(8,128)S(1)} %get-tuple-element.54), channel_id=1, source_target_pairs={{0,32},{32,0},{64,96},{96,64},{128,160},{160,128},{192,224},{224,1... | collective-permute-start | bytes 294920 | tf_op jit(solution)/shard_map/ppermute | solution.py:453
  55.0 3.9 %copy-start.5 = (f32[16,24,128]{2,1,0:T(8,128)S(1)}, f32[16,24,128]{2,1,0:T(8,128)}, u32[]{:S(2)}) copy-start(f32[16,24,128]{2,1,0:T(8,128)} %older.4) | copy-start | bytes 589828
  56.6 2.3 %copy-start = (bf16[4,16,24,128]{3,2,1,0:T(8,128)(2,1)S(1)}, bf16[4,16,24,128]{3,2,1,0:T(8,128)(2,1)}, u32[]{:S(2)}) copy-start(bf16[4,16,24,128]{3,2,1,0:T(8,128)(2,1)} %forward.7) | copy-start | bytes 1179652
  56.6 2.3 %copy-start.1 = (f32[16,24,128]{2,1,0:T(8,128)S(1)}, f32[16,24,128]{2,1,0:T(8,128)}, u32[]{:S(2)}) copy-start(f32[16,24,128]{2,1,0:T(8,128)} %stiff.9) | copy-start | bytes 589828
  60.2 10.4 %collective-permute-start.10 = (f32[10,24,128]{2,1,0:T(8,128)S(1)}, f32[10,24,128]{2,1,0:T(8,128)S(1)}, u32[]{:S(2)}, u32[]{:S(2)}) collective-permute-start(f32[10,24,128]{2,1,0:T(8,128)S(1)} %get-tuple-element.65), channel_id=1, source_target_pairs={{1,2},{2,1},{3,4},{4,3},{5,6},{6,5},{9,10},{10,9},{11,12},{12,11},... | collective-permute-start | bytes 368648 | tf_op jit(solution)/shard_map/ppermute | solution.py:453
  62.3 8.3 %collective-permute-start.8 = (f32[20,8,128]{2,1,0:T(8,128)S(1)}, f32[20,8,128]{2,1,0:T(8,128)S(1)}, u32[]{:S(2)}, u32[]{:S(2)}) collective-permute-start(f32[20,8,128]{2,1,0:T(8,128)S(1)} %get-tuple-element.63), channel_id=1, source_target_pairs={{32,64},{64,32},{96,128},{128,96},{160,192},{192,160},{224,256},{2... | collective-permute-start | bytes 245768 | tf_op jit(solution)/shard_map/ppermute | solution.py:453
  63.0 7.6 %collective-permute-start.9 = (f32[20,8,128]{2,1,0:T(8,128)S(1)}, f32[20,8,128]{2,1,0:T(8,128)S(1)}, u32[]{:S(2)}, u32[]{:S(2)}) collective-permute-start(f32[20,8,128]{2,1,0:T(8,128)S(1)} %get-tuple-element.64), channel_id=1, source_target_pairs={{0,32},{32,0},{64,96},{96,64},{128,160},{160,128},{192,224},{224,1... | collective-permute-start | bytes 245768 | tf_op jit(solution)/shard_map/ppermute | solution.py:453
  71.9 13.2 %collective-permute-start.13 = (f32[9,24,128]{2,1,0:T(8,128)S(1)}, f32[9,24,128]{2,1,0:T(8,128)S(1)}, u32[]{:S(2)}, u32[]{:S(2)}) collective-permute-start(f32[9,24,128]{2,1,0:T(8,128)S(1)} %get-tuple-element.75), channel_id=1, source_target_pairs={{1,2},{2,1},{3,4},{4,3},{5,6},{6,5},{9,10},{10,9},{11,12},{12,11},... | collective-permute-start | bytes 331784 | tf_op jit(solution)/shard_map/ppermute | solution.py:453
  75.9 9.2 %collective-permute-start.11 = (f32[18,8,128]{2,1,0:T(8,128)S(1)}, f32[18,8,128]{2,1,0:T(8,128)S(1)}, u32[]{:S(2)}, u32[]{:S(2)}) collective-permute-start(f32[18,8,128]{2,1,0:T(8,128)S(1)} %get-tuple-element.73), channel_id=1, source_target_pairs={{32,64},{64,32},{96,128},{128,96},{160,192},{192,160},{224,256},{2... | collective-permute-start | bytes 221192 | tf_op jit(solution)/shard_map/ppermute | solution.py:453
  76.6 8.5 %collective-permute-start.12 = (f32[18,8,128]{2,1,0:T(8,128)S(1)}, f32[18,8,128]{2,1,0:T(8,128)S(1)}, u32[]{:S(2)}, u32[]{:S(2)}) collective-permute-start(f32[18,8,128]{2,1,0:T(8,128)S(1)} %get-tuple-element.74), channel_id=1, source_target_pairs={{0,32},{32,0},{64,96},{96,64},{128,160},{160,128},{192,224},{224,1... | collective-permute-start | bytes 221192 | tf_op jit(solution)/shard_map/ppermute | solution.py:453
  86.2 12.8 %collective-permute-start.16 = (f32[8,24,128]{2,1,0:T(8,128)S(1)}, f32[8,24,128]{2,1,0:T(8,128)S(1)}, u32[]{:S(2)}, u32[]{:S(2)}) collective-permute-start(f32[8,24,128]{2,1,0:T(8,128)S(1)} %get-tuple-element.84), channel_id=1, source_target_pairs={{1,2},{2,1},{3,4},{4,3},{5,6},{6,5},{9,10},{10,9},{11,12},{12,11},... | collective-permute-start | bytes 294920 | tf_op jit(solution)/shard_map/ppermute | solution.py:453
  89.2 9.8 %collective-permute-start.14 = (f32[16,8,128]{2,1,0:T(8,128)S(1)}, f32[16,8,128]{2,1,0:T(8,128)S(1)}, u32[]{:S(2)}, u32[]{:S(2)}) collective-permute-start(f32[16,8,128]{2,1,0:T(8,128)S(1)} %get-tuple-element.82), channel_id=1, source_target_pairs={{32,64},{64,32},{96,128},{128,96},{160,192},{192,160},{224,256},{2... | collective-permute-start | bytes 196616 | tf_op jit(solution)/shard_map/ppermute | solution.py:453
  89.9 9.1 %collective-permute-start.15 = (f32[16,8,128]{2,1,0:T(8,128)S(1)}, f32[16,8,128]{2,1,0:T(8,128)S(1)}, u32[]{:S(2)}, u32[]{:S(2)}) collective-permute-start(f32[16,8,128]{2,1,0:T(8,128)S(1)} %get-tuple-element.83), channel_id=1, source_target_pairs={{0,32},{32,0},{64,96},{96,64},{128,160},{160,128},{192,224},{224,1... | collective-permute-start | bytes 196616 | tf_op jit(solution)/shard_map/ppermute | solution.py:453

commit v8 on v7

--- a/solution.py
+++ b/solution.py
@@ -91,17 +91,9 @@
 
 
 def prepare_kernel(span_y, tiles, ids, residuals, owners, cells, wave, older, stiff, packets,
-                   even, odd, held, sems):
-    copies = [
-        pltpu.make_async_copy(field, held.at[number], sems.at[number])
-        for number, field in enumerate((wave, older, stiff))
-    ]
-    for copy in copies:
-        copy.start()
+                   even, odd):
     pack_slots(span_y, tiles, residuals, owners, cells, packets)
-    for copy in copies:
-        copy.wait()
-    pack_strips(ids, held.at[0], held.at[1], held.at[2], even, odd)
+    pack_strips(ids, wave, older, stiff, even, odd)
 
 
 def pack_slots(span_y, tiles, residuals, owner_row, cell_row, out):
@@ -270,7 +262,8 @@
     chunks = wave.shape[0] // quarters
     for number, side in enumerate((wave_side, older_side, stiff_side)):
         for chunk in range(chunks):
-            one, two = even[number * chunks + chunk], odd[number * chunks + chunk]
+            one = even[1 - parity, number * chunks + chunk]
+            two = odd[number * chunks + chunk]
             for turn in range(quarters):
                 back = (LANES - STRIP * turn) % LANES
                 first = pltpu.roll(one, back, 1) if back else one
@@ -499,18 +492,18 @@
         [shaped(tiles, LANES), strips, strips],
         [ids, residuals, owners.reshape(1, -1), receivers.reshape(1, -1), wave_now, older_wave,
          stiffness],
-        scratch=[pltpu.VMEM((3, depth, rows, LANES), F32), pltpu.SemaphoreType.DMA((3,))],
-        in_specs=[smem()] + [pl.BlockSpec()] * 3 + [pl.BlockSpec(memory_space=pl.ANY)] * 3,
+        in_specs=[smem()] + [pl.BlockSpec()] * 6,
         grant=60,
     )
     packets = lax.all_to_all(packets, ("gx", "gy"), 0, 0, tiled=True)
-    packets, even, odd = lax.optimization_barrier((packets, even, odd))
-    even, odd = (swap(strip, "gy", parity) for parity, strip in enumerate((even, odd)))
+    odd = swap(odd, "gy", 1)
+    even = pair_gather(even, "gy", 0)
     side, older_side, stiff_side, *faces = call(
         strip_unpack_kernel,
         [block] * 3 + faces_out(0),
         [ids, even, odd, wave_now],
     )
+    packets, faces = lax.optimization_barrier((packets, faces))
     cores = 2
     packets = [packets] + [
         lax.ppermute(packets, "gz", [(chip + core, core) for core in range(cores)])

time: 102 us -> 99.6 us (0.976)
  starting transfers between devices: 43.4 us -> 62.9 us
  blocking collectives: 36.1 us -> 19 us
  waiting for transfers between devices: 4.2 us -> 0.04 us
    all_to_all x1 -> x0, blocking collectives: 28 us -> none  [on_device(): packets = lax.all_to_all(packets, ('gx', 'gy'), 0, 0, tiled=True)]
    all_to_all x0 -> x1, starting transfers between devices: none -> 19.5 us  [on_device(): packets = lax.all_to_all(packets, ('gx', 'gy'), 0, 0, tiled=True)]
    all_gather x4 -> x5, blocking collectives: 8.17 us -> 19 us  [pair_gather(): lax.all_gather(block, axis, axis=0, tiled=False, axis_index_groups=groups)]
    ppermute x14 -> x13, waiting for transfers between devices: 4.2 us -> 0.03 us  [swap(): return lax.ppermute(block, axis, pairs)]
    ppermute x14 -> x13, starting transfers between devices: 39.5 us -> 39.4 us  [swap(): return lax.ppermute(block, axis, pairs)]
  transfers between devices with their start and end apart: 17 -> 17, of which waited for: 1 -> 0; matrix products, arithmetic and copies ran while one was open for 0% -> 0% of each run, Pallas kernels for 6% -> 7%
where the time goes in v8:
time: 99.6 us; the launch traced here: 98.6 us
  starting transfers between devices  62.9 us (63%)
  blocking collectives  19 us (19%)
  Pallas kernels  13.8 us (14%)
  between operations  1.6 us (2%)
    ppermute x13, starting transfers between devices, swap(): return lax.ppermute(block, axis, pairs)  39.4 us
    all_to_all x1, starting transfers between devices, on_device(): packets = lax.all_to_all(packets, ('gx', 'gy'), 0, 0, tiled=True)  19.5 us
    all_gather x5, blocking collectives, pair_gather(): lax.all_gather(block, axis, axis=0, tiled=False, axis_index_groups=groups)  19 us
    pallas_call x11, Pallas kernels, call(): pl.pallas_call(body, out_shape=outs, in_specs=in_specs or [smem()] + [vme...  13.8 us
    ppermute x3, starting transfers between devices, on_device(): lax.ppermute(packets, 'gz', [(chip + core, core) for core in range(cores)])  3.88 us
  transfers between devices with their start and end apart: 17, of which 0 were waited for; matrix products, arithmetic and copies ran while one was open for 0% of the time, Pallas kernels for 7%

profile of v8, /device:TPU:1, one launch (start us, length us, event | category | flops | bytes accessed | tf_op | source)
XLA Modules:
  0.0 98.6 jit_solution(17971115744831872484)
XLA Ops:
  1.3 2.3 %shard_map.121 = (f32[64,128]{1,0:T(8,128)}, f32[12,24,128]{2,1,0:T(8,128)}, f32[12,24,128]{2,1,0:T(8,128)}) custom-call(s32[3]{0:T(128)} %pad_add_fusion.ids, f32[4,128]{1,0:T(4,128)} %residuals.1, s32[1,128]{1,0:T(1,128)} %bitcast.24, s32[1,128]{1,0:T(1,128)} %bitcast.25, f32[16,24,128]{2,1,0:T(8,128)} %older.5, f32[16,24,128]{2,1,0:T(8,128)} %older.4, ...), custom_call_target="tpu_custom_call" | custom-call | flops 1000000 | bytes 2000000 | tf_op jit(solution)/shard_map/pallas_call | solution.py:67
  4.2 19.5 %all-to-all-start = ((f32[64,1,128]{2,1,0:T(1,128)}), f32[64,1,128]{2,1,0:T(1,128)S(1)}, u32[]{:S(2)}, u32[]{:S(2)}) async-start(f32[64,1,128]{2,1,0:T(1,128)} %bitcast.23), calls=%async_computation | async-start | bytes 65536 | tf_op jit(solution)/shard_map/all_to_all | solution.py:498
  23.8 10.8 %all-gather = f32[24,24,128]{2,1,0:T(8,128)S(1)} all-gather(f32[12,24,128]{2,1,0:T(8,128)} %get-tuple-element.51), channel_id=2, replica_groups={{0,8},{16,24},{1,9},{17,25},{2,10},{18,26},{3,11},{19,27},{4,12},{20,28..., dimensions={0}, use_global_device_ids=true | all-gather | bytes 442368 | tf_op jit(solution)/shard_map/all_gather | solution.py:455
  36.1 1.3 %collective-permute-start.4 = (f32[64,128]{1,0:T(8,128)S(1)}, f32[64,128]{1,0:T(8,128)S(1)}, u32[]{:S(2)}, u32[]{:S(2)}) collective-permute-start(f32[64,128]{1,0:T(8,128)S(1)} %bitcast.19), channel_id=1, source_target_pairs={{2,0},{3,1},{10,8},{11,9},{18,16},{19,17},{26,24},{27,25},{34,32},... | collective-permute-start | bytes 98312 | tf_op jit(solution)/shard_map/ppermute | solution.py:509
  37.4 1.3 %collective-permute-start.5 = (f32[64,128]{1,0:T(8,128)S(1)}, f32[64,128]{1,0:T(8,128)S(1)}, u32[]{:S(2)}, u32[]{:S(2)}) collective-permute-start(f32[64,128]{1,0:T(8,128)S(1)} %bitcast.20), channel_id=1, source_target_pairs={{4,0},{5,1},{12,8},{13,9},{20,16},{21,17},{28,24},{29,25},{36,32},... | collective-permute-start | bytes 98312 | tf_op jit(solution)/shard_map/ppermute | solution.py:509
  38.7 1.3 %collective-permute-start.6 = (f32[64,128]{1,0:T(8,128)S(1)}, f32[64,128]{1,0:T(8,128)S(1)}, u32[]{:S(2)}, u32[]{:S(2)}) collective-permute-start(f32[64,128]{1,0:T(8,128)S(1)} %bitcast.21), channel_id=1, source_target_pairs={{6,0},{7,1},{14,8},{15,9},{22,16},{23,17},{30,24},{31,25},{38,32},... | collective-permute-start | bytes 98312 | tf_op jit(solution)/shard_map/ppermute | solution.py:509
  40.0 4.0 %collective-permute-start.3 = (f32[12,24,128]{2,1,0:T(8,128)S(1)}, f32[12,24,128]{2,1,0:T(8,128)S(1)}, u32[]{:S(2)}, u32[]{:S(2)}) collective-permute-start(f32[12,24,128]{2,1,0:T(8,128)S(1)} %get-tuple-element.59), channel_id=1, source_target_pairs={{1,2},{2,1},{3,4},{4,3},{5,6},{6,5},{9,10},{10,9},{11,12},{12,11},... | collective-permute-start | bytes 442376 | tf_op jit(solution)/shard_map/ppermute | solution.py:446
  45.8 5.3 %collective-permute-start.2 = (f32[24,8,128]{2,1,0:T(8,128)S(1)}, f32[24,8,128]{2,1,0:T(8,128)S(1)}, u32[]{:S(2)}, u32[]{:S(2)}) collective-permute-start(f32[24,8,128]{2,1,0:T(8,128)S(1)} %get-tuple-element.58), channel_id=1, source_target_pairs={{0,32},{32,0},{64,96},{96,64},{128,160},{160,128},{192,224},{224,1... | collective-permute-start | bytes 294920 | tf_op jit(solution)/shard_map/ppermute | solution.py:446
  51.1 1.6 %shard_map.123 = f32[20,24,128]{2,1,0:T(8,128)S(1)} custom-call(s32[3]{0:T(128)S(1)} %copy-done.6, f32[12,24,128]{2,1,0:T(8,128)S(1)} %get-tuple-element.60.z_even, f32[64,128]{1,0:T(8,128)S(1)} %bitcast.22, f32[64,128]{1,0:T(8,128)S(1)} %collective-permute-done.4.refs_1_, f32[64,128]{1,0:T(8,128)S(1)} %collective-permute-done.5.refs_2_, ...), custom_call_target="tpu_custom_call" | custom-call | flops 1000000 | bytes 2000000 | tf_op jit(solution)/shard_map/pallas_call | solution.py:67
  52.7 2.3 %all-gather.1 = f32[40,24,128]{2,1,0:T(8,128)S(1)} all-gather(f32[20,24,128]{2,1,0:T(8,128)S(1)} %shard_map.123), channel_id=3, replica_groups={{0,1},{2,3},{4,5},{6,7},{8,9},{10,11},{12,13},{14,15},{16,17},{18,19},{..., dimensions={0}, use_global_device_ids=true | all-gather | bytes 737280 | tf_op jit(solution)/shard_map/all_gather | solution.py:455
  55.0 1.2 %shard_map.125 = (f32[8,24,128]{2,1,0:T(8,128)S(1)}, f32[16,24,128]{2,1,0:T(8,128)S(1)}, f32[16,24,128]{2,1,0:T(8,128)S(1)}, f32[16,24,128]{2,1,0:T(8,128)S(1)},...) custom-call(s32[3]{0:T(128)S(1)} %copy-done.6, ...), custom_call_target="tpu_custom_call" | custom-call | flops 1000000 | bytes 2000000 | tf_op jit(solution)/shard_map/pallas_call | solution.py:67
  56.3 2.7 %collective-permute-start.9 = (f32[10,24,128]{2,1,0:T(8,128)S(1)}, f32[10,24,128]{2,1,0:T(8,128)S(1)}, u32[]{:S(2)}, u32[]{:S(2)}) collective-permute-start(f32[10,24,128]{2,1,0:T(8,128)S(1)} %get-tuple-element.69), channel_id=1, source_target_pairs={{1,2},{2,1},{3,4},{4,3},{5,6},{6,5},{9,10},{10,9},{11,12},{12,11},... | collective-permute-start | bytes 368648 | tf_op jit(solution)/shard_map/ppermute | solution.py:446
  59.6 5.5 %collective-permute-start.8 = (f32[20,8,128]{2,1,0:T(8,128)S(1)}, f32[20,8,128]{2,1,0:T(8,128)S(1)}, u32[]{:S(2)}, u32[]{:S(2)}) collective-permute-start(f32[20,8,128]{2,1,0:T(8,128)S(1)} %get-tuple-element.68), channel_id=1, source_target_pairs={{0,32},{32,0},{64,96},{96,64},{128,160},{160,128},{192,224},{224,1... | collective-permute-start | bytes 245768 | tf_op jit(solution)/shard_map/ppermute | solution.py:446
  66.1 2.0 %all-gather.2 = f32[20,24,128]{2,1,0:T(8,128)S(1)} all-gather(f32[10,24,128]{2,1,0:T(8,128)S(1)} %get-tuple-element.70), channel_id=4, replica_groups={{0,1},{2,3},{4,5},{6,7},{8,9},{10,11},{12,13},{14,15},{16,17},{18,19},{..., dimensions={0}, use_global_device_ids=true | all-gather | bytes 368640 | tf_op jit(solution)/shard_map/all_gather | solution.py:455
  68.1 1.3 %shard_map.127 = (f32[16,24,128]{2,1,0:T(8,128)S(1)}, f32[16,24,128]{2,1,0:T(8,128)S(1)}, f32[16,24,128]{2,1,0:T(8,128)S(1)}, f32[9,24,128]{2,1,0:T(8,128)S(1)},...) custom-call(s32[3]{0:T(128)S(1)} %copy-done.6, ...), custom_call_target="tpu_custom_call" | custom-call | flops 1000000 | bytes 2000000 | tf_op jit(solution)/shard_map/pallas_call | solution.py:67
  69.4 3.7 %collective-permute-start.12 = (f32[9,24,128]{2,1,0:T(8,128)S(1)}, f32[9,24,128]{2,1,0:T(8,128)S(1)}, u32[]{:S(2)}, u32[]{:S(2)}) collective-permute-start(f32[9,24,128]{2,1,0:T(8,128)S(1)} %get-tuple-element.79), channel_id=1, source_target_pairs={{1,2},{2,1},{3,4},{4,3},{5,6},{6,5},{9,10},{10,9},{11,12},{12,11},... | collective-permute-start | bytes 331784 | tf_op jit(solution)/shard_map/ppermute | solution.py:446
  73.8 5.5 %collective-permute-start.11 = (f32[18,8,128]{2,1,0:T(8,128)S(1)}, f32[18,8,128]{2,1,0:T(8,128)S(1)}, u32[]{:S(2)}, u32[]{:S(2)}) collective-permute-start(f32[18,8,128]{2,1,0:T(8,128)S(1)} %get-tuple-element.78), channel_id=1, source_target_pairs={{0,32},{32,0},{64,96},{96,64},{128,160},{160,128},{192,224},{224,1... | collective-permute-start | bytes 221192 | tf_op jit(solution)/shard_map/ppermute | solution.py:446
  80.2 2.0 %all-gather.3 = f32[18,24,128]{2,1,0:T(8,128)S(1)} all-gather(f32[9,24,128]{2,1,0:T(8,128)S(1)} %get-tuple-element.80), channel_id=5, replica_groups={{0,1},{2,3},{4,5},{6,7},{8,9},{10,11},{12,13},{14,15},{16,17},{18,19},{..., dimensions={0}, use_global_device_ids=true | all-gather | bytes 331776 | tf_op jit(solution)/shard_map/all_gather | solution.py:455
  82.2 1.1 %shard_map.129 = (f32[16,24,128]{2,1,0:T(8,128)S(1)}, f32[16,24,128]{2,1,0:T(8,128)S(1)}, f32[16,24,128]{2,1,0:T(8,128)S(1)}, f32[8,24,128]{2,1,0:T(8,128)S(1)},...) custom-call(s32[3]{0:T(128)S(1)} %copy-done.6, ...), custom_call_target="tpu_custom_call" | custom-call | flops 1000000 | bytes 2000000 | tf_op jit(solution)/shard_map/pallas_call | solution.py:67
  83.3 2.6 %collective-permute-start.15 = (f32[8,24,128]{2,1,0:T(8,128)S(1)}, f32[8,24,128]{2,1,0:T(8,128)S(1)}, u32[]{:S(2)}, u32[]{:S(2)}) collective-permute-start(f32[8,24,128]{2,1,0:T(8,128)S(1)} %get-tuple-element.88), channel_id=1, source_target_pairs={{1,2},{2,1},{3,4},{4,3},{5,6},{6,5},{9,10},{10,9},{11,12},{12,11},... | collective-permute-start | bytes 294920 | tf_op jit(solution)/shard_map/ppermute | solution.py:446
  86.6 6.7 %collective-permute-start.14 = (f32[16,8,128]{2,1,0:T(8,128)S(1)}, f32[16,8,128]{2,1,0:T(8,128)S(1)}, u32[]{:S(2)}, u32[]{:S(2)}) collective-permute-start(f32[16,8,128]{2,1,0:T(8,128)S(1)} %get-tuple-element.87), channel_id=1, source_target_pairs={{0,32},{32,0},{64,96},{96,64},{128,160},{160,128},{192,224},{224,1... | collective-permute-start | bytes 196616 | tf_op jit(solution)/shard_map/ppermute | solution.py:446
  93.9 1.2 %shard_map.130 = (f32[16,24,128]{2,1,0:T(8,128)S(1)}, f32[16,24,128]{2,1,0:T(8,128)}) custom-call(f32[16,24,128]{2,1,0:T(8,128)S(1)} %get-tuple-element.90.wave, f32[16,24,128]{2,1,0:T(8,128)S(1)} %get-tuple-element.91.side, bf16[256,256]{1,0:T(8,128)(2,1)S(1)} %copy-done.3, bf16[256,256]{1,0:T(8,128)(2,1)S(1)} %copy-done.4), custom_call_target="tpu_custom_call" | custom-call | flops 1000000 | bytes 2000000 | tf_op jit(solution)/shard_map/pallas_call | solution.py:67
  95.1 1.9 %all-gather.4 = f32[16,24,128]{2,1,0:T(8,128)S(1)} all-gather(f32[8,24,128]{2,1,0:T(8,128)S(1)} %get-tuple-element.89), channel_id=6, replica_groups={{0,1},{2,3},{4,5},{6,7},{8,9},{10,11},{12,13},{14,15},{16,17},{18,19},{..., dimensions={0}, use_global_device_ids=true | all-gather | bytes 294912 | tf_op jit(solution)/shard_map/all_gather | solution.py:455
  97.0 1.5 %shard_map.131 = (f32[16,24,128]{2,1,0:T(8,128)}, f32[16,24,128]{2,1,0:T(8,128)}) custom-call(s32[3]{0:T(128)S(1)} %copy-done.6, f32[16,8,128]{2,1,0:T(8,128)S(1)} %collective-permute-done.13.x_odd_in, f32[16,8,128]{2,1,0:T(8,128)S(1)} %collective-permute-done.14.x_even_in, f32[8,24,128]{2,1,0:T(8,128)S(1)} %collective-permute-done.15.z_odd_in, ...), custom_call_target="tpu_custom_call" | custom-call | flops 1000000 | bytes 2000000 | tf_op jit(solution)/shard_map/pallas_call | solution.py:67
  (41 shorter events, 8.3 us)
Async XLA Ops:
  3.5 31.1 %collective-permute-start = (f32[12,24,128]{2,1,0:T(8,128)}, f32[12,24,128]{2,1,0:T(8,128)S(1)}, u32[]{:S(2)}, u32[]{:S(2)}) collective-permute-start(f32[12,24,128]{2,1,0:T(8,128)} %get-tuple-element.52), channel_id=1, source_target_pairs={{8,16},{16,8},{9,17},{17,9},{10,18},{18,10},{11,19},{19,11},{12,20... | collective-permute-start | bytes 442376 | tf_op jit(solution)/shard_map/ppermute | solution.py:446
  4.2 31.9 %all-to-all-start = ((f32[64,1,128]{2,1,0:T(1,128)}), f32[64,1,128]{2,1,0:T(1,128)S(1)}, u32[]{:S(2)}, u32[]{:S(2)}) async-start(f32[64,1,128]{2,1,0:T(1,128)} %bitcast.23), calls=%async_computation | async-start | bytes 65536 | tf_op jit(solution)/shard_map/all_to_all | solution.py:498
  23.8 10.8 %copy-start.2 = (f32[16,24,128]{2,1,0:T(8,128)S(1)}, f32[16,24,128]{2,1,0:T(8,128)}, u32[]{:S(2)}) copy-start(f32[16,24,128]{2,1,0:T(8,128)} %older.5) | copy-start | bytes 589828
  34.6 0.6 copy-start.6
  35.2 9.5 %copy-start.3 = (bf16[256,256]{1,0:T(8,128)(2,1)S(1)}, bf16[256,256]{1,0:T(8,128)(2,1)}, u32[]{:S(2)}) copy-start(bf16[256,256]{1,0:T(8,128)(2,1)} %constant.18.clone.band_high) | copy-start | bytes 393220
  35.2 9.5 %copy-start.4 = (bf16[256,256]{1,0:T(8,128)(2,1)S(1)}, bf16[256,256]{1,0:T(8,128)(2,1)}, u32[]{:S(2)}) copy-start(bf16[256,256]{1,0:T(8,128)(2,1)} %constant.19.clone.band_low) | copy-start | bytes 393220
  36.1 9.6 %collective-permute-start.4 = (f32[64,128]{1,0:T(8,128)S(1)}, f32[64,128]{1,0:T(8,128)S(1)}, u32[]{:S(2)}, u32[]{:S(2)}) collective-permute-start(f32[64,128]{1,0:T(8,128)S(1)} %bitcast.19), channel_id=1, source_target_pairs={{2,0},{3,1},{10,8},{11,9},{18,16},{19,17},{26,24},{27,25},{34,32},... | collective-permute-start | bytes 98312 | tf_op jit(solution)/shard_map/ppermute | solution.py:509
  37.4 13.7 %collective-permute-start.5 = (f32[64,128]{1,0:T(8,128)S(1)}, f32[64,128]{1,0:T(8,128)S(1)}, u32[]{:S(2)}, u32[]{:S(2)}) collective-permute-start(f32[64,128]{1,0:T(8,128)S(1)} %bitcast.20), channel_id=1, source_target_pairs={{4,0},{5,1},{12,8},{13,9},{20,16},{21,17},{28,24},{29,25},{36,32},... | collective-permute-start | bytes 98312 | tf_op jit(solution)/shard_map/ppermute | solution.py:509
  38.7 12.4 %collective-permute-start.6 = (f32[64,128]{1,0:T(8,128)S(1)}, f32[64,128]{1,0:T(8,128)S(1)}, u32[]{:S(2)}, u32[]{:S(2)}) collective-permute-start(f32[64,128]{1,0:T(8,128)S(1)} %bitcast.21), channel_id=1, source_target_pairs={{6,0},{7,1},{14,8},{15,9},{22,16},{23,17},{30,24},{31,25},{38,32},... | collective-permute-start | bytes 98312 | tf_op jit(solution)/shard_map/ppermute | solution.py:509
  40.0 15.0 %collective-permute-start.3 = (f32[12,24,128]{2,1,0:T(8,128)S(1)}, f32[12,24,128]{2,1,0:T(8,128)S(1)}, u32[]{:S(2)}, u32[]{:S(2)}) collective-permute-start(f32[12,24,128]{2,1,0:T(8,128)S(1)} %get-tuple-element.59), channel_id=1, source_target_pairs={{1,2},{2,1},{3,4},{4,3},{5,6},{6,5},{9,10},{10,9},{11,12},{12,11},... | collective-permute-start | bytes 442376 | tf_op jit(solution)/shard_map/ppermute | solution.py:446
  44.1 10.9 %collective-permute-start.1 = (f32[24,8,128]{2,1,0:T(8,128)S(1)}, f32[24,8,128]{2,1,0:T(8,128)S(1)}, u32[]{:S(2)}, u32[]{:S(2)}) collective-permute-start(f32[24,8,128]{2,1,0:T(8,128)S(1)} %get-tuple-element.57), channel_id=1, source_target_pairs={{32,64},{64,32},{96,128},{128,96},{160,192},{192,160},{224,256},{2... | collective-permute-start | bytes 294920 | tf_op jit(solution)/shard_map/ppermute | solution.py:446
  45.8 9.3 %collective-permute-start.2 = (f32[24,8,128]{2,1,0:T(8,128)S(1)}, f32[24,8,128]{2,1,0:T(8,128)S(1)}, u32[]{:S(2)}, u32[]{:S(2)}) collective-permute-start(f32[24,8,128]{2,1,0:T(8,128)S(1)} %get-tuple-element.58), channel_id=1, source_target_pairs={{0,32},{32,0},{64,96},{96,64},{128,160},{160,128},{192,224},{224,1... | collective-permute-start | bytes 294920 | tf_op jit(solution)/shard_map/ppermute | solution.py:446
  51.1 3.9 %copy-start.5 = (f32[16,24,128]{2,1,0:T(8,128)S(1)}, f32[16,24,128]{2,1,0:T(8,128)}, u32[]{:S(2)}) copy-start(f32[16,24,128]{2,1,0:T(8,128)} %older.4) | copy-start | bytes 589828
  52.7 2.3 %copy-start = (bf16[4,16,24,128]{3,2,1,0:T(8,128)(2,1)S(1)}, bf16[4,16,24,128]{3,2,1,0:T(8,128)(2,1)}, u32[]{:S(2)}) copy-start(bf16[4,16,24,128]{3,2,1,0:T(8,128)(2,1)} %forward.7) | copy-start | bytes 1179652
  52.7 2.3 %copy-start.1 = (f32[16,24,128]{2,1,0:T(8,128)S(1)}, f32[16,24,128]{2,1,0:T(8,128)}, u32[]{:S(2)}) copy-start(f32[16,24,128]{2,1,0:T(8,128)} %stiff.9) | copy-start | bytes 589828
  56.3 11.9 %collective-permute-start.9 = (f32[10,24,128]{2,1,0:T(8,128)S(1)}, f32[10,24,128]{2,1,0:T(8,128)S(1)}, u32[]{:S(2)}, u32[]{:S(2)}) collective-permute-start(f32[10,24,128]{2,1,0:T(8,128)S(1)} %get-tuple-element.69), channel_id=1, source_target_pairs={{1,2},{2,1},{3,4},{4,3},{5,6},{6,5},{9,10},{10,9},{11,12},{12,11},... | collective-permute-start | bytes 368648 | tf_op jit(solution)/shard_map/ppermute | solution.py:446
  59.0 9.1 %collective-permute-start.7 = (f32[20,8,128]{2,1,0:T(8,128)S(1)}, f32[20,8,128]{2,1,0:T(8,128)S(1)}, u32[]{:S(2)}, u32[]{:S(2)}) collective-permute-start(f32[20,8,128]{2,1,0:T(8,128)S(1)} %get-tuple-element.67), channel_id=1, source_target_pairs={{32,64},{64,32},{96,128},{128,96},{160,192},{192,160},{224,256},{2... | collective-permute-start | bytes 245768 | tf_op jit(solution)/shard_map/ppermute | solution.py:446
  59.6 8.5 %collective-permute-start.8 = (f32[20,8,128]{2,1,0:T(8,128)S(1)}, f32[20,8,128]{2,1,0:T(8,128)S(1)}, u32[]{:S(2)}, u32[]{:S(2)}) collective-permute-start(f32[20,8,128]{2,1,0:T(8,128)S(1)} %get-tuple-element.68), channel_id=1, source_target_pairs={{0,32},{32,0},{64,96},{96,64},{128,160},{160,128},{192,224},{224,1... | collective-permute-start | bytes 245768 | tf_op jit(solution)/shard_map/ppermute | solution.py:446
  69.4 12.8 %collective-permute-start.12 = (f32[9,24,128]{2,1,0:T(8,128)S(1)}, f32[9,24,128]{2,1,0:T(8,128)S(1)}, u32[]{:S(2)}, u32[]{:S(2)}) collective-permute-start(f32[9,24,128]{2,1,0:T(8,128)S(1)} %get-tuple-element.79), channel_id=1, source_target_pairs={{1,2},{2,1},{3,4},{4,3},{5,6},{6,5},{9,10},{10,9},{11,12},{12,11},... | collective-permute-start | bytes 331784 | tf_op jit(solution)/shard_map/ppermute | solution.py:446
  73.1 9.1 %collective-permute-start.10 = (f32[18,8,128]{2,1,0:T(8,128)S(1)}, f32[18,8,128]{2,1,0:T(8,128)S(1)}, u32[]{:S(2)}, u32[]{:S(2)}) collective-permute-start(f32[18,8,128]{2,1,0:T(8,128)S(1)} %get-tuple-element.77), channel_id=1, source_target_pairs={{32,64},{64,32},{96,128},{128,96},{160,192},{192,160},{224,256},{2... | collective-permute-start | bytes 221192 | tf_op jit(solution)/shard_map/ppermute | solution.py:446
  73.8 8.4 %collective-permute-start.11 = (f32[18,8,128]{2,1,0:T(8,128)S(1)}, f32[18,8,128]{2,1,0:T(8,128)S(1)}, u32[]{:S(2)}, u32[]{:S(2)}) collective-permute-start(f32[18,8,128]{2,1,0:T(8,128)S(1)} %get-tuple-element.78), channel_id=1, source_target_pairs={{0,32},{32,0},{64,96},{96,64},{128,160},{160,128},{192,224},{224,1... | collective-permute-start | bytes 221192 | tf_op jit(solution)/shard_map/ppermute | solution.py:446
  83.3 13.7 %collective-permute-start.15 = (f32[8,24,128]{2,1,0:T(8,128)S(1)}, f32[8,24,128]{2,1,0:T(8,128)S(1)}, u32[]{:S(2)}, u32[]{:S(2)}) collective-permute-start(f32[8,24,128]{2,1,0:T(8,128)S(1)} %get-tuple-element.88), channel_id=1, source_target_pairs={{1,2},{2,1},{3,4},{4,3},{5,6},{6,5},{9,10},{10,9},{11,12},{12,11},... | collective-permute-start | bytes 294920 | tf_op jit(solution)/shard_map/ppermute | solution.py:446
  85.9 11.1 %collective-permute-start.13 = (f32[16,8,128]{2,1,0:T(8,128)S(1)}, f32[16,8,128]{2,1,0:T(8,128)S(1)}, u32[]{:S(2)}, u32[]{:S(2)}) collective-permute-start(f32[16,8,128]{2,1,0:T(8,128)S(1)} %get-tuple-element.86), channel_id=1, source_target_pairs={{32,64},{64,32},{96,128},{128,96},{160,192},{192,160},{224,256},{2... | collective-permute-start | bytes 196616 | tf_op jit(solution)/shard_map/ppermute | solution.py:446
  86.6 10.4 %collective-permute-start.14 = (f32[16,8,128]{2,1,0:T(8,128)S(1)}, f32[16,8,128]{2,1,0:T(8,128)S(1)}, u32[]{:S(2)}, u32[]{:S(2)}) collective-permute-start(f32[16,8,128]{2,1,0:T(8,128)S(1)} %get-tuple-element.87), channel_id=1, source_target_pairs={{0,32},{32,0},{64,96},{96,64},{128,160},{160,128},{192,224},{224,1... | collective-permute-start | bytes 196616 | tf_op jit(solution)/shard_map/ppermute | solution.py:446

commit v9 on v8

--- a/solution.py
+++ b/solution.py
@@ -67,7 +67,7 @@
     return pl.pallas_call(
         body,
         out_shape=outs,
-        in_specs=in_specs or [smem()] + [vmem()] * (len(ins) - 1),
+        in_specs=in_specs or [vmem()] * len(ins),
         out_specs=out_specs or jax.tree.map(lambda _: vmem(), outs),
         scratch_shapes=list(scratch),
         compiler_params=pltpu.CompilerParams(vmem_limit_bytes=grant * 1024 * 1024),
@@ -90,10 +90,14 @@
     return lax.dot_general(left, right, (((1,), (1,)), ((), ())), preferred_element_type=F32)
 
 
-def prepare_kernel(span_y, tiles, ids, residuals, owners, cells, wave, older, stiff, packets,
+def place():
+    return tuple(lax.axis_index(axis) for axis in ("gz", "gx", "gy"))
+
+
+def prepare_kernel(span_y, tiles, residuals, owners, cells, wave, older, stiff, packets,
                    even, odd):
     pack_slots(span_y, tiles, residuals, owners, cells, packets)
-    pack_strips(ids, wave, older, stiff, even, odd)
+    pack_strips(place(), wave, older, stiff, even, odd)
 
 
 def pack_slots(span_y, tiles, residuals, owner_row, cell_row, out):
@@ -133,12 +137,12 @@
     out[...] = total
 
 
-def plane_kernel(face, rows, ids, z_even, *refs):
+def plane_kernel(face, rows, z_even, *refs):
     *packets, out, turned = refs
     out[pl.ds(0, face)] = z_even[...]
     out[pl.ds(face, 2 * STEPS)] = jnp.zeros((2 * STEPS, rows, LANES), F32)
 
-    @pl.when(ids[0] < 2)
+    @pl.when(place()[0] < 2)
     def _():
         count = turned.shape[1]
         share = count // len(packets)
@@ -252,8 +256,9 @@
 
 
 def strip_unpack_kernel(
-    ids, even, odd, wave, wave_side, older_side, stiff_side, z_even, z_odd, x_even, x_odd
+    even, odd, wave, wave_side, older_side, stiff_side, z_even, z_odd, x_even, x_odd
 ):
+    ids = place()
     parity = ids[2] & 1
     quarters = LANES // STRIP
     quarter = lane_of(wave.shape[1:]) // STRIP
@@ -395,8 +400,9 @@
     return jnp.minimum(1.0, distance / 576.0)
 
 
-def step_kernel(step, total_y, ids, x_odd_in, x_even_in, z_odd_in, z_even_in, wave, side, older,
+def step_kernel(step, total_y, x_odd_in, x_even_in, z_odd_in, z_even_in, wave, side, older,
                 older_side, stiff, stiff_side, forward, own, *rest):
+    ids = place()
     last = step == STEPS - 1
     own_side = image_in = None
     if not last:
@@ -470,13 +476,6 @@
     depth, rows, cols = wave_now.shape
     span_x, span_y, span_z = (lax.axis_size(axis) for axis in ("gx", "gy", "gz"))
     tiles = span_x * span_y
-    ids = jnp.stack(
-        [
-            lax.axis_index("gz"),
-            lax.axis_index("gx"),
-            lax.axis_index("gy"),
-        ]
-    ).astype(jnp.int32)
     band_high, band_low = (jnp.asarray(part) for part in band())
     block = shaped(depth, rows, LANES)
 
@@ -490,9 +489,9 @@
     packets, even, odd = call(
         functools.partial(prepare_kernel, span_y, tiles),
         [shaped(tiles, LANES), strips, strips],
-        [ids, residuals, owners.reshape(1, -1), receivers.reshape(1, -1), wave_now, older_wave,
+        [residuals, owners.reshape(1, -1), receivers.reshape(1, -1), wave_now, older_wave,
          stiffness],
-        in_specs=[smem()] + [pl.BlockSpec()] * 6,
+        in_specs=[pl.BlockSpec()] * 6,
         grant=60,
     )
     packets = lax.all_to_all(packets, ("gx", "gy"), 0, 0, tiled=True)
@@ -501,7 +500,7 @@
     side, older_side, stiff_side, *faces = call(
         strip_unpack_kernel,
         [block] * 3 + faces_out(0),
-        [ids, even, odd, wave_now],
+        [even, odd, wave_now],
     )
     packets, faces = lax.optimization_barrier((packets, faces))
     cores = 2
@@ -513,7 +512,7 @@
     faces[0] = call(
         functools.partial(plane_kernel, face, rows),
         shaped(face + 2 * STEPS, rows, LANES),
-        [ids, faces[0], *packets],
+        [faces[0], *packets],
         scratch=[pltpu.VMEM((LANES, span_z // cores * tiles), F32)],
     )
 
@@ -530,12 +529,11 @@
             [block, block],
             [wave, side, band_high, band_low],
             scratch=[pltpu.VMEM((depth * rows, 2 * LANES), F32)],
-            in_specs=[vmem()] * 4,
         )
         if last:
             *own, last_older = own
         faces = exchange(faces)
-        ins = [ids, *faces[::-1], wave, side, older, older_side, stiffness, stiff_side, forward_wave,
+        ins = [*faces[::-1], wave, side, older, older_side, stiffness, stiff_side, forward_wave,
                *own]
         outs = [block, block]
         if step:
@@ -547,7 +545,7 @@
         room, in_specs, out_specs = scratch, None, None
         if last:
             ins.append(source_cell)
-            in_specs = [smem()] + [vmem()] * (len(ins) - 2) + [smem()]
+            in_specs = [vmem()] * (len(ins) - 1) + [smem()]
             out_specs = [pl.BlockSpec(memory_space=pl.ANY)] * 2
             held = pltpu.VMEM((depth, rows, LANES), F32)
             room = scratch + [held, held, pltpu.SemaphoreType.DMA((2, depth // CHUNK))]

time: 99.6 us -> 95.5 us (0.959)
  Pallas kernels: 13.8 us -> 10.4 us
    pallas_call x11, Pallas kernels: 13.8 us -> 10.4 us  [call(): pl.pallas_call(body, out_shape=outs, in_specs=in_specs or [vmem()] * len(...]
  transfers between devices with their start and end apart: 17 -> 17, of which waited for: 0 -> 0; matrix products, arithmetic and copies ran while one was open for 0% -> 0% of each run, Pallas kernels for 7% -> 6%
where the time goes in v9:
time: 95.5 us; the launch traced here: 94 us
  starting transfers between devices  62.9 us (66%)
  blocking collectives  19 us (20%)
  Pallas kernels  10.4 us (11%)
  between operations  1.6 us (2%)
    ppermute x13, starting transfers between devices, swap(): return lax.ppermute(block, axis, pairs)  39.5 us
    all_to_all x1, starting transfers between devices, on_device(): packets = lax.all_to_all(packets, ('gx', 'gy'), 0, 0, tiled=True)  19.5 us
    all_gather x5, blocking collectives, pair_gather(): lax.all_gather(block, axis, axis=0, tiled=False, axis_index_groups=groups)  19 us
    pallas_call x11, Pallas kernels, call(): pl.pallas_call(body, out_shape=outs, in_specs=in_specs or [vmem()] * len(...  10.4 us
    ppermute x3, starting transfers between devices, on_device(): lax.ppermute(packets, 'gz', [(chip + core, core) for core in range(cores)])  3.88 us
  transfers between devices with their start and end apart: 17, of which 0 were waited for; matrix products, arithmetic and copies ran while one was open for 0% of the time, Pallas kernels for 6%

profile of v9, /device:TPU:1, one launch (start us, length us, event | category | flops | bytes accessed | tf_op | source)
XLA Modules:
  0.0 94.0 jit_solution(2032045058582067090)
XLA Ops:
  0.6 2.3 %shard_map.121 = (f32[64,128]{1,0:T(8,128)}, f32[12,24,128]{2,1,0:T(8,128)}, f32[12,24,128]{2,1,0:T(8,128)}) custom-call(f32[4,128]{1,0:T(4,128)} %residuals.1, s32[1,128]{1,0:T(1,128)} %bitcast.21, s32[1,128]{1,0:T(1,128)} %bitcast.22, f32[16,24,128]{2,1,0:T(8,128)} %older.5, f32[16,24,128]{2,1,0:T(8,128)} %older.4, f32[16,24,128]{2,1,0:T(8,128)} %stiff.9), custom_call_target="tpu_custom_call" | custom-call | flops 1000000 | bytes 2000000 | tf_op jit(solution)/shard_map/pallas_call | solution.py:67
  3.6 19.5 %all-to-all-start = ((f32[64,1,128]{2,1,0:T(1,128)}), f32[64,1,128]{2,1,0:T(1,128)S(1)}, u32[]{:S(2)}, u32[]{:S(2)}) async-start(f32[64,1,128]{2,1,0:T(1,128)} %bitcast.20), calls=%async_computation | async-start | bytes 65536 | tf_op jit(solution)/shard_map/all_to_all | solution.py:497
  23.1 10.8 %all-gather = f32[24,24,128]{2,1,0:T(8,128)S(1)} all-gather(f32[12,24,128]{2,1,0:T(8,128)} %get-tuple-element.51), channel_id=2, replica_groups={{0,8},{16,24},{1,9},{17,25},{2,10},{18,26},{3,11},{19,27},{4,12},{20,28..., dimensions={0}, use_global_device_ids=true | all-gather | bytes 442368 | tf_op jit(solution)/shard_map/all_gather | solution.py:461
  34.4 1.3 %collective-permute-start.4 = (f32[64,128]{1,0:T(8,128)S(1)}, f32[64,128]{1,0:T(8,128)S(1)}, u32[]{:S(2)}, u32[]{:S(2)}) collective-permute-start(f32[64,128]{1,0:T(8,128)S(1)} %bitcast.16), channel_id=1, source_target_pairs={{2,0},{3,1},{10,8},{11,9},{18,16},{19,17},{26,24},{27,25},{34,32},... | collective-permute-start | bytes 98312 | tf_op jit(solution)/shard_map/ppermute | solution.py:508
  35.7 1.3 %collective-permute-start.5 = (f32[64,128]{1,0:T(8,128)S(1)}, f32[64,128]{1,0:T(8,128)S(1)}, u32[]{:S(2)}, u32[]{:S(2)}) collective-permute-start(f32[64,128]{1,0:T(8,128)S(1)} %bitcast.17), channel_id=1, source_target_pairs={{4,0},{5,1},{12,8},{13,9},{20,16},{21,17},{28,24},{29,25},{36,32},... | collective-permute-start | bytes 98312 | tf_op jit(solution)/shard_map/ppermute | solution.py:508
  37.0 1.3 %collective-permute-start.6 = (f32[64,128]{1,0:T(8,128)S(1)}, f32[64,128]{1,0:T(8,128)S(1)}, u32[]{:S(2)}, u32[]{:S(2)}) collective-permute-start(f32[64,128]{1,0:T(8,128)S(1)} %bitcast.18), channel_id=1, source_target_pairs={{6,0},{7,1},{14,8},{15,9},{22,16},{23,17},{30,24},{31,25},{38,32},... | collective-permute-start | bytes 98312 | tf_op jit(solution)/shard_map/ppermute | solution.py:508
  38.3 4.9 %collective-permute-start.3 = (f32[12,24,128]{2,1,0:T(8,128)S(1)}, f32[12,24,128]{2,1,0:T(8,128)S(1)}, u32[]{:S(2)}, u32[]{:S(2)}) collective-permute-start(f32[12,24,128]{2,1,0:T(8,128)S(1)} %get-tuple-element.59), channel_id=1, source_target_pairs={{1,2},{2,1},{3,4},{4,3},{5,6},{6,5},{9,10},{10,9},{11,12},{12,11},... | collective-permute-start | bytes 442376 | tf_op jit(solution)/shard_map/ppermute | solution.py:452
  43.8 0.9 shard_map.124
  44.8 4.7 %collective-permute-start.2 = (f32[24,8,128]{2,1,0:T(8,128)S(1)}, f32[24,8,128]{2,1,0:T(8,128)S(1)}, u32[]{:S(2)}, u32[]{:S(2)}) collective-permute-start(f32[24,8,128]{2,1,0:T(8,128)S(1)} %get-tuple-element.58), channel_id=1, source_target_pairs={{0,32},{32,0},{64,96},{96,64},{128,160},{160,128},{192,224},{224,1... | collective-permute-start | bytes 294920 | tf_op jit(solution)/shard_map/ppermute | solution.py:452
  49.5 1.0 %shard_map.123 = f32[20,24,128]{2,1,0:T(8,128)S(1)} custom-call(f32[12,24,128]{2,1,0:T(8,128)S(1)} %get-tuple-element.60.z_even, f32[64,128]{1,0:T(8,128)S(1)} %bitcast.19, f32[64,128]{1,0:T(8,128)S(1)} %collective-permute-done.4.refs_1_, f32[64,128]{1,0:T(8,128)S(1)} %collective-permute-done.5.refs_2_, f32[64,128]{1,0:T(8,128)S(1)} %collective-permute-done.6.refs_3_), custom_call_target="tpu_custom_call" | custom-call | flops 1000000 | bytes 2000000 | tf_op jit(solution)/shard_map/pallas_call | solution.py:67
  50.5 2.3 %all-gather.1 = f32[40,24,128]{2,1,0:T(8,128)S(1)} all-gather(f32[20,24,128]{2,1,0:T(8,128)S(1)} %shard_map.123), channel_id=3, replica_groups={{0,1},{2,3},{4,5},{6,7},{8,9},{10,11},{12,13},{14,15},{16,17},{18,19},{..., dimensions={0}, use_global_device_ids=true | all-gather | bytes 737280 | tf_op jit(solution)/shard_map/all_gather | solution.py:461
  53.5 2.7 %collective-permute-start.9 = (f32[10,24,128]{2,1,0:T(8,128)S(1)}, f32[10,24,128]{2,1,0:T(8,128)S(1)}, u32[]{:S(2)}, u32[]{:S(2)}) collective-permute-start(f32[10,24,128]{2,1,0:T(8,128)S(1)} %get-tuple-element.69), channel_id=1, source_target_pairs={{1,2},{2,1},{3,4},{4,3},{5,6},{6,5},{9,10},{10,9},{11,12},{12,11},... | collective-permute-start | bytes 368648 | tf_op jit(solution)/shard_map/ppermute | solution.py:452
  56.9 5.3 %collective-permute-start.8 = (f32[20,8,128]{2,1,0:T(8,128)S(1)}, f32[20,8,128]{2,1,0:T(8,128)S(1)}, u32[]{:S(2)}, u32[]{:S(2)}) collective-permute-start(f32[20,8,128]{2,1,0:T(8,128)S(1)} %get-tuple-element.68), channel_id=1, source_target_pairs={{0,32},{32,0},{64,96},{96,64},{128,160},{160,128},{192,224},{224,1... | collective-permute-start | bytes 245768 | tf_op jit(solution)/shard_map/ppermute | solution.py:452
  62.2 0.9 shard_map.126
  63.2 2.0 %all-gather.2 = f32[20,24,128]{2,1,0:T(8,128)S(1)} all-gather(f32[10,24,128]{2,1,0:T(8,128)S(1)} %get-tuple-element.70), channel_id=4, replica_groups={{0,1},{2,3},{4,5},{6,7},{8,9},{10,11},{12,13},{14,15},{16,17},{18,19},{..., dimensions={0}, use_global_device_ids=true | all-gather | bytes 368640 | tf_op jit(solution)/shard_map/all_gather | solution.py:461
  65.8 3.9 %collective-permute-start.12 = (f32[9,24,128]{2,1,0:T(8,128)S(1)}, f32[9,24,128]{2,1,0:T(8,128)S(1)}, u32[]{:S(2)}, u32[]{:S(2)}) collective-permute-start(f32[9,24,128]{2,1,0:T(8,128)S(1)} %get-tuple-element.79), channel_id=1, source_target_pairs={{1,2},{2,1},{3,4},{4,3},{5,6},{6,5},{9,10},{10,9},{11,12},{12,11},... | collective-permute-start | bytes 331784 | tf_op jit(solution)/shard_map/ppermute | solution.py:452
  70.3 5.1 %collective-permute-start.11 = (f32[18,8,128]{2,1,0:T(8,128)S(1)}, f32[18,8,128]{2,1,0:T(8,128)S(1)}, u32[]{:S(2)}, u32[]{:S(2)}) collective-permute-start(f32[18,8,128]{2,1,0:T(8,128)S(1)} %get-tuple-element.78), channel_id=1, source_target_pairs={{0,32},{32,0},{64,96},{96,64},{128,160},{160,128},{192,224},{224,1... | collective-permute-start | bytes 221192 | tf_op jit(solution)/shard_map/ppermute | solution.py:452
  75.5 0.9 shard_map.128
  76.4 2.0 %all-gather.3 = f32[18,24,128]{2,1,0:T(8,128)S(1)} all-gather(f32[9,24,128]{2,1,0:T(8,128)S(1)} %get-tuple-element.80), channel_id=5, replica_groups={{0,1},{2,3},{4,5},{6,7},{8,9},{10,11},{12,13},{14,15},{16,17},{18,19},{..., dimensions={0}, use_global_device_ids=true | all-gather | bytes 331776 | tf_op jit(solution)/shard_map/all_gather | solution.py:461
  79.0 3.5 %collective-permute-start.15 = (f32[8,24,128]{2,1,0:T(8,128)S(1)}, f32[8,24,128]{2,1,0:T(8,128)S(1)}, u32[]{:S(2)}, u32[]{:S(2)}) collective-permute-start(f32[8,24,128]{2,1,0:T(8,128)S(1)} %get-tuple-element.88), channel_id=1, source_target_pairs={{1,2},{2,1},{3,4},{4,3},{5,6},{6,5},{9,10},{10,9},{11,12},{12,11},... | collective-permute-start | bytes 294920 | tf_op jit(solution)/shard_map/ppermute | solution.py:452
  83.2 6.1 %collective-permute-start.14 = (f32[16,8,128]{2,1,0:T(8,128)S(1)}, f32[16,8,128]{2,1,0:T(8,128)S(1)}, u32[]{:S(2)}, u32[]{:S(2)}) collective-permute-start(f32[16,8,128]{2,1,0:T(8,128)S(1)} %get-tuple-element.87), channel_id=1, source_target_pairs={{0,32},{32,0},{64,96},{96,64},{128,160},{160,128},{192,224},{224,1... | collective-permute-start | bytes 196616 | tf_op jit(solution)/shard_map/ppermute | solution.py:452
  89.9 1.1 %shard_map.130 = (f32[16,24,128]{2,1,0:T(8,128)S(1)}, f32[16,24,128]{2,1,0:T(8,128)}) custom-call(f32[16,24,128]{2,1,0:T(8,128)S(1)} %get-tuple-element.90.wave, f32[16,24,128]{2,1,0:T(8,128)S(1)} %get-tuple-element.91.side, bf16[256,256]{1,0:T(8,128)(2,1)S(1)} %copy-done.3, bf16[256,256]{1,0:T(8,128)(2,1)S(1)} %copy-done.4), custom_call_target="tpu_custom_call" | custom-call | flops 1000000 | bytes 2000000 | tf_op jit(solution)/shard_map/pallas_call | solution.py:67
  91.1 1.9 %all-gather.4 = f32[16,24,128]{2,1,0:T(8,128)S(1)} all-gather(f32[8,24,128]{2,1,0:T(8,128)S(1)} %get-tuple-element.89), channel_id=6, replica_groups={{0,1},{2,3},{4,5},{6,7},{8,9},{10,11},{12,13},{14,15},{16,17},{18,19},{..., dimensions={0}, use_global_device_ids=true | all-gather | bytes 294912 | tf_op jit(solution)/shard_map/all_gather | solution.py:461
  93.0 1.0 %shard_map.131 = (f32[16,24,128]{2,1,0:T(8,128)}, f32[16,24,128]{2,1,0:T(8,128)}) custom-call(f32[16,8,128]{2,1,0:T(8,128)S(1)} %collective-permute-done.13.x_odd_in, f32[16,8,128]{2,1,0:T(8,128)S(1)} %collective-permute-done.14.x_even_in, f32[8,24,128]{2,1,0:T(8,128)S(1)} %collective-permute-done.15.z_odd_in, f32[2,8,24,128]{3,2,1,0:T(8,128)S(1)} %bitcast.15, ...), custom_call_target="tpu_custom_call" | custom-call | flops 1000000 | bytes 2000000 | tf_op jit(solution)/shard_map/pallas_call | solution.py:67
  (38 shorter events, 5.6 us)
Async XLA Ops:
  2.9 31.1 %collective-permute-start = (f32[12,24,128]{2,1,0:T(8,128)}, f32[12,24,128]{2,1,0:T(8,128)S(1)}, u32[]{:S(2)}, u32[]{:S(2)}) collective-permute-start(f32[12,24,128]{2,1,0:T(8,128)} %get-tuple-element.52), channel_id=1, source_target_pairs={{8,16},{16,8},{9,17},{17,9},{10,18},{18,10},{11,19},{19,11},{12,20... | collective-permute-start | bytes 442376 | tf_op jit(solution)/shard_map/ppermute | solution.py:452
  3.6 30.8 %all-to-all-start = ((f32[64,1,128]{2,1,0:T(1,128)}), f32[64,1,128]{2,1,0:T(1,128)S(1)}, u32[]{:S(2)}, u32[]{:S(2)}) async-start(f32[64,1,128]{2,1,0:T(1,128)} %bitcast.20), calls=%async_computation | async-start | bytes 65536 | tf_op jit(solution)/shard_map/all_to_all | solution.py:497
  23.1 10.8 %copy-start.1 = (f32[16,24,128]{2,1,0:T(8,128)S(1)}, f32[16,24,128]{2,1,0:T(8,128)}, u32[]{:S(2)}) copy-start(f32[16,24,128]{2,1,0:T(8,128)} %older.5) | copy-start | bytes 589828
  34.0 9.8 %copy-start.3 = (bf16[256,256]{1,0:T(8,128)(2,1)S(1)}, bf16[256,256]{1,0:T(8,128)(2,1)}, u32[]{:S(2)}) copy-start(bf16[256,256]{1,0:T(8,128)(2,1)} %constant.4.clone.band_high) | copy-start | bytes 393220
  34.0 9.8 %copy-start.4 = (bf16[256,256]{1,0:T(8,128)(2,1)S(1)}, bf16[256,256]{1,0:T(8,128)(2,1)}, u32[]{:S(2)}) copy-start(bf16[256,256]{1,0:T(8,128)(2,1)} %constant.5.clone.band_low) | copy-start | bytes 393220
  34.4 10.4 %collective-permute-start.4 = (f32[64,128]{1,0:T(8,128)S(1)}, f32[64,128]{1,0:T(8,128)S(1)}, u32[]{:S(2)}, u32[]{:S(2)}) collective-permute-start(f32[64,128]{1,0:T(8,128)S(1)} %bitcast.16), channel_id=1, source_target_pairs={{2,0},{3,1},{10,8},{11,9},{18,16},{19,17},{26,24},{27,25},{34,32},... | collective-permute-start | bytes 98312 | tf_op jit(solution)/shard_map/ppermute | solution.py:508
  35.7 13.8 %collective-permute-start.5 = (f32[64,128]{1,0:T(8,128)S(1)}, f32[64,128]{1,0:T(8,128)S(1)}, u32[]{:S(2)}, u32[]{:S(2)}) collective-permute-start(f32[64,128]{1,0:T(8,128)S(1)} %bitcast.17), channel_id=1, source_target_pairs={{4,0},{5,1},{12,8},{13,9},{20,16},{21,17},{28,24},{29,25},{36,32},... | collective-permute-start | bytes 98312 | tf_op jit(solution)/shard_map/ppermute | solution.py:508
  37.0 12.5 %collective-permute-start.6 = (f32[64,128]{1,0:T(8,128)S(1)}, f32[64,128]{1,0:T(8,128)S(1)}, u32[]{:S(2)}, u32[]{:S(2)}) collective-permute-start(f32[64,128]{1,0:T(8,128)S(1)} %bitcast.18), channel_id=1, source_target_pairs={{6,0},{7,1},{14,8},{15,9},{22,16},{23,17},{30,24},{31,25},{38,32},... | collective-permute-start | bytes 98312 | tf_op jit(solution)/shard_map/ppermute | solution.py:508
  38.3 14.6 %collective-permute-start.3 = (f32[12,24,128]{2,1,0:T(8,128)S(1)}, f32[12,24,128]{2,1,0:T(8,128)S(1)}, u32[]{:S(2)}, u32[]{:S(2)}) collective-permute-start(f32[12,24,128]{2,1,0:T(8,128)S(1)} %get-tuple-element.59), channel_id=1, source_target_pairs={{1,2},{2,1},{3,4},{4,3},{5,6},{6,5},{9,10},{10,9},{11,12},{12,11},... | collective-permute-start | bytes 442376 | tf_op jit(solution)/shard_map/ppermute | solution.py:452
  43.1 9.7 %collective-permute-start.1 = (f32[24,8,128]{2,1,0:T(8,128)S(1)}, f32[24,8,128]{2,1,0:T(8,128)S(1)}, u32[]{:S(2)}, u32[]{:S(2)}) collective-permute-start(f32[24,8,128]{2,1,0:T(8,128)S(1)} %get-tuple-element.57), channel_id=1, source_target_pairs={{32,64},{64,32},{96,128},{128,96},{160,192},{192,160},{224,256},{2... | collective-permute-start | bytes 294920 | tf_op jit(solution)/shard_map/ppermute | solution.py:452
  44.8 8.1 %collective-permute-start.2 = (f32[24,8,128]{2,1,0:T(8,128)S(1)}, f32[24,8,128]{2,1,0:T(8,128)S(1)}, u32[]{:S(2)}, u32[]{:S(2)}) collective-permute-start(f32[24,8,128]{2,1,0:T(8,128)S(1)} %get-tuple-element.58), channel_id=1, source_target_pairs={{0,32},{32,0},{64,96},{96,64},{128,160},{160,128},{192,224},{224,1... | collective-permute-start | bytes 294920 | tf_op jit(solution)/shard_map/ppermute | solution.py:452
  49.5 3.4 %copy-start.5 = (f32[16,24,128]{2,1,0:T(8,128)S(1)}, f32[16,24,128]{2,1,0:T(8,128)}, u32[]{:S(2)}) copy-start(f32[16,24,128]{2,1,0:T(8,128)} %older.4) | copy-start | bytes 589828
  50.5 2.3 %copy-start = (bf16[4,16,24,128]{3,2,1,0:T(8,128)(2,1)S(1)}, bf16[4,16,24,128]{3,2,1,0:T(8,128)(2,1)}, u32[]{:S(2)}) copy-start(bf16[4,16,24,128]{3,2,1,0:T(8,128)(2,1)} %forward.7) | copy-start | bytes 1179652
  50.5 2.3 %copy-start.2 = (f32[16,24,128]{2,1,0:T(8,128)S(1)}, f32[16,24,128]{2,1,0:T(8,128)}, u32[]{:S(2)}) copy-start(f32[16,24,128]{2,1,0:T(8,128)} %stiff.9) | copy-start | bytes 589828
  53.5 11.7 %collective-permute-start.9 = (f32[10,24,128]{2,1,0:T(8,128)S(1)}, f32[10,24,128]{2,1,0:T(8,128)S(1)}, u32[]{:S(2)}, u32[]{:S(2)}) collective-permute-start(f32[10,24,128]{2,1,0:T(8,128)S(1)} %get-tuple-element.69), channel_id=1, source_target_pairs={{1,2},{2,1},{3,4},{4,3},{5,6},{6,5},{9,10},{10,9},{11,12},{12,11},... | collective-permute-start | bytes 368648 | tf_op jit(solution)/shard_map/ppermute | solution.py:452
  56.2 8.9 %collective-permute-start.7 = (f32[20,8,128]{2,1,0:T(8,128)S(1)}, f32[20,8,128]{2,1,0:T(8,128)S(1)}, u32[]{:S(2)}, u32[]{:S(2)}) collective-permute-start(f32[20,8,128]{2,1,0:T(8,128)S(1)} %get-tuple-element.67), channel_id=1, source_target_pairs={{32,64},{64,32},{96,128},{128,96},{160,192},{192,160},{224,256},{2... | collective-permute-start | bytes 245768 | tf_op jit(solution)/shard_map/ppermute | solution.py:452
  56.9 8.2 %collective-permute-start.8 = (f32[20,8,128]{2,1,0:T(8,128)S(1)}, f32[20,8,128]{2,1,0:T(8,128)S(1)}, u32[]{:S(2)}, u32[]{:S(2)}) collective-permute-start(f32[20,8,128]{2,1,0:T(8,128)S(1)} %get-tuple-element.68), channel_id=1, source_target_pairs={{0,32},{32,0},{64,96},{96,64},{128,160},{160,128},{192,224},{224,1... | collective-permute-start | bytes 245768 | tf_op jit(solution)/shard_map/ppermute | solution.py:452
  65.8 12.6 %collective-permute-start.12 = (f32[9,24,128]{2,1,0:T(8,128)S(1)}, f32[9,24,128]{2,1,0:T(8,128)S(1)}, u32[]{:S(2)}, u32[]{:S(2)}) collective-permute-start(f32[9,24,128]{2,1,0:T(8,128)S(1)} %get-tuple-element.79), channel_id=1, source_target_pairs={{1,2},{2,1},{3,4},{4,3},{5,6},{6,5},{9,10},{10,9},{11,12},{12,11},... | collective-permute-start | bytes 331784 | tf_op jit(solution)/shard_map/ppermute | solution.py:452
  69.7 8.7 %collective-permute-start.10 = (f32[18,8,128]{2,1,0:T(8,128)S(1)}, f32[18,8,128]{2,1,0:T(8,128)S(1)}, u32[]{:S(2)}, u32[]{:S(2)}) collective-permute-start(f32[18,8,128]{2,1,0:T(8,128)S(1)} %get-tuple-element.77), channel_id=1, source_target_pairs={{32,64},{64,32},{96,128},{128,96},{160,192},{192,160},{224,256},{2... | collective-permute-start | bytes 221192 | tf_op jit(solution)/shard_map/ppermute | solution.py:452
  70.3 8.1 %collective-permute-start.11 = (f32[18,8,128]{2,1,0:T(8,128)S(1)}, f32[18,8,128]{2,1,0:T(8,128)S(1)}, u32[]{:S(2)}, u32[]{:S(2)}) collective-permute-start(f32[18,8,128]{2,1,0:T(8,128)S(1)} %get-tuple-element.78), channel_id=1, source_target_pairs={{0,32},{32,0},{64,96},{96,64},{128,160},{160,128},{192,224},{224,1... | collective-permute-start | bytes 221192 | tf_op jit(solution)/shard_map/ppermute | solution.py:452
  79.0 14.0 %collective-permute-start.15 = (f32[8,24,128]{2,1,0:T(8,128)S(1)}, f32[8,24,128]{2,1,0:T(8,128)S(1)}, u32[]{:S(2)}, u32[]{:S(2)}) collective-permute-start(f32[8,24,128]{2,1,0:T(8,128)S(1)} %get-tuple-element.88), channel_id=1, source_target_pairs={{1,2},{2,1},{3,4},{4,3},{5,6},{6,5},{9,10},{10,9},{11,12},{12,11},... | collective-permute-start | bytes 294920 | tf_op jit(solution)/shard_map/ppermute | solution.py:452
  82.6 10.5 %collective-permute-start.13 = (f32[16,8,128]{2,1,0:T(8,128)S(1)}, f32[16,8,128]{2,1,0:T(8,128)S(1)}, u32[]{:S(2)}, u32[]{:S(2)}) collective-permute-start(f32[16,8,128]{2,1,0:T(8,128)S(1)} %get-tuple-element.86), channel_id=1, source_target_pairs={{32,64},{64,32},{96,128},{128,96},{160,192},{192,160},{224,256},{2... | collective-permute-start | bytes 196616 | tf_op jit(solution)/shard_map/ppermute | solution.py:452
  83.2 9.8 %collective-permute-start.14 = (f32[16,8,128]{2,1,0:T(8,128)S(1)}, f32[16,8,128]{2,1,0:T(8,128)S(1)}, u32[]{:S(2)}, u32[]{:S(2)}) collective-permute-start(f32[16,8,128]{2,1,0:T(8,128)S(1)} %get-tuple-element.87), channel_id=1, source_target_pairs={{0,32},{32,0},{64,96},{96,64},{128,160},{160,128},{192,224},{224,1... | collective-permute-start | bytes 196616 | tf_op jit(solution)/shard_map/ppermute | solution.py:452

commit v10 on v9

--- a/solution.py
+++ b/solution.py
@@ -57,10 +57,6 @@
 
 def vmem():
     return pl.BlockSpec(memory_space=pltpu.VMEM)
-
-
-def smem():
-    return pl.BlockSpec(memory_space=pltpu.SMEM)
 
 
 def call(body, outs, ins, scratch=(), in_specs=None, grant=32, out_specs=None):
@@ -172,26 +168,39 @@
             out[pl.ds(face + STEPS * part, STEPS)] = total.reshape(STEPS, rows, LANES)
 
 
+def strip_places(depth):
+    short = STRIP - RADIUS
+    planes = []
+    for pair in range(depth // 2):
+        pieces = [(0, pair, STRIP, 0)]
+        for number in range(4):
+            pieces.append((1 + number // 2, 2 * pair + number % 2, short, STRIP + short * number))
+        planes.append(pieces)
+    quarters = LANES // STRIP
+    for first in range(depth // 2, depth, quarters):
+        planes.append([(0, first + turn, STRIP, STRIP * turn) for turn in range(quarters)])
+    return planes
+
+
+def turn_lanes(value, by):
+    by = by % LANES
+    return pltpu.roll(value, by, 1) if by else value
+
+
 def pack_strips(ids, wave, older, stiff, even, odd):
     parity = ids[2] & 1
-    quarter = lane_of(wave.shape[1:]) // STRIP
-    low, high = quarter == 0, quarter == 3
-    quarters = LANES // STRIP
-    for number, field in enumerate((wave, older, stiff)):
-        for chunk in range(field.shape[0] // quarters):
-            lows = highs = None
-            for turn in range(quarters):
-                value = field[quarters * chunk + turn]
-                one = jnp.where(low, value, 0.0)
-                two = jnp.where(high, value, 0.0)
-                if turn:
-                    one = pltpu.roll(one, STRIP * turn, 1)
-                    two = pltpu.roll(two, STRIP * turn, 1)
-                lows = one if lows is None else lows + one
-                highs = two if highs is None else highs + two
-            place = number * (field.shape[0] // quarters) + chunk
-            even[place] = jnp.where(parity == 0, highs, lows)
-            odd[place] = jnp.where(parity == 0, lows, highs)
+    lane = lane_of(wave.shape[1:])
+    fields = (wave, older, stiff)
+    for plane, pieces in enumerate(strip_places(wave.shape[0])):
+        lows = highs = None
+        for field, z, cells, start in pieces:
+            value = fields[field][z]
+            one = turn_lanes(jnp.where(lane < cells, value, 0.0), start)
+            two = turn_lanes(jnp.where(lane >= LANES - cells, value, 0.0), start + cells)
+            lows = one if lows is None else lows + one
+            highs = two if highs is None else highs + two
+        even[plane] = jnp.where(parity == 0, highs, lows)
+        odd[plane] = jnp.where(parity == 0, lows, highs)
 
 
 def strip_width(step):
@@ -260,22 +269,18 @@
 ):
     ids = place()
     parity = ids[2] & 1
-    quarters = LANES // STRIP
-    quarter = lane_of(wave.shape[1:]) // STRIP
-    from_even = quarter == 3 * parity
-    from_odd = quarter == 3 * (1 - parity)
-    chunks = wave.shape[0] // quarters
-    for number, side in enumerate((wave_side, older_side, stiff_side)):
-        for chunk in range(chunks):
-            one = even[1 - parity, number * chunks + chunk]
-            two = odd[number * chunks + chunk]
-            for turn in range(quarters):
-                back = (LANES - STRIP * turn) % LANES
-                first = pltpu.roll(one, back, 1) if back else one
-                second = pltpu.roll(two, back, 1) if back else two
-                side[quarters * chunk + turn] = jnp.where(
-                    from_even, first, jnp.where(from_odd, second, 0.0)
-                )
+    lane = lane_of(wave.shape[1:])
+    sides = (wave_side, older_side, stiff_side)
+    for plane, pieces in enumerate(strip_places(wave.shape[0])):
+        one, two = even[1 - parity, plane], odd[plane]
+        after = jnp.where(parity == 0, one, two)
+        before = jnp.where(parity == 0, two, one)
+        for field, z, cells, start in pieces:
+            sides[field][z] = jnp.where(
+                lane < cells,
+                turn_lanes(after, -start),
+                jnp.where(lane >= LANES - cells, turn_lanes(before, -start - cells), 0.0),
+            )
     write_faces(STRIP, ids, wave, wave_side, z_even, z_odd, x_even, x_odd)
 
 
@@ -419,7 +424,8 @@
     if last:
         (source, image_out, wave_out, z_halo, x_halo, image, fresh, sems) = rest
         fresh_side = None
-        shot = (lax.div(source[0], total_y), lax.rem(source[0], total_y))
+        cell = source[0, 0]
+        shot = (lax.div(cell, total_y), lax.rem(cell, total_y))
 
         def done(z):
             if (z + 1) % CHUNK:
@@ -485,7 +491,7 @@
         x_face = shaped(depth + folded(depth, width), RADIUS, LANES)
         return [z_face, z_face, x_face, x_face]
 
-    strips = shaped(3 * depth * STRIP // LANES, rows, LANES)
+    strips = shaped(len(strip_places(depth)), rows, LANES)
     packets, even, odd = call(
         functools.partial(prepare_kernel, span_y, tiles),
         [shaped(tiles, LANES), strips, strips],
@@ -544,8 +550,7 @@
             outs += [block] + faces_out(step + 1)
         room, in_specs, out_specs = scratch, None, None
         if last:
-            ins.append(source_cell)
-            in_specs = [vmem()] * (len(ins) - 1) + [smem()]
+            ins.append(source_cell.reshape(1, 1))
             out_specs = [pl.BlockSpec(memory_space=pl.ANY)] * 2
             held = pltpu.VMEM((depth, rows, LANES), F32)
             room = scratch + [held, held, pltpu.SemaphoreType.DMA((2, depth // CHUNK))]

time: 95.5 us -> 94.5 us (0.990)
  blocking collectives: 19 us -> 17.9 us
    all_gather x5, blocking collectives: 19 us -> 17.9 us  [pair_gather(): lax.all_gather(block, axis, axis=0, tiled=False, axis_index_groups=groups)]
  transfers between devices with their start and end apart: 17 -> 17, of which waited for: 0 -> 1; matrix products, arithmetic and copies ran while one was open for 0% -> 0% of each run, Pallas kernels for 6% -> 6%
where the time goes in v10:
time: 94.5 us; the launch traced here: 93 us
  starting transfers between devices  62.4 us (66%)
  blocking collectives  17.9 us (19%)
  Pallas kernels  10.5 us (11%)
  between operations  1.59 us (2%)
    ppermute x13, starting transfers between devices, swap(): return lax.ppermute(block, axis, pairs)  39 us
    all_to_all x1, starting transfers between devices, on_device(): packets = lax.all_to_all(packets, ('gx', 'gy'), 0, 0, tiled=True)  19.6 us
    all_gather x5, blocking collectives, pair_gather(): lax.all_gather(block, axis, axis=0, tiled=False, axis_index_groups=groups)  17.9 us
    pallas_call x11, Pallas kernels, call(): pl.pallas_call(body, out_shape=outs, in_specs=in_specs or [vmem()] * len(...  10.5 us
    ppermute x3, starting transfers between devices, on_device(): lax.ppermute(packets, 'gz', [(chip + core, core) for core in range(cores)])  3.86 us
  transfers between devices with their start and end apart: 17, of which 1 were waited for; matrix products, arithmetic and copies ran while one was open for 0% of the time, Pallas kernels for 6%

profile of v10, /device:TPU:1, one launch (start us, length us, event | category | flops | bytes accessed | tf_op | source)
XLA Modules:
  0.0 93.0 jit_solution(18399257118639770929)
XLA Ops:
  0.6 2.3 %shard_map.121 = (f32[64,128]{1,0:T(8,128)}, f32[10,24,128]{2,1,0:T(8,128)}, f32[10,24,128]{2,1,0:T(8,128)}) custom-call(f32[4,128]{1,0:T(4,128)} %residuals.1, s32[1,128]{1,0:T(1,128)} %bitcast.23, s32[1,128]{1,0:T(1,128)} %bitcast.24, f32[16,24,128]{2,1,0:T(8,128)} %older.5, f32[16,24,128]{2,1,0:T(8,128)} %older.4, f32[16,24,128]{2,1,0:T(8,128)} %stiff.9), custom_call_target="tpu_custom_call" | custom-call | flops 1000000 | bytes 2000000 | tf_op jit(solution)/shard_map/pallas_call | solution.py:63
  3.6 19.6 %all-to-all-start = ((f32[64,1,128]{2,1,0:T(1,128)}), f32[64,1,128]{2,1,0:T(1,128)S(1)}, u32[]{:S(2)}, u32[]{:S(2)}) async-start(f32[64,1,128]{2,1,0:T(1,128)} %bitcast.22), calls=%async_computation | async-start | bytes 65536 | tf_op jit(solution)/shard_map/all_to_all | solution.py:503
  23.1 9.7 %all-gather = f32[20,24,128]{2,1,0:T(8,128)S(1)} all-gather(f32[10,24,128]{2,1,0:T(8,128)} %get-tuple-element.51), channel_id=2, replica_groups={{0,8},{16,24},{1,9},{17,25},{2,10},{18,26},{3,11},{19,27},{4,12},{20,28..., dimensions={0}, use_global_device_ids=true | all-gather | bytes 368640 | tf_op jit(solution)/shard_map/all_gather | solution.py:467
  33.9 1.3 %collective-permute-start.4 = (f32[64,128]{1,0:T(8,128)S(1)}, f32[64,128]{1,0:T(8,128)S(1)}, u32[]{:S(2)}, u32[]{:S(2)}) collective-permute-start(f32[64,128]{1,0:T(8,128)S(1)} %bitcast.18), channel_id=1, source_target_pairs={{2,0},{3,1},{10,8},{11,9},{18,16},{19,17},{26,24},{27,25},{34,32},... | collective-permute-start | bytes 98312 | tf_op jit(solution)/shard_map/ppermute | solution.py:514
  35.2 1.3 %collective-permute-start.5 = (f32[64,128]{1,0:T(8,128)S(1)}, f32[64,128]{1,0:T(8,128)S(1)}, u32[]{:S(2)}, u32[]{:S(2)}) collective-permute-start(f32[64,128]{1,0:T(8,128)S(1)} %bitcast.19), channel_id=1, source_target_pairs={{4,0},{5,1},{12,8},{13,9},{20,16},{21,17},{28,24},{29,25},{36,32},... | collective-permute-start | bytes 98312 | tf_op jit(solution)/shard_map/ppermute | solution.py:514
  36.5 1.3 %collective-permute-start.6 = (f32[64,128]{1,0:T(8,128)S(1)}, f32[64,128]{1,0:T(8,128)S(1)}, u32[]{:S(2)}, u32[]{:S(2)}) collective-permute-start(f32[64,128]{1,0:T(8,128)S(1)} %bitcast.20), channel_id=1, source_target_pairs={{6,0},{7,1},{14,8},{15,9},{22,16},{23,17},{30,24},{31,25},{38,32},... | collective-permute-start | bytes 98312 | tf_op jit(solution)/shard_map/ppermute | solution.py:514
  37.8 5.3 %collective-permute-start.3 = (f32[12,24,128]{2,1,0:T(8,128)S(1)}, f32[12,24,128]{2,1,0:T(8,128)S(1)}, u32[]{:S(2)}, u32[]{:S(2)}) collective-permute-start(f32[12,24,128]{2,1,0:T(8,128)S(1)} %get-tuple-element.59), channel_id=1, source_target_pairs={{1,2},{2,1},{3,4},{4,3},{5,6},{6,5},{9,10},{10,9},{11,12},{12,11},... | collective-permute-start | bytes 442376 | tf_op jit(solution)/shard_map/ppermute | solution.py:458
  43.8 0.9 shard_map.124
  44.7 4.7 %collective-permute-start.2 = (f32[24,8,128]{2,1,0:T(8,128)S(1)}, f32[24,8,128]{2,1,0:T(8,128)S(1)}, u32[]{:S(2)}, u32[]{:S(2)}) collective-permute-start(f32[24,8,128]{2,1,0:T(8,128)S(1)} %get-tuple-element.58), channel_id=1, source_target_pairs={{0,32},{32,0},{64,96},{96,64},{128,160},{160,128},{192,224},{224,1... | collective-permute-start | bytes 294920 | tf_op jit(solution)/shard_map/ppermute | solution.py:458
  49.4 1.0 %shard_map.123 = f32[20,24,128]{2,1,0:T(8,128)S(1)} custom-call(f32[12,24,128]{2,1,0:T(8,128)S(1)} %get-tuple-element.60.z_even, f32[64,128]{1,0:T(8,128)S(1)} %bitcast.21, f32[64,128]{1,0:T(8,128)S(1)} %collective-permute-done.4.refs_1_, f32[64,128]{1,0:T(8,128)S(1)} %collective-permute-done.5.refs_2_, f32[64,128]{1,0:T(8,128)S(1)} %collective-permute-done.6.refs_3_), custom_call_target="tpu_custom_call" | custom-call | flops 1000000 | bytes 2000000 | tf_op jit(solution)/shard_map/pallas_call | solution.py:63
  50.5 2.3 %all-gather.1 = f32[40,24,128]{2,1,0:T(8,128)S(1)} all-gather(f32[20,24,128]{2,1,0:T(8,128)S(1)} %shard_map.123), channel_id=3, replica_groups={{0,1},{2,3},{4,5},{6,7},{8,9},{10,11},{12,13},{14,15},{16,17},{18,19},{..., dimensions={0}, use_global_device_ids=true | all-gather | bytes 737280 | tf_op jit(solution)/shard_map/all_gather | solution.py:467
  53.5 2.7 %collective-permute-start.9 = (f32[10,24,128]{2,1,0:T(8,128)S(1)}, f32[10,24,128]{2,1,0:T(8,128)S(1)}, u32[]{:S(2)}, u32[]{:S(2)}) collective-permute-start(f32[10,24,128]{2,1,0:T(8,128)S(1)} %get-tuple-element.69), channel_id=1, source_target_pairs={{1,2},{2,1},{3,4},{4,3},{5,6},{6,5},{9,10},{10,9},{11,12},{12,11},... | collective-permute-start | bytes 368648 | tf_op jit(solution)/shard_map/ppermute | solution.py:458
  56.9 5.1 %collective-permute-start.8 = (f32[20,8,128]{2,1,0:T(8,128)S(1)}, f32[20,8,128]{2,1,0:T(8,128)S(1)}, u32[]{:S(2)}, u32[]{:S(2)}) collective-permute-start(f32[20,8,128]{2,1,0:T(8,128)S(1)} %get-tuple-element.68), channel_id=1, source_target_pairs={{0,32},{32,0},{64,96},{96,64},{128,160},{160,128},{192,224},{224,1... | collective-permute-start | bytes 245768 | tf_op jit(solution)/shard_map/ppermute | solution.py:458
  62.0 0.9 shard_map.126
  62.9 2.0 %all-gather.2 = f32[20,24,128]{2,1,0:T(8,128)S(1)} all-gather(f32[10,24,128]{2,1,0:T(8,128)S(1)} %get-tuple-element.70), channel_id=4, replica_groups={{0,1},{2,3},{4,5},{6,7},{8,9},{10,11},{12,13},{14,15},{16,17},{18,19},{..., dimensions={0}, use_global_device_ids=true | all-gather | bytes 368640 | tf_op jit(solution)/shard_map/all_gather | solution.py:467
  65.6 4.1 %collective-permute-start.12 = (f32[9,24,128]{2,1,0:T(8,128)S(1)}, f32[9,24,128]{2,1,0:T(8,128)S(1)}, u32[]{:S(2)}, u32[]{:S(2)}) collective-permute-start(f32[9,24,128]{2,1,0:T(8,128)S(1)} %get-tuple-element.79), channel_id=1, source_target_pairs={{1,2},{2,1},{3,4},{4,3},{5,6},{6,5},{9,10},{10,9},{11,12},{12,11},... | collective-permute-start | bytes 331784 | tf_op jit(solution)/shard_map/ppermute | solution.py:458
  70.3 4.6 %collective-permute-start.11 = (f32[18,8,128]{2,1,0:T(8,128)S(1)}, f32[18,8,128]{2,1,0:T(8,128)S(1)}, u32[]{:S(2)}, u32[]{:S(2)}) collective-permute-start(f32[18,8,128]{2,1,0:T(8,128)S(1)} %get-tuple-element.78), channel_id=1, source_target_pairs={{0,32},{32,0},{64,96},{96,64},{128,160},{160,128},{192,224},{224,1... | collective-permute-start | bytes 221192 | tf_op jit(solution)/shard_map/ppermute | solution.py:458
  75.0 0.9 %shard_map.128 = (f32[16,24,128]{2,1,0:T(8,128)S(1)}, f32[16,24,128]{2,1,0:T(8,128)S(1)}) custom-call(f32[16,24,128]{2,1,0:T(8,128)S(1)} %get-tuple-element.81.wave.older, f32[16,24,128]{2,1,0:T(8,128)S(1)} %get-tuple-element.82.side.older_side, bf16[256,256]{1,0:T(8,128)(2,1)S(1)} %copy-done.3, bf16[256,256]{1,0:T(8,128)(2,1)S(1)} %copy-done.4), custom_call_target="tpu_custom_call" | custom-call | flops 1000000 | bytes 2000000 | tf_op jit(solution)/shard_map/pallas_call | solution.py:63
  75.9 2.0 %all-gather.3 = f32[18,24,128]{2,1,0:T(8,128)S(1)} all-gather(f32[9,24,128]{2,1,0:T(8,128)S(1)} %get-tuple-element.80), channel_id=5, replica_groups={{0,1},{2,3},{4,5},{6,7},{8,9},{10,11},{12,13},{14,15},{16,17},{18,19},{..., dimensions={0}, use_global_device_ids=true | all-gather | bytes 331776 | tf_op jit(solution)/shard_map/all_gather | solution.py:467
  78.5 4.1 %collective-permute-start.15 = (f32[8,24,128]{2,1,0:T(8,128)S(1)}, f32[8,24,128]{2,1,0:T(8,128)S(1)}, u32[]{:S(2)}, u32[]{:S(2)}) collective-permute-start(f32[8,24,128]{2,1,0:T(8,128)S(1)} %get-tuple-element.88), channel_id=1, source_target_pairs={{1,2},{2,1},{3,4},{4,3},{5,6},{6,5},{9,10},{10,9},{11,12},{12,11},... | collective-permute-start | bytes 294920 | tf_op jit(solution)/shard_map/ppermute | solution.py:458
  83.2 5.1 %collective-permute-start.14 = (f32[16,8,128]{2,1,0:T(8,128)S(1)}, f32[16,8,128]{2,1,0:T(8,128)S(1)}, u32[]{:S(2)}, u32[]{:S(2)}) collective-permute-start(f32[16,8,128]{2,1,0:T(8,128)S(1)} %get-tuple-element.87), channel_id=1, source_target_pairs={{0,32},{32,0},{64,96},{96,64},{128,160},{160,128},{192,224},{224,1... | collective-permute-start | bytes 196616 | tf_op jit(solution)/shard_map/ppermute | solution.py:458
  89.0 1.1 %shard_map.130 = (f32[16,24,128]{2,1,0:T(8,128)S(1)}, f32[16,24,128]{2,1,0:T(8,128)}) custom-call(f32[16,24,128]{2,1,0:T(8,128)S(1)} %get-tuple-element.90.wave, f32[16,24,128]{2,1,0:T(8,128)S(1)} %get-tuple-element.91.side, bf16[256,256]{1,0:T(8,128)(2,1)S(1)} %copy-done.3, bf16[256,256]{1,0:T(8,128)(2,1)S(1)} %copy-done.4), custom_call_target="tpu_custom_call" | custom-call | flops 1000000 | bytes 2000000 | tf_op jit(solution)/shard_map/pallas_call | solution.py:63
  90.1 1.9 %all-gather.4 = f32[16,24,128]{2,1,0:T(8,128)S(1)} all-gather(f32[8,24,128]{2,1,0:T(8,128)S(1)} %get-tuple-element.89), channel_id=6, replica_groups={{0,1},{2,3},{4,5},{6,7},{8,9},{10,11},{12,13},{14,15},{16,17},{18,19},{..., dimensions={0}, use_global_device_ids=true | all-gather | bytes 294912 | tf_op jit(solution)/shard_map/all_gather | solution.py:467
  92.1 1.0 %shard_map.131 = (f32[16,24,128]{2,1,0:T(8,128)}, f32[16,24,128]{2,1,0:T(8,128)}) custom-call(f32[16,8,128]{2,1,0:T(8,128)S(1)} %collective-permute-done.13.x_odd_in, f32[16,8,128]{2,1,0:T(8,128)S(1)} %collective-permute-done.14.x_even_in, f32[8,24,128]{2,1,0:T(8,128)S(1)} %collective-permute-done.15.z_odd_in, f32[2,8,24,128]{3,2,1,0:T(8,128)S(1)} %bitcast.17, ...), custom_call_target="tpu_custom_call" | custom-call | flops 1000000 | bytes 2000000 | tf_op jit(solution)/shard_map/pallas_call | solution.py:63
  (38 shorter events, 6.3 us)
Async XLA Ops:
  2.9 29.9 %collective-permute-start = (f32[10,24,128]{2,1,0:T(8,128)}, f32[10,24,128]{2,1,0:T(8,128)S(1)}, u32[]{:S(2)}, u32[]{:S(2)}) collective-permute-start(f32[10,24,128]{2,1,0:T(8,128)} %get-tuple-element.52), channel_id=1, source_target_pairs={{8,16},{16,8},{9,17},{17,9},{10,18},{18,10},{11,19},{19,11},{12,20... | collective-permute-start | bytes 368648 | tf_op jit(solution)/shard_map/ppermute | solution.py:458
  3.6 30.4 %all-to-all-start = ((f32[64,1,128]{2,1,0:T(1,128)}), f32[64,1,128]{2,1,0:T(1,128)S(1)}, u32[]{:S(2)}, u32[]{:S(2)}) async-start(f32[64,1,128]{2,1,0:T(1,128)} %bitcast.22), calls=%async_computation | async-start | bytes 65536 | tf_op jit(solution)/shard_map/all_to_all | solution.py:503
  23.1 9.7 %copy-start.1 = (f32[16,24,128]{2,1,0:T(8,128)S(1)}, f32[16,24,128]{2,1,0:T(8,128)}, u32[]{:S(2)}) copy-start(f32[16,24,128]{2,1,0:T(8,128)} %older.5) | copy-start | bytes 589828
  32.8 10.9 %copy-start.3 = (bf16[256,256]{1,0:T(8,128)(2,1)S(1)}, bf16[256,256]{1,0:T(8,128)(2,1)}, u32[]{:S(2)}) copy-start(bf16[256,256]{1,0:T(8,128)(2,1)} %constant.4.clone.band_high) | copy-start | bytes 393220
  32.8 10.9 %copy-start.4 = (bf16[256,256]{1,0:T(8,128)(2,1)S(1)}, bf16[256,256]{1,0:T(8,128)(2,1)}, u32[]{:S(2)}) copy-start(bf16[256,256]{1,0:T(8,128)(2,1)} %constant.5.clone.band_low) | copy-start | bytes 393220
  33.9 10.8 %collective-permute-start.4 = (f32[64,128]{1,0:T(8,128)S(1)}, f32[64,128]{1,0:T(8,128)S(1)}, u32[]{:S(2)}, u32[]{:S(2)}) collective-permute-start(f32[64,128]{1,0:T(8,128)S(1)} %bitcast.18), channel_id=1, source_target_pairs={{2,0},{3,1},{10,8},{11,9},{18,16},{19,17},{26,24},{27,25},{34,32},... | collective-permute-start | bytes 98312 | tf_op jit(solution)/shard_map/ppermute | solution.py:514
  35.2 14.2 %collective-permute-start.5 = (f32[64,128]{1,0:T(8,128)S(1)}, f32[64,128]{1,0:T(8,128)S(1)}, u32[]{:S(2)}, u32[]{:S(2)}) collective-permute-start(f32[64,128]{1,0:T(8,128)S(1)} %bitcast.19), channel_id=1, source_target_pairs={{4,0},{5,1},{12,8},{13,9},{20,16},{21,17},{28,24},{29,25},{36,32},... | collective-permute-start | bytes 98312 | tf_op jit(solution)/shard_map/ppermute | solution.py:514
  36.5 12.9 %collective-permute-start.6 = (f32[64,128]{1,0:T(8,128)S(1)}, f32[64,128]{1,0:T(8,128)S(1)}, u32[]{:S(2)}, u32[]{:S(2)}) collective-permute-start(f32[64,128]{1,0:T(8,128)S(1)} %bitcast.20), channel_id=1, source_target_pairs={{6,0},{7,1},{14,8},{15,9},{22,16},{23,17},{30,24},{31,25},{38,32},... | collective-permute-start | bytes 98312 | tf_op jit(solution)/shard_map/ppermute | solution.py:514
  37.8 15.0 %collective-permute-start.3 = (f32[12,24,128]{2,1,0:T(8,128)S(1)}, f32[12,24,128]{2,1,0:T(8,128)S(1)}, u32[]{:S(2)}, u32[]{:S(2)}) collective-permute-start(f32[12,24,128]{2,1,0:T(8,128)S(1)} %get-tuple-element.59), channel_id=1, source_target_pairs={{1,2},{2,1},{3,4},{4,3},{5,6},{6,5},{9,10},{10,9},{11,12},{12,11},... | collective-permute-start | bytes 442376 | tf_op jit(solution)/shard_map/ppermute | solution.py:458
  43.1 9.7 %collective-permute-start.1 = (f32[24,8,128]{2,1,0:T(8,128)S(1)}, f32[24,8,128]{2,1,0:T(8,128)S(1)}, u32[]{:S(2)}, u32[]{:S(2)}) collective-permute-start(f32[24,8,128]{2,1,0:T(8,128)S(1)} %get-tuple-element.57), channel_id=1, source_target_pairs={{32,64},{64,32},{96,128},{128,96},{160,192},{192,160},{224,256},{2... | collective-permute-start | bytes 294920 | tf_op jit(solution)/shard_map/ppermute | solution.py:458
  44.7 8.1 %collective-permute-start.2 = (f32[24,8,128]{2,1,0:T(8,128)S(1)}, f32[24,8,128]{2,1,0:T(8,128)S(1)}, u32[]{:S(2)}, u32[]{:S(2)}) collective-permute-start(f32[24,8,128]{2,1,0:T(8,128)S(1)} %get-tuple-element.58), channel_id=1, source_target_pairs={{0,32},{32,0},{64,96},{96,64},{128,160},{160,128},{192,224},{224,1... | collective-permute-start | bytes 294920 | tf_op jit(solution)/shard_map/ppermute | solution.py:458
  49.4 3.4 %copy-start.5 = (f32[16,24,128]{2,1,0:T(8,128)S(1)}, f32[16,24,128]{2,1,0:T(8,128)}, u32[]{:S(2)}) copy-start(f32[16,24,128]{2,1,0:T(8,128)} %older.4) | copy-start | bytes 589828
  50.5 2.3 %copy-start = (bf16[4,16,24,128]{3,2,1,0:T(8,128)(2,1)S(1)}, bf16[4,16,24,128]{3,2,1,0:T(8,128)(2,1)}, u32[]{:S(2)}) copy-start(bf16[4,16,24,128]{3,2,1,0:T(8,128)(2,1)} %forward.7) | copy-start | bytes 1179652
  50.5 2.3 %copy-start.2 = (f32[16,24,128]{2,1,0:T(8,128)S(1)}, f32[16,24,128]{2,1,0:T(8,128)}, u32[]{:S(2)}) copy-start(f32[16,24,128]{2,1,0:T(8,128)} %stiff.9) | copy-start | bytes 589828
  53.5 11.4 %collective-permute-start.9 = (f32[10,24,128]{2,1,0:T(8,128)S(1)}, f32[10,24,128]{2,1,0:T(8,128)S(1)}, u32[]{:S(2)}, u32[]{:S(2)}) collective-permute-start(f32[10,24,128]{2,1,0:T(8,128)S(1)} %get-tuple-element.69), channel_id=1, source_target_pairs={{1,2},{2,1},{3,4},{4,3},{5,6},{6,5},{9,10},{10,9},{11,12},{12,11},... | collective-permute-start | bytes 368648 | tf_op jit(solution)/shard_map/ppermute | solution.py:458
  56.2 8.7 %collective-permute-start.7 = (f32[20,8,128]{2,1,0:T(8,128)S(1)}, f32[20,8,128]{2,1,0:T(8,128)S(1)}, u32[]{:S(2)}, u32[]{:S(2)}) collective-permute-start(f32[20,8,128]{2,1,0:T(8,128)S(1)} %get-tuple-element.67), channel_id=1, source_target_pairs={{32,64},{64,32},{96,128},{128,96},{160,192},{192,160},{224,256},{2... | collective-permute-start | bytes 245768 | tf_op jit(solution)/shard_map/ppermute | solution.py:458
  56.9 8.0 %collective-permute-start.8 = (f32[20,8,128]{2,1,0:T(8,128)S(1)}, f32[20,8,128]{2,1,0:T(8,128)S(1)}, u32[]{:S(2)}, u32[]{:S(2)}) collective-permute-start(f32[20,8,128]{2,1,0:T(8,128)S(1)} %get-tuple-element.68), channel_id=1, source_target_pairs={{0,32},{32,0},{64,96},{96,64},{128,160},{160,128},{192,224},{224,1... | collective-permute-start | bytes 245768 | tf_op jit(solution)/shard_map/ppermute | solution.py:458
  65.6 12.3 %collective-permute-start.12 = (f32[9,24,128]{2,1,0:T(8,128)S(1)}, f32[9,24,128]{2,1,0:T(8,128)S(1)}, u32[]{:S(2)}, u32[]{:S(2)}) collective-permute-start(f32[9,24,128]{2,1,0:T(8,128)S(1)} %get-tuple-element.79), channel_id=1, source_target_pairs={{1,2},{2,1},{3,4},{4,3},{5,6},{6,5},{9,10},{10,9},{11,12},{12,11},... | collective-permute-start | bytes 331784 | tf_op jit(solution)/shard_map/ppermute | solution.py:458
  69.7 8.2 %collective-permute-start.10 = (f32[18,8,128]{2,1,0:T(8,128)S(1)}, f32[18,8,128]{2,1,0:T(8,128)S(1)}, u32[]{:S(2)}, u32[]{:S(2)}) collective-permute-start(f32[18,8,128]{2,1,0:T(8,128)S(1)} %get-tuple-element.77), channel_id=1, source_target_pairs={{32,64},{64,32},{96,128},{128,96},{160,192},{192,160},{224,256},{2... | collective-permute-start | bytes 221192 | tf_op jit(solution)/shard_map/ppermute | solution.py:458
  70.3 7.6 %collective-permute-start.11 = (f32[18,8,128]{2,1,0:T(8,128)S(1)}, f32[18,8,128]{2,1,0:T(8,128)S(1)}, u32[]{:S(2)}, u32[]{:S(2)}) collective-permute-start(f32[18,8,128]{2,1,0:T(8,128)S(1)} %get-tuple-element.78), channel_id=1, source_target_pairs={{0,32},{32,0},{64,96},{96,64},{128,160},{160,128},{192,224},{224,1... | collective-permute-start | bytes 221192 | tf_op jit(solution)/shard_map/ppermute | solution.py:458
  78.5 13.6 %collective-permute-start.15 = (f32[8,24,128]{2,1,0:T(8,128)S(1)}, f32[8,24,128]{2,1,0:T(8,128)S(1)}, u32[]{:S(2)}, u32[]{:S(2)}) collective-permute-start(f32[8,24,128]{2,1,0:T(8,128)S(1)} %get-tuple-element.88), channel_id=1, source_target_pairs={{1,2},{2,1},{3,4},{4,3},{5,6},{6,5},{9,10},{10,9},{11,12},{12,11},... | collective-permute-start | bytes 294920 | tf_op jit(solution)/shard_map/ppermute | solution.py:458
  82.6 9.5 %collective-permute-start.13 = (f32[16,8,128]{2,1,0:T(8,128)S(1)}, f32[16,8,128]{2,1,0:T(8,128)S(1)}, u32[]{:S(2)}, u32[]{:S(2)}) collective-permute-start(f32[16,8,128]{2,1,0:T(8,128)S(1)} %get-tuple-element.86), channel_id=1, source_target_pairs={{32,64},{64,32},{96,128},{128,96},{160,192},{192,160},{224,256},{2... | collective-permute-start | bytes 196616 | tf_op jit(solution)/shard_map/ppermute | solution.py:458
  83.2 8.8 %collective-permute-start.14 = (f32[16,8,128]{2,1,0:T(8,128)S(1)}, f32[16,8,128]{2,1,0:T(8,128)S(1)}, u32[]{:S(2)}, u32[]{:S(2)}) collective-permute-start(f32[16,8,128]{2,1,0:T(8,128)S(1)} %get-tuple-element.87), channel_id=1, source_target_pairs={{0,32},{32,0},{64,96},{96,64},{128,160},{160,128},{192,224},{224,1... | collective-permute-start | bytes 196616 | tf_op jit(solution)/shard_map/ppermute | solution.py:458

commit v11 on v10

--- a/solution.py
+++ b/solution.py
@@ -306,12 +306,9 @@
                 x_halo[1, plane + span * turn, pl.ds(start, RADIUS), :] = unfold(both, turn, width)
 
 
-def own_kernel(last, wave, side, band_high, band_low, *rest):
+def own_kernel(wave, side, band_high, band_low, *rest):
     *outs, y_terms = rest
     depth, rows, _ = wave.shape
-    if last:
-        outs, kept = outs[:1], outs[1]
-        kept[...] = wave[...]
     width = LANES * len(outs)
     both = jnp.concatenate(
         [wave[...].reshape(depth * rows, LANES), side[...].reshape(depth * rows, LANES)], axis=1
@@ -422,8 +419,11 @@
     shot = done = None
     copies = []
     if last:
-        (source, image_out, wave_out, z_halo, x_halo, image, fresh, sems) = rest
+        (source, image_out, wave_out, older_out, z_halo, x_halo, image, fresh, sems,
+         older_sem) = rest
         fresh_side = None
+        copies.append(pltpu.make_async_copy(wave, older_out, older_sem))
+        copies[-1].start()
         cell = source[0, 0]
         shot = (lax.div(cell, total_y), lax.rem(cell, total_y))
 
@@ -531,13 +531,11 @@
     for step in range(STEPS):
         last = step == STEPS - 1
         own = call(
-            functools.partial(own_kernel, last),
-            [block, block],
+            own_kernel,
+            [block] if last else [block, block],
             [wave, side, band_high, band_low],
             scratch=[pltpu.VMEM((depth * rows, 2 * LANES), F32)],
         )
-        if last:
-            *own, last_older = own
         faces = exchange(faces)
         ins = [*faces[::-1], wave, side, older, older_side, stiffness, stiff_side, forward_wave,
                *own]
@@ -551,9 +549,11 @@
         room, in_specs, out_specs = scratch, None, None
         if last:
             ins.append(source_cell.reshape(1, 1))
-            out_specs = [pl.BlockSpec(memory_space=pl.ANY)] * 2
+            outs.append(block)
+            out_specs = [pl.BlockSpec(memory_space=pl.ANY)] * 3
             held = pltpu.VMEM((depth, rows, LANES), F32)
-            room = scratch + [held, held, pltpu.SemaphoreType.DMA((2, depth // CHUNK))]
+            room = scratch + [held, held, pltpu.SemaphoreType.DMA((2, depth // CHUNK)),
+                              pltpu.SemaphoreType.DMA]
         rest = call(
             functools.partial(step_kernel, step, cols * span_y), outs, ins, room, in_specs,
             out_specs=out_specs,
@@ -565,7 +565,7 @@
         if not last:
             older_side, side = side, rest[0]
             faces = rest[1:]
-    return image, last_older, wave
+    return image, rest[0], wave
 
 
 def solution(mesh):

time: 94.5 us -> 94 us (level)
  transfers between devices with their start and end apart: 17 -> 17, of which waited for: 1 -> 1; matrix products, arithmetic and copies ran while one was open for 0% -> 0% of each run, Pallas kernels for 6% -> 5%
where the time goes in v11:
time: 94 us; the launch traced here: 92.5 us
  starting transfers between devices  62.4 us (66%)
  blocking collectives  17.9 us (19%)
  Pallas kernels  9.87 us (10%)
  between operations  1.6 us (2%)
    ppermute x13, starting transfers between devices, swap(): return lax.ppermute(block, axis, pairs)  39 us
    all_to_all x1, starting transfers between devices, on_device(): packets = lax.all_to_all(packets, ('gx', 'gy'), 0, 0, tiled=True)  19.6 us
    all_gather x5, blocking collectives, pair_gather(): lax.all_gather(block, axis, axis=0, tiled=False, axis_index_groups=groups)  17.9 us
    pallas_call x11, Pallas kernels, call(): pl.pallas_call(body, out_shape=outs, in_specs=in_specs or [vmem()] * len(...  9.87 us
    ppermute x3, starting transfers between devices, on_device(): lax.ppermute(packets, 'gz', [(chip + core, core) for core in range(cores)])  3.86 us
  transfers between devices with their start and end apart: 17, of which 1 were waited for; matrix products, arithmetic and copies ran while one was open for 0% of the time, Pallas kernels for 5%

profile of v11, /device:TPU:1, one launch (start us, length us, event | category | flops | bytes accessed | tf_op | source)
XLA Modules:
  0.0 92.5 jit_solution(16309959296013590215)
XLA Ops:
  0.6 2.3 %shard_map.121 = (f32[64,128]{1,0:T(8,128)}, f32[10,24,128]{2,1,0:T(8,128)}, f32[10,24,128]{2,1,0:T(8,128)}) custom-call(f32[4,128]{1,0:T(4,128)} %residuals.1, s32[1,128]{1,0:T(1,128)} %bitcast.23, s32[1,128]{1,0:T(1,128)} %bitcast.24, f32[16,24,128]{2,1,0:T(8,128)} %older.5, f32[16,24,128]{2,1,0:T(8,128)} %older.4, f32[16,24,128]{2,1,0:T(8,128)} %stiff.9), custom_call_target="tpu_custom_call" | custom-call | flops 1000000 | bytes 2000000 | tf_op jit(solution)/shard_map/pallas_call | solution.py:63
  3.6 19.6 %all-to-all-start = ((f32[64,1,128]{2,1,0:T(1,128)}), f32[64,1,128]{2,1,0:T(1,128)S(1)}, u32[]{:S(2)}, u32[]{:S(2)}) async-start(f32[64,1,128]{2,1,0:T(1,128)} %bitcast.22), calls=%async_computation | async-start | bytes 65536 | tf_op jit(solution)/shard_map/all_to_all | solution.py:503
  23.1 9.7 %all-gather = f32[20,24,128]{2,1,0:T(8,128)S(1)} all-gather(f32[10,24,128]{2,1,0:T(8,128)} %get-tuple-element.50), channel_id=2, replica_groups={{0,8},{16,24},{1,9},{17,25},{2,10},{18,26},{3,11},{19,27},{4,12},{20,28..., dimensions={0}, use_global_device_ids=true | all-gather | bytes 368640 | tf_op jit(solution)/shard_map/all_gather | solution.py:467
  33.9 1.3 %collective-permute-start.4 = (f32[64,128]{1,0:T(8,128)S(1)}, f32[64,128]{1,0:T(8,128)S(1)}, u32[]{:S(2)}, u32[]{:S(2)}) collective-permute-start(f32[64,128]{1,0:T(8,128)S(1)} %bitcast.18), channel_id=1, source_target_pairs={{2,0},{3,1},{10,8},{11,9},{18,16},{19,17},{26,24},{27,25},{34,32},... | collective-permute-start | bytes 98312 | tf_op jit(solution)/shard_map/ppermute | solution.py:514
  35.2 1.3 %collective-permute-start.5 = (f32[64,128]{1,0:T(8,128)S(1)}, f32[64,128]{1,0:T(8,128)S(1)}, u32[]{:S(2)}, u32[]{:S(2)}) collective-permute-start(f32[64,128]{1,0:T(8,128)S(1)} %bitcast.19), channel_id=1, source_target_pairs={{4,0},{5,1},{12,8},{13,9},{20,16},{21,17},{28,24},{29,25},{36,32},... | collective-permute-start | bytes 98312 | tf_op jit(solution)/shard_map/ppermute | solution.py:514
  36.5 1.3 %collective-permute-start.6 = (f32[64,128]{1,0:T(8,128)S(1)}, f32[64,128]{1,0:T(8,128)S(1)}, u32[]{:S(2)}, u32[]{:S(2)}) collective-permute-start(f32[64,128]{1,0:T(8,128)S(1)} %bitcast.20), channel_id=1, source_target_pairs={{6,0},{7,1},{14,8},{15,9},{22,16},{23,17},{30,24},{31,25},{38,32},... | collective-permute-start | bytes 98312 | tf_op jit(solution)/shard_map/ppermute | solution.py:514
  37.8 5.3 %collective-permute-start.3 = (f32[12,24,128]{2,1,0:T(8,128)S(1)}, f32[12,24,128]{2,1,0:T(8,128)S(1)}, u32[]{:S(2)}, u32[]{:S(2)}) collective-permute-start(f32[12,24,128]{2,1,0:T(8,128)S(1)} %get-tuple-element.58), channel_id=1, source_target_pairs={{1,2},{2,1},{3,4},{4,3},{5,6},{6,5},{9,10},{10,9},{11,12},{12,11},... | collective-permute-start | bytes 442376 | tf_op jit(solution)/shard_map/ppermute | solution.py:458
  43.1 0.7 collective-permute-start.1
  43.8 0.9 shard_map.124
  44.7 4.7 %collective-permute-start.2 = (f32[24,8,128]{2,1,0:T(8,128)S(1)}, f32[24,8,128]{2,1,0:T(8,128)S(1)}, u32[]{:S(2)}, u32[]{:S(2)}) collective-permute-start(f32[24,8,128]{2,1,0:T(8,128)S(1)} %get-tuple-element.57), channel_id=1, source_target_pairs={{0,32},{32,0},{64,96},{96,64},{128,160},{160,128},{192,224},{224,1... | collective-permute-start | bytes 294920 | tf_op jit(solution)/shard_map/ppermute | solution.py:458
  49.4 1.0 %shard_map.123 = f32[20,24,128]{2,1,0:T(8,128)S(1)} custom-call(f32[12,24,128]{2,1,0:T(8,128)S(1)} %get-tuple-element.59.z_even, f32[64,128]{1,0:T(8,128)S(1)} %bitcast.21, f32[64,128]{1,0:T(8,128)S(1)} %collective-permute-done.4.refs_1_, f32[64,128]{1,0:T(8,128)S(1)} %collective-permute-done.5.refs_2_, f32[64,128]{1,0:T(8,128)S(1)} %collective-permute-done.6.refs_3_), custom_call_target="tpu_custom_call" | custom-call | flops 1000000 | bytes 2000000 | tf_op jit(solution)/shard_map/pallas_call | solution.py:63
  50.5 2.3 %all-gather.1 = f32[40,24,128]{2,1,0:T(8,128)S(1)} all-gather(f32[20,24,128]{2,1,0:T(8,128)S(1)} %shard_map.123), channel_id=3, replica_groups={{0,1},{2,3},{4,5},{6,7},{8,9},{10,11},{12,13},{14,15},{16,17},{18,19},{..., dimensions={0}, use_global_device_ids=true | all-gather | bytes 737280 | tf_op jit(solution)/shard_map/all_gather | solution.py:467
  53.5 2.7 %collective-permute-start.9 = (f32[10,24,128]{2,1,0:T(8,128)S(1)}, f32[10,24,128]{2,1,0:T(8,128)S(1)}, u32[]{:S(2)}, u32[]{:S(2)}) collective-permute-start(f32[10,24,128]{2,1,0:T(8,128)S(1)} %get-tuple-element.68), channel_id=1, source_target_pairs={{1,2},{2,1},{3,4},{4,3},{5,6},{6,5},{9,10},{10,9},{11,12},{12,11},... | collective-permute-start | bytes 368648 | tf_op jit(solution)/shard_map/ppermute | solution.py:458
  56.9 5.1 %collective-permute-start.8 = (f32[20,8,128]{2,1,0:T(8,128)S(1)}, f32[20,8,128]{2,1,0:T(8,128)S(1)}, u32[]{:S(2)}, u32[]{:S(2)}) collective-permute-start(f32[20,8,128]{2,1,0:T(8,128)S(1)} %get-tuple-element.67), channel_id=1, source_target_pairs={{0,32},{32,0},{64,96},{96,64},{128,160},{160,128},{192,224},{224,1... | collective-permute-start | bytes 245768 | tf_op jit(solution)/shard_map/ppermute | solution.py:458
  62.0 0.9 shard_map.126
  62.9 2.0 %all-gather.2 = f32[20,24,128]{2,1,0:T(8,128)S(1)} all-gather(f32[10,24,128]{2,1,0:T(8,128)S(1)} %get-tuple-element.69), channel_id=4, replica_groups={{0,1},{2,3},{4,5},{6,7},{8,9},{10,11},{12,13},{14,15},{16,17},{18,19},{..., dimensions={0}, use_global_device_ids=true | all-gather | bytes 368640 | tf_op jit(solution)/shard_map/all_gather | solution.py:467
  65.5 4.1 %collective-permute-start.12 = (f32[9,24,128]{2,1,0:T(8,128)S(1)}, f32[9,24,128]{2,1,0:T(8,128)S(1)}, u32[]{:S(2)}, u32[]{:S(2)}) collective-permute-start(f32[9,24,128]{2,1,0:T(8,128)S(1)} %get-tuple-element.78), channel_id=1, source_target_pairs={{1,2},{2,1},{3,4},{4,3},{5,6},{6,5},{9,10},{10,9},{11,12},{12,11},... | collective-permute-start | bytes 331784 | tf_op jit(solution)/shard_map/ppermute | solution.py:458
  70.3 4.6 %collective-permute-start.11 = (f32[18,8,128]{2,1,0:T(8,128)S(1)}, f32[18,8,128]{2,1,0:T(8,128)S(1)}, u32[]{:S(2)}, u32[]{:S(2)}) collective-permute-start(f32[18,8,128]{2,1,0:T(8,128)S(1)} %get-tuple-element.77), channel_id=1, source_target_pairs={{0,32},{32,0},{64,96},{96,64},{128,160},{160,128},{192,224},{224,1... | collective-permute-start | bytes 221192 | tf_op jit(solution)/shard_map/ppermute | solution.py:458
  75.0 0.9 %shard_map.128 = (f32[16,24,128]{2,1,0:T(8,128)S(1)}, f32[16,24,128]{2,1,0:T(8,128)S(1)}) custom-call(f32[16,24,128]{2,1,0:T(8,128)S(1)} %get-tuple-element.80.wave.older, f32[16,24,128]{2,1,0:T(8,128)S(1)} %get-tuple-element.81.side.older_side, bf16[256,256]{1,0:T(8,128)(2,1)S(1)} %copy-done.3, bf16[256,256]{1,0:T(8,128)(2,1)S(1)} %copy-done.4), custom_call_target="tpu_custom_call" | custom-call | flops 1000000 | bytes 2000000 | tf_op jit(solution)/shard_map/pallas_call | solution.py:63
  75.9 2.0 %all-gather.3 = f32[18,24,128]{2,1,0:T(8,128)S(1)} all-gather(f32[9,24,128]{2,1,0:T(8,128)S(1)} %get-tuple-element.79), channel_id=5, replica_groups={{0,1},{2,3},{4,5},{6,7},{8,9},{10,11},{12,13},{14,15},{16,17},{18,19},{..., dimensions={0}, use_global_device_ids=true | all-gather | bytes 331776 | tf_op jit(solution)/shard_map/all_gather | solution.py:467
  78.5 4.1 %collective-permute-start.15 = (f32[8,24,128]{2,1,0:T(8,128)S(1)}, f32[8,24,128]{2,1,0:T(8,128)S(1)}, u32[]{:S(2)}, u32[]{:S(2)}) collective-permute-start(f32[8,24,128]{2,1,0:T(8,128)S(1)} %get-tuple-element.87), channel_id=1, source_target_pairs={{1,2},{2,1},{3,4},{4,3},{5,6},{6,5},{9,10},{10,9},{11,12},{12,11},... | collective-permute-start | bytes 294920 | tf_op jit(solution)/shard_map/ppermute | solution.py:458
  83.2 5.1 %collective-permute-start.14 = (f32[16,8,128]{2,1,0:T(8,128)S(1)}, f32[16,8,128]{2,1,0:T(8,128)S(1)}, u32[]{:S(2)}, u32[]{:S(2)}) collective-permute-start(f32[16,8,128]{2,1,0:T(8,128)S(1)} %get-tuple-element.86), channel_id=1, source_target_pairs={{0,32},{32,0},{64,96},{96,64},{128,160},{160,128},{192,224},{224,1... | collective-permute-start | bytes 196616 | tf_op jit(solution)/shard_map/ppermute | solution.py:458
  89.5 1.9 %all-gather.4 = f32[16,24,128]{2,1,0:T(8,128)S(1)} all-gather(f32[8,24,128]{2,1,0:T(8,128)S(1)} %get-tuple-element.88), channel_id=6, replica_groups={{0,1},{2,3},{4,5},{6,7},{8,9},{10,11},{12,13},{14,15},{16,17},{18,19},{..., dimensions={0}, use_global_device_ids=true | all-gather | bytes 294912 | tf_op jit(solution)/shard_map/all_gather | solution.py:467
  91.5 1.0 %shard_map.131 = (f32[16,24,128]{2,1,0:T(8,128)}, f32[16,24,128]{2,1,0:T(8,128)}, f32[16,24,128]{2,1,0:T(8,128)}) custom-call(f32[16,8,128]{2,1,0:T(8,128)S(1)} %collective-permute-done.13.x_odd_in, f32[16,8,128]{2,1,0:T(8,128)S(1)} %collective-permute-done.14.x_even_in, f32[8,24,128]{2,1,0:T(8,128)S(1)} %collective-permute-done.15.z_odd_in, ...), custom_call_target="tpu_custom_call" | custom-call | flops 1000000 | bytes 2000000 | tf_op jit(solution)/shard_map/pallas_call | solution.py:63
  (38 shorter events, 6.2 us)
Async XLA Ops:
  2.9 29.9 %collective-permute-start = (f32[10,24,128]{2,1,0:T(8,128)}, f32[10,24,128]{2,1,0:T(8,128)S(1)}, u32[]{:S(2)}, u32[]{:S(2)}) collective-permute-start(f32[10,24,128]{2,1,0:T(8,128)} %get-tuple-element.51), channel_id=1, source_target_pairs={{8,16},{16,8},{9,17},{17,9},{10,18},{18,10},{11,19},{19,11},{12,20... | collective-permute-start | bytes 368648 | tf_op jit(solution)/shard_map/ppermute | solution.py:458
  3.6 30.4 %all-to-all-start = ((f32[64,1,128]{2,1,0:T(1,128)}), f32[64,1,128]{2,1,0:T(1,128)S(1)}, u32[]{:S(2)}, u32[]{:S(2)}) async-start(f32[64,1,128]{2,1,0:T(1,128)} %bitcast.22), calls=%async_computation | async-start | bytes 65536 | tf_op jit(solution)/shard_map/all_to_all | solution.py:503
  23.1 9.7 %copy-start.1 = (f32[16,24,128]{2,1,0:T(8,128)S(1)}, f32[16,24,128]{2,1,0:T(8,128)}, u32[]{:S(2)}) copy-start(f32[16,24,128]{2,1,0:T(8,128)} %older.5) | copy-start | bytes 589828
  32.8 10.9 %copy-start.3 = (bf16[256,256]{1,0:T(8,128)(2,1)S(1)}, bf16[256,256]{1,0:T(8,128)(2,1)}, u32[]{:S(2)}) copy-start(bf16[256,256]{1,0:T(8,128)(2,1)} %constant.4.clone.band_high) | copy-start | bytes 393220
  32.8 10.9 %copy-start.4 = (bf16[256,256]{1,0:T(8,128)(2,1)S(1)}, bf16[256,256]{1,0:T(8,128)(2,1)}, u32[]{:S(2)}) copy-start(bf16[256,256]{1,0:T(8,128)(2,1)} %constant.5.clone.band_low) | copy-start | bytes 393220
  33.9 10.8 %collective-permute-start.4 = (f32[64,128]{1,0:T(8,128)S(1)}, f32[64,128]{1,0:T(8,128)S(1)}, u32[]{:S(2)}, u32[]{:S(2)}) collective-permute-start(f32[64,128]{1,0:T(8,128)S(1)} %bitcast.18), channel_id=1, source_target_pairs={{2,0},{3,1},{10,8},{11,9},{18,16},{19,17},{26,24},{27,25},{34,32},... | collective-permute-start | bytes 98312 | tf_op jit(solution)/shard_map/ppermute | solution.py:514
  35.2 14.2 %collective-permute-start.5 = (f32[64,128]{1,0:T(8,128)S(1)}, f32[64,128]{1,0:T(8,128)S(1)}, u32[]{:S(2)}, u32[]{:S(2)}) collective-permute-start(f32[64,128]{1,0:T(8,128)S(1)} %bitcast.19), channel_id=1, source_target_pairs={{4,0},{5,1},{12,8},{13,9},{20,16},{21,17},{28,24},{29,25},{36,32},... | collective-permute-start | bytes 98312 | tf_op jit(solution)/shard_map/ppermute | solution.py:514
  36.5 12.9 %collective-permute-start.6 = (f32[64,128]{1,0:T(8,128)S(1)}, f32[64,128]{1,0:T(8,128)S(1)}, u32[]{:S(2)}, u32[]{:S(2)}) collective-permute-start(f32[64,128]{1,0:T(8,128)S(1)} %bitcast.20), channel_id=1, source_target_pairs={{6,0},{7,1},{14,8},{15,9},{22,16},{23,17},{30,24},{31,25},{38,32},... | collective-permute-start | bytes 98312 | tf_op jit(solution)/shard_map/ppermute | solution.py:514
  37.8 15.0 %collective-permute-start.3 = (f32[12,24,128]{2,1,0:T(8,128)S(1)}, f32[12,24,128]{2,1,0:T(8,128)S(1)}, u32[]{:S(2)}, u32[]{:S(2)}) collective-permute-start(f32[12,24,128]{2,1,0:T(8,128)S(1)} %get-tuple-element.58), channel_id=1, source_target_pairs={{1,2},{2,1},{3,4},{4,3},{5,6},{6,5},{9,10},{10,9},{11,12},{12,11},... | collective-permute-start | bytes 442376 | tf_op jit(solution)/shard_map/ppermute | solution.py:458
  43.1 9.7 %collective-permute-start.1 = (f32[24,8,128]{2,1,0:T(8,128)S(1)}, f32[24,8,128]{2,1,0:T(8,128)S(1)}, u32[]{:S(2)}, u32[]{:S(2)}) collective-permute-start(f32[24,8,128]{2,1,0:T(8,128)S(1)} %get-tuple-element.56), channel_id=1, source_target_pairs={{32,64},{64,32},{96,128},{128,96},{160,192},{192,160},{224,256},{2... | collective-permute-start | bytes 294920 | tf_op jit(solution)/shard_map/ppermute | solution.py:458
  44.7 8.1 %collective-permute-start.2 = (f32[24,8,128]{2,1,0:T(8,128)S(1)}, f32[24,8,128]{2,1,0:T(8,128)S(1)}, u32[]{:S(2)}, u32[]{:S(2)}) collective-permute-start(f32[24,8,128]{2,1,0:T(8,128)S(1)} %get-tuple-element.57), channel_id=1, source_target_pairs={{0,32},{32,0},{64,96},{96,64},{128,160},{160,128},{192,224},{224,1... | collective-permute-start | bytes 294920 | tf_op jit(solution)/shard_map/ppermute | solution.py:458
  49.4 3.4 %copy-start.5 = (f32[16,24,128]{2,1,0:T(8,128)S(1)}, f32[16,24,128]{2,1,0:T(8,128)}, u32[]{:S(2)}) copy-start(f32[16,24,128]{2,1,0:T(8,128)} %older.4) | copy-start | bytes 589828
  50.5 2.3 %copy-start = (bf16[4,16,24,128]{3,2,1,0:T(8,128)(2,1)S(1)}, bf16[4,16,24,128]{3,2,1,0:T(8,128)(2,1)}, u32[]{:S(2)}) copy-start(bf16[4,16,24,128]{3,2,1,0:T(8,128)(2,1)} %forward.7) | copy-start | bytes 1179652
  50.5 2.3 %copy-start.2 = (f32[16,24,128]{2,1,0:T(8,128)S(1)}, f32[16,24,128]{2,1,0:T(8,128)}, u32[]{:S(2)}) copy-start(f32[16,24,128]{2,1,0:T(8,128)} %stiff.9) | copy-start | bytes 589828
  53.5 11.4 %collective-permute-start.9 = (f32[10,24,128]{2,1,0:T(8,128)S(1)}, f32[10,24,128]{2,1,0:T(8,128)S(1)}, u32[]{:S(2)}, u32[]{:S(2)}) collective-permute-start(f32[10,24,128]{2,1,0:T(8,128)S(1)} %get-tuple-element.68), channel_id=1, source_target_pairs={{1,2},{2,1},{3,4},{4,3},{5,6},{6,5},{9,10},{10,9},{11,12},{12,11},... | collective-permute-start | bytes 368648 | tf_op jit(solution)/shard_map/ppermute | solution.py:458
  56.2 8.7 %collective-permute-start.7 = (f32[20,8,128]{2,1,0:T(8,128)S(1)}, f32[20,8,128]{2,1,0:T(8,128)S(1)}, u32[]{:S(2)}, u32[]{:S(2)}) collective-permute-start(f32[20,8,128]{2,1,0:T(8,128)S(1)} %get-tuple-element.66), channel_id=1, source_target_pairs={{32,64},{64,32},{96,128},{128,96},{160,192},{192,160},{224,256},{2... | collective-permute-start | bytes 245768 | tf_op jit(solution)/shard_map/ppermute | solution.py:458
  56.9 8.0 %collective-permute-start.8 = (f32[20,8,128]{2,1,0:T(8,128)S(1)}, f32[20,8,128]{2,1,0:T(8,128)S(1)}, u32[]{:S(2)}, u32[]{:S(2)}) collective-permute-start(f32[20,8,128]{2,1,0:T(8,128)S(1)} %get-tuple-element.67), channel_id=1, source_target_pairs={{0,32},{32,0},{64,96},{96,64},{128,160},{160,128},{192,224},{224,1... | collective-permute-start | bytes 245768 | tf_op jit(solution)/shard_map/ppermute | solution.py:458
  65.5 12.3 %collective-permute-start.12 = (f32[9,24,128]{2,1,0:T(8,128)S(1)}, f32[9,24,128]{2,1,0:T(8,128)S(1)}, u32[]{:S(2)}, u32[]{:S(2)}) collective-permute-start(f32[9,24,128]{2,1,0:T(8,128)S(1)} %get-tuple-element.78), channel_id=1, source_target_pairs={{1,2},{2,1},{3,4},{4,3},{5,6},{6,5},{9,10},{10,9},{11,12},{12,11},... | collective-permute-start | bytes 331784 | tf_op jit(solution)/shard_map/ppermute | solution.py:458
  69.7 8.2 %collective-permute-start.10 = (f32[18,8,128]{2,1,0:T(8,128)S(1)}, f32[18,8,128]{2,1,0:T(8,128)S(1)}, u32[]{:S(2)}, u32[]{:S(2)}) collective-permute-start(f32[18,8,128]{2,1,0:T(8,128)S(1)} %get-tuple-element.76), channel_id=1, source_target_pairs={{32,64},{64,32},{96,128},{128,96},{160,192},{192,160},{224,256},{2... | collective-permute-start | bytes 221192 | tf_op jit(solution)/shard_map/ppermute | solution.py:458
  70.3 7.6 %collective-permute-start.11 = (f32[18,8,128]{2,1,0:T(8,128)S(1)}, f32[18,8,128]{2,1,0:T(8,128)S(1)}, u32[]{:S(2)}, u32[]{:S(2)}) collective-permute-start(f32[18,8,128]{2,1,0:T(8,128)S(1)} %get-tuple-element.77), channel_id=1, source_target_pairs={{0,32},{32,0},{64,96},{96,64},{128,160},{160,128},{192,224},{224,1... | collective-permute-start | bytes 221192 | tf_op jit(solution)/shard_map/ppermute | solution.py:458
  78.5 13.0 %collective-permute-start.15 = (f32[8,24,128]{2,1,0:T(8,128)S(1)}, f32[8,24,128]{2,1,0:T(8,128)S(1)}, u32[]{:S(2)}, u32[]{:S(2)}) collective-permute-start(f32[8,24,128]{2,1,0:T(8,128)S(1)} %get-tuple-element.87), channel_id=1, source_target_pairs={{1,2},{2,1},{3,4},{4,3},{5,6},{6,5},{9,10},{10,9},{11,12},{12,11},... | collective-permute-start | bytes 294920 | tf_op jit(solution)/shard_map/ppermute | solution.py:458
  82.6 8.9 %collective-permute-start.13 = (f32[16,8,128]{2,1,0:T(8,128)S(1)}, f32[16,8,128]{2,1,0:T(8,128)S(1)}, u32[]{:S(2)}, u32[]{:S(2)}) collective-permute-start(f32[16,8,128]{2,1,0:T(8,128)S(1)} %get-tuple-element.85), channel_id=1, source_target_pairs={{32,64},{64,32},{96,128},{128,96},{160,192},{192,160},{224,256},{2... | collective-permute-start | bytes 196616 | tf_op jit(solution)/shard_map/ppermute | solution.py:458
  83.2 8.2 %collective-permute-start.14 = (f32[16,8,128]{2,1,0:T(8,128)S(1)}, f32[16,8,128]{2,1,0:T(8,128)S(1)}, u32[]{:S(2)}, u32[]{:S(2)}) collective-permute-start(f32[16,8,128]{2,1,0:T(8,128)S(1)} %get-tuple-element.86), channel_id=1, source_target_pairs={{0,32},{32,0},{64,96},{96,64},{128,160},{160,128},{192,224},{224,1... | collective-permute-start | bytes 196616 | tf_op jit(solution)/shard_map/ppermute | solution.py:458

commit v12 on v11

--- a/solution.py
+++ b/solution.py
@@ -532,13 +532,13 @@
         last = step == STEPS - 1
         own = call(
             own_kernel,
-            [block] if last else [block, block],
+            [block, block],
             [wave, side, band_high, band_low],
             scratch=[pltpu.VMEM((depth * rows, 2 * LANES), F32)],
         )
         faces = exchange(faces)
         ins = [*faces[::-1], wave, side, older, older_side, stiffness, stiff_side, forward_wave,
-               *own]
+               *(own[:1] if last else own)]
         outs = [block, block]
         if step:
             ins += [planes, image]

time: 94 us -> 95 us (1.011)
  Pallas kernels: 9.87 us -> 10.9 us
    pallas_call x11, Pallas kernels: 9.87 us -> 10.9 us  [call(): pl.pallas_call(body, out_shape=outs, in_specs=in_specs or [vmem()] * len(...]
  transfers between devices with their start and end apart: 17 -> 17, of which waited for: 1 -> 1; matrix products, arithmetic and copies ran while one was open for 0% -> 0% of each run, Pallas kernels for 5% -> 6%
where the time goes in v12:
time: 95 us; the launch traced here: 93.5 us
  starting transfers between devices  62.4 us (66%)
  blocking collectives  17.9 us (19%)
  Pallas kernels  10.9 us (11%)
  between operations  1.59 us (2%)
    ppermute x13, starting transfers between devices, swap(): return lax.ppermute(block, axis, pairs)  39 us
    all_to_all x1, starting transfers between devices, on_device(): packets = lax.all_to_all(packets, ('gx', 'gy'), 0, 0, tiled=True)  19.6 us
    all_gather x5, blocking collectives, pair_gather(): lax.all_gather(block, axis, axis=0, tiled=False, axis_index_groups=groups)  17.9 us
    pallas_call x11, Pallas kernels, call(): pl.pallas_call(body, out_shape=outs, in_specs=in_specs or [vmem()] * len(...  10.9 us
    ppermute x3, starting transfers between devices, on_device(): lax.ppermute(packets, 'gz', [(chip + core, core) for core in range(cores)])  3.86 us
  transfers between devices with their start and end apart: 17, of which 1 were waited for; matrix products, arithmetic and copies ran while one was open for 0% of the time, Pallas kernels for 6%

profile of v12, /device:TPU:1, one launch (start us, length us, event | category | flops | bytes accessed | tf_op | source)
XLA Modules:
  0.0 93.5 jit_solution(9463135262642877965)
XLA Ops:
  0.6 2.3 %shard_map.121 = (f32[64,128]{1,0:T(8,128)}, f32[10,24,128]{2,1,0:T(8,128)}, f32[10,24,128]{2,1,0:T(8,128)}) custom-call(f32[4,128]{1,0:T(4,128)} %residuals.1, s32[1,128]{1,0:T(1,128)} %bitcast.23, s32[1,128]{1,0:T(1,128)} %bitcast.24, f32[16,24,128]{2,1,0:T(8,128)} %older.5, f32[16,24,128]{2,1,0:T(8,128)} %older.4, f32[16,24,128]{2,1,0:T(8,128)} %stiff.9), custom_call_target="tpu_custom_call" | custom-call | flops 1000000 | bytes 2000000 | tf_op jit(solution)/shard_map/pallas_call | solution.py:63
  3.6 19.6 %all-to-all-start = ((f32[64,1,128]{2,1,0:T(1,128)}), f32[64,1,128]{2,1,0:T(1,128)S(1)}, u32[]{:S(2)}, u32[]{:S(2)}) async-start(f32[64,1,128]{2,1,0:T(1,128)} %bitcast.22), calls=%async_computation | async-start | bytes 65536 | tf_op jit(solution)/shard_map/all_to_all | solution.py:503
  23.1 9.7 %all-gather = f32[20,24,128]{2,1,0:T(8,128)S(1)} all-gather(f32[10,24,128]{2,1,0:T(8,128)} %get-tuple-element.51), channel_id=2, replica_groups={{0,8},{16,24},{1,9},{17,25},{2,10},{18,26},{3,11},{19,27},{4,12},{20,28..., dimensions={0}, use_global_device_ids=true | all-gather | bytes 368640 | tf_op jit(solution)/shard_map/all_gather | solution.py:467
  33.9 1.3 %collective-permute-start.4 = (f32[64,128]{1,0:T(8,128)S(1)}, f32[64,128]{1,0:T(8,128)S(1)}, u32[]{:S(2)}, u32[]{:S(2)}) collective-permute-start(f32[64,128]{1,0:T(8,128)S(1)} %bitcast.18), channel_id=1, source_target_pairs={{2,0},{3,1},{10,8},{11,9},{18,16},{19,17},{26,24},{27,25},{34,32},... | collective-permute-start | bytes 98312 | tf_op jit(solution)/shard_map/ppermute | solution.py:514
  35.2 1.3 %collective-permute-start.5 = (f32[64,128]{1,0:T(8,128)S(1)}, f32[64,128]{1,0:T(8,128)S(1)}, u32[]{:S(2)}, u32[]{:S(2)}) collective-permute-start(f32[64,128]{1,0:T(8,128)S(1)} %bitcast.19), channel_id=1, source_target_pairs={{4,0},{5,1},{12,8},{13,9},{20,16},{21,17},{28,24},{29,25},{36,32},... | collective-permute-start | bytes 98312 | tf_op jit(solution)/shard_map/ppermute | solution.py:514
  36.5 1.3 %collective-permute-start.6 = (f32[64,128]{1,0:T(8,128)S(1)}, f32[64,128]{1,0:T(8,128)S(1)}, u32[]{:S(2)}, u32[]{:S(2)}) collective-permute-start(f32[64,128]{1,0:T(8,128)S(1)} %bitcast.20), channel_id=1, source_target_pairs={{6,0},{7,1},{14,8},{15,9},{22,16},{23,17},{30,24},{31,25},{38,32},... | collective-permute-start | bytes 98312 | tf_op jit(solution)/shard_map/ppermute | solution.py:514
  37.8 5.3 %collective-permute-start.3 = (f32[12,24,128]{2,1,0:T(8,128)S(1)}, f32[12,24,128]{2,1,0:T(8,128)S(1)}, u32[]{:S(2)}, u32[]{:S(2)}) collective-permute-start(f32[12,24,128]{2,1,0:T(8,128)S(1)} %get-tuple-element.59), channel_id=1, source_target_pairs={{1,2},{2,1},{3,4},{4,3},{5,6},{6,5},{9,10},{10,9},{11,12},{12,11},... | collective-permute-start | bytes 442376 | tf_op jit(solution)/shard_map/ppermute | solution.py:458
  43.8 0.9 shard_map.124
  44.7 4.7 %collective-permute-start.2 = (f32[24,8,128]{2,1,0:T(8,128)S(1)}, f32[24,8,128]{2,1,0:T(8,128)S(1)}, u32[]{:S(2)}, u32[]{:S(2)}) collective-permute-start(f32[24,8,128]{2,1,0:T(8,128)S(1)} %get-tuple-element.58), channel_id=1, source_target_pairs={{0,32},{32,0},{64,96},{96,64},{128,160},{160,128},{192,224},{224,1... | collective-permute-start | bytes 294920 | tf_op jit(solution)/shard_map/ppermute | solution.py:458
  49.4 1.0 %shard_map.123 = f32[20,24,128]{2,1,0:T(8,128)S(1)} custom-call(f32[12,24,128]{2,1,0:T(8,128)S(1)} %get-tuple-element.60.z_even, f32[64,128]{1,0:T(8,128)S(1)} %bitcast.21, f32[64,128]{1,0:T(8,128)S(1)} %collective-permute-done.4.refs_1_, f32[64,128]{1,0:T(8,128)S(1)} %collective-permute-done.5.refs_2_, f32[64,128]{1,0:T(8,128)S(1)} %collective-permute-done.6.refs_3_), custom_call_target="tpu_custom_call" | custom-call | flops 1000000 | bytes 2000000 | tf_op jit(solution)/shard_map/pallas_call | solution.py:63
  50.5 2.3 %all-gather.1 = f32[40,24,128]{2,1,0:T(8,128)S(1)} all-gather(f32[20,24,128]{2,1,0:T(8,128)S(1)} %shard_map.123), channel_id=3, replica_groups={{0,1},{2,3},{4,5},{6,7},{8,9},{10,11},{12,13},{14,15},{16,17},{18,19},{..., dimensions={0}, use_global_device_ids=true | all-gather | bytes 737280 | tf_op jit(solution)/shard_map/all_gather | solution.py:467
  53.5 2.7 %collective-permute-start.9 = (f32[10,24,128]{2,1,0:T(8,128)S(1)}, f32[10,24,128]{2,1,0:T(8,128)S(1)}, u32[]{:S(2)}, u32[]{:S(2)}) collective-permute-start(f32[10,24,128]{2,1,0:T(8,128)S(1)} %get-tuple-element.69), channel_id=1, source_target_pairs={{1,2},{2,1},{3,4},{4,3},{5,6},{6,5},{9,10},{10,9},{11,12},{12,11},... | collective-permute-start | bytes 368648 | tf_op jit(solution)/shard_map/ppermute | solution.py:458
  56.9 5.1 %collective-permute-start.8 = (f32[20,8,128]{2,1,0:T(8,128)S(1)}, f32[20,8,128]{2,1,0:T(8,128)S(1)}, u32[]{:S(2)}, u32[]{:S(2)}) collective-permute-start(f32[20,8,128]{2,1,0:T(8,128)S(1)} %get-tuple-element.68), channel_id=1, source_target_pairs={{0,32},{32,0},{64,96},{96,64},{128,160},{160,128},{192,224},{224,1... | collective-permute-start | bytes 245768 | tf_op jit(solution)/shard_map/ppermute | solution.py:458
  62.0 0.9 shard_map.126
  62.9 2.0 %all-gather.2 = f32[20,24,128]{2,1,0:T(8,128)S(1)} all-gather(f32[10,24,128]{2,1,0:T(8,128)S(1)} %get-tuple-element.70), channel_id=4, replica_groups={{0,1},{2,3},{4,5},{6,7},{8,9},{10,11},{12,13},{14,15},{16,17},{18,19},{..., dimensions={0}, use_global_device_ids=true | all-gather | bytes 368640 | tf_op jit(solution)/shard_map/all_gather | solution.py:467
  65.6 4.1 %collective-permute-start.12 = (f32[9,24,128]{2,1,0:T(8,128)S(1)}, f32[9,24,128]{2,1,0:T(8,128)S(1)}, u32[]{:S(2)}, u32[]{:S(2)}) collective-permute-start(f32[9,24,128]{2,1,0:T(8,128)S(1)} %get-tuple-element.79), channel_id=1, source_target_pairs={{1,2},{2,1},{3,4},{4,3},{5,6},{6,5},{9,10},{10,9},{11,12},{12,11},... | collective-permute-start | bytes 331784 | tf_op jit(solution)/shard_map/ppermute | solution.py:458
  70.3 4.6 %collective-permute-start.11 = (f32[18,8,128]{2,1,0:T(8,128)S(1)}, f32[18,8,128]{2,1,0:T(8,128)S(1)}, u32[]{:S(2)}, u32[]{:S(2)}) collective-permute-start(f32[18,8,128]{2,1,0:T(8,128)S(1)} %get-tuple-element.78), channel_id=1, source_target_pairs={{0,32},{32,0},{64,96},{96,64},{128,160},{160,128},{192,224},{224,1... | collective-permute-start | bytes 221192 | tf_op jit(solution)/shard_map/ppermute | solution.py:458
  75.0 0.9 shard_map.128
  75.9 2.0 %all-gather.3 = f32[18,24,128]{2,1,0:T(8,128)S(1)} all-gather(f32[9,24,128]{2,1,0:T(8,128)S(1)} %get-tuple-element.80), channel_id=5, replica_groups={{0,1},{2,3},{4,5},{6,7},{8,9},{10,11},{12,13},{14,15},{16,17},{18,19},{..., dimensions={0}, use_global_device_ids=true | all-gather | bytes 331776 | tf_op jit(solution)/shard_map/all_gather | solution.py:467
  78.5 4.1 %collective-permute-start.15 = (f32[8,24,128]{2,1,0:T(8,128)S(1)}, f32[8,24,128]{2,1,0:T(8,128)S(1)}, u32[]{:S(2)}, u32[]{:S(2)}) collective-permute-start(f32[8,24,128]{2,1,0:T(8,128)S(1)} %get-tuple-element.88), channel_id=1, source_target_pairs={{1,2},{2,1},{3,4},{4,3},{5,6},{6,5},{9,10},{10,9},{11,12},{12,11},... | collective-permute-start | bytes 294920 | tf_op jit(solution)/shard_map/ppermute | solution.py:458
  83.2 5.1 %collective-permute-start.14 = (f32[16,8,128]{2,1,0:T(8,128)S(1)}, f32[16,8,128]{2,1,0:T(8,128)S(1)}, u32[]{:S(2)}, u32[]{:S(2)}) collective-permute-start(f32[16,8,128]{2,1,0:T(8,128)S(1)} %get-tuple-element.87), channel_id=1, source_target_pairs={{0,32},{32,0},{64,96},{96,64},{128,160},{160,128},{192,224},{224,1... | collective-permute-start | bytes 196616 | tf_op jit(solution)/shard_map/ppermute | solution.py:458
  89.0 1.6 %shard_map.130 = (f32[16,24,128]{2,1,0:T(8,128)S(1)}, f32[16,24,128]{2,1,0:T(8,128)}) custom-call(f32[16,24,128]{2,1,0:T(8,128)S(1)} %get-tuple-element.90.wave, f32[16,24,128]{2,1,0:T(8,128)S(1)} %get-tuple-element.91.side, bf16[256,256]{1,0:T(8,128)(2,1)S(1)} %copy-done.3, bf16[256,256]{1,0:T(8,128)(2,1)S(1)} %copy-done.4), custom_call_target="tpu_custom_call" | custom-call | flops 1000000 | bytes 2000000 | tf_op jit(solution)/shard_map/pallas_call | solution.py:63
  90.6 1.9 %all-gather.4 = f32[16,24,128]{2,1,0:T(8,128)S(1)} all-gather(f32[8,24,128]{2,1,0:T(8,128)S(1)} %get-tuple-element.89), channel_id=6, replica_groups={{0,1},{2,3},{4,5},{6,7},{8,9},{10,11},{12,13},{14,15},{16,17},{18,19},{..., dimensions={0}, use_global_device_ids=true | all-gather | bytes 294912 | tf_op jit(solution)/shard_map/all_gather | solution.py:467
  92.5 1.0 %shard_map.131 = (f32[16,24,128]{2,1,0:T(8,128)}, f32[16,24,128]{2,1,0:T(8,128)}, f32[16,24,128]{2,1,0:T(8,128)}) custom-call(f32[16,8,128]{2,1,0:T(8,128)S(1)} %collective-permute-done.13.x_odd_in, f32[16,8,128]{2,1,0:T(8,128)S(1)} %collective-permute-done.14.x_even_in, f32[8,24,128]{2,1,0:T(8,128)S(1)} %collective-permute-done.15.z_odd_in, ...), custom_call_target="tpu_custom_call" | custom-call | flops 1000000 | bytes 2000000 | tf_op jit(solution)/shard_map/pallas_call | solution.py:63
  (38 shorter events, 6.3 us)
Async XLA Ops:
  2.9 29.9 %collective-permute-start = (f32[10,24,128]{2,1,0:T(8,128)}, f32[10,24,128]{2,1,0:T(8,128)S(1)}, u32[]{:S(2)}, u32[]{:S(2)}) collective-permute-start(f32[10,24,128]{2,1,0:T(8,128)} %get-tuple-element.52), channel_id=1, source_target_pairs={{8,16},{16,8},{9,17},{17,9},{10,18},{18,10},{11,19},{19,11},{12,20... | collective-permute-start | bytes 368648 | tf_op jit(solution)/shard_map/ppermute | solution.py:458
  3.6 30.4 %all-to-all-start = ((f32[64,1,128]{2,1,0:T(1,128)}), f32[64,1,128]{2,1,0:T(1,128)S(1)}, u32[]{:S(2)}, u32[]{:S(2)}) async-start(f32[64,1,128]{2,1,0:T(1,128)} %bitcast.22), calls=%async_computation | async-start | bytes 65536 | tf_op jit(solution)/shard_map/all_to_all | solution.py:503
  23.1 9.7 %copy-start.1 = (f32[16,24,128]{2,1,0:T(8,128)S(1)}, f32[16,24,128]{2,1,0:T(8,128)}, u32[]{:S(2)}) copy-start(f32[16,24,128]{2,1,0:T(8,128)} %older.5) | copy-start | bytes 589828
  32.8 10.9 %copy-start.3 = (bf16[256,256]{1,0:T(8,128)(2,1)S(1)}, bf16[256,256]{1,0:T(8,128)(2,1)}, u32[]{:S(2)}) copy-start(bf16[256,256]{1,0:T(8,128)(2,1)} %constant.4.clone.band_high) | copy-start | bytes 393220
  32.8 10.9 %copy-start.4 = (bf16[256,256]{1,0:T(8,128)(2,1)S(1)}, bf16[256,256]{1,0:T(8,128)(2,1)}, u32[]{:S(2)}) copy-start(bf16[256,256]{1,0:T(8,128)(2,1)} %constant.5.clone.band_low) | copy-start | bytes 393220
  33.9 10.8 %collective-permute-start.4 = (f32[64,128]{1,0:T(8,128)S(1)}, f32[64,128]{1,0:T(8,128)S(1)}, u32[]{:S(2)}, u32[]{:S(2)}) collective-permute-start(f32[64,128]{1,0:T(8,128)S(1)} %bitcast.18), channel_id=1, source_target_pairs={{2,0},{3,1},{10,8},{11,9},{18,16},{19,17},{26,24},{27,25},{34,32},... | collective-permute-start | bytes 98312 | tf_op jit(solution)/shard_map/ppermute | solution.py:514
  35.2 14.2 %collective-permute-start.5 = (f32[64,128]{1,0:T(8,128)S(1)}, f32[64,128]{1,0:T(8,128)S(1)}, u32[]{:S(2)}, u32[]{:S(2)}) collective-permute-start(f32[64,128]{1,0:T(8,128)S(1)} %bitcast.19), channel_id=1, source_target_pairs={{4,0},{5,1},{12,8},{13,9},{20,16},{21,17},{28,24},{29,25},{36,32},... | collective-permute-start | bytes 98312 | tf_op jit(solution)/shard_map/ppermute | solution.py:514
  36.5 12.9 %collective-permute-start.6 = (f32[64,128]{1,0:T(8,128)S(1)}, f32[64,128]{1,0:T(8,128)S(1)}, u32[]{:S(2)}, u32[]{:S(2)}) collective-permute-start(f32[64,128]{1,0:T(8,128)S(1)} %bitcast.20), channel_id=1, source_target_pairs={{6,0},{7,1},{14,8},{15,9},{22,16},{23,17},{30,24},{31,25},{38,32},... | collective-permute-start | bytes 98312 | tf_op jit(solution)/shard_map/ppermute | solution.py:514
  37.8 15.0 %collective-permute-start.3 = (f32[12,24,128]{2,1,0:T(8,128)S(1)}, f32[12,24,128]{2,1,0:T(8,128)S(1)}, u32[]{:S(2)}, u32[]{:S(2)}) collective-permute-start(f32[12,24,128]{2,1,0:T(8,128)S(1)} %get-tuple-element.59), channel_id=1, source_target_pairs={{1,2},{2,1},{3,4},{4,3},{5,6},{6,5},{9,10},{10,9},{11,12},{12,11},... | collective-permute-start | bytes 442376 | tf_op jit(solution)/shard_map/ppermute | solution.py:458
  43.1 9.7 %collective-permute-start.1 = (f32[24,8,128]{2,1,0:T(8,128)S(1)}, f32[24,8,128]{2,1,0:T(8,128)S(1)}, u32[]{:S(2)}, u32[]{:S(2)}) collective-permute-start(f32[24,8,128]{2,1,0:T(8,128)S(1)} %get-tuple-element.57), channel_id=1, source_target_pairs={{32,64},{64,32},{96,128},{128,96},{160,192},{192,160},{224,256},{2... | collective-permute-start | bytes 294920 | tf_op jit(solution)/shard_map/ppermute | solution.py:458
  44.7 8.1 %collective-permute-start.2 = (f32[24,8,128]{2,1,0:T(8,128)S(1)}, f32[24,8,128]{2,1,0:T(8,128)S(1)}, u32[]{:S(2)}, u32[]{:S(2)}) collective-permute-start(f32[24,8,128]{2,1,0:T(8,128)S(1)} %get-tuple-element.58), channel_id=1, source_target_pairs={{0,32},{32,0},{64,96},{96,64},{128,160},{160,128},{192,224},{224,1... | collective-permute-start | bytes 294920 | tf_op jit(solution)/shard_map/ppermute | solution.py:458
  49.4 3.4 %copy-start.5 = (f32[16,24,128]{2,1,0:T(8,128)S(1)}, f32[16,24,128]{2,1,0:T(8,128)}, u32[]{:S(2)}) copy-start(f32[16,24,128]{2,1,0:T(8,128)} %older.4) | copy-start | bytes 589828
  50.5 2.3 %copy-start = (bf16[4,16,24,128]{3,2,1,0:T(8,128)(2,1)S(1)}, bf16[4,16,24,128]{3,2,1,0:T(8,128)(2,1)}, u32[]{:S(2)}) copy-start(bf16[4,16,24,128]{3,2,1,0:T(8,128)(2,1)} %forward.7) | copy-start | bytes 1179652
  50.5 2.3 %copy-start.2 = (f32[16,24,128]{2,1,0:T(8,128)S(1)}, f32[16,24,128]{2,1,0:T(8,128)}, u32[]{:S(2)}) copy-start(f32[16,24,128]{2,1,0:T(8,128)} %stiff.9) | copy-start | bytes 589828
  53.5 11.4 %collective-permute-start.9 = (f32[10,24,128]{2,1,0:T(8,128)S(1)}, f32[10,24,128]{2,1,0:T(8,128)S(1)}, u32[]{:S(2)}, u32[]{:S(2)}) collective-permute-start(f32[10,24,128]{2,1,0:T(8,128)S(1)} %get-tuple-element.69), channel_id=1, source_target_pairs={{1,2},{2,1},{3,4},{4,3},{5,6},{6,5},{9,10},{10,9},{11,12},{12,11},... | collective-permute-start | bytes 368648 | tf_op jit(solution)/shard_map/ppermute | solution.py:458
  56.2 8.7 %collective-permute-start.7 = (f32[20,8,128]{2,1,0:T(8,128)S(1)}, f32[20,8,128]{2,1,0:T(8,128)S(1)}, u32[]{:S(2)}, u32[]{:S(2)}) collective-permute-start(f32[20,8,128]{2,1,0:T(8,128)S(1)} %get-tuple-element.67), channel_id=1, source_target_pairs={{32,64},{64,32},{96,128},{128,96},{160,192},{192,160},{224,256},{2... | collective-permute-start | bytes 245768 | tf_op jit(solution)/shard_map/ppermute | solution.py:458
  56.9 8.0 %collective-permute-start.8 = (f32[20,8,128]{2,1,0:T(8,128)S(1)}, f32[20,8,128]{2,1,0:T(8,128)S(1)}, u32[]{:S(2)}, u32[]{:S(2)}) collective-permute-start(f32[20,8,128]{2,1,0:T(8,128)S(1)} %get-tuple-element.68), channel_id=1, source_target_pairs={{0,32},{32,0},{64,96},{96,64},{128,160},{160,128},{192,224},{224,1... | collective-permute-start | bytes 245768 | tf_op jit(solution)/shard_map/ppermute | solution.py:458
  65.6 12.3 %collective-permute-start.12 = (f32[9,24,128]{2,1,0:T(8,128)S(1)}, f32[9,24,128]{2,1,0:T(8,128)S(1)}, u32[]{:S(2)}, u32[]{:S(2)}) collective-permute-start(f32[9,24,128]{2,1,0:T(8,128)S(1)} %get-tuple-element.79), channel_id=1, source_target_pairs={{1,2},{2,1},{3,4},{4,3},{5,6},{6,5},{9,10},{10,9},{11,12},{12,11},... | collective-permute-start | bytes 331784 | tf_op jit(solution)/shard_map/ppermute | solution.py:458
  69.7 8.2 %collective-permute-start.10 = (f32[18,8,128]{2,1,0:T(8,128)S(1)}, f32[18,8,128]{2,1,0:T(8,128)S(1)}, u32[]{:S(2)}, u32[]{:S(2)}) collective-permute-start(f32[18,8,128]{2,1,0:T(8,128)S(1)} %get-tuple-element.77), channel_id=1, source_target_pairs={{32,64},{64,32},{96,128},{128,96},{160,192},{192,160},{224,256},{2... | collective-permute-start | bytes 221192 | tf_op jit(solution)/shard_map/ppermute | solution.py:458
  70.3 7.6 %collective-permute-start.11 = (f32[18,8,128]{2,1,0:T(8,128)S(1)}, f32[18,8,128]{2,1,0:T(8,128)S(1)}, u32[]{:S(2)}, u32[]{:S(2)}) collective-permute-start(f32[18,8,128]{2,1,0:T(8,128)S(1)} %get-tuple-element.78), channel_id=1, source_target_pairs={{0,32},{32,0},{64,96},{96,64},{128,160},{160,128},{192,224},{224,1... | collective-permute-start | bytes 221192 | tf_op jit(solution)/shard_map/ppermute | solution.py:458
  78.5 14.0 %collective-permute-start.15 = (f32[8,24,128]{2,1,0:T(8,128)S(1)}, f32[8,24,128]{2,1,0:T(8,128)S(1)}, u32[]{:S(2)}, u32[]{:S(2)}) collective-permute-start(f32[8,24,128]{2,1,0:T(8,128)S(1)} %get-tuple-element.88), channel_id=1, source_target_pairs={{1,2},{2,1},{3,4},{4,3},{5,6},{6,5},{9,10},{10,9},{11,12},{12,11},... | collective-permute-start | bytes 294920 | tf_op jit(solution)/shard_map/ppermute | solution.py:458
  82.6 9.9 %collective-permute-start.13 = (f32[16,8,128]{2,1,0:T(8,128)S(1)}, f32[16,8,128]{2,1,0:T(8,128)S(1)}, u32[]{:S(2)}, u32[]{:S(2)}) collective-permute-start(f32[16,8,128]{2,1,0:T(8,128)S(1)} %get-tuple-element.86), channel_id=1, source_target_pairs={{32,64},{64,32},{96,128},{128,96},{160,192},{192,160},{224,256},{2... | collective-permute-start | bytes 196616 | tf_op jit(solution)/shard_map/ppermute | solution.py:458
  83.2 9.3 %collective-permute-start.14 = (f32[16,8,128]{2,1,0:T(8,128)S(1)}, f32[16,8,128]{2,1,0:T(8,128)S(1)}, u32[]{:S(2)}, u32[]{:S(2)}) collective-permute-start(f32[16,8,128]{2,1,0:T(8,128)S(1)} %get-tuple-element.87), channel_id=1, source_target_pairs={{0,32},{32,0},{64,96},{96,64},{128,160},{160,128},{192,224},{224,1... | collective-permute-start | bytes 196616 | tf_op jit(solution)/shard_map/ppermute | solution.py:458
